TPU v7x, 32 devices: a whole 2x2x4 slice. The times are simulated.
32 devices in a mesh: dp: 2 (over core), fsdp: 16 (over z, y, x).
Axes of the slice: x: 2, y: 2, z: 4, core: 2. Of those that a mesh axis runs over, the one named last changes fastest.
Arguments:
- patches: bfloat16 [64, 4, 117, 128], P(('dp', 'fsdp')), may hold values from -6 to 6
- prompts: bfloat16 [8, 10, 128], replicated, may hold values from -6 to 6
- cls_token: bfloat16 [128], replicated, may hold values from -6 to 6
- attention_input_weights: bfloat16 [2, 2, 128, 384], P(None, None, 'fsdp'), may hold values from -0.5 to 0.5
- attention_output_weights: bfloat16 [2, 2, 128, 128], P(None, None, 'fsdp'), may hold values from -2 to 2
- feed_input_weights: bfloat16 [2, 128, 1024], P(None, 'fsdp'), may hold values from -0.5 to 0.5
- feed_output_weights: bfloat16 [2, 512, 128], P(None, 'fsdp'), may hold values from -0.25 to 0.25
- token_operator: bfloat16 [2, 128, 128], replicated, may hold values from -0.5 to 0.5
- norm_gains: float32 [2, 4, 128], replicated, may hold values from 0.5 to 1.5
- branch_scales: float32 [2, 4, 128], replicated, may hold values from 0.1 to 1.9
- var_counts: int32 [8], replicated, may hold values from 1 to 4, as said below
- dataset_ids: int32 [64], P(('dp', 'fsdp')), may hold values from 0 to 7
- cotangent: bfloat16 [64, 4, 128, 128], P(('dp', 'fsdp')), may hold values from -40 to 40
- adjust_cotangent: bfloat16 [64, 4, 128, 128], P(('dp', 'fsdp')), may hold values from -40 to 40
Outputs:
- output: bfloat16 [64, 4, 128, 128], P(('dp', 'fsdp'))
- patch_grad: float32 [64, 4, 117, 128], P(('dp', 'fsdp'))
- prompt_grad: float32 [8, 10, 128], replicated
- cls_grad: float32 [128], replicated
- attn_in_grad: float32 [2, 2, 128, 384], P(None, None, 'fsdp')
- attn_out_grad: float32 [2, 2, 128, 128], P(None, None, 'fsdp')
- mix_in_grad: float32 [2, 128, 1024], P(None, 'fsdp')
- mix_out_grad: float32 [2, 512, 128], P(None, 'fsdp')
- token_mix_grad: float32 [2, 128, 128], replicated
- gains_grad: float32 [2, 4, 128], replicated
- scales_grad: float32 [2, 4, 128], replicated
- adjust_prompt_grad: float32 [8, 10, 128], replicated
- adjust_cls_grad: float32 [128], replicated
Inputs may be any that keep to these rules, and one draw needn't show every extreme that they name: `var_counts`: some dataset has exactly 4 variables and another exactly 1.
All inputs are finite; a program needn't handle non-finite values.
Results may differ from a plain program's by a relative error of at most 0.02.
Values may be sent and summed in bfloat16 or wider, within the bound.
No kernel may reach another device: no remote copies, remote signals or barrier semaphores. Data moves between devices by JAX's collectives and lax.ppermute only.
A program may use at most 192 MiB of HBM per device.

v0:
```python
import jax
import jax.numpy as jnp
from jax import lax
from jax.sharding import PartitionSpec as P

HEADS = 8


EPSILON = 1e-05
NEG_FILL = -1000000000.0


def norm_rows(stream, gain_vec):
    centered = stream - jnp.mean(stream, axis=-1, keepdims=True)
    inv_std = lax.rsqrt(jnp.mean(centered * centered, axis=-1, keepdims=True) + EPSILON)
    unit_rows = centered * inv_std
    return (unit_rows * gain_vec, unit_rows, inv_std)


def norm_back(grad_norm, gain_vec, unit_rows, inv_std):
    grad_unit = grad_norm * gain_vec
    grad_gain = jnp.sum(grad_norm * unit_rows, axis=(0, 1, 2))
    first_mean = jnp.mean(grad_unit, axis=-1, keepdims=True)
    second_mean = jnp.mean(grad_unit * unit_rows, axis=-1, keepdims=True)
    return (inv_std * (grad_unit - first_mean - unit_rows * second_mean), grad_gain)


def project(input_rows, weight_matrix):
    return jnp.einsum(
        "mfxu,uz->mfxz", input_rows, weight_matrix, preferred_element_type=jnp.float32
    )


def weight_grad(input_rows, gradient_tree):
    return jnp.einsum(
        "fzak,fzax->kx", input_rows, gradient_tree, preferred_element_type=jnp.float32
    )


def back_project(gradient_tree, weight_matrix):
    return jnp.einsum(
        "sxkc,ac->sxka", gradient_tree, weight_matrix, preferred_element_type=jnp.float32
    )


def heads_of(block):
    return block.reshape(block.shape[:-1] + (HEADS, block.shape[-1] // HEADS))


def thirds(query_key_value_rows):
    model_width = query_key_value_rows.shape[-1] // 3
    return (
        heads_of(query_key_value_rows[..., :model_width]),
        heads_of(query_key_value_rows[..., model_width : 2 * model_width]),
        heads_of(query_key_value_rows[..., 2 * model_width :]),
    )


def head_factor(query_key_value_rows):
    return (query_key_value_rows.shape[-1] // (3 * HEADS)) ** (-0.5)


def joined_heads(grad_query, grad_key, grad_value):
    joined = jnp.concatenate([grad_query, grad_key, grad_value], axis=-2)
    return joined.reshape(joined.shape[:-2] + (-1,)).astype(jnp.bfloat16)


def time_item(qkv_item):
    queries, key_rows, value_rows = thirds(qkv_item)
    scores = jnp.einsum(
        "vqhc,vkhc->vhqk", queries, key_rows, preferred_element_type=jnp.float32
    ) * head_factor(qkv_item)
    row_max = jnp.max(scores, axis=-1, keepdims=True)
    shifted_exp = jnp.exp(scores - row_max)
    row_total = jnp.sum(shifted_exp, axis=-1, keepdims=True)
    attn_prob = (shifted_exp / row_total).astype(jnp.bfloat16)
    mixed_state = jnp.einsum(
        "vhqk,vkhc->vqhc", attn_prob, value_rows, preferred_element_type=jnp.float32
    )
    mixed_state = mixed_state.reshape(mixed_state.shape[:2] + (-1,)).astype(jnp.bfloat16)
    return (mixed_state, (row_max + jnp.log(row_total))[..., 0])


def time_back_item(operands):
    qkv_item, log_total, grad_mixed = operands
    queries, key_rows, value_rows = thirds(qkv_item)
    factor = head_factor(qkv_item)
    scores = (
        jnp.einsum("vqhc,vkhc->vhqk", queries, key_rows, preferred_element_type=jnp.float32)
        * factor
    )
    attn_prob = jnp.exp(scores - log_total[..., None])
    grad_heads = heads_of(grad_mixed)
    grad_prob = jnp.einsum(
        "vqhc,vkhc->vhqk", grad_heads, value_rows, preferred_element_type=jnp.float32
    )
    grad_value = jnp.einsum(
        "vhqk,vqhc->vkhc",
        attn_prob.astype(jnp.bfloat16),
        grad_heads,
        preferred_element_type=jnp.float32,
    )
    grad_score = attn_prob * (grad_prob - jnp.sum(attn_prob * grad_prob, axis=-1, keepdims=True))
    grad_score = grad_score.astype(jnp.bfloat16)
    grad_query = (
        jnp.einsum("vhqk,vkhc->vqhc", grad_score, key_rows, preferred_element_type=jnp.float32)
        * factor
    )
    grad_key = (
        jnp.einsum("vhqk,vqhc->vkhc", grad_score, queries, preferred_element_type=jnp.float32)
        * factor
    )
    return joined_heads(grad_query, grad_key, grad_value)


def var_forward(query_key_value_rows, key_mask):
    queries, key_rows, value_rows = thirds(query_key_value_rows)
    scores = jnp.einsum(
        "bqlhc,bklhc->blhqk", queries, key_rows, preferred_element_type=jnp.float32
    ) * head_factor(query_key_value_rows)
    scores = jnp.where(key_mask[:, None, None, None, :], scores, NEG_FILL)
    attn_prob = jax.nn.softmax(scores, axis=-1)
    mixed_state = jnp.einsum(
        "blhqk,bklhc->bqlhc",
        attn_prob.astype(jnp.bfloat16),
        value_rows,
        preferred_element_type=jnp.float32,
    )
    return (mixed_state.reshape(mixed_state.shape[:3] + (-1,)).astype(jnp.bfloat16), attn_prob)


def var_back(query_key_value_rows, attn_prob, grad_mixed):
    queries, key_rows, value_rows = thirds(query_key_value_rows)
    factor = head_factor(query_key_value_rows)
    grad_heads = heads_of(grad_mixed)
    grad_prob = jnp.einsum(
        "bqlhc,bklhc->blhqk", grad_heads, value_rows, preferred_element_type=jnp.float32
    )
    grad_value = jnp.einsum(
        "blhqk,bqlhc->bklhc",
        attn_prob.astype(jnp.bfloat16),
        grad_heads,
        preferred_element_type=jnp.float32,
    )
    grad_score = attn_prob * (grad_prob - jnp.sum(attn_prob * grad_prob, axis=-1, keepdims=True))
    grad_score = grad_score.astype(jnp.bfloat16)
    grad_query = (
        jnp.einsum("blhqk,bklhc->bqlhc", grad_score, key_rows, preferred_element_type=jnp.float32)
        * factor
    )
    grad_key = (
        jnp.einsum("blhqk,bqlhc->bklhc", grad_score, queries, preferred_element_type=jnp.float32)
        * factor
    )
    return joined_heads(grad_query, grad_key, grad_value)


def layer_forward(stream, weights, token_operator_weight, gain_vec, scale_vec, key_mask):
    w_attn_in, w_attn_out, w_mix_in, down_weight = weights
    first_in = stream
    normalized_rows = norm_rows(stream, gain_vec[0])[0].astype(jnp.bfloat16)
    qkv_time = project(normalized_rows, w_attn_in[0]).astype(jnp.bfloat16)
    mixed_time, log_total = lax.map(time_item, qkv_time)
    branch_time = project(mixed_time, w_attn_out[0])
    stream = stream + scale_vec[0] * branch_time
    second_in = stream
    normalized_rows = norm_rows(stream, gain_vec[1])[0].astype(jnp.bfloat16)
    qkv_var = project(normalized_rows, w_attn_in[1]).astype(jnp.bfloat16)
    mixed_var, prob_var = var_forward(qkv_var, key_mask)
    branch_var = project(mixed_var, w_attn_out[1])
    stream = stream + scale_vec[1] * branch_var
    third_in = stream
    normalized_rows = norm_rows(stream, gain_vec[2])[0].astype(jnp.bfloat16)
    branch_tok = jnp.einsum(
        "xf,pyfi->pyxi", token_operator_weight, normalized_rows, preferred_element_type=jnp.float32
    )
    stream = stream + scale_vec[2] * branch_tok
    fourth_in = stream
    normalized_rows = norm_rows(stream, gain_vec[3])[0].astype(jnp.bfloat16)
    joint_rows = project(normalized_rows, w_mix_in)
    half_width = joint_rows.shape[-1] // 2
    hidden_state = (
        jax.nn.silu(joint_rows[..., :half_width]) * joint_rows[..., half_width:]
    ).astype(jnp.bfloat16)
    branch_feed_mix = jnp.einsum(
        "mkni,ix->mknx", hidden_state, down_weight, preferred_element_type=jnp.float32
    )
    stream = stream + scale_vec[3] * branch_feed_mix
    kept_state = (
        first_in,
        second_in,
        third_in,
        fourth_in,
        qkv_time,
        mixed_time,
        log_total,
        branch_time,
        qkv_var,
        mixed_var,
        prob_var,
        branch_var,
        branch_tok,
        joint_rows,
        branch_feed_mix,
    )
    return (stream, kept_state)


def layer_backward(upstream, kept_state, weights, token_operator_weight, gain_vec, scale_vec, full):
    (
        first_in,
        second_in,
        third_in,
        fourth_in,
        qkv_time,
        mixed_time,
        log_total,
        branch_time,
        qkv_var,
        mixed_var,
        prob_var,
        branch_var,
        branch_tok,
        joint_rows,
        branch_feed_mix,
    ) = kept_state
    w_attn_in, w_attn_out, w_mix_in, down_weight = weights
    axes_rows = (0, 1, 2)
    normalized_rows, unit_rows, inv_std = norm_rows(fourth_in, gain_vec[3])
    normalized_rows = normalized_rows.astype(jnp.bfloat16)
    half_width = joint_rows.shape[-1] // 2
    gate_pre = joint_rows[..., :half_width]
    up_pre = joint_rows[..., half_width:]
    gate_sig = jax.nn.sigmoid(gate_pre)
    gate_act = jax.nn.silu(gate_pre)
    branch_gradient = (scale_vec[3] * upstream).astype(jnp.bfloat16)
    grad_hidden = jnp.einsum(
        "zhim,wm->zhiw", branch_gradient, down_weight, preferred_element_type=jnp.float32
    )
    grad_joint = jnp.concatenate(
        [
            grad_hidden * up_pre * gate_sig * (1.0 + gate_pre * (1.0 - gate_sig)),
            grad_hidden * gate_act,
        ],
        axis=-1,
    ).astype(jnp.bfloat16)
    if full:
        hidden_state = (gate_act * up_pre).astype(jnp.bfloat16)
        scale_mix = jnp.sum(branch_feed_mix * upstream, axis=axes_rows)
        grad_mix_out = jnp.einsum(
            "khup,khuo->po", hidden_state, branch_gradient, preferred_element_type=jnp.float32
        )
        grad_mix_in = weight_grad(normalized_rows, grad_joint)
    returned, gain_mix = norm_back(
        back_project(grad_joint, w_mix_in), gain_vec[3], unit_rows, inv_std
    )
    upstream = upstream + returned
    normalized_rows, unit_rows, inv_std = norm_rows(third_in, gain_vec[2])
    normalized_rows = normalized_rows.astype(jnp.bfloat16)
    branch_gradient = (scale_vec[2] * upstream).astype(jnp.bfloat16)
    if full:
        scale_tok = jnp.sum(branch_tok * upstream, axis=axes_rows)
        grad_token = jnp.einsum(
            "egnh,egoh->no", branch_gradient, normalized_rows, preferred_element_type=jnp.float32
        )
    grad_normed = jnp.einsum(
        "hf,cshg->csfg", token_operator_weight, branch_gradient, preferred_element_type=jnp.float32
    )
    returned, gain_tok = norm_back(grad_normed, gain_vec[2], unit_rows, inv_std)
    upstream = upstream + returned
    normalized_rows, unit_rows, inv_std = norm_rows(second_in, gain_vec[1])
    normalized_rows = normalized_rows.astype(jnp.bfloat16)
    branch_gradient = (scale_vec[1] * upstream).astype(jnp.bfloat16)
    if full:
        scale_var = jnp.sum(branch_var * upstream, axis=axes_rows)
        grad_out_var = weight_grad(mixed_var, branch_gradient)
    grad_mixed = back_project(branch_gradient, w_attn_out[1]).astype(jnp.bfloat16)
    grad_qkv = var_back(qkv_var, prob_var, grad_mixed)
    if full:
        grad_in_var = weight_grad(normalized_rows, grad_qkv)
    returned, gain_var = norm_back(
        back_project(grad_qkv, w_attn_in[1]), gain_vec[1], unit_rows, inv_std
    )
    upstream = upstream + returned
    normalized_rows, unit_rows, inv_std = norm_rows(first_in, gain_vec[0])
    normalized_rows = normalized_rows.astype(jnp.bfloat16)
    branch_gradient = (scale_vec[0] * upstream).astype(jnp.bfloat16)
    if full:
        scale_time = jnp.sum(branch_time * upstream, axis=axes_rows)
        grad_out_time = weight_grad(mixed_time, branch_gradient)
    grad_mixed = back_project(branch_gradient, w_attn_out[0]).astype(jnp.bfloat16)
    grad_qkv = lax.map(time_back_item, (qkv_time, log_total, grad_mixed))
    if full:
        grad_in_time = weight_grad(normalized_rows, grad_qkv)
    returned, gain_time = norm_back(
        back_project(grad_qkv, w_attn_in[0]), gain_vec[0], unit_rows, inv_std
    )
    upstream = upstream + returned
    if not full:
        return (upstream, None, None)
    matrix_grads = (
        jnp.stack([grad_in_time, grad_in_var]),
        jnp.stack([grad_out_time, grad_out_var]),
        grad_mix_in,
        grad_mix_out,
    )
    small_grads = (
        grad_token,
        jnp.stack([gain_time, gain_var, gain_tok, gain_mix]),
        jnp.stack([scale_time, scale_var, scale_tok, scale_mix]),
    )
    return (upstream, matrix_grads, small_grads)


def tower_terms(upstream, chosen_float, prompt_len):
    prompt_part = jnp.sum(upstream[:, :, :prompt_len], axis=1)
    prompt_local = jnp.einsum(
        "bn,bpd->npd", chosen_float, prompt_part, precision=lax.Precision.HIGHEST
    )
    cls_local = jnp.sum(upstream[:, :, -1], axis=(0, 1))
    return (prompt_local, cls_local)


def per_device(
    patches,
    prompts,
    cls_token,
    attention_input_weights,
    attention_output_weights,
    feed_input_weights,
    feed_output_weights,
    token_operator,
    norm_gains,
    branch_scales,
    var_counts,
    dataset_ids,
    cotangent,
    adjust_cotangent,
):
    item_count, var_slots, patch_len, model_width = patches.shape
    data_count, prompt_len, _ = prompts.shape
    layer_count = attention_input_weights.shape[0]
    chosen = dataset_ids[:, None] == jnp.arange(data_count, dtype=jnp.int32)[None, :]
    chosen_rows = chosen.astype(jnp.bfloat16)
    counts_item = jnp.sum(jnp.where(chosen, var_counts[None, :], 0), axis=1)
    key_mask = jnp.arange(var_slots, dtype=jnp.int32)[None, :] < counts_item[:, None]
    prompt_rows = jnp.einsum(
        "bn,npd->bpd", chosen_rows, prompts, preferred_element_type=jnp.float32
    )
    prompt_rows = jnp.broadcast_to(
        prompt_rows[:, None], (item_count, var_slots, prompt_len, model_width)
    )
    cls_rows = jnp.broadcast_to(
        cls_token.astype(jnp.float32), (item_count, var_slots, 1, model_width)
    )
    stream = jnp.concatenate([prompt_rows, patches.astype(jnp.float32), cls_rows], axis=2)
    gathered = []
    kept_layers = []
    for layer_idx in range(layer_count):
        weights = (
            lax.all_gather(attention_input_weights[layer_idx], "fsdp", axis=1, tiled=True),
            lax.all_gather(attention_output_weights[layer_idx], "fsdp", axis=1, tiled=True),
            lax.all_gather(feed_input_weights[layer_idx], "fsdp", axis=0, tiled=True),
            lax.all_gather(feed_output_weights[layer_idx], "fsdp", axis=0, tiled=True),
        )
        stream, kept_state = layer_forward(
            stream,
            weights,
            token_operator[layer_idx],
            norm_gains[layer_idx],
            branch_scales[layer_idx],
            key_mask,
        )
        gathered.append(weights)
        kept_layers.append(kept_state)
    output = stream.astype(jnp.bfloat16)
    upstream = cotangent.astype(jnp.float32)
    adjust_upstream = adjust_cotangent.astype(jnp.float32)
    owned_layers = [None] * layer_count
    small_layers = [None] * layer_count
    for layer_idx in range(layer_count - 1, -1, -1):
        weights = (
            lax.all_gather(attention_input_weights[layer_idx], "fsdp", axis=1, tiled=True),
            lax.all_gather(attention_output_weights[layer_idx], "fsdp", axis=1, tiled=True),
            lax.all_gather(feed_input_weights[layer_idx], "fsdp", axis=0, tiled=True),
            lax.all_gather(feed_output_weights[layer_idx], "fsdp", axis=0, tiled=True),
        )
        upstream, matrix_grads, small_grads = layer_backward(
            upstream,
            kept_layers[layer_idx],
            weights,
            token_operator[layer_idx],
            norm_gains[layer_idx],
            branch_scales[layer_idx],
            True,
        )
        adjust_upstream = layer_backward(
            adjust_upstream,
            kept_layers[layer_idx],
            weights,
            token_operator[layer_idx],
            norm_gains[layer_idx],
            branch_scales[layer_idx],
            False,
        )[0]
        owned = (
            lax.psum_scatter(matrix_grads[0], "fsdp", scatter_dimension=1, tiled=True),
            lax.psum_scatter(matrix_grads[1], "fsdp", scatter_dimension=1, tiled=True),
            lax.psum_scatter(matrix_grads[2], "fsdp", scatter_dimension=0, tiled=True),
            lax.psum_scatter(matrix_grads[3], "fsdp", scatter_dimension=0, tiled=True),
        )
        owned = lax.psum(owned, "dp")
        owned_layers[layer_idx] = owned
        small_layers[layer_idx] = small_grads
    patch_grad = upstream[:, :, prompt_len : prompt_len + patch_len]
    chosen_float = chosen.astype(jnp.float32)
    prompt_local, cls_local = tower_terms(upstream, chosen_float, prompt_len)
    adjust_prompt_local, adjust_cls_local = tower_terms(adjust_upstream, chosen_float, prompt_len)
    token_local = jnp.stack([entry[0] for entry in small_layers])
    gains_local = jnp.stack([entry[1] for entry in small_layers])
    scales_local = jnp.stack([entry[2] for entry in small_layers])
    (
        token_grad,
        gains_grad,
        scales_grad,
        prompt_grad,
        cls_grad,
        adjust_prompt_grad,
        adjust_cls_grad,
    ) = lax.psum(
        (
            token_local,
            gains_local,
            scales_local,
            prompt_local,
            cls_local,
            adjust_prompt_local,
            adjust_cls_local,
        ),
        ("dp", "fsdp"),
    )
    attn_in_grad = jnp.stack([entry[0] for entry in owned_layers])
    attn_out_grad = jnp.stack([entry[1] for entry in owned_layers])
    mix_in_grad = jnp.stack([entry[2] for entry in owned_layers])
    mix_out_grad = jnp.stack([entry[3] for entry in owned_layers])
    return (
        output,
        patch_grad,
        prompt_grad,
        cls_grad,
        attn_in_grad,
        attn_out_grad,
        mix_in_grad,
        mix_out_grad,
        token_grad,
        gains_grad,
        scales_grad,
        adjust_prompt_grad,
        adjust_cls_grad,
    )


def solution(mesh):
    return jax.shard_map(
        per_device,
        mesh=mesh,
        in_specs=(
            P(("dp", "fsdp"), None, None, None),
            P(),
            P(),
            P(None, None, "fsdp", None),
            P(None, None, "fsdp", None),
            P(None, "fsdp", None),
            P(None, "fsdp", None),
            P(),
            P(),
            P(),
            P(),
            P(("dp", "fsdp")),
            P(("dp", "fsdp"), None, None, None),
            P(("dp", "fsdp"), None, None, None),
        ),
        out_specs=(
            P(("dp", "fsdp"), None, None, None),
            P(("dp", "fsdp"), None, None, None),
            P(),
            P(),
            P(None, None, "fsdp", None),
            P(None, None, "fsdp", None),
            P(None, "fsdp", None),
            P(None, "fsdp", None),
            P(),
            P(),
            P(),
            P(),
            P(),
        ),
        check_vma=False,
    )
```

profile of v0, /device:TPU:0, one launch (start us, length us, event | category | flops | bytes accessed | tf_op | source)
XLA Modules:
  0.0 1602.7 jit_solution(8137210346536687448)
XLA Ops:
  11.9 42.7 %all-gather.5 = bf16[1,2,128,128]{3,2,1,0:T(8,128)(2,1)S(1)} all-gather(bf16[1,2,8,128]{3,2,1,0:T(8,128)(2,1)S(1)} %get-tuple-element.511), channel_id=7, replica_groups=mesh['dp'=2,'fsdp'=16] {'fsdp'}, dimensions={2}, use_global_device_ids=true | all-gather | bytes 69632 | tf_op jit(solution)/shard_map/all_gather | solution.py:362
  54.6 35.8 %all-gather.1 = bf16[1,2,128,128]{3,2,1,0:T(8,128)(2,1)S(1)} all-gather(bf16[1,2,8,128]{3,2,1,0:T(8,128)(2,1)S(1)} %get-tuple-element.512), channel_id=3, replica_groups=mesh['dp'=2,'fsdp'=16] {'fsdp'}, dimensions={2}, use_global_device_ids=true | all-gather | bytes 69632 | tf_op jit(solution)/shard_map/all_gather | solution.py:362
  90.4 40.5 %all-gather.7 = bf16[1,512,128]{2,1,0:T(8,128)(2,1)} all-gather(bf16[1,32,128]{2,1,0:T(8,128)(2,1)S(1)} %get-tuple-element.509), channel_id=9, replica_groups=mesh['dp'=2,'fsdp'=16] {'fsdp'}, dimensions={1}, use_global_device_ids=true | all-gather | bytes 139264 | tf_op jit(solution)/shard_map/all_gather | solution.py:364
  130.9 38.5 %all-gather.3 = bf16[1,512,128]{2,1,0:T(8,128)(2,1)} all-gather(bf16[1,32,128]{2,1,0:T(8,128)(2,1)S(1)} %get-tuple-element.510), channel_id=5, replica_groups=mesh['dp'=2,'fsdp'=16] {'fsdp'}, dimensions={1}, use_global_device_ids=true | all-gather | bytes 139264 | tf_op jit(solution)/shard_map/all_gather | solution.py:364
  169.4 38.5 %all-gather.4 = bf16[1,2,128,384]{3,2,1,0:T(8,128)(2,1)S(1)} all-gather(bf16[1,2,8,384]{3,2,1,0:T(8,128)(2,1)S(1)} %get-tuple-element.507), channel_id=6, replica_groups=mesh['dp'=2,'fsdp'=16] {'fsdp'}, dimensions={2}, use_global_device_ids=true | all-gather | bytes 208896 | tf_op jit(solution)/shard_map/all_gather | solution.py:361
  207.9 36.7 %all-gather = bf16[1,2,128,384]{3,2,1,0:T(8,128)(2,1)S(1)} all-gather(bf16[1,2,8,384]{3,2,1,0:T(8,128)(2,1)S(1)} %get-tuple-element.508), channel_id=2, replica_groups=mesh['dp'=2,'fsdp'=16] {'fsdp'}, dimensions={2}, use_global_device_ids=true | all-gather | bytes 208896 | tf_op jit(solution)/shard_map/all_gather | solution.py:361
  244.6 41.2 %all-gather.6 = bf16[1,128,1024]{2,1,0:T(8,128)(2,1)} all-gather(bf16[1,8,1024]{2,1,0:T(8,128)(2,1)S(1)} %get-tuple-element.505), channel_id=8, replica_groups=mesh['dp'=2,'fsdp'=16] {'fsdp'}, dimensions={1}, use_global_device_ids=true | all-gather | bytes 278528 | tf_op jit(solution)/shard_map/all_gather | solution.py:363
  285.8 36.8 %all-gather.2 = bf16[1,128,1024]{2,1,0:T(8,128)(2,1)S(1)} all-gather(bf16[1,8,1024]{2,1,0:T(8,128)(2,1)S(1)} %get-tuple-element.506), channel_id=4, replica_groups=mesh['dp'=2,'fsdp'=16] {'fsdp'}, dimensions={1}, use_global_device_ids=true | all-gather | bytes 278528 | tf_op jit(solution)/shard_map/all_gather | solution.py:363
  326.7 4.6 while.64
  340.2 4.3 copy.228
  347.4 11.8 fusion.167
  364.3 4.3 convert_bitcast_fusion.3
  392.2 4.1 copy.239
  396.3 4.2 copy.240
  400.5 11.9 fusion.168
  421.3 4.4 copy.243
  451.2 4.1 copy.246
  455.3 6.6 convolution_bitcast_fusion.1
  461.9 4.3 fusion.177
  467.8 4.5 copy.289
  472.4 6.5 convert_bitcast_fusion.1
  478.9 13.5 multiply_reduce_fusion.7
  492.4 7.6 multiply_convert_fusion.9
  515.0 4.3 copy.297
  529.2 4.4 copy.253
  533.6 4.2 copy.252
  548.1 11.4 while.68
  562.8 11.2 while.66
  594.1 6.6 convolution_bitcast_fusion
  600.8 4.3 fusion.178
  606.0 4.3 copy.303
  610.3 6.5 convert_bitcast_fusion
  616.7 13.6 multiply_reduce_fusion.6
  630.3 7.6 multiply_convert_fusion.6
  653.0 4.3 copy.311
  659.9 4.3 copy.310
  691.3 10.9 while.67
  713.8 9.2 while.69
  732.4 22.5 %reduce-scatter.13.cloned.1.call-done = f32[2,8,128]{2,1,0:T(8,128)} async-done(((f32[2,128,128]{2,1,0:T(8,128)}), f32[2,8,128]{2,1,0:T(8,128)}) %reduce-scatter.13.cloned.1.call-update) | async-done | bytes 8208 | tf_op jit(solution)/shard_map/reduce_scatter | solution.py:408
  754.9 74.7 %reduce-scatter.23.cloned.1.call-done = f32[32,128]{1,0:T(8,128)} async-done(((f32[512,128]{1,0:T(8,128)}), f32[32,128]{1,0:T(8,128)}) %reduce-scatter.23.cloned.1.call-update) | async-done | bytes 16400 | tf_op jit(solution)/shard_map/reduce_scatter | solution.py:410
  829.6 74.7 %reduce-scatter.21.cloned.1.call-done = f32[32,128]{1,0:T(8,128)} async-done(((f32[512,128]{1,0:T(8,128)}), f32[32,128]{1,0:T(8,128)}) %reduce-scatter.21.cloned.1.call-update) | async-done | bytes 16400 | tf_op jit(solution)/shard_map/reduce_scatter | solution.py:410
  904.3 123.0 %reduce-scatter.11.cloned.1.call-done = f32[2,8,384]{2,1,0:T(8,128)} async-done(((f32[2,128,384]{2,1,0:T(8,128)}), f32[2,8,384]{2,1,0:T(8,128)}) %reduce-scatter.11.cloned.1.call-update) | async-done | bytes 24592 | tf_op jit(solution)/shard_map/reduce_scatter | solution.py:407
  1027.3 127.0 %reduce-scatter.9.cloned.1.call-done = f32[2,8,384]{2,1,0:T(8,128)} async-done(((f32[2,128,384]{2,1,0:T(8,128)}), f32[2,8,384]{2,1,0:T(8,128)}) %reduce-scatter.9.cloned.1.call-update) | async-done | bytes 24592 | tf_op jit(solution)/shard_map/reduce_scatter | solution.py:407
  1154.4 77.9 %reduce-scatter.19.cloned.1.call-done = f32[8,1024]{1,0:T(8,128)} async-done(((f32[128,1024]{1,0:T(8,128)}), f32[8,1024]{1,0:T(8,128)}) %reduce-scatter.19.cloned.1.call-update) | async-done | bytes 32784 | tf_op jit(solution)/shard_map/reduce_scatter | solution.py:409
  1232.3 75.3 %reduce-scatter.17.cloned.1.call-done = f32[8,1024]{1,0:T(8,128)} async-done(((f32[128,1024]{1,0:T(8,128)}), f32[8,1024]{1,0:T(8,128)}) %reduce-scatter.17.cloned.1.call-update) | async-done | bytes 32784 | tf_op jit(solution)/shard_map/reduce_scatter | solution.py:409
  1314.3 11.1 all-reduce.10.cloned.1.call-done
  1330.8 126.3 %all-reduce.8.cloned.1.call-done = (f32[8,10,128]{2,0,1:T(8,128)}, f32[128]{0:T(128)}, f32[2,4,128]{2,1,0:T(4,128)}, f32[2,4,128]{2,1,0:T(4,128)}, f32[8,10,128]{2,0,1:T(8,128)}, /*index=5*/f32[128]{0:T(128)}) async-done(((f32[8,10,128]{2,0,1:T(8,128)}, f32[128]{0:T(128)}, f32[2,4,128]{2,1,0:T(4,128)}, f32[2,4,128]{2,1,0:T(4,128)}, f32[8,10,128]{2,0,1:T(8,128)}, /*index=5*/f32[128]{0:T(128)}), ...) | async-done | bytes 91152 | tf_op jit(solution)/shard_map/psum | solution.py:430
  1457.1 129.7 %all-reduce.6.cloned.1.call-done = f32[2,128,128]{2,1,0:T(8,128)} async-done(((f32[2,128,128]{2,1,0:T(8,128)}), f32[2,128,128]{2,1,0:T(8,128)}) %all-reduce.6.cloned.1.call-update) | async-done | bytes 131088 | tf_op jit(solution)/shard_map/psum | solution.py:430
  (760 shorter events, 278.2 us)
Async XLA Ops:
  7.2 316.5 %copy-start.183 = (bf16[128]{0:T(256)(128)(2,1)S(1)}, bf16[128]{0:T(256)(128)(2,1)}, u32[]{:S(2)}) copy-start(bf16[128]{0:T(256)(128)(2,1)} %param.28) | copy-start | bytes 772
  7.2 317.2 %copy-start.169 = (f32[2,4,128]{2,1,0:T(4,128)S(1)}, f32[2,4,128]{2,1,0:T(4,128)}, u32[]{:S(2)}) copy-start(f32[2,4,128]{2,1,0:T(4,128)} %param.35) | copy-start | bytes 12292
  7.2 317.2 %copy-start.168 = (f32[2,4,128]{2,1,0:T(4,128)S(1)}, f32[2,4,128]{2,1,0:T(4,128)}, u32[]{:S(2)}) copy-start(f32[2,4,128]{2,1,0:T(4,128)} %param.34) | copy-start | bytes 12292
  7.2 725.2 %reduce-scatter.15.cloned.1.call-start = ((), (), s32[]{:S(2)}) async-start(), calls=%async_computation.11 | async-start | bytes 139264 | tf_op jit(solution)/shard_map/reduce_scatter | solution.py:408
  90.4 281.6 %copy-start.88 = (bf16[1,2,128,128]{3,2,1,0:T(8,128)(2,1)}, bf16[1,2,128,128]{3,2,1,0:T(8,128)(2,1)S(1)}, u32[]{:S(2)}) copy-start(bf16[1,2,128,128]{3,2,1,0:T(8,128)(2,1)S(1)} %all-gather.1) | copy-start | bytes 196612
  207.9 178.0 %copy-start.56 = (bf16[1,2,128,384]{3,2,1,0:T(8,128)(2,1)}, bf16[1,2,128,384]{3,2,1,0:T(8,128)(2,1)S(1)}, u32[]{:S(2)}) copy-start(bf16[1,2,128,384]{3,2,1,0:T(8,128)(2,1)S(1)} %all-gather.4) | copy-start | bytes 589828
  244.6 88.3 %copy-start.60 = (bf16[1,2,128,384]{3,2,1,0:T(8,128)(2,1)}, bf16[1,2,128,384]{3,2,1,0:T(8,128)(2,1)S(1)}, u32[]{:S(2)}) copy-start(bf16[1,2,128,384]{3,2,1,0:T(8,128)(2,1)S(1)} %all-gather) | copy-start | bytes 589828
  322.6 53.1 %copy-start.94 = (bf16[1,128,1024]{2,1,0:T(8,128)(2,1)}, bf16[1,128,1024]{2,1,0:T(8,128)(2,1)S(1)}, u32[]{:S(2)}) copy-start(bf16[1,128,1024]{2,1,0:T(8,128)(2,1)S(1)} %all-gather.2) | copy-start | bytes 786436
  325.0 47.0 %copy-start.156 = (f32[128]{0:T(128)}, f32[128]{0:T(128)S(1)}, u32[]{:S(2)}) copy-start(f32[128]{0:T(128)S(1)} %get-tuple-element.552) | copy-start | bytes 1540
  325.0 48.5 %copy-start.138 = (f32[128]{0:T(128)}, f32[128]{0:T(128)S(1)}, u32[]{:S(2)}) copy-start(f32[128]{0:T(128)S(1)} %get-tuple-element.525) | copy-start | bytes 1540
  325.0 48.5 %copy-start.150 = (f32[128]{0:T(128)}, f32[128]{0:T(128)S(1)}, u32[]{:S(2)}) copy-start(f32[128]{0:T(128)S(1)} %get-tuple-element.553) | copy-start | bytes 1540
  325.1 50.7 %copy-start.163 = (f32[128]{0:T(128)}, f32[128]{0:T(128)S(1)}, u32[]{:S(2)}) copy-start(f32[128]{0:T(128)S(1)} %get-tuple-element.524) | copy-start | bytes 1540
  325.1 53.4 %copy-start.166 = (f32[128]{0:T(128)}, f32[128]{0:T(128)S(1)}, u32[]{:S(2)}) copy-start(f32[128]{0:T(128)S(1)} %get-tuple-element.554) | copy-start | bytes 1540
  325.1 55.1 %copy-start.143 = (f32[128]{0:T(128)}, f32[128]{0:T(128)S(1)}, u32[]{:S(2)}) copy-start(f32[128]{0:T(128)S(1)} %get-tuple-element.523) | copy-start | bytes 1540
  325.1 59.2 %copy-start.158 = (f32[128]{0:T(128)}, f32[128]{0:T(128)S(1)}, u32[]{:S(2)}) copy-start(f32[128]{0:T(128)S(1)} %get-tuple-element.555) | copy-start | bytes 1540
  325.1 60.7 %copy-start.145 = (f32[128]{0:T(128)}, f32[128]{0:T(128)S(1)}, u32[]{:S(2)}) copy-start(f32[128]{0:T(128)S(1)} %get-tuple-element.522) | copy-start | bytes 1540
  325.1 102.6 %copy-start.148 = (f32[128]{0:T(128)}, f32[128]{0:T(128)S(1)}, u32[]{:S(2)}) copy-start(f32[128]{0:T(128)S(1)} %get-tuple-element.528) | copy-start | bytes 1540
  332.4 39.6 %copy-start.8 = (f32[2,4,128,128]{3,2,1,0:T(8,128)}, f32[2,4,128,128]{3,2,1,0:T(8,128)S(1)}, u32[]{:S(2)}) copy-start(f32[2,4,128,128]{3,2,1,0:T(8,128)S(1)} %get-tuple-element.431) | copy-start | bytes 1572868
  340.2 22.2 %copy-start.6 = (bf16[2,4,128,8,16]{4,1,3,2,0:T(4,128)(2,1)}, bf16[2,4,128,8,16]{4,1,3,2,0:T(4,128)(2,1)S(1)}, u32[]{:S(2)}) copy-start(bf16[2,4,128,8,16]{4,1,3,2,0:T(4,128)(2,1)S(1)} %copy.230) | copy-start | bytes 786436
  427.3 17.6 %copy-start.22 = (f32[2,4,128,128]{3,2,1,0:T(8,128)}, f32[2,4,128,128]{3,2,1,0:T(8,128)S(1)}, u32[]{:S(2)}) copy-start(f32[2,4,128,128]{3,2,1,0:T(8,128)S(1)} %get-tuple-element.421) | copy-start | bytes 1572868
  427.3 17.6 %copy-start.116 = (f32[2,4,128]{2,1,0:T(4,128)}, f32[2,4,128]{2,1,0:T(4,128)S(1)}, u32[]{:S(2)}) copy-start(f32[2,4,128]{2,1,0:T(4,128)S(1)} %broadcast_multiply_fusion.33) | copy-start | bytes 12292
  427.7 17.2 %copy-start.128 = (f32[2,4,128]{2,1,0:T(4,128)}, f32[2,4,128]{2,1,0:T(4,128)S(1)}, u32[]{:S(2)}) copy-start(f32[2,4,128]{2,1,0:T(4,128)S(1)} %add_rsqrt_fusion.1) | copy-start | bytes 12292
  429.1 15.8 copy-start.12
  429.1 15.8 copy-start.106
  429.5 15.4 copy-start.118
  545.2 209.8 %reduce-scatter.13.cloned.1.call-start = ((), (), s32[]{:S(2)}) async-start(), calls=%async_computation.10 | async-start | bytes 139264 | tf_op jit(solution)/shard_map/reduce_scatter | solution.py:408
  681.1 148.5 %reduce-scatter.23.cloned.1.call-start = ((), (), s32[]{:S(2)}) async-start(), calls=%async_computation.15 | async-start | bytes 278528 | tf_op jit(solution)/shard_map/reduce_scatter | solution.py:410
  683.7 220.6 %reduce-scatter.21.cloned.1.call-start = ((), (), s32[]{:S(2)}) async-start(), calls=%async_computation.14 | async-start | bytes 278528 | tf_op jit(solution)/shard_map/reduce_scatter | solution.py:410
  686.4 341.0 %reduce-scatter.11.cloned.1.call-start = ((), (), s32[]{:S(2)}) async-start(), calls=%async_computation.9 | async-start | bytes 417792 | tf_op jit(solution)/shard_map/reduce_scatter | solution.py:407
  689.9 464.5 %reduce-scatter.9.cloned.1.call-start = ((), (), s32[]{:S(2)}) async-start(), calls=%async_computation.8 | async-start | bytes 417792 | tf_op jit(solution)/shard_map/reduce_scatter | solution.py:407
  691.2 12.4 copy-start.25
  691.2 12.4 copy-start.109
  691.2 12.4 copy-start.131
  691.2 12.4 copy-start.136
  706.5 525.7 %reduce-scatter.19.cloned.1.call-start = ((), (), s32[]{:S(2)}) async-start(), calls=%async_computation.13 | async-start | bytes 557056 | tf_op jit(solution)/shard_map/reduce_scatter | solution.py:409
  709.8 597.7 %reduce-scatter.17.cloned.1.call-start = ((), (), s32[]{:S(2)}) async-start(), calls=%async_computation.12 | async-start | bytes 557056 | tf_op jit(solution)/shard_map/reduce_scatter | solution.py:409
  713.4 612.0 %all-reduce.10.cloned.1.call-start = ((), (), s32[]{:S(2)}) async-start(), calls=%async_computation.18 | async-start | bytes 327680 | tf_op jit(solution)/shard_map/psum | solution.py:412
  728.1 582.1 %copy-start.23 = (f32[2,4,128,128]{3,2,1,0:T(8,128)S(1)}, f32[2,4,128,128]{3,2,1,0:T(8,128)}, u32[]{:S(2)}) copy-start(f32[2,4,128,128]{3,2,1,0:T(8,128)} %copy-done.22) | copy-start | bytes 1572868
  728.1 582.1 %copy-start.35 = (f32[2,4,128,128]{3,2,1,0:T(8,128)S(1)}, f32[2,4,128,128]{3,2,1,0:T(8,128)}, u32[]{:S(2)}) copy-start(f32[2,4,128,128]{3,2,1,0:T(8,128)} %copy-done.34) | copy-start | bytes 1572868
  728.1 582.1 %copy-start.117 = (f32[2,4,128]{2,1,0:T(4,128)S(1)}, f32[2,4,128]{2,1,0:T(4,128)}, u32[]{:S(2)}) copy-start(f32[2,4,128]{2,1,0:T(4,128)} %copy-done.116) | copy-start | bytes 12292
  728.1 582.1 %copy-start.129 = (f32[2,4,128]{2,1,0:T(4,128)S(1)}, f32[2,4,128]{2,1,0:T(4,128)}, u32[]{:S(2)}) copy-start(f32[2,4,128]{2,1,0:T(4,128)} %copy-done.128) | copy-start | bytes 12292
  728.1 583.3 %copy-start.16 = (f32[2,4,128,128]{3,2,1,0:T(8,128)S(1)}, f32[2,4,128,128]{3,2,1,0:T(8,128)}, u32[]{:S(2)}) copy-start(f32[2,4,128,128]{3,2,1,0:T(8,128)} %copy-done.14) | copy-start | bytes 1572868
  728.2 583.3 %copy-start.29 = (f32[2,4,128,128]{3,2,1,0:T(8,128)S(1)}, f32[2,4,128,128]{3,2,1,0:T(8,128)}, u32[]{:S(2)}) copy-start(f32[2,4,128,128]{3,2,1,0:T(8,128)} %copy-done.28) | copy-start | bytes 1572868
  728.2 583.3 %copy-start.140 = (f32[128]{0:T(128)S(1)}, f32[128]{0:T(128)}, u32[]{:S(2)}) copy-start(f32[128]{0:T(128)} %copy-done.138) | copy-start | bytes 1540
  730.1 583.2 %copy-start.74 = (f32[2,4,128,128]{3,2,1,0:T(8,128)S(1)}, f32[2,4,128,128]{3,2,1,0:T(8,128)}, u32[]{:S(2)}) copy-start(f32[2,4,128,128]{3,2,1,0:T(8,128)} %copy-done.73) | copy-start | bytes 1572868
  1307.5 149.5 %all-reduce.8.cloned.1.call-start = ((), (), s32[]{:S(2)}) async-start(), calls=%async_computation.17 | async-start | bytes 182272 | tf_op jit(solution)/shard_map/psum | solution.py:430
  1310.2 276.6 %all-reduce.6.cloned.1.call-start = ((), (), s32[]{:S(2)}) async-start(), calls=%async_computation.16 | async-start | bytes 262144 | tf_op jit(solution)/shard_map/psum | solution.py:430
  1310.3 285.7 %copy-start.1 = (bf16[8,10,128]{2,0,1:T(8,128)(2,1)S(1)}, bf16[8,10,128]{2,0,1:T(8,128)(2,1)}, u32[]{:S(2)}) copy-start(bf16[8,10,128]{2,0,1:T(8,128)(2,1)} %param.27) | copy-start | bytes 61444
  (161 other events, 579.0 us)
Sparse Core Ops, SparseCore 0:
  545.3 73.8 reduce-scatter.14
  681.2 73.6 reduce-scatter.12
  757.2 72.4 reduce-scatter.22
  831.8 72.4 reduce-scatter.20
  909.4 117.9 reduce-scatter.10
  1032.6 121.7 reduce-scatter.8
  1156.6 75.5 reduce-scatter.18
  1234.6 72.8 reduce-scatter.16
  1310.4 14.9 all-reduce.9
  1332.8 124.2 all-reduce.7
  1463.2 123.5 all-reduce.5
where the time goes:
time: 1610 us; the launch traced here: 1600 us
  waiting for transfers between devices  842 us (52%)
  blocking collectives  311 us (19%)
  matrix products  229 us (14%)
  local copies, waits for them, and re-layouts  136 us (8%)
  other arithmetic  66 us (4%)
  between operations  16.8 us (1%)
    psum x2, waiting for transfers between devices, per_device(): lax.psum((token_local, gains_local, scales_local, prompt_local, cls_local...  256 us
    reduce_scatter x2, waiting for transfers between devices, per_device(): lax.psum_scatter(matrix_grads[0], 'fsdp', scatter_dimension=1, tiled=True)  250 us
    reduce_scatter x2, waiting for transfers between devices, per_device(): lax.psum_scatter(matrix_grads[2], 'fsdp', scatter_dimension=0, tiled=True)  153 us
    reduce_scatter x2, waiting for transfers between devices, per_device(): lax.psum_scatter(matrix_grads[3], 'fsdp', scatter_dimension=0, tiled=True)  149 us
    all_gather x2, blocking collectives, per_device(): lax.all_gather(feed_output_weights[layer_idx], 'fsdp', axis=0, tiled=True)  78.9 us
    all_gather x2, blocking collectives, per_device(): lax.all_gather(attention_output_weights[layer_idx], 'fsdp', axis=1, tiled...  78.5 us
    all_gather x2, blocking collectives, per_device(): lax.all_gather(feed_input_weights[layer_idx], 'fsdp', axis=0, tiled=True)  78 us
    all_gather x2, blocking collectives, per_device(): lax.all_gather(attention_input_weights[layer_idx], 'fsdp', axis=1, tiled=...  75.2 us
  transfers between devices with their start and end apart: 11, of which 10 were waited for; matrix products, arithmetic and copies ran while one was open for 12% of the time, Pallas kernels for 0%

commit v1 on v0

v1 whole, which is shorter than its diff:
```python
import functools

import jax
import jax.numpy as jnp
from jax import lax
from jax.experimental import pallas as pl
from jax.experimental.pallas import tpu as pltpu
from jax.sharding import PartitionSpec as P

HEADS = 8
EPSILON = 1e-05
NEG_FILL = -1000000000.0
BF = jnp.bfloat16
F32 = jnp.float32

COL_IN = (0, 384)
COL_OUT = (768, 896)
COL_FEED = 1024
COL_DOWN = 2048
COLS = 2560
SHARDS = 16
STEP_BITS = (2, 3, 0, 1)


def dot_nn(a, b):
    return lax.dot_general(a, b, (((1,), (0,)), ((), ())), preferred_element_type=F32)


def dot_nt(a, b):
    return lax.dot_general(a, b, (((1,), (1,)), ((), ())), preferred_element_type=F32)


def norm_cols(x):
    centered = x - jnp.mean(x, axis=0, keepdims=True)
    inv = lax.rsqrt(jnp.mean(centered * centered, axis=0, keepdims=True) + EPSILON)
    return centered * inv, inv


def norm_cols_back(dn, gain, xhat, inv):
    e = dn * gain
    m1 = jnp.mean(e, axis=0, keepdims=True)
    m2 = jnp.mean(e * xhat, axis=0, keepdims=True)
    return inv * (e - m1 - xhat * m2)


def fold(part):
    return part[:, :128] + part[:, 128:]


def dp_of(split):
    return lax.axis_index("dp") if split else 0


def pack_kernel(attn_in_ref, attn_out_ref, feed_in_ref, feed_out_ref, out_ref):
    l = lax.axis_index("dp")
    down = feed_out_ref[l].astype(F32)
    parts = [attn_in_ref[l, 0], attn_in_ref[l, 1], attn_out_ref[l, 0], attn_out_ref[l, 1], feed_in_ref[l]]
    parts = [part.astype(F32) for part in parts] + [down[8 * a : 8 * a + 8] for a in range(4)]
    row = jnp.concatenate(parts, axis=1).astype(BF)
    for f in range(SHARDS):
        out_ref[f] = row


def tower_kernel(
    split,
    ids_ref, counts_ref, wmine_ref, wother_ref, tok_ref, gains_ref, scales_ref, patches_ref, prompts_ref,
    cls_ref, cot_ref, adj_ref,
    out_ref, pgrad_ref, gbig_ref, gsmall_ref,
    w_ref, wd_ref, wt_ref, wdt_ref, colb_ref, tokscr_ref, h_ref, g_ref, xh_ref, inv_ref,
    qkvt_ref, pb_ref, ot_ref, qkvv_ref, pv_ref, ov_ref, qbd_ref, dob_ref, hid_ref, du_ref, dqkv_ref,
    dov_ref, ga_ref, gd_ref, gt_ref, gacc_ref,
):
    dp = dp_of(split)
    layers = 2
    chunks = 4
    items = 2

    for l in range(layers):
        for pair in range(SHARDS // 2):
            lo = jnp.where(dp == l, wmine_ref[2 * pair].astype(F32), wother_ref[2 * pair].astype(F32))
            hi = jnp.where(dp == l, wmine_ref[2 * pair + 1].astype(F32), wother_ref[2 * pair + 1].astype(F32))
            w_ref[l, 16 * pair : 16 * pair + 16, :] = jnp.concatenate([lo[:, :COL_DOWN], hi[:, :COL_DOWN]], axis=0).astype(BF)
            for half, part in enumerate((lo, hi)):
                base = 64 * pair + 32 * half
                wd_ref[l, base : base + 32, :] = jnp.concatenate(
                    [part[:, COL_DOWN + 128 * a : COL_DOWN + 128 * a + 128] for a in range(4)], axis=0
                ).astype(BF)
        for block in range(COL_DOWN // 128):
            wt_ref[l, 128 * block : 128 * block + 128, :] = w_ref[l, :, 128 * block : 128 * block + 128].T
        for block in range(4):
            wdt_ref[l, :, 128 * block : 128 * block + 128] = wd_ref[l, 128 * block : 128 * block + 128, :].T
        for k in range(4):
            for offset, rows in ((0, gains_ref), (4, scales_ref)):
                col = jnp.broadcast_to(rows[l, k : k + 1, :], (128, 128)).T
                colb_ref[l * 8 + offset + k, :, 0:128] = col
                colb_ref[l * 8 + offset + k, :, 128:256] = col

    for b in range(items):
        ident = ids_ref[b]
        for v in range(4):
            bv = 4 * b + v
            tokscr_ref[bv, 0:10, :] = prompts_ref[ident].astype(F32)
            tokscr_ref[bv, 10:127, :] = patches_ref[b, v].astype(F32)
            tokscr_ref[bv, 127:128, :] = cls_ref[...].astype(F32)
            lanes = slice(128 * (v % 2), 128 * (v % 2) + 128)
            h_ref[2 * b + v // 2, :, lanes] = tokscr_ref[bv].T
            g_ref[0, 2 * b + v // 2, :, lanes] = cot_ref[b, v].astype(F32).T
            g_ref[1, 2 * b + v // 2, :, lanes] = adj_ref[b, v].astype(F32).T

    qbd_ref[...] = jnp.zeros_like(qbd_ref)
    dob_ref[...] = jnp.zeros_like(dob_ref)

    head_row = lax.broadcasted_iota(jnp.int32, (8, 256), 0)
    head_col = (lax.broadcasted_iota(jnp.int32, (8, 256), 1) % 128) // 16
    gather_heads = jnp.where(head_row == head_col, 1.0, 0.0).astype(BF)
    spread_row = lax.broadcasted_iota(jnp.int32, (128, 8), 0) // 16
    spread_col = lax.broadcasted_iota(jnp.int32, (128, 8), 1)
    spread_heads = jnp.where(spread_row == spread_col, 1.0, 0.0).astype(BF)

    def head_sums(left, rights):
        his, los = [], []
        for right in rights:
            prod = left * right
            hi = prod.astype(BF)
            his.append(hi)
            los.append((prod - hi.astype(F32)).astype(BF))
        both = jnp.concatenate([jnp.concatenate(his, axis=1), jnp.concatenate(los, axis=1)], axis=0)
        return dot_nn(gather_heads, both)

    def diag_heads(target_ref, s, rows):
        for head in range(HEADS):
            target_ref[s, 16 * head : 16 * head + 16, 128 * head : 128 * head + 128] = rows[16 * head : 16 * head + 16]

    def gain(l, k):
        return colb_ref[l * 8 + k]

    def scale(l, k):
        return colb_ref[l * 8 + 4 + k]

    def keep_norm(l, k, c, x):
        xhat, inv = norm_cols(x)
        xh_ref[l * 4 + k, c] = xhat
        inv_ref[l * 4 + k, c] = inv
        return (xhat * gain(l, k)).astype(BF)

    def time_forward(l, c):
        x = h_ref[c]
        n = keep_norm(l, 0, c, x)
        qkv = dot_nn(wt_ref[l, 0:384, :], n)
        queries = (qkv[:128] * 0.25).astype(BF)
        keys = qkv[128:256].astype(BF)
        values = qkv[256:].astype(BF)
        qkvt_ref[l, c, 0:128, :] = queries
        qkvt_ref[l, c, 128:256, :] = keys
        qkvt_ref[l, c, 256:384, :] = values
        for s in range(2):
            lanes = slice(128 * s, 128 * s + 128)
            diag_heads(qbd_ref, s, queries[:, lanes])
            key_rows = keys[:, lanes].T
            for hp in range(4):
                span = slice(256 * hp, 256 * hp + 256)
                rows = slice(32 * hp, 32 * hp + 32)
                scores = dot_nn(key_rows, qbd_ref[s, :, span])
                shifted = jnp.exp(scores - jnp.max(scores, axis=0, keepdims=True))
                prob = (shifted * (1.0 / jnp.sum(shifted, axis=0, keepdims=True))).astype(BF)
                pb_ref[l, 2 * c + s, :, span] = prob
                mixed = dot_nn(values[rows, lanes], prob)
                ot_ref[l, c, 32 * hp : 32 * hp + 16, lanes] = mixed[:16, :128].astype(BF)
                ot_ref[l, c, 32 * hp + 16 : 32 * hp + 32, lanes] = mixed[16:, 128:].astype(BF)
        branch = dot_nn(wt_ref[l, COL_OUT[0] : COL_OUT[0] + 128, :], ot_ref[l, c])
        h_ref[c] = x + scale(l, 0) * branch

    def var_forward(l, b):
        for cc in range(2):
            c = 2 * b + cc
            n = keep_norm(l, 1, c, h_ref[c])
            qkv = dot_nn(wt_ref[l, COL_IN[1] : COL_IN[1] + 384, :], n)
            qkvv_ref[l, c, 0:128, :] = (qkv[:128] * 0.25).astype(BF)
            qkvv_ref[l, c, 128:384, :] = qkv[128:].astype(BF)
        count = counts_ref[ids_ref[b]]

        def slot(first, i):
            lanes = slice(128 * (i % 2), 128 * (i % 2) + 128)
            return qkvv_ref[l, 2 * b + i // 2, first : first + 128, lanes].astype(F32)

        key_slots = [slot(128, j) for j in range(4)]
        value_slots = [slot(256, j) for j in range(4)]
        for i in range(4):
            scores = head_sums(slot(0, i), key_slots)
            parts = [scores[:, 128 * j : 128 * j + 128] for j in range(4)]
            parts = [jnp.where(jnp.full((8, 128), count, jnp.int32) > j, parts[j], NEG_FILL) for j in range(4)]
            top = jnp.maximum(jnp.maximum(parts[0], parts[1]), jnp.maximum(parts[2], parts[3]))
            shifted = [jnp.exp(part - top) for part in parts]
            total = 1.0 / ((shifted[0] + shifted[1]) + (shifted[2] + shifted[3]))
            prob = jnp.concatenate([part * total for part in shifted], axis=1)
            pv_ref[l, b, i] = prob
            spread = dot_nn(spread_heads, prob.astype(BF))
            mixed = spread[:, :128] * value_slots[0]
            for j in range(1, 4):
                mixed = mixed + spread[:, 128 * j : 128 * j + 128] * value_slots[j]
            lanes = slice(128 * (i % 2), 128 * (i % 2) + 128)
            ov_ref[l, 2 * b + i // 2, :, lanes] = mixed.astype(BF)
        for cc in range(2):
            c = 2 * b + cc
            branch = dot_nn(wt_ref[l, COL_OUT[1] : COL_OUT[1] + 128, :], ov_ref[l, c])
            h_ref[c] = h_ref[c] + scale(l, 1) * branch

    def tail_forward(l, c):
        x = h_ref[c]
        n = keep_norm(l, 2, c, x)
        mix = [dot_nt(n[:, 128 * s : 128 * s + 128], tok_ref[l]) for s in range(2)]
        x = x + scale(l, 2) * jnp.concatenate(mix, axis=1)
        n = keep_norm(l, 3, c, x)
        for z in range(4):
            gate = dot_nn(wt_ref[l, COL_FEED + 128 * z : COL_FEED + 128 * z + 128, :], n)
            up = dot_nn(wt_ref[l, COL_FEED + 512 + 128 * z : COL_FEED + 640 + 128 * z, :], n)
            sig = 0.5 * jnp.tanh(0.5 * gate) + 0.5
            hid_ref[128 * z : 128 * z + 128, :] = (gate * sig * up).astype(BF)
        h_ref[c] = x + scale(l, 3) * dot_nn(wdt_ref[l], hid_ref[...])

    def norm_of(l, k, c):
        xhat = xh_ref[l * 4 + k, c]
        return xhat, inv_ref[l * 4 + k, c], (xhat * gain(l, k)).astype(BF)

    def pass_on(l, k, c, x, dn, xhat, inv):
        if x == 0:
            gacc_ref[l * 4 + k] += fold(dn * xhat)
        g_ref[x, c] += norm_cols_back(dn, gain(l, k), xhat, inv)

    def feed_backward(l, c):
        xhat, inv, n = norm_of(l, 3, c)
        dz = [(scale(l, 3) * g_ref[x, c]).astype(BF) for x in range(2)]
        for z in range(4):
            rows = slice(128 * z, 128 * z + 128)
            gate = dot_nn(wt_ref[l, COL_FEED + 128 * z : COL_FEED + 128 * z + 128, :], n)
            up = dot_nn(wt_ref[l, COL_FEED + 512 + 128 * z : COL_FEED + 640 + 128 * z, :], n)
            sig = 0.5 * jnp.tanh(0.5 * gate) + 0.5
            act = gate * sig
            hid_ref[rows, :] = (act * up).astype(BF)
            slope = up * (sig * (1.0 + gate * (1.0 - sig)))
            for x in range(2):
                dhid = dot_nn(wd_ref[l, rows, :], dz[x])
                du_ref[x, 128 * z : 128 * z + 128, :] = (dhid * slope).astype(BF)
                du_ref[x, 512 + 128 * z : 640 + 128 * z, :] = (dhid * act).astype(BF)
        ga_ref[:, COL_FEED:COL_DOWN] += dot_nt(n, du_ref[0])
        gd_ref[...] += dot_nt(hid_ref[...], dz[0])
        for x in range(2):
            dn = dot_nn(w_ref[l, :, COL_FEED:COL_DOWN], du_ref[x])
            pass_on(l, 3, c, x, dn, xhat, inv)

    def token_backward(l, c):
        xhat, inv, n = norm_of(l, 2, c)
        for x in range(2):
            dy = (scale(l, 2) * g_ref[x, c]).astype(BF)
            dn = []
            for s in range(2):
                part = dy[:, 128 * s : 128 * s + 128]
                dn.append(dot_nn(part, tok_ref[l]))
                if x == 0:
                    gt_ref[l] += dot_nn(part.T, n[:, 128 * s : 128 * s + 128])
            pass_on(l, 2, c, x, jnp.concatenate(dn, axis=1), xhat, inv)

    def var_backward(l, b):
        def slot(first, i):
            lanes = slice(128 * (i % 2), 128 * (i % 2) + 128)
            return qkvv_ref[l, 2 * b + i // 2, first : first + 128, lanes].astype(F32)

        for x in range(2):
            for cc in range(2):
                c = 2 * b + cc
                dt = (scale(l, 1) * g_ref[x, c]).astype(BF)
                dov_ref[cc] = dot_nn(w_ref[l, :, COL_OUT[1] : COL_OUT[1] + 128], dt).astype(BF)
                if x == 0:
                    ga_ref[:, COL_OUT[1] : COL_OUT[1] + 128] += dot_nt(ov_ref[l, c], dt)
            value_slots = [slot(256, j) for j in range(4)]
            dkeys = [None] * 4
            dvalues = [None] * 4
            for i in range(4):
                lanes = slice(128 * (i % 2), 128 * (i % 2) + 128)
                grad = dov_ref[i // 2, :, lanes].astype(F32)
                query = slot(0, i)
                prob = pv_ref[l, b, i]
                weighted = prob * head_sums(grad, value_slots)
                total = (weighted[:, :128] + weighted[:, 128:256]) + (weighted[:, 256:384] + weighted[:, 384:])
                ds = weighted - prob * jnp.concatenate([total] * 4, axis=1)
                ds_wide = dot_nn(spread_heads, ds.astype(BF))
                p_wide = dot_nn(spread_heads, prob.astype(BF))
                dquery = None
                for j in range(4):
                    ds_j = ds_wide[:, 128 * j : 128 * j + 128]
                    p_j = p_wide[:, 128 * j : 128 * j + 128]
                    terms = (ds_j * slot(128, j), ds_j * query, p_j * grad)
                    dquery = terms[0] if dquery is None else dquery + terms[0]
                    dkeys[j] = terms[1] if dkeys[j] is None else dkeys[j] + terms[1]
                    dvalues[j] = terms[2] if dvalues[j] is None else dvalues[j] + terms[2]
                dqkv_ref[i // 2, 0:128, lanes] = (0.25 * dquery).astype(BF)
            for j in range(4):
                lanes = slice(128 * (j % 2), 128 * (j % 2) + 128)
                dqkv_ref[j // 2, 128:256, lanes] = dkeys[j].astype(BF)
                dqkv_ref[j // 2, 256:384, lanes] = dvalues[j].astype(BF)
            for cc in range(2):
                c = 2 * b + cc
                xhat, inv, n = norm_of(l, 1, c)
                dqkv = dqkv_ref[cc]
                if x == 0:
                    ga_ref[:, COL_IN[1] : COL_IN[1] + 384] += dot_nt(n, dqkv)
                pass_on(l, 1, c, x, dot_nn(w_ref[l, :, COL_IN[1] : COL_IN[1] + 384], dqkv), xhat, inv)

    def time_backward(l, c):
        xhat, inv, n = norm_of(l, 0, c)
        queries = qkvt_ref[l, c, 0:128, :]
        keys = qkvt_ref[l, c, 128:256, :]
        values = qkvt_ref[l, c, 256:384, :]
        grads = []
        for x in range(2):
            dt = (scale(l, 0) * g_ref[x, c]).astype(BF)
            grads.append(dot_nn(w_ref[l, :, COL_OUT[0] : COL_OUT[0] + 128], dt).astype(BF))
            if x == 0:
                ga_ref[:, COL_OUT[0] : COL_OUT[0] + 128] += dot_nt(ot_ref[l, c], dt)
        for s in range(2):
            lanes = slice(128 * s, 128 * s + 128)
            diag_heads(qbd_ref, s, queries[:, lanes])
            value_rows = values[:, lanes].T
            for x in range(2):
                diag_heads(dob_ref, 2 * x + s, grads[x][:, lanes])
            for hp in range(4):
                span = slice(256 * hp, 256 * hp + 256)
                rows = slice(32 * hp, 32 * hp + 32)
                prob_bf = pb_ref[l, 2 * c + s, :, span]
                prob = prob_bf.astype(F32)
                for x in range(2):
                    weighted = prob * dot_nn(value_rows, dob_ref[2 * x + s, :, span])
                    ds = (weighted - prob * jnp.sum(weighted, axis=0, keepdims=True)).astype(BF)
                    dvalue = dot_nt(dob_ref[2 * x + s, rows, span], prob_bf)
                    dquery = dot_nn(keys[rows, lanes], ds) * 0.25
                    dkey = dot_nt(qbd_ref[s, rows, span], ds)
                    dqkv_ref[x, 32 * hp : 32 * hp + 16, lanes] = dquery[:16, :128].astype(BF)
                    dqkv_ref[x, 32 * hp + 16 : 32 * hp + 32, lanes] = dquery[16:, 128:].astype(BF)
                    dqkv_ref[x, 128 + 32 * hp : 160 + 32 * hp, lanes] = dkey.astype(BF)
                    dqkv_ref[x, 256 + 32 * hp : 288 + 32 * hp, lanes] = dvalue.astype(BF)
        ga_ref[:, COL_IN[0] : COL_IN[0] + 384] += dot_nt(n, dqkv_ref[0])
        for x in range(2):
            pass_on(l, 0, c, x, dot_nn(w_ref[l, :, COL_IN[0] : COL_IN[0] + 384], dqkv_ref[x]), xhat, inv)

    def each(count, stage, l):
        lax.fori_loop(0, count, lambda i, carry: (stage(l, i), carry)[1], 0)

    def forward_layer(l, carry):
        each(chunks, time_forward, l)
        each(items, var_forward, l)
        each(chunks, tail_forward, l)
        return carry

    lax.fori_loop(0, layers, forward_layer, 0)
    for b in range(items):
        for v in range(4):
            lanes = slice(128 * (v % 2), 128 * (v % 2) + 128)
            out_ref[b, v] = h_ref[2 * b + v // 2, :, lanes].T.astype(BF)

    gacc_ref[...] = jnp.zeros_like(gacc_ref)
    gt_ref[...] = jnp.zeros_like(gt_ref)
    gsmall_ref[...] = jnp.zeros_like(gsmall_ref)
    rest = 1 ^ dp
    def backward_layer(step, carry):
        l = layers - 1 - step
        ga_ref[...] = jnp.zeros_like(ga_ref)
        gd_ref[...] = jnp.zeros_like(gd_ref)
        each(chunks, feed_backward, l)
        each(chunks, token_backward, l)
        each(items, var_backward, l)
        each(chunks, time_backward, l)
        l_at = l ^ dp
        for f in range(SHARDS):
            down = jnp.concatenate([gd_ref[32 * f + 8 * a : 32 * f + 8 * a + 8, :] for a in range(4)], axis=1)
            block = jnp.concatenate([ga_ref[8 * f : 8 * f + 8, :], down], axis=1)
            gbig_ref[l_at, f] = block.astype(BF)
        gains_rows = [jnp.sum(gacc_ref[l * 4 + k].T, axis=0, keepdims=True) for k in range(4)]
        sums = [
            jnp.sum(w_ref[l, :, COL_OUT[k] : COL_OUT[k] + 128].astype(F32) * ga_ref[:, COL_OUT[k] : COL_OUT[k] + 128], axis=0, keepdims=True)
            for k in range(2)
        ]
        sums.append(gains_ref[l, 2:3, :] * gains_rows[2])
        sums.append(jnp.sum(wd_ref[l].astype(F32) * gd_ref[...], axis=0, keepdims=True))
        for k in range(4):
            gsmall_ref[rest, l * 4 + k, 10:11, :] = gains_rows[k]
            gsmall_ref[rest, l * 4 + k, 11:12, :] = sums[k] / scales_ref[l, k : k + 1, :]
        for block in range(8):
            gsmall_ref[dp, 8 * l + block] = gt_ref[l, 16 * block : 16 * block + 16, :]
        return carry

    lax.fori_loop(0, layers, backward_layer, 0)

    for x in range(2):
        cls_sum = None
        for b in range(items):
            prompt_sum = None
            for v in range(4):
                lanes = slice(128 * (v % 2), 128 * (v % 2) + 128)
                tokscr_ref[4 * b + v] = g_ref[x, 2 * b + v // 2, :, lanes].T
                head = tokscr_ref[4 * b + v, 0:10, :]
                last = tokscr_ref[4 * b + v, 127:128, :]
                prompt_sum = head if prompt_sum is None else prompt_sum + head
                cls_sum = last if cls_sum is None else cls_sum + last
                if x == 0:
                    pgrad_ref[b, v] = tokscr_ref[4 * b + v, 10:127, :]
            gsmall_ref[rest, 8 * x + ids_ref[b], 0:10, :] += prompt_sum
        gsmall_ref[rest, 8 * x, 12:13, :] = cls_sum


def run_tower(split, *operands):
    vmem = pl.BlockSpec(memory_space=pltpu.VMEM)
    smem = pl.BlockSpec(memory_space=pltpu.SMEM)
    return pl.pallas_call(
        functools.partial(tower_kernel, split),
        out_shape=(
            jax.ShapeDtypeStruct((2, 4, 128, 128), BF),
            jax.ShapeDtypeStruct((2, 4, 117, 128), F32),
            jax.ShapeDtypeStruct((2, SHARDS, 8, COLS), BF),
            jax.ShapeDtypeStruct((2, 16, 16, 128), F32),
        ),
        in_specs=[smem, smem] + [vmem] * 10,
        out_specs=[vmem] * 4,
        scratch_shapes=[
            pltpu.VMEM((2, 128, COL_DOWN), BF),
            pltpu.VMEM((2, 512, 128), BF),
            pltpu.VMEM((2, COL_DOWN, 128), BF),
            pltpu.VMEM((2, 128, 512), BF),
            pltpu.VMEM((16, 128, 256), F32),
            pltpu.VMEM((8, 128, 128), F32),
            pltpu.VMEM((4, 128, 256), F32),
            pltpu.VMEM((2, 4, 128, 256), F32),
            pltpu.VMEM((8, 4, 128, 256), F32),
            pltpu.VMEM((8, 4, 1, 256), F32),
            pltpu.VMEM((2, 4, 384, 256), BF),
            pltpu.VMEM((2, 8, 128, 1024), BF),
            pltpu.VMEM((2, 4, 128, 256), BF),
            pltpu.VMEM((2, 4, 384, 256), BF),
            pltpu.VMEM((2, 2, 4, 8, 512), F32),
            pltpu.VMEM((2, 4, 128, 256), BF),
            pltpu.VMEM((2, 128, 1024), BF),
            pltpu.VMEM((4, 128, 1024), BF),
            pltpu.VMEM((512, 256), BF),
            pltpu.VMEM((2, 1024, 256), BF),
            pltpu.VMEM((2, 384, 256), BF),
            pltpu.VMEM((2, 128, 256), BF),
            pltpu.VMEM((128, COL_DOWN), F32),
            pltpu.VMEM((512, 128), F32),
            pltpu.VMEM((2, 128, 128), F32),
            pltpu.VMEM((8, 128, 128), F32),
        ],
        compiler_params=pltpu.CompilerParams(vmem_limit_bytes=56 * 1024 * 1024),
        name="tower",
    )(*operands)


def pack_rows(attn_in, attn_out, feed_in, feed_out):
    layers, _, rows, _ = attn_in.shape
    down = feed_out.reshape(layers, 4, rows, 128)
    return jnp.concatenate(
        [attn_in[:, 0], attn_in[:, 1], attn_out[:, 0], attn_out[:, 1], feed_in] + [down[:, a] for a in range(4)], axis=2
    )


def unpack_rows(packed):
    layers, rows, _ = packed.shape
    attn_in = jnp.stack([packed[:, :, at : at + 384] for at in COL_IN], axis=1)
    attn_out = jnp.stack([packed[:, :, at : at + 128] for at in COL_OUT], axis=1)
    feed_in = packed[:, :, COL_FEED:COL_DOWN]
    feed_out = jnp.stack([packed[:, :, COL_DOWN + 128 * a : COL_DOWN + 128 * a + 128] for a in range(4)], axis=1)
    return attn_in, attn_out, feed_in, feed_out.reshape(layers, 4 * rows, 128)


def flip(array, axis, bit, size):
    return lax.ppermute(array, axis, [(i, i ^ (1 << bit)) for i in range(size)])


def gather_rows(attn_in, attn_out, feed_in, feed_out):
    vmem = pl.BlockSpec(memory_space=pltpu.VMEM)
    row = pl.pallas_call(
        pack_kernel, out_shape=jax.ShapeDtypeStruct((SHARDS, 8, COLS), BF), in_specs=[vmem] * 4, out_specs=vmem, name="pack",
    )(attn_in, attn_out, feed_in, feed_out)
    mine = lax.all_to_all(row, "fsdp", 0, 0, tiled=True)
    return mine, flip(mine, "dp", 0, 2)


def reduce_big(big):
    held = big[0].astype(F32) + flip(big[1], "dp", 0, 2).astype(F32)
    parts = lax.all_to_all(held.astype(BF), "fsdp", 0, 0, tiled=True)
    return jnp.sum(parts.astype(F32), axis=0)


def reduce_small(small):
    held = small[0] + flip(small[1].astype(BF), "dp", 0, 2).astype(F32)
    for bit in STEP_BITS[::-1]:
        mine = held.astype(BF)
        held = mine.astype(F32) + flip(mine, "fsdp", bit, SHARDS).astype(F32)
    return held


def both_cores(mine, dp):
    other = flip(mine, "dp", 0, 2)
    return jnp.where(dp == 0, mine, other), jnp.where(dp == 0, other, mine)


def per_device(shard_count, patches, prompts, cls_token, attn_in, attn_out, feed_in, feed_out, token_operator,
               norm_gains, branch_scales, var_counts, dataset_ids, cotangent, adjust_cotangent):
    dp = lax.axis_index("dp")
    fast = shard_count == SHARDS
    if fast:
        mine, other = gather_rows(attn_in, attn_out, feed_in, feed_out)
    else:
        whole_down = lax.all_gather(feed_out, "fsdp", axis=1, tiled=True)
        whole_down = whole_down.reshape(2, SHARDS, 4, 8, 128).transpose(0, 2, 1, 3, 4).reshape(2, 512, 128)
        rows = pack_rows(
            lax.all_gather(attn_in, "fsdp", axis=2, tiled=True),
            lax.all_gather(attn_out, "fsdp", axis=2, tiled=True),
            lax.all_gather(feed_in, "fsdp", axis=1, tiled=True),
            whole_down,
        )
        rows = rows.reshape(2, SHARDS, 8, COLS).transpose(1, 0, 2, 3)
        mine, other = rows[:, 0], rows[:, 1]
    output, patch_grad, big, small = run_tower(
        fast, dataset_ids, var_counts, mine, other, token_operator, norm_gains, branch_scales, patches, prompts,
        cls_token.reshape(1, -1), cotangent, adjust_cotangent,
    )
    if fast:
        layer_grads = both_cores(reduce_big(big), dp)
        grads = unpack_rows(jnp.stack(layer_grads))
        tokens, rest = both_cores(reduce_small(small), dp)
    else:
        rows = big.astype(F32).reshape(2, 128, COLS)
        attn_in_g, attn_out_g, feed_in_g, feed_out_g = unpack_rows(rows)
        feed_out_g = feed_out_g.reshape(2, 4, SHARDS, 8, 128).transpose(0, 2, 1, 3, 4).reshape(2, 512, 128)
        grads = (
            lax.psum_scatter(lax.psum(attn_in_g, "dp"), "fsdp", scatter_dimension=2, tiled=True),
            lax.psum_scatter(lax.psum(attn_out_g, "dp"), "fsdp", scatter_dimension=2, tiled=True),
            lax.psum_scatter(lax.psum(feed_in_g, "dp"), "fsdp", scatter_dimension=1, tiled=True),
            lax.psum_scatter(lax.psum(feed_out_g, "dp"), "fsdp", scatter_dimension=1, tiled=True),
        )
        tokens, rest = lax.psum(small, ("dp", "fsdp"))
    token_grad = tokens.reshape(2, 128, 128)
    gains_grad = rest[:8, 10].reshape(2, 4, 128)
    scales_grad = rest[:8, 11].reshape(2, 4, 128)
    return (
        output, patch_grad, rest[:8, :10], rest[0, 12], *grads, token_grad, gains_grad, scales_grad,
        rest[8:, :10], rest[8, 12],
    )


def solution(mesh):
    batch = P(("dp", "fsdp"), None, None, None)
    wide = P(None, None, "fsdp", None)
    tall = P(None, "fsdp", None)
    return jax.shard_map(
        functools.partial(per_device, mesh.shape["fsdp"]),
        mesh=mesh,
        in_specs=(batch, P(), P(), wide, wide, tall, tall, P(), P(), P(), P(), P(("dp", "fsdp")), batch, batch),
        out_specs=(batch, batch, P(), P(), wide, wide, tall, tall, P(), P(), P(), P(), P()),
        check_vma=False,
    )
```

time: 1610 us -> 141 us (0.09)
  waiting for transfers between devices: 842 us -> 19.2 us
  blocking collectives: 311 us -> 27 us
  matrix products: 229 us -> 0 us
  local copies, waits for them, and re-layouts: 136 us -> 8.96 us
  Pallas kernels: 0 us -> 71.6 us
  other arithmetic: 66 us -> 4.08 us
    reduce_scatter x8 -> x0, waiting for transfers between devices: 575 us -> none  [the longest x2 250 us: per_device(): lax.psum_scatter(matrix_grads[0], 'fsdp', scatter_dimension=1, tiled=True)]
    all_gather x8 -> x0, blocking collectives: 311 us -> none  [the longest x2 78.9 us: per_device(): lax.all_gather(feed_output_weights[layer_idx], 'fsdp', axis=0, tiled=True)]
    psum x3 -> x0, waiting for transfers between devices: 267 us -> none  [the longest x2 256 us: per_device(): lax.psum((token_local, gains_local, scales_local, prompt_local, cls_local...]
    dot_general x125 -> x0, matrix products: 205 us -> none  [the longest x4 35.7 us: var_back(): jnp.einsum('bqlhc,bklhc->blhqk', grad_heads, value_rows, preferred_elemen...]
    pallas_call x0 -> x2, Pallas kernels: none -> 71.6 us  [the longest x1 69.8 us: run_tower(): pl.pallas_call(functools.partial(tower_kernel, split), out_shape=(jax.Sha...]
    reshape x10 -> x0, local copies, waits for them, and re-layouts: 37.6 us -> none  [heads_of(): return block.reshape(block.shape[:-1] + (HEADS, block.shape[-1] // HEADS))]
    mul x9 -> x0, local copies, waits for them, and re-layouts: 30 us -> none  [the longest x4 15.4 us: var_back(): jnp.einsum('blhqk,bqlhc->bklhc', grad_score, queries, preferred_element_t...]
    all_to_all x0 -> x1, blocking collectives: none -> 27 us  [gather_rows(): mine = lax.all_to_all(row, 'fsdp', 0, 0, tiled=True)]
  transfers between devices with their start and end apart: 11 -> 10, of which waited for: 10 -> 7; matrix products, arithmetic and copies ran while one was open for 12% -> 6% of each run, Pallas kernels for 0% -> 0%
where the time goes in v1:
time: 141 us; the launch traced here: 140 us
  Pallas kernels  71.6 us (51%)
  blocking collectives  27 us (19%)
  waiting for transfers between devices  19.2 us (14%)
  local copies, waits for them, and re-layouts  8.96 us (6%)
  starting transfers between devices  8.77 us (6%)
  other arithmetic  4.08 us (3%)
    pallas_call x1, Pallas kernels, run_tower(): pl.pallas_call(functools.partial(tower_kernel, split), out_shape=(jax.Sha...  69.8 us
    all_to_all x1, blocking collectives, gather_rows(): mine = lax.all_to_all(row, 'fsdp', 0, 0, tiled=True)  27 us
    ppermute x9, waiting for transfers between devices, flip(): return lax.ppermute(array, axis, [(i, i ^ 1 << bit) for i in range(size)])  16.8 us
    unnamed x19, local copies, waits for them, and re-layouts  5.69 us
    ppermute x9, starting transfers between devices, flip(): return lax.ppermute(array, axis, [(i, i ^ 1 << bit) for i in range(size)])  4.53 us
    all_to_all x1, starting transfers between devices, reduce_big(): parts = lax.all_to_all(held.astype(BF), 'fsdp', 0, 0, tiled=True)  4.23 us
  transfers between devices with their start and end apart: 10, of which 7 were waited for; matrix products, arithmetic and copies ran while one was open for 6% of the time, Pallas kernels for 0%

profile of v1, /device:TPU:0, one launch (start us, length us, event | category | flops | bytes accessed | tf_op | source)
XLA Modules:
  0.0 140.4 jit_solution(1724547520172546205)
XLA Ops:
  0.6 0.0 copy-start.4
  0.7 0.0 copy-start.5
  0.7 1.8 %pack.1 = bf16[16,8,2560]{2,1,0:T(8,128)(2,1)} custom-call(bf16[2,2,8,384]{3,2,1,0:T(8,128)(2,1)} %attn_in_ref.1, bf16[2,2,8,128]{3,2,1,0:T(8,128)(2,1)} %attn_out_ref.1, bf16[2,8,1024]{2,1,0:T(8,128)(2,1)} %feed_in_ref.1, bf16[2,32,128]{2,1,0:T(8,128)(2,1)} %feed_out_ref.1), custom_call_target="tpu_custom_call" | custom-call | tf_op jit(solution)/shard_map/pack/pallas_call | solution.py:479
  2.4 27.0 %all_to_all.10.wmine_ref = bf16[16,8,2560]{2,1,0:T(8,128)(2,1)S(1)} all-to-all(bf16[16,8,2560]{2,1,0:T(8,128)(2,1)} %pack.1), channel_id=1, replica_groups=mesh['dp'=2,'fsdp'=16] {'fsdp'}, dimensions={0} | all-to-all | bytes 1310720 | tf_op jit(solution)/shard_map/all_to_all | solution.py:482
  29.5 0.0 collective-permute-start
  29.5 0.0 copy-done.4
  29.5 0.8 copy.27.patches_ref
  30.3 0.0 copy-done.5
  30.3 0.6 copy.28.prompts_ref
  30.9 0.6 collective-permute-done.wother_ref
  31.6 0.0 copy-done
  31.6 0.8 copy-done.2
  32.4 69.8 %tower.1 = (bf16[2,4,128,128]{3,2,1,0:T(8,128)(2,1)}, f32[2,4,117,128]{3,2,1,0:T(8,128)}, bf16[2,16,8,2560]{3,2,1,0:T(8,128)(2,1)}, f32[2,16,16,128]{3,2,1,0:T(8,128)}) custom-call(s32[2]{0:T(128)} %ids_ref.1, s32[8]{0:T(128)} %counts_ref.1, bf16[16,8,2560]{2,1,0:T(8,128)(2,1)} %copy-done, bf16[16,8,2560]{2,1,0:T(8,128)(2,1)} %copy-done.2, ...), custom_call_target="tpu_custom_call" | custom-call | tf_op jit(solution)/shard_map/tower/pallas_call | solution.py:413
  102.2 1.0 fusion.2
  103.3 0.2 collective-permute-start.1
  103.5 1.1 slice_bitcast_fusion
  104.6 0.4 collective-permute-start.7
  105.0 0.0 collective-permute-done.1
  105.0 0.9 fusion.1
  106.0 0.7 collective-permute-start.2
  106.7 3.6 %collective-permute-done.2 = bf16[16,16,128]{2,1,0:T(8,128)(2,1)S(1)} collective-permute-done((bf16[16,16,128]{2,1,0:T(8,128)(2,1)S(1)}, bf16[16,16,128]{2,1,0:T(8,128)(2,1)S(1)}, u32[]{:S(2)}, u32[]{:S(2)}) %collective-permute-start.2) | collective-permute-done | bytes 65568 | tf_op jit(solution)/shard_map/ppermute | solution.py:474
  110.3 0.6 collective-permute-start.3
  111.0 3.7 %collective-permute-done.3 = bf16[16,16,128]{2,1,0:T(8,128)(2,1)S(1)} collective-permute-done((bf16[16,16,128]{2,1,0:T(8,128)(2,1)S(1)}, bf16[16,16,128]{2,1,0:T(8,128)(2,1)S(1)}, u32[]{:S(2)}, u32[]{:S(2)}) %collective-permute-start.3) | collective-permute-done | bytes 65568 | tf_op jit(solution)/shard_map/ppermute | solution.py:474
  114.7 0.5 collective-permute-start.4
  115.2 0.0 collective-permute-done.7
  115.2 0.0 copy-done.1
  115.2 1.0 fusion
  116.2 4.2 %all-to-all-start.1 = ((bf16[16,8,2560]{2,1,0:T(8,128)(2,1)}), bf16[16,8,2560]{2,1,0:T(8,128)(2,1)S(1)}, u32[]{:S(2)}, u32[]{:S(2)}) async-start(bf16[16,8,2560]{2,1,0:T(8,128)(2,1)} %fusion), calls=%async_computation.1 | async-start | bytes 1310720 | tf_op jit(solution)/shard_map/all_to_all | solution.py:488
  120.5 0.1 collective-permute-done.4
  120.6 1.9 %collective-permute-start.5 = (bf16[16,16,128]{2,1,0:T(8,128)(2,1)S(1)}, bf16[16,16,128]{2,1,0:T(8,128)(2,1)S(1)}, u32[]{:S(2)}, u32[]{:S(2)}) collective-permute-start(bf16[16,16,128]{2,1,0:T(8,128)(2,1)S(1)} %add_convert_fusion), channel_id=1, source_target_pairs={{0,4},{1,5},{2,6},{3,7},{4,0},{5,1},{6,2},{7,3},{8,12},{9,13},{10,... | collective-permute-start | bytes 196616 | tf_op jit(solution)/shard_map/ppermute | solution.py:474
  122.5 8.3 %collective-permute-done.5 = bf16[16,16,128]{2,1,0:T(8,128)(2,1)S(1)} collective-permute-done((bf16[16,16,128]{2,1,0:T(8,128)(2,1)S(1)}, bf16[16,16,128]{2,1,0:T(8,128)(2,1)S(1)}, u32[]{:S(2)}, u32[]{:S(2)}) %collective-permute-start.5) | collective-permute-done | bytes 65568 | tf_op jit(solution)/shard_map/ppermute | solution.py:474
  130.8 0.1 collective-permute-start.6
  130.9 0.0 copy-done.3
  130.9 0.9 copy.30
  131.8 0.4 collective-permute-done.6
  132.2 0.7 broadcast_select_fusion
  132.9 0.6 fusion.20
  133.5 2.4 %all-to-all-done.1 = bf16[16,8,2560]{2,1,0:T(8,128)(2,1)S(1)} async-done(((bf16[16,8,2560]{2,1,0:T(8,128)(2,1)}), bf16[16,8,2560]{2,1,0:T(8,128)(2,1)S(1)}, u32[]{:S(2)}, u32[]{:S(2)}) %all-to-all-start.1) | async-done | bytes 655392 | tf_op jit(solution)/shard_map/all_to_all | solution.py:488
  135.9 0.1 convert_reduce_fusion
  136.0 0.1 collective-permute-start.8
  136.1 0.5 slice_bitcast_fusion.1
  136.6 0.6 copy.31
  137.3 0.6 copy.34
  137.9 0.0 collective-permute-done.8
  137.9 0.6 fusion.3
  138.6 0.6 copy.33
  139.2 0.6 copy.32
  139.8 0.6 copy_bitcast_fusion
  (14 shorter events, 0.1 us)
Async XLA Ops:
  0.6 28.8 %copy-start.4 = (bf16[2,4,117,128]{3,1,2,0:T(4,128)(2,1)S(1)}, bf16[2,4,117,128]{3,1,2,0:T(4,128)(2,1)}, u32[]{:S(2)}) copy-start(bf16[2,4,117,128]{3,1,2,0:T(4,128)(2,1)} %param.14) | copy-start | bytes 718852
  0.7 29.6 %copy-start.5 = (bf16[8,10,128]{2,0,1:T(8,128)(2,1)S(1)}, bf16[8,10,128]{2,0,1:T(8,128)(2,1)}, u32[]{:S(2)}) copy-start(bf16[8,10,128]{2,0,1:T(8,128)(2,1)} %param.15) | copy-start | bytes 61444
  29.5 2.1 %copy-start = (bf16[16,8,2560]{2,1,0:T(8,128)(2,1)}, bf16[16,8,2560]{2,1,0:T(8,128)(2,1)S(1)}, u32[]{:S(2)}) copy-start(bf16[16,8,2560]{2,1,0:T(8,128)(2,1)S(1)} %all_to_all.10.wmine_ref) | copy-start | bytes 1966084
  29.5 2.1 %collective-permute-start = (bf16[16,8,2560]{2,1,0:T(8,128)(2,1)S(1)}, bf16[16,8,2560]{2,1,0:T(8,128)(2,1)S(1)}, u32[]{:S(2)}, u32[]{:S(2)}) collective-permute-start(bf16[16,8,2560]{2,1,0:T(8,128)(2,1)S(1)} %all_to_all.10.wmine_ref), channel_id=1, source_target_pairs={{0,16},{16,0},{1,17},{17,1},{2,18},{18,2},{3,19},{19,3},{4,20},{20... | collective-permute-start | bytes 1966088 | tf_op jit(solution)/shard_map/ppermute | solution.py:474
  31.6 0.8 copy-start.2
  102.2 13.0 %copy-start.1 = (bf16[2,16,8,2560]{3,2,1,0:T(8,128)(2,1)S(1)}, bf16[2,16,8,2560]{3,2,1,0:T(8,128)(2,1)}, u32[]{:S(2)}) copy-start(bf16[2,16,8,2560]{3,2,1,0:T(8,128)(2,1)} %get-tuple-element.20) | copy-start | bytes 3932164
  103.3 1.8 %collective-permute-start.1 = (bf16[16,16,128]{2,1,0:T(8,128)(2,1)S(1)}, bf16[16,16,128]{2,1,0:T(8,128)(2,1)S(1)}, u32[]{:S(2)}, u32[]{:S(2)}) collective-permute-start(bf16[16,16,128]{2,1,0:T(8,128)(2,1)S(1)} %fusion.2), channel_id=1, source_target_pairs={{0,16},{16,0},{1,17},{17,1},{2,18},{18,2},{3,19},{19,3},{4,20},{20... | collective-permute-start | bytes 196616 | tf_op jit(solution)/shard_map/ppermute | solution.py:474
  104.6 10.6 %collective-permute-start.7 = (bf16[16,8,2560]{2,1,0:T(8,128)(2,1)S(1)}, bf16[16,8,2560]{2,1,0:T(8,128)(2,1)S(1)}, u32[]{:S(2)}, u32[]{:S(2)}) collective-permute-start(bf16[16,8,2560]{2,1,0:T(8,128)(2,1)S(1)} %slice_bitcast_fusion), channel_id=1, source_target_pairs={{0,16},{16,0},{1,17},{17,1},{2,18},{18,2},{3,19},{19,3},{4,20},{20... | collective-permute-start | bytes 1966088 | tf_op jit(solution)/shard_map/ppermute | solution.py:474
  106.0 4.3 %collective-permute-start.2 = (bf16[16,16,128]{2,1,0:T(8,128)(2,1)S(1)}, bf16[16,16,128]{2,1,0:T(8,128)(2,1)S(1)}, u32[]{:S(2)}, u32[]{:S(2)}) collective-permute-start(bf16[16,16,128]{2,1,0:T(8,128)(2,1)S(1)} %fusion.1), channel_id=1, source_target_pairs={{0,2},{1,3},{2,0},{3,1},{4,6},{5,7},{6,4},{7,5},{8,10},{9,11},{10,... | collective-permute-start | bytes 196616 | tf_op jit(solution)/shard_map/ppermute | solution.py:474
  110.3 4.3 %collective-permute-start.3 = (bf16[16,16,128]{2,1,0:T(8,128)(2,1)S(1)}, bf16[16,16,128]{2,1,0:T(8,128)(2,1)S(1)}, u32[]{:S(2)}, u32[]{:S(2)}) collective-permute-start(bf16[16,16,128]{2,1,0:T(8,128)(2,1)S(1)} %add_convert_fusion.2), channel_id=1, source_target_pairs={{0,1},{1,0},{2,3},{3,2},{4,5},{5,4},{6,7},{7,6},{8,9},{9,8},{10,11... | collective-permute-start | bytes 196616 | tf_op jit(solution)/shard_map/ppermute | solution.py:474
  114.7 5.9 %collective-permute-start.4 = (bf16[16,16,128]{2,1,0:T(8,128)(2,1)S(1)}, bf16[16,16,128]{2,1,0:T(8,128)(2,1)S(1)}, u32[]{:S(2)}, u32[]{:S(2)}) collective-permute-start(bf16[16,16,128]{2,1,0:T(8,128)(2,1)S(1)} %add_convert_fusion.1), channel_id=1, source_target_pairs={{0,8},{1,9},{2,10},{3,11},{4,12},{5,13},{6,14},{7,15},{8,0},{9,1},... | collective-permute-start | bytes 196616 | tf_op jit(solution)/shard_map/ppermute | solution.py:474
  116.2 14.7 %copy-start.3 = (f32[2,4,117,128]{3,2,1,0:T(8,128)S(1)}, f32[2,4,117,128]{3,2,1,0:T(8,128)}, u32[]{:S(2)}) copy-start(f32[2,4,117,128]{3,2,1,0:T(8,128)} %get-tuple-element.22) | copy-start | bytes 1437700
  116.2 19.7 %all-to-all-start.1 = ((bf16[16,8,2560]{2,1,0:T(8,128)(2,1)}), bf16[16,8,2560]{2,1,0:T(8,128)(2,1)S(1)}, u32[]{:S(2)}, u32[]{:S(2)}) async-start(bf16[16,8,2560]{2,1,0:T(8,128)(2,1)} %fusion), calls=%async_computation.1 | async-start | bytes 1310720 | tf_op jit(solution)/shard_map/all_to_all | solution.py:488
  120.6 10.1 %collective-permute-start.5 = (bf16[16,16,128]{2,1,0:T(8,128)(2,1)S(1)}, bf16[16,16,128]{2,1,0:T(8,128)(2,1)S(1)}, u32[]{:S(2)}, u32[]{:S(2)}) collective-permute-start(bf16[16,16,128]{2,1,0:T(8,128)(2,1)S(1)} %add_convert_fusion), channel_id=1, source_target_pairs={{0,4},{1,5},{2,6},{3,7},{4,0},{5,1},{6,2},{7,3},{8,12},{9,13},{10,... | collective-permute-start | bytes 196616 | tf_op jit(solution)/shard_map/ppermute | solution.py:474
  130.8 1.4 %collective-permute-start.6 = (f32[16,16,128]{2,1,0:T(8,128)S(1)}, f32[16,16,128]{2,1,0:T(8,128)S(1)}, u32[]{:S(2)}, u32[]{:S(2)}) collective-permute-start(f32[16,16,128]{2,1,0:T(8,128)S(1)} %convert_add_fusion.1), channel_id=1, source_target_pairs={{0,16},{16,0},{1,17},{17,1},{2,18},{18,2},{3,19},{19,3},{4,20},{20... | collective-permute-start | bytes 393224 | tf_op jit(solution)/shard_map/ppermute | solution.py:474
  136.0 1.9 %collective-permute-start.8 = (f32[8,2560]{1,0:T(8,128)S(1)}, f32[8,2560]{1,0:T(8,128)S(1)}, u32[]{:S(2)}, u32[]{:S(2)}) collective-permute-start(f32[8,2560]{1,0:T(8,128)S(1)} %convert_reduce_fusion), channel_id=1, source_target_pairs={{0,16},{16,0},{1,17},{17,1},{2,18},{18,2},{3,19},{19,3},{4,20},{20... | collective-permute-start | bytes 245768 | tf_op jit(solution)/shard_map/ppermute | solution.py:474

commit v2 on v1

--- a/solution.py
+++ b/solution.py
@@ -67,7 +67,7 @@
     cls_ref, cot_ref, adj_ref,
     out_ref, pgrad_ref, gbig_ref, gsmall_ref,
     w_ref, wd_ref, wt_ref, wdt_ref, colb_ref, tokscr_ref, h_ref, g_ref, xh_ref, inv_ref,
-    qkvt_ref, pb_ref, ot_ref, qkvv_ref, pv_ref, ov_ref, qbd_ref, dob_ref, hid_ref, du_ref, dqkv_ref,
+    qkvt_ref, pb_ref, ot_ref, qkvv_ref, pv_ref, ov_ref, pw_ref, hid_ref, du_ref, dqkv_ref,
     dov_ref, ga_ref, gd_ref, gt_ref, gacc_ref,
 ):
     dp = dp_of(split)
@@ -86,7 +86,8 @@
                     [part[:, COL_DOWN + 128 * a : COL_DOWN + 128 * a + 128] for a in range(4)], axis=0
                 ).astype(BF)
         for block in range(COL_DOWN // 128):
-            wt_ref[l, 128 * block : 128 * block + 128, :] = w_ref[l, :, 128 * block : 128 * block + 128].T
+            target = block if block < 8 else 8 + (0, 1, 4, 5, 2, 3, 6, 7)[block - 8]
+            wt_ref[l, 128 * target : 128 * target + 128, :] = w_ref[l, :, 128 * block : 128 * block + 128].T
         for block in range(4):
             wdt_ref[l, :, 128 * block : 128 * block + 128] = wd_ref[l, 128 * block : 128 * block + 128, :].T
         for k in range(4):
@@ -107,29 +108,25 @@
             g_ref[0, 2 * b + v // 2, :, lanes] = cot_ref[b, v].astype(F32).T
             g_ref[1, 2 * b + v // 2, :, lanes] = adj_ref[b, v].astype(F32).T
 
-    qbd_ref[...] = jnp.zeros_like(qbd_ref)
-    dob_ref[...] = jnp.zeros_like(dob_ref)
-
-    head_row = lax.broadcasted_iota(jnp.int32, (8, 256), 0)
-    head_col = (lax.broadcasted_iota(jnp.int32, (8, 256), 1) % 128) // 16
+    head_row = lax.broadcasted_iota(jnp.int32, (8, 128), 0)
+    head_col = lax.broadcasted_iota(jnp.int32, (8, 128), 1) // 16
     gather_heads = jnp.where(head_row == head_col, 1.0, 0.0).astype(BF)
     spread_row = lax.broadcasted_iota(jnp.int32, (128, 8), 0) // 16
     spread_col = lax.broadcasted_iota(jnp.int32, (128, 8), 1)
     spread_heads = jnp.where(spread_row == spread_col, 1.0, 0.0).astype(BF)
 
     def head_sums(left, rights):
-        his, los = [], []
-        for right in rights:
-            prod = left * right
-            hi = prod.astype(BF)
-            his.append(hi)
-            los.append((prod - hi.astype(F32)).astype(BF))
-        both = jnp.concatenate([jnp.concatenate(his, axis=1), jnp.concatenate(los, axis=1)], axis=0)
-        return dot_nn(gather_heads, both)
-
-    def diag_heads(target_ref, s, rows):
-        for head in range(HEADS):
-            target_ref[s, 16 * head : 16 * head + 16, 128 * head : 128 * head + 128] = rows[16 * head : 16 * head + 16]
+        return dot_nn(gather_heads, jnp.concatenate([left * right for right in rights], axis=1))
+
+    blank = jnp.zeros((16, 128), BF)
+
+    def diag_pair(rows):
+        upper = jnp.concatenate([rows[:16], blank], axis=1)
+        return jnp.concatenate([upper, jnp.concatenate([blank, rows[16:]], axis=1)], axis=0)
+
+    def diag_full(pair, hp):
+        parts = [pair if at == hp else jnp.zeros_like(pair) for at in range(4)]
+        return jnp.concatenate(parts, axis=0)
 
     def gain(l, k):
         return colb_ref[l * 8 + k]
@@ -155,12 +152,11 @@
         qkvt_ref[l, c, 256:384, :] = values
         for s in range(2):
             lanes = slice(128 * s, 128 * s + 128)
-            diag_heads(qbd_ref, s, queries[:, lanes])
             key_rows = keys[:, lanes].T
             for hp in range(4):
                 span = slice(256 * hp, 256 * hp + 256)
                 rows = slice(32 * hp, 32 * hp + 32)
-                scores = dot_nn(key_rows, qbd_ref[s, :, span])
+                scores = dot_nn(key_rows, diag_full(diag_pair(queries[rows, lanes]), hp))
                 shifted = jnp.exp(scores - jnp.max(scores, axis=0, keepdims=True))
                 prob = (shifted * (1.0 / jnp.sum(shifted, axis=0, keepdims=True))).astype(BF)
                 pb_ref[l, 2 * c + s, :, span] = prob
@@ -181,10 +177,10 @@
 
         def slot(first, i):
             lanes = slice(128 * (i % 2), 128 * (i % 2) + 128)
-            return qkvv_ref[l, 2 * b + i // 2, first : first + 128, lanes].astype(F32)
+            return qkvv_ref[l, 2 * b + i // 2, first : first + 128, lanes]
 
         key_slots = [slot(128, j) for j in range(4)]
-        value_slots = [slot(256, j) for j in range(4)]
+        value_slots = [slot(256, j).astype(F32) for j in range(4)]
         for i in range(4):
             scores = head_sums(slot(0, i), key_slots)
             parts = [scores[:, 128 * j : 128 * j + 128] for j in range(4)]
@@ -195,6 +191,7 @@
             prob = jnp.concatenate([part * total for part in shifted], axis=1)
             pv_ref[l, b, i] = prob
             spread = dot_nn(spread_heads, prob.astype(BF))
+            pw_ref[l, b, i] = spread.astype(BF)
             mixed = spread[:, :128] * value_slots[0]
             for j in range(1, 4):
                 mixed = mixed + spread[:, 128 * j : 128 * j + 128] * value_slots[j]
@@ -205,18 +202,26 @@
             branch = dot_nn(wt_ref[l, COL_OUT[1] : COL_OUT[1] + 128, :], ov_ref[l, c])
             h_ref[c] = h_ref[c] + scale(l, 1) * branch
 
+    def stacked(rows):
+        return jnp.concatenate([rows[:, :128], rows[:, 128:]], axis=0)
+
+    def unstacked(rows):
+        return jnp.concatenate([rows[:128], rows[128:]], axis=1)
+
+    def gate_and_up(l, z, n):
+        joint = dot_nn(wt_ref[l, COL_FEED + 512 * z : COL_FEED + 512 * z + 512, :], n)
+        gate, up = joint[:256], joint[256:]
+        return gate, up, 0.5 * jnp.tanh(0.5 * gate) + 0.5
+
     def tail_forward(l, c):
         x = h_ref[c]
         n = keep_norm(l, 2, c, x)
-        mix = [dot_nt(n[:, 128 * s : 128 * s + 128], tok_ref[l]) for s in range(2)]
-        x = x + scale(l, 2) * jnp.concatenate(mix, axis=1)
+        x = x + scale(l, 2) * unstacked(dot_nt(stacked(n), tok_ref[l]))
         n = keep_norm(l, 3, c, x)
-        for z in range(4):
-            gate = dot_nn(wt_ref[l, COL_FEED + 128 * z : COL_FEED + 128 * z + 128, :], n)
-            up = dot_nn(wt_ref[l, COL_FEED + 512 + 128 * z : COL_FEED + 640 + 128 * z, :], n)
-            sig = 0.5 * jnp.tanh(0.5 * gate) + 0.5
-            hid_ref[128 * z : 128 * z + 128, :] = (gate * sig * up).astype(BF)
-        h_ref[c] = x + scale(l, 3) * dot_nn(wdt_ref[l], hid_ref[...])
+        for z in range(2):
+            gate, up, sig = gate_and_up(l, z, n)
+            hid_ref[c % 2, 256 * z : 256 * z + 256, :] = (gate * sig * up).astype(BF)
+        h_ref[c] = x + scale(l, 3) * dot_nn(wdt_ref[l], hid_ref[c % 2])
 
     def norm_of(l, k, c):
         xhat = xh_ref[l * 4 + k, c]
@@ -230,78 +235,70 @@
     def feed_backward(l, c):
         xhat, inv, n = norm_of(l, 3, c)
         dz = [(scale(l, 3) * g_ref[x, c]).astype(BF) for x in range(2)]
-        for z in range(4):
-            rows = slice(128 * z, 128 * z + 128)
-            gate = dot_nn(wt_ref[l, COL_FEED + 128 * z : COL_FEED + 128 * z + 128, :], n)
-            up = dot_nn(wt_ref[l, COL_FEED + 512 + 128 * z : COL_FEED + 640 + 128 * z, :], n)
-            sig = 0.5 * jnp.tanh(0.5 * gate) + 0.5
+        for z in range(2):
+            rows = slice(256 * z, 256 * z + 256)
+            gate, up, sig = gate_and_up(l, z, n)
             act = gate * sig
-            hid_ref[rows, :] = (act * up).astype(BF)
+            hid_ref[c % 2, rows, :] = (act * up).astype(BF)
             slope = up * (sig * (1.0 + gate * (1.0 - sig)))
             for x in range(2):
                 dhid = dot_nn(wd_ref[l, rows, :], dz[x])
-                du_ref[x, 128 * z : 128 * z + 128, :] = (dhid * slope).astype(BF)
-                du_ref[x, 512 + 128 * z : 640 + 128 * z, :] = (dhid * act).astype(BF)
-        ga_ref[:, COL_FEED:COL_DOWN] += dot_nt(n, du_ref[0])
-        gd_ref[...] += dot_nt(hid_ref[...], dz[0])
+                du_ref[2 * (c % 2) + x, 256 * z : 256 * z + 256, :] = (dhid * slope).astype(BF)
+                du_ref[2 * (c % 2) + x, 512 + 256 * z : 768 + 256 * z, :] = (dhid * act).astype(BF)
+        ga_ref[:, COL_FEED:COL_DOWN] += dot_nt(n, du_ref[2 * (c % 2)])
+        gd_ref[...] += dot_nt(hid_ref[c % 2], dz[0])
         for x in range(2):
-            dn = dot_nn(w_ref[l, :, COL_FEED:COL_DOWN], du_ref[x])
+            dn = dot_nn(w_ref[l, :, COL_FEED:COL_DOWN], du_ref[2 * (c % 2) + x])
             pass_on(l, 3, c, x, dn, xhat, inv)
 
     def token_backward(l, c):
         xhat, inv, n = norm_of(l, 2, c)
         for x in range(2):
-            dy = (scale(l, 2) * g_ref[x, c]).astype(BF)
-            dn = []
-            for s in range(2):
-                part = dy[:, 128 * s : 128 * s + 128]
-                dn.append(dot_nn(part, tok_ref[l]))
-                if x == 0:
-                    gt_ref[l] += dot_nn(part.T, n[:, 128 * s : 128 * s + 128])
-            pass_on(l, 2, c, x, jnp.concatenate(dn, axis=1), xhat, inv)
+            dy = stacked((scale(l, 2) * g_ref[x, c]).astype(BF))
+            if x == 0:
+                turned = jnp.concatenate([dy[:128].T, dy[128:].T], axis=1)
+                gt_ref[l] += dot_nn(turned, stacked(n))
+            pass_on(l, 2, c, x, unstacked(dot_nn(dy, tok_ref[l])), xhat, inv)
 
     def var_backward(l, b):
         def slot(first, i):
             lanes = slice(128 * (i % 2), 128 * (i % 2) + 128)
-            return qkvv_ref[l, 2 * b + i // 2, first : first + 128, lanes].astype(F32)
+            return qkvv_ref[l, 2 * b + i // 2, first : first + 128, lanes]
 
         for x in range(2):
             for cc in range(2):
                 c = 2 * b + cc
                 dt = (scale(l, 1) * g_ref[x, c]).astype(BF)
-                dov_ref[cc] = dot_nn(w_ref[l, :, COL_OUT[1] : COL_OUT[1] + 128], dt).astype(BF)
+                dov_ref[4 * b + 2 * x + cc] = dot_nn(w_ref[l, :, COL_OUT[1] : COL_OUT[1] + 128], dt).astype(BF)
                 if x == 0:
                     ga_ref[:, COL_OUT[1] : COL_OUT[1] + 128] += dot_nt(ov_ref[l, c], dt)
             value_slots = [slot(256, j) for j in range(4)]
-            dkeys = [None] * 4
-            dvalues = [None] * 4
+            dkeys = [[] for _ in range(4)]
+            dvalues = [[] for _ in range(4)]
             for i in range(4):
                 lanes = slice(128 * (i % 2), 128 * (i % 2) + 128)
-                grad = dov_ref[i // 2, :, lanes].astype(F32)
+                grad = dov_ref[4 * b + 2 * x + i // 2, :, lanes]
                 query = slot(0, i)
                 prob = pv_ref[l, b, i]
                 weighted = prob * head_sums(grad, value_slots)
                 total = (weighted[:, :128] + weighted[:, 128:256]) + (weighted[:, 256:384] + weighted[:, 384:])
                 ds = weighted - prob * jnp.concatenate([total] * 4, axis=1)
-                ds_wide = dot_nn(spread_heads, ds.astype(BF))
-                p_wide = dot_nn(spread_heads, prob.astype(BF))
-                dquery = None
+                ds_wide = dot_nn(spread_heads, ds.astype(BF)).astype(BF)
+                ds_slots = [ds_wide[:, 128 * j : 128 * j + 128] for j in range(4)]
+                terms = [ds_slots[j] * slot(128, j) for j in range(4)]
+                dquery = (terms[0] + terms[1]) + (terms[2] + terms[3])
                 for j in range(4):
-                    ds_j = ds_wide[:, 128 * j : 128 * j + 128]
-                    p_j = p_wide[:, 128 * j : 128 * j + 128]
-                    terms = (ds_j * slot(128, j), ds_j * query, p_j * grad)
-                    dquery = terms[0] if dquery is None else dquery + terms[0]
-                    dkeys[j] = terms[1] if dkeys[j] is None else dkeys[j] + terms[1]
-                    dvalues[j] = terms[2] if dvalues[j] is None else dvalues[j] + terms[2]
-                dqkv_ref[i // 2, 0:128, lanes] = (0.25 * dquery).astype(BF)
+                    dkeys[j].append(ds_slots[j] * query)
+                    dvalues[j].append(pw_ref[l, b, i, :, 128 * j : 128 * j + 128] * grad)
+                dqkv_ref[4 * b + 2 * x + i // 2, 0:128, lanes] = dquery * jnp.asarray(0.25, BF)
             for j in range(4):
                 lanes = slice(128 * (j % 2), 128 * (j % 2) + 128)
-                dqkv_ref[j // 2, 128:256, lanes] = dkeys[j].astype(BF)
-                dqkv_ref[j // 2, 256:384, lanes] = dvalues[j].astype(BF)
+                dqkv_ref[4 * b + 2 * x + j // 2, 128:256, lanes] = (dkeys[j][0] + dkeys[j][1]) + (dkeys[j][2] + dkeys[j][3])
+                dqkv_ref[4 * b + 2 * x + j // 2, 256:384, lanes] = (dvalues[j][0] + dvalues[j][1]) + (dvalues[j][2] + dvalues[j][3])
             for cc in range(2):
                 c = 2 * b + cc
                 xhat, inv, n = norm_of(l, 1, c)
-                dqkv = dqkv_ref[cc]
+                dqkv = dqkv_ref[4 * b + 2 * x + cc]
                 if x == 0:
                     ga_ref[:, COL_IN[1] : COL_IN[1] + 384] += dot_nt(n, dqkv)
                 pass_on(l, 1, c, x, dot_nn(w_ref[l, :, COL_IN[1] : COL_IN[1] + 384], dqkv), xhat, inv)
@@ -319,31 +316,31 @@
                 ga_ref[:, COL_OUT[0] : COL_OUT[0] + 128] += dot_nt(ot_ref[l, c], dt)
         for s in range(2):
             lanes = slice(128 * s, 128 * s + 128)
-            diag_heads(qbd_ref, s, queries[:, lanes])
             value_rows = values[:, lanes].T
-            for x in range(2):
-                diag_heads(dob_ref, 2 * x + s, grads[x][:, lanes])
             for hp in range(4):
                 span = slice(256 * hp, 256 * hp + 256)
                 rows = slice(32 * hp, 32 * hp + 32)
                 prob_bf = pb_ref[l, 2 * c + s, :, span]
                 prob = prob_bf.astype(F32)
+                query_pair = diag_pair(queries[rows, lanes])
                 for x in range(2):
-                    weighted = prob * dot_nn(value_rows, dob_ref[2 * x + s, :, span])
+                    grad_pair = diag_pair(grads[x][rows, lanes])
+                    weighted = prob * dot_nn(value_rows, diag_full(grad_pair, hp))
                     ds = (weighted - prob * jnp.sum(weighted, axis=0, keepdims=True)).astype(BF)
-                    dvalue = dot_nt(dob_ref[2 * x + s, rows, span], prob_bf)
+                    dvalue = dot_nt(grad_pair, prob_bf)
                     dquery = dot_nn(keys[rows, lanes], ds) * 0.25
-                    dkey = dot_nt(qbd_ref[s, rows, span], ds)
-                    dqkv_ref[x, 32 * hp : 32 * hp + 16, lanes] = dquery[:16, :128].astype(BF)
-                    dqkv_ref[x, 32 * hp + 16 : 32 * hp + 32, lanes] = dquery[16:, 128:].astype(BF)
-                    dqkv_ref[x, 128 + 32 * hp : 160 + 32 * hp, lanes] = dkey.astype(BF)
-                    dqkv_ref[x, 256 + 32 * hp : 288 + 32 * hp, lanes] = dvalue.astype(BF)
-        ga_ref[:, COL_IN[0] : COL_IN[0] + 384] += dot_nt(n, dqkv_ref[0])
+                    dkey = dot_nt(query_pair, ds)
+                    dqkv_ref[2 * c + x, 32 * hp : 32 * hp + 16, lanes] = dquery[:16, :128].astype(BF)
+                    dqkv_ref[2 * c + x, 32 * hp + 16 : 32 * hp + 32, lanes] = dquery[16:, 128:].astype(BF)
+                    dqkv_ref[2 * c + x, 128 + 32 * hp : 160 + 32 * hp, lanes] = dkey.astype(BF)
+                    dqkv_ref[2 * c + x, 256 + 32 * hp : 288 + 32 * hp, lanes] = dvalue.astype(BF)
+        ga_ref[:, COL_IN[0] : COL_IN[0] + 384] += dot_nt(n, dqkv_ref[2 * c])
         for x in range(2):
-            pass_on(l, 0, c, x, dot_nn(w_ref[l, :, COL_IN[0] : COL_IN[0] + 384], dqkv_ref[x]), xhat, inv)
+            pass_on(l, 0, c, x, dot_nn(w_ref[l, :, COL_IN[0] : COL_IN[0] + 384], dqkv_ref[2 * c + x]), xhat, inv)
 
     def each(count, stage, l):
-        lax.fori_loop(0, count, lambda i, carry: (stage(l, i), carry)[1], 0)
+        for i in range(count):
+            stage(l, i)
 
     def forward_layer(l, carry):
         each(chunks, time_forward, l)
@@ -437,12 +434,11 @@
             pltpu.VMEM((2, 4, 384, 256), BF),
             pltpu.VMEM((2, 2, 4, 8, 512), F32),
             pltpu.VMEM((2, 4, 128, 256), BF),
-            pltpu.VMEM((2, 128, 1024), BF),
-            pltpu.VMEM((4, 128, 1024), BF),
-            pltpu.VMEM((512, 256), BF),
-            pltpu.VMEM((2, 1024, 256), BF),
-            pltpu.VMEM((2, 384, 256), BF),
-            pltpu.VMEM((2, 128, 256), BF),
+            pltpu.VMEM((2, 2, 4, 128, 512), BF),
+            pltpu.VMEM((2, 512, 256), BF),
+            pltpu.VMEM((4, 1024, 256), BF),
+            pltpu.VMEM((8, 384, 256), BF),
+            pltpu.VMEM((8, 128, 256), BF),
             pltpu.VMEM((128, COL_DOWN), F32),
             pltpu.VMEM((512, 128), F32),
             pltpu.VMEM((2, 128, 128), F32),

time: 141 us -> 138 us (0.979)
  Pallas kernels: 71.6 us -> 68.9 us
    pallas_call x1, Pallas kernels: 69.8 us -> 67.1 us  [run_tower(): pl.pallas_call(functools.partial(tower_kernel, split), out_shape=(jax.Sha...]
where the time goes in v2:
time: 138 us
  Pallas kernels  68.9 us (50%)
  blocking collectives  27 us (20%)
  waiting for transfers between devices  19.2 us (14%)
  local copies, waits for them, and re-layouts  8.96 us (6%)
  starting transfers between devices  8.75 us (6%)
  other arithmetic  4.08 us (3%)
    pallas_call x1, Pallas kernels, run_tower(): pl.pallas_call(functools.partial(tower_kernel, split), out_shape=(jax.Sha...  67.1 us
    all_to_all x1, blocking collectives, gather_rows(): mine = lax.all_to_all(row, 'fsdp', 0, 0, tiled=True)  27 us
    ppermute x9, waiting for transfers between devices, flip(): return lax.ppermute(array, axis, [(i, i ^ 1 << bit) for i in range(size)])  16.8 us
    unnamed x19, local copies, waits for them, and re-layouts  5.69 us
    ppermute x9, starting transfers between devices, flip(): return lax.ppermute(array, axis, [(i, i ^ 1 << bit) for i in range(size)])  4.53 us
    all_to_all x1, starting transfers between devices, reduce_big(): parts = lax.all_to_all(held.astype(BF), 'fsdp', 0, 0, tiled=True)  4.23 us
  transfers between devices with their start and end apart: 10, of which 7 were waited for; matrix products, arithmetic and copies ran while one was open for 6% of the time, Pallas kernels for 0%

profile of v2, /device:TPU:0, one launch (start us, length us, event | category | flops | bytes accessed | tf_op | source)
XLA Modules:
  0.0 137.7 jit_solution(15928932566589208426)
XLA Ops:
  0.6 0.0 copy-start.4
  0.7 0.0 copy-start.5
  0.7 1.8 %pack.1 = bf16[16,8,2560]{2,1,0:T(8,128)(2,1)} custom-call(bf16[2,2,8,384]{3,2,1,0:T(8,128)(2,1)} %attn_in_ref.1, bf16[2,2,8,128]{3,2,1,0:T(8,128)(2,1)} %attn_out_ref.1, bf16[2,8,1024]{2,1,0:T(8,128)(2,1)} %feed_in_ref.1, bf16[2,32,128]{2,1,0:T(8,128)(2,1)} %feed_out_ref.1), custom_call_target="tpu_custom_call" | custom-call | tf_op jit(solution)/shard_map/pack/pallas_call | solution.py:475
  2.4 27.0 %all_to_all.10.wmine_ref = bf16[16,8,2560]{2,1,0:T(8,128)(2,1)S(1)} all-to-all(bf16[16,8,2560]{2,1,0:T(8,128)(2,1)} %pack.1), channel_id=1, replica_groups=mesh['dp'=2,'fsdp'=16] {'fsdp'}, dimensions={0} | all-to-all | bytes 1310720 | tf_op jit(solution)/shard_map/all_to_all | solution.py:478
  29.5 0.0 collective-permute-start
  29.5 0.0 copy-done.4
  29.5 0.8 copy.27.patches_ref
  30.3 0.0 copy-done.5
  30.3 0.6 copy.28.prompts_ref
  30.9 0.6 collective-permute-done.wother_ref
  31.6 0.0 copy-done
  31.6 0.8 copy-done.2
  32.4 67.1 %tower.1 = (bf16[2,4,128,128]{3,2,1,0:T(8,128)(2,1)}, f32[2,4,117,128]{3,2,1,0:T(8,128)}, bf16[2,16,8,2560]{3,2,1,0:T(8,128)(2,1)}, f32[2,16,16,128]{3,2,1,0:T(8,128)}) custom-call(s32[2]{0:T(128)} %ids_ref.1, s32[8]{0:T(128)} %counts_ref.1, bf16[16,8,2560]{2,1,0:T(8,128)(2,1)} %copy-done, bf16[16,8,2560]{2,1,0:T(8,128)(2,1)} %copy-done.2, ...), custom_call_target="tpu_custom_call" | custom-call | tf_op jit(solution)/shard_map/tower/pallas_call | solution.py:410
  99.5 1.0 fusion.2
  100.6 0.2 collective-permute-start.1
  100.8 1.1 slice_bitcast_fusion
  101.9 0.4 collective-permute-start.7
  102.3 0.0 collective-permute-done.1
  102.3 0.9 fusion.1
  103.3 0.7 collective-permute-start.2
  104.0 3.6 %collective-permute-done.2 = bf16[16,16,128]{2,1,0:T(8,128)(2,1)S(1)} collective-permute-done((bf16[16,16,128]{2,1,0:T(8,128)(2,1)S(1)}, bf16[16,16,128]{2,1,0:T(8,128)(2,1)S(1)}, u32[]{:S(2)}, u32[]{:S(2)}) %collective-permute-start.2) | collective-permute-done | bytes 65568 | tf_op jit(solution)/shard_map/ppermute | solution.py:470
  107.6 0.6 collective-permute-start.3
  108.2 3.7 %collective-permute-done.3 = bf16[16,16,128]{2,1,0:T(8,128)(2,1)S(1)} collective-permute-done((bf16[16,16,128]{2,1,0:T(8,128)(2,1)S(1)}, bf16[16,16,128]{2,1,0:T(8,128)(2,1)S(1)}, u32[]{:S(2)}, u32[]{:S(2)}) %collective-permute-start.3) | collective-permute-done | bytes 65568 | tf_op jit(solution)/shard_map/ppermute | solution.py:470
  112.0 0.5 collective-permute-start.4
  112.5 0.0 collective-permute-done.7
  112.5 0.0 copy-done.1
  112.5 1.0 fusion
  113.5 4.2 %all-to-all-start.1 = ((bf16[16,8,2560]{2,1,0:T(8,128)(2,1)}), bf16[16,8,2560]{2,1,0:T(8,128)(2,1)S(1)}, u32[]{:S(2)}, u32[]{:S(2)}) async-start(bf16[16,8,2560]{2,1,0:T(8,128)(2,1)} %fusion), calls=%async_computation.1 | async-start | bytes 1310720 | tf_op jit(solution)/shard_map/all_to_all | solution.py:484
  117.8 0.1 collective-permute-done.4
  117.9 1.9 %collective-permute-start.5 = (bf16[16,16,128]{2,1,0:T(8,128)(2,1)S(1)}, bf16[16,16,128]{2,1,0:T(8,128)(2,1)S(1)}, u32[]{:S(2)}, u32[]{:S(2)}) collective-permute-start(bf16[16,16,128]{2,1,0:T(8,128)(2,1)S(1)} %add_convert_fusion), channel_id=1, source_target_pairs={{0,4},{1,5},{2,6},{3,7},{4,0},{5,1},{6,2},{7,3},{8,12},{9,13},{10,... | collective-permute-start | bytes 196616 | tf_op jit(solution)/shard_map/ppermute | solution.py:470
  119.8 8.3 %collective-permute-done.5 = bf16[16,16,128]{2,1,0:T(8,128)(2,1)S(1)} collective-permute-done((bf16[16,16,128]{2,1,0:T(8,128)(2,1)S(1)}, bf16[16,16,128]{2,1,0:T(8,128)(2,1)S(1)}, u32[]{:S(2)}, u32[]{:S(2)}) %collective-permute-start.5) | collective-permute-done | bytes 65568 | tf_op jit(solution)/shard_map/ppermute | solution.py:470
  128.1 0.1 collective-permute-start.6
  128.2 0.0 copy-done.3
  128.2 0.9 copy.30
  129.1 0.4 collective-permute-done.6
  129.5 0.7 broadcast_select_fusion
  130.2 0.6 fusion.20
  130.8 2.4 %all-to-all-done.1 = bf16[16,8,2560]{2,1,0:T(8,128)(2,1)S(1)} async-done(((bf16[16,8,2560]{2,1,0:T(8,128)(2,1)}), bf16[16,8,2560]{2,1,0:T(8,128)(2,1)S(1)}, u32[]{:S(2)}, u32[]{:S(2)}) %all-to-all-start.1) | async-done | bytes 655392 | tf_op jit(solution)/shard_map/all_to_all | solution.py:484
  133.2 0.1 convert_reduce_fusion
  133.3 0.1 collective-permute-start.8
  133.4 0.5 slice_bitcast_fusion.1
  133.9 0.6 copy.31
  134.6 0.6 copy.34
  135.2 0.0 collective-permute-done.8
  135.2 0.6 fusion.3
  135.9 0.6 copy.33
  136.5 0.6 copy.32
  137.1 0.6 copy_bitcast_fusion
  (14 shorter events, 0.1 us)
Async XLA Ops:
  0.6 28.8 %copy-start.4 = (bf16[2,4,117,128]{3,1,2,0:T(4,128)(2,1)S(1)}, bf16[2,4,117,128]{3,1,2,0:T(4,128)(2,1)}, u32[]{:S(2)}) copy-start(bf16[2,4,117,128]{3,1,2,0:T(4,128)(2,1)} %param.14) | copy-start | bytes 718852
  0.7 29.6 %copy-start.5 = (bf16[8,10,128]{2,0,1:T(8,128)(2,1)S(1)}, bf16[8,10,128]{2,0,1:T(8,128)(2,1)}, u32[]{:S(2)}) copy-start(bf16[8,10,128]{2,0,1:T(8,128)(2,1)} %param.15) | copy-start | bytes 61444
  29.5 2.1 %copy-start = (bf16[16,8,2560]{2,1,0:T(8,128)(2,1)}, bf16[16,8,2560]{2,1,0:T(8,128)(2,1)S(1)}, u32[]{:S(2)}) copy-start(bf16[16,8,2560]{2,1,0:T(8,128)(2,1)S(1)} %all_to_all.10.wmine_ref) | copy-start | bytes 1966084
  29.5 2.1 %collective-permute-start = (bf16[16,8,2560]{2,1,0:T(8,128)(2,1)S(1)}, bf16[16,8,2560]{2,1,0:T(8,128)(2,1)S(1)}, u32[]{:S(2)}, u32[]{:S(2)}) collective-permute-start(bf16[16,8,2560]{2,1,0:T(8,128)(2,1)S(1)} %all_to_all.10.wmine_ref), channel_id=1, source_target_pairs={{0,16},{16,0},{1,17},{17,1},{2,18},{18,2},{3,19},{19,3},{4,20},{20... | collective-permute-start | bytes 1966088 | tf_op jit(solution)/shard_map/ppermute | solution.py:470
  31.6 0.8 copy-start.2
  99.5 13.0 %copy-start.1 = (bf16[2,16,8,2560]{3,2,1,0:T(8,128)(2,1)S(1)}, bf16[2,16,8,2560]{3,2,1,0:T(8,128)(2,1)}, u32[]{:S(2)}) copy-start(bf16[2,16,8,2560]{3,2,1,0:T(8,128)(2,1)} %get-tuple-element.20) | copy-start | bytes 3932164
  100.6 1.8 %collective-permute-start.1 = (bf16[16,16,128]{2,1,0:T(8,128)(2,1)S(1)}, bf16[16,16,128]{2,1,0:T(8,128)(2,1)S(1)}, u32[]{:S(2)}, u32[]{:S(2)}) collective-permute-start(bf16[16,16,128]{2,1,0:T(8,128)(2,1)S(1)} %fusion.2), channel_id=1, source_target_pairs={{0,16},{16,0},{1,17},{17,1},{2,18},{18,2},{3,19},{19,3},{4,20},{20... | collective-permute-start | bytes 196616 | tf_op jit(solution)/shard_map/ppermute | solution.py:470
  101.9 10.6 %collective-permute-start.7 = (bf16[16,8,2560]{2,1,0:T(8,128)(2,1)S(1)}, bf16[16,8,2560]{2,1,0:T(8,128)(2,1)S(1)}, u32[]{:S(2)}, u32[]{:S(2)}) collective-permute-start(bf16[16,8,2560]{2,1,0:T(8,128)(2,1)S(1)} %slice_bitcast_fusion), channel_id=1, source_target_pairs={{0,16},{16,0},{1,17},{17,1},{2,18},{18,2},{3,19},{19,3},{4,20},{20... | collective-permute-start | bytes 1966088 | tf_op jit(solution)/shard_map/ppermute | solution.py:470
  103.3 4.3 %collective-permute-start.2 = (bf16[16,16,128]{2,1,0:T(8,128)(2,1)S(1)}, bf16[16,16,128]{2,1,0:T(8,128)(2,1)S(1)}, u32[]{:S(2)}, u32[]{:S(2)}) collective-permute-start(bf16[16,16,128]{2,1,0:T(8,128)(2,1)S(1)} %fusion.1), channel_id=1, source_target_pairs={{0,2},{1,3},{2,0},{3,1},{4,6},{5,7},{6,4},{7,5},{8,10},{9,11},{10,... | collective-permute-start | bytes 196616 | tf_op jit(solution)/shard_map/ppermute | solution.py:470
  107.6 4.3 %collective-permute-start.3 = (bf16[16,16,128]{2,1,0:T(8,128)(2,1)S(1)}, bf16[16,16,128]{2,1,0:T(8,128)(2,1)S(1)}, u32[]{:S(2)}, u32[]{:S(2)}) collective-permute-start(bf16[16,16,128]{2,1,0:T(8,128)(2,1)S(1)} %add_convert_fusion.2), channel_id=1, source_target_pairs={{0,1},{1,0},{2,3},{3,2},{4,5},{5,4},{6,7},{7,6},{8,9},{9,8},{10,11... | collective-permute-start | bytes 196616 | tf_op jit(solution)/shard_map/ppermute | solution.py:470
  112.0 5.9 %collective-permute-start.4 = (bf16[16,16,128]{2,1,0:T(8,128)(2,1)S(1)}, bf16[16,16,128]{2,1,0:T(8,128)(2,1)S(1)}, u32[]{:S(2)}, u32[]{:S(2)}) collective-permute-start(bf16[16,16,128]{2,1,0:T(8,128)(2,1)S(1)} %add_convert_fusion.1), channel_id=1, source_target_pairs={{0,8},{1,9},{2,10},{3,11},{4,12},{5,13},{6,14},{7,15},{8,0},{9,1},... | collective-permute-start | bytes 196616 | tf_op jit(solution)/shard_map/ppermute | solution.py:470
  113.5 14.7 %copy-start.3 = (f32[2,4,117,128]{3,2,1,0:T(8,128)S(1)}, f32[2,4,117,128]{3,2,1,0:T(8,128)}, u32[]{:S(2)}) copy-start(f32[2,4,117,128]{3,2,1,0:T(8,128)} %get-tuple-element.22) | copy-start | bytes 1437700
  113.5 19.7 %all-to-all-start.1 = ((bf16[16,8,2560]{2,1,0:T(8,128)(2,1)}), bf16[16,8,2560]{2,1,0:T(8,128)(2,1)S(1)}, u32[]{:S(2)}, u32[]{:S(2)}) async-start(bf16[16,8,2560]{2,1,0:T(8,128)(2,1)} %fusion), calls=%async_computation.1 | async-start | bytes 1310720 | tf_op jit(solution)/shard_map/all_to_all | solution.py:484
  117.9 10.1 %collective-permute-start.5 = (bf16[16,16,128]{2,1,0:T(8,128)(2,1)S(1)}, bf16[16,16,128]{2,1,0:T(8,128)(2,1)S(1)}, u32[]{:S(2)}, u32[]{:S(2)}) collective-permute-start(bf16[16,16,128]{2,1,0:T(8,128)(2,1)S(1)} %add_convert_fusion), channel_id=1, source_target_pairs={{0,4},{1,5},{2,6},{3,7},{4,0},{5,1},{6,2},{7,3},{8,12},{9,13},{10,... | collective-permute-start | bytes 196616 | tf_op jit(solution)/shard_map/ppermute | solution.py:470
  128.1 1.4 %collective-permute-start.6 = (f32[16,16,128]{2,1,0:T(8,128)S(1)}, f32[16,16,128]{2,1,0:T(8,128)S(1)}, u32[]{:S(2)}, u32[]{:S(2)}) collective-permute-start(f32[16,16,128]{2,1,0:T(8,128)S(1)} %convert_add_fusion.1), channel_id=1, source_target_pairs={{0,16},{16,0},{1,17},{17,1},{2,18},{18,2},{3,19},{19,3},{4,20},{20... | collective-permute-start | bytes 393224 | tf_op jit(solution)/shard_map/ppermute | solution.py:470
  133.3 1.9 %collective-permute-start.8 = (f32[8,2560]{1,0:T(8,128)S(1)}, f32[8,2560]{1,0:T(8,128)S(1)}, u32[]{:S(2)}, u32[]{:S(2)}) collective-permute-start(f32[8,2560]{1,0:T(8,128)S(1)} %convert_reduce_fusion), channel_id=1, source_target_pairs={{0,16},{16,0},{1,17},{17,1},{2,18},{18,2},{3,19},{19,3},{4,20},{20... | collective-permute-start | bytes 245768 | tf_op jit(solution)/shard_map/ppermute | solution.py:470

commit v3 on v2

--- a/solution.py
+++ b/solution.py
@@ -47,38 +47,40 @@
     return part[:, :128] + part[:, 128:]
 
 
-def dp_of(split):
-    return lax.axis_index("dp") if split else 0
-
-
 def pack_kernel(attn_in_ref, attn_out_ref, feed_in_ref, feed_out_ref, out_ref):
     l = lax.axis_index("dp")
     down = feed_out_ref[l].astype(F32)
     parts = [attn_in_ref[l, 0], attn_in_ref[l, 1], attn_out_ref[l, 0], attn_out_ref[l, 1], feed_in_ref[l]]
     parts = [part.astype(F32) for part in parts] + [down[8 * a : 8 * a + 8] for a in range(4)]
-    row = jnp.concatenate(parts, axis=1).astype(BF)
-    for f in range(SHARDS):
-        out_ref[f] = row
+    out_ref[0] = jnp.concatenate(parts, axis=1).astype(BF)
 
 
 def tower_kernel(
     split,
-    ids_ref, counts_ref, wmine_ref, wother_ref, tok_ref, gains_ref, scales_ref, patches_ref, prompts_ref,
+    ids_ref, counts_ref, wmine0_ref, wmine1_ref, wmine2_ref, wmine3_ref, wother0_ref, wother1_ref, wother2_ref, wother3_ref,
+    tok_ref, gains_ref, scales_ref, patches_ref, prompts_ref,
     cls_ref, cot_ref, adj_ref,
     out_ref, pgrad_ref, gbig_ref, gsmall_ref,
-    w_ref, wd_ref, wt_ref, wdt_ref, colb_ref, tokscr_ref, h_ref, g_ref, xh_ref, inv_ref,
+    stage_ref, w_ref, wd_ref, wt_ref, wdt_ref, colb_ref, tokscr_ref, h_ref, g_ref, xh_ref, inv_ref,
     qkvt_ref, pb_ref, ot_ref, qkvv_ref, pv_ref, ov_ref, pw_ref, hid_ref, du_ref, dqkv_ref,
     dov_ref, ga_ref, gd_ref, gt_ref, gacc_ref,
 ):
-    dp = dp_of(split)
+    dp = lax.axis_index("dp") if split else 0
+    me = lax.axis_index("fsdp") if split else 0
     layers = 2
     chunks = 4
     items = 2
 
+    for rel in range(SHARDS):
+        rows = pl.ds(pl.multiple_of(8 * (me ^ rel), 8), 8)
+        mine_ref = (wmine0_ref, wmine1_ref, wmine2_ref, wmine3_ref)[rel % 4]
+        other_ref = (wother0_ref, wother1_ref, wother2_ref, wother3_ref)[rel % 4]
+        stage_ref[dp, rows, :] = mine_ref[rel // 4].astype(F32)
+        stage_ref[1 - dp, rows, :] = other_ref[rel // 4].astype(F32)
     for l in range(layers):
         for pair in range(SHARDS // 2):
-            lo = jnp.where(dp == l, wmine_ref[2 * pair].astype(F32), wother_ref[2 * pair].astype(F32))
-            hi = jnp.where(dp == l, wmine_ref[2 * pair + 1].astype(F32), wother_ref[2 * pair + 1].astype(F32))
+            lo = stage_ref[l, 16 * pair : 16 * pair + 8, :]
+            hi = stage_ref[l, 16 * pair + 8 : 16 * pair + 16, :]
             w_ref[l, 16 * pair : 16 * pair + 16, :] = jnp.concatenate([lo[:, :COL_DOWN], hi[:, :COL_DOWN]], axis=0).astype(BF)
             for half, part in enumerate((lo, hi)):
                 base = 64 * pair + 32 * half
@@ -86,8 +88,7 @@
                     [part[:, COL_DOWN + 128 * a : COL_DOWN + 128 * a + 128] for a in range(4)], axis=0
                 ).astype(BF)
         for block in range(COL_DOWN // 128):
-            target = block if block < 8 else 8 + (0, 1, 4, 5, 2, 3, 6, 7)[block - 8]
-            wt_ref[l, 128 * target : 128 * target + 128, :] = w_ref[l, :, 128 * block : 128 * block + 128].T
+            wt_ref[l, 128 * block : 128 * block + 128, :] = w_ref[l, :, 128 * block : 128 * block + 128].T
         for block in range(4):
             wdt_ref[l, :, 128 * block : 128 * block + 128] = wd_ref[l, 128 * block : 128 * block + 128, :].T
         for k in range(4):
@@ -116,7 +117,7 @@
     spread_heads = jnp.where(spread_row == spread_col, 1.0, 0.0).astype(BF)
 
     def head_sums(left, rights):
-        return dot_nn(gather_heads, jnp.concatenate([left * right for right in rights], axis=1))
+        return dot_nn(gather_heads, jnp.concatenate([(left * right).astype(BF) for right in rights], axis=1))
 
     blank = jnp.zeros((16, 128), BF)
 
@@ -177,10 +178,10 @@
 
         def slot(first, i):
             lanes = slice(128 * (i % 2), 128 * (i % 2) + 128)
-            return qkvv_ref[l, 2 * b + i // 2, first : first + 128, lanes]
+            return qkvv_ref[l, 2 * b + i // 2, first : first + 128, lanes].astype(F32)
 
         key_slots = [slot(128, j) for j in range(4)]
-        value_slots = [slot(256, j).astype(F32) for j in range(4)]
+        value_slots = [slot(256, j) for j in range(4)]
         for i in range(4):
             scores = head_sums(slot(0, i), key_slots)
             parts = [scores[:, 128 * j : 128 * j + 128] for j in range(4)]
@@ -202,25 +203,17 @@
             branch = dot_nn(wt_ref[l, COL_OUT[1] : COL_OUT[1] + 128, :], ov_ref[l, c])
             h_ref[c] = h_ref[c] + scale(l, 1) * branch
 
-    def stacked(rows):
-        return jnp.concatenate([rows[:, :128], rows[:, 128:]], axis=0)
-
-    def unstacked(rows):
-        return jnp.concatenate([rows[:128], rows[128:]], axis=1)
-
-    def gate_and_up(l, z, n):
-        joint = dot_nn(wt_ref[l, COL_FEED + 512 * z : COL_FEED + 512 * z + 512, :], n)
-        gate, up = joint[:256], joint[256:]
-        return gate, up, 0.5 * jnp.tanh(0.5 * gate) + 0.5
-
     def tail_forward(l, c):
         x = h_ref[c]
         n = keep_norm(l, 2, c, x)
-        x = x + scale(l, 2) * unstacked(dot_nt(stacked(n), tok_ref[l]))
+        mix = [dot_nt(n[:, 128 * s : 128 * s + 128], tok_ref[l]) for s in range(2)]
+        x = x + scale(l, 2) * jnp.concatenate(mix, axis=1)
         n = keep_norm(l, 3, c, x)
-        for z in range(2):
-            gate, up, sig = gate_and_up(l, z, n)
-            hid_ref[c % 2, 256 * z : 256 * z + 256, :] = (gate * sig * up).astype(BF)
+        for z in range(4):
+            gate = dot_nn(wt_ref[l, COL_FEED + 128 * z : COL_FEED + 128 * z + 128, :], n)
+            up = dot_nn(wt_ref[l, COL_FEED + 512 + 128 * z : COL_FEED + 640 + 128 * z, :], n)
+            sig = 0.5 * jnp.tanh(0.5 * gate) + 0.5
+            hid_ref[c % 2, 128 * z : 128 * z + 128, :] = (gate * sig * up).astype(BF)
         h_ref[c] = x + scale(l, 3) * dot_nn(wdt_ref[l], hid_ref[c % 2])
 
     def norm_of(l, k, c):
@@ -235,16 +228,18 @@
     def feed_backward(l, c):
         xhat, inv, n = norm_of(l, 3, c)
         dz = [(scale(l, 3) * g_ref[x, c]).astype(BF) for x in range(2)]
-        for z in range(2):
-            rows = slice(256 * z, 256 * z + 256)
-            gate, up, sig = gate_and_up(l, z, n)
+        for z in range(4):
+            rows = slice(128 * z, 128 * z + 128)
+            gate = dot_nn(wt_ref[l, COL_FEED + 128 * z : COL_FEED + 128 * z + 128, :], n)
+            up = dot_nn(wt_ref[l, COL_FEED + 512 + 128 * z : COL_FEED + 640 + 128 * z, :], n)
+            sig = 0.5 * jnp.tanh(0.5 * gate) + 0.5
             act = gate * sig
             hid_ref[c % 2, rows, :] = (act * up).astype(BF)
             slope = up * (sig * (1.0 + gate * (1.0 - sig)))
             for x in range(2):
                 dhid = dot_nn(wd_ref[l, rows, :], dz[x])
-                du_ref[2 * (c % 2) + x, 256 * z : 256 * z + 256, :] = (dhid * slope).astype(BF)
-                du_ref[2 * (c % 2) + x, 512 + 256 * z : 768 + 256 * z, :] = (dhid * act).astype(BF)
+                du_ref[2 * (c % 2) + x, 128 * z : 128 * z + 128, :] = (dhid * slope).astype(BF)
+                du_ref[2 * (c % 2) + x, 512 + 128 * z : 640 + 128 * z, :] = (dhid * act).astype(BF)
         ga_ref[:, COL_FEED:COL_DOWN] += dot_nt(n, du_ref[2 * (c % 2)])
         gd_ref[...] += dot_nt(hid_ref[c % 2], dz[0])
         for x in range(2):
@@ -254,16 +249,19 @@
     def token_backward(l, c):
         xhat, inv, n = norm_of(l, 2, c)
         for x in range(2):
-            dy = stacked((scale(l, 2) * g_ref[x, c]).astype(BF))
-            if x == 0:
-                turned = jnp.concatenate([dy[:128].T, dy[128:].T], axis=1)
-                gt_ref[l] += dot_nn(turned, stacked(n))
-            pass_on(l, 2, c, x, unstacked(dot_nn(dy, tok_ref[l])), xhat, inv)
+            dy = (scale(l, 2) * g_ref[x, c]).astype(BF)
+            dn = []
+            for s in range(2):
+                part = dy[:, 128 * s : 128 * s + 128]
+                dn.append(dot_nn(part, tok_ref[l]))
+                if x == 0:
+                    gt_ref[l] += dot_nn(part.T, n[:, 128 * s : 128 * s + 128])
+            pass_on(l, 2, c, x, jnp.concatenate(dn, axis=1), xhat, inv)
 
     def var_backward(l, b):
         def slot(first, i):
             lanes = slice(128 * (i % 2), 128 * (i % 2) + 128)
-            return qkvv_ref[l, 2 * b + i // 2, first : first + 128, lanes]
+            return qkvv_ref[l, 2 * b + i // 2, first : first + 128, lanes].astype(F32)
 
         for x in range(2):
             for cc in range(2):
@@ -273,28 +271,28 @@
                 if x == 0:
                     ga_ref[:, COL_OUT[1] : COL_OUT[1] + 128] += dot_nt(ov_ref[l, c], dt)
             value_slots = [slot(256, j) for j in range(4)]
-            dkeys = [[] for _ in range(4)]
-            dvalues = [[] for _ in range(4)]
+            dkeys = [0.0] * 4
+            dvalues = [0.0] * 4
             for i in range(4):
                 lanes = slice(128 * (i % 2), 128 * (i % 2) + 128)
-                grad = dov_ref[4 * b + 2 * x + i // 2, :, lanes]
+                grad = dov_ref[4 * b + 2 * x + i // 2, :, lanes].astype(F32)
                 query = slot(0, i)
                 prob = pv_ref[l, b, i]
                 weighted = prob * head_sums(grad, value_slots)
                 total = (weighted[:, :128] + weighted[:, 128:256]) + (weighted[:, 256:384] + weighted[:, 384:])
                 ds = weighted - prob * jnp.concatenate([total] * 4, axis=1)
-                ds_wide = dot_nn(spread_heads, ds.astype(BF)).astype(BF)
+                ds_wide = dot_nn(spread_heads, ds.astype(BF))
                 ds_slots = [ds_wide[:, 128 * j : 128 * j + 128] for j in range(4)]
                 terms = [ds_slots[j] * slot(128, j) for j in range(4)]
                 dquery = (terms[0] + terms[1]) + (terms[2] + terms[3])
                 for j in range(4):
-                    dkeys[j].append(ds_slots[j] * query)
-                    dvalues[j].append(pw_ref[l, b, i, :, 128 * j : 128 * j + 128] * grad)
-                dqkv_ref[4 * b + 2 * x + i // 2, 0:128, lanes] = dquery * jnp.asarray(0.25, BF)
+                    dkeys[j] = dkeys[j] + ds_slots[j] * query
+                    dvalues[j] = dvalues[j] + pw_ref[l, b, i, :, 128 * j : 128 * j + 128].astype(F32) * grad
+                dqkv_ref[4 * b + 2 * x + i // 2, 0:128, lanes] = (dquery * 0.25).astype(BF)
             for j in range(4):
                 lanes = slice(128 * (j % 2), 128 * (j % 2) + 128)
-                dqkv_ref[4 * b + 2 * x + j // 2, 128:256, lanes] = (dkeys[j][0] + dkeys[j][1]) + (dkeys[j][2] + dkeys[j][3])
-                dqkv_ref[4 * b + 2 * x + j // 2, 256:384, lanes] = (dvalues[j][0] + dvalues[j][1]) + (dvalues[j][2] + dvalues[j][3])
+                dqkv_ref[4 * b + 2 * x + j // 2, 128:256, lanes] = dkeys[j].astype(BF)
+                dqkv_ref[4 * b + 2 * x + j // 2, 256:384, lanes] = dvalues[j].astype(BF)
             for cc in range(2):
                 c = 2 * b + cc
                 xhat, inv, n = norm_of(l, 1, c)
@@ -415,9 +413,10 @@
             jax.ShapeDtypeStruct((2, SHARDS, 8, COLS), BF),
             jax.ShapeDtypeStruct((2, 16, 16, 128), F32),
         ),
-        in_specs=[smem, smem] + [vmem] * 10,
+        in_specs=[smem, smem] + [vmem] * 16,
         out_specs=[vmem] * 4,
         scratch_shapes=[
+            pltpu.VMEM((2, 128, COLS), F32),
             pltpu.VMEM((2, 128, COL_DOWN), BF),
             pltpu.VMEM((2, 512, 128), BF),
             pltpu.VMEM((2, COL_DOWN, 128), BF),
@@ -470,13 +469,18 @@
     return lax.ppermute(array, axis, [(i, i ^ (1 << bit)) for i in range(size)])
 
 
+def swap(array, mask):
+    return lax.ppermute(array, "fsdp", [(i, i ^ mask) for i in range(SHARDS)])
+
+
 def gather_rows(attn_in, attn_out, feed_in, feed_out):
     vmem = pl.BlockSpec(memory_space=pltpu.VMEM)
     row = pl.pallas_call(
-        pack_kernel, out_shape=jax.ShapeDtypeStruct((SHARDS, 8, COLS), BF), in_specs=[vmem] * 4, out_specs=vmem, name="pack",
+        pack_kernel, out_shape=jax.ShapeDtypeStruct((1, 8, COLS), BF), in_specs=[vmem] * 4, out_specs=vmem, name="pack",
     )(attn_in, attn_out, feed_in, feed_out)
-    mine = lax.all_to_all(row, "fsdp", 0, 0, tiled=True)
-    return mine, flip(mine, "dp", 0, 2)
+    column = jnp.concatenate([row] + [swap(row, 4 * z) for z in range(1, 4)], axis=0)
+    mine = [column] + [swap(column, xy) for xy in range(1, 4)]
+    return mine + [flip(part, "dp", 0, 2) for part in mine]
 
 
 def reduce_big(big):
@@ -503,7 +507,7 @@
     dp = lax.axis_index("dp")
     fast = shard_count == SHARDS
     if fast:
-        mine, other = gather_rows(attn_in, attn_out, feed_in, feed_out)
+        gathered = gather_rows(attn_in, attn_out, feed_in, feed_out)
     else:
         whole_down = lax.all_gather(feed_out, "fsdp", axis=1, tiled=True)
         whole_down = whole_down.reshape(2, SHARDS, 4, 8, 128).transpose(0, 2, 1, 3, 4).reshape(2, 512, 128)
@@ -514,9 +518,9 @@
             whole_down,
         )
         rows = rows.reshape(2, SHARDS, 8, COLS).transpose(1, 0, 2, 3)
-        mine, other = rows[:, 0], rows[:, 1]
+        gathered = [rows[:, l].reshape(4, 4, 8, COLS)[:, xy] for l in range(2) for xy in range(4)]
     output, patch_grad, big, small = run_tower(
-        fast, dataset_ids, var_counts, mine, other, token_operator, norm_gains, branch_scales, patches, prompts,
+        fast, dataset_ids, var_counts, *gathered, token_operator, norm_gains, branch_scales, patches, prompts,
         cls_token.reshape(1, -1), cotangent, adjust_cotangent,
     )
     if fast:

time: 138 us -> 135 us (0.978)
  blocking collectives: 27 us -> 0 us
  waiting for transfers between devices: 19.2 us -> 30.5 us
  starting transfers between devices: 8.75 us -> 18.8 us
  local copies, waits for them, and re-layouts: 8.96 us -> 10.5 us
    all_to_all x1 -> x0, blocking collectives: 27 us -> none  [gather_rows(): mine = lax.all_to_all(row, 'fsdp', 0, 0, tiled=True)]
    ppermute x0 -> x6, waiting for transfers between devices: none -> 12.2 us  [swap(): return lax.ppermute(array, 'fsdp', [(i, i ^ mask) for i in range(SHARDS)])]
    ppermute x0 -> x6, starting transfers between devices: none -> 9.17 us  [swap(): return lax.ppermute(array, 'fsdp', [(i, i ^ mask) for i in range(SHARDS)])]
    unnamed x19 -> x27, local copies, waits for them, and re-layouts: 5.69 us -> 7.2 us
    ppermute x9 -> x12, waiting for transfers between devices: 16.8 us -> 15.8 us  [flip(): return lax.ppermute(array, axis, [(i, i ^ 1 << bit) for i in range(size)])]
    ppermute x9 -> x12, starting transfers between devices: 4.53 us -> 4.81 us  [flip(): return lax.ppermute(array, axis, [(i, i ^ 1 << bit) for i in range(size)])]
  transfers between devices with their start and end apart: 10 -> 19, of which waited for: 7 -> 9; matrix products, arithmetic and copies ran while one was open for 6% -> 8% of each run, Pallas kernels for 0% -> 0%
where the time goes in v3:
time: 135 us; the launch traced here: 134 us
  Pallas kernels  68.7 us (51%)
  waiting for transfers between devices  30.5 us (23%)
  starting transfers between devices  18.8 us (14%)
  local copies, waits for them, and re-layouts  10.5 us (8%)
  other arithmetic  4.85 us (4%)
    pallas_call x1, Pallas kernels, run_tower(): pl.pallas_call(functools.partial(tower_kernel, split), out_shape=(jax.Sha...  67.2 us
    ppermute x12, waiting for transfers between devices, flip(): return lax.ppermute(array, axis, [(i, i ^ 1 << bit) for i in range(size)])  15.8 us
    ppermute x6, waiting for transfers between devices, swap(): return lax.ppermute(array, 'fsdp', [(i, i ^ mask) for i in range(SHARDS)])  12.2 us
    ppermute x6, starting transfers between devices, swap(): return lax.ppermute(array, 'fsdp', [(i, i ^ mask) for i in range(SHARDS)])  9.17 us
    unnamed x27, local copies, waits for them, and re-layouts  7.2 us
    all_to_all x1, starting transfers between devices, reduce_big(): parts = lax.all_to_all(held.astype(BF), 'fsdp', 0, 0, tiled=True)  4.86 us
    ppermute x12, starting transfers between devices, flip(): return lax.ppermute(array, axis, [(i, i ^ 1 << bit) for i in range(size)])  4.81 us
  transfers between devices with their start and end apart: 19, of which 9 were waited for; matrix products, arithmetic and copies ran while one was open for 8% of the time, Pallas kernels for 0%

profile of v3, /device:TPU:0, one launch (start us, length us, event | category | flops | bytes accessed | tf_op | source)
XLA Modules:
  0.0 134.2 jit_solution(9779651790425109859)
XLA Ops:
  0.6 1.4 %pack.1 = bf16[1,8,2560]{2,1,0:T(8,128)(2,1)} custom-call(bf16[2,2,8,384]{3,2,1,0:T(8,128)(2,1)} %attn_in_ref.1, bf16[2,2,8,128]{3,2,1,0:T(8,128)(2,1)} %attn_out_ref.1, bf16[2,8,1024]{2,1,0:T(8,128)(2,1)} %feed_in_ref.1, bf16[2,32,128]{2,1,0:T(8,128)(2,1)} %feed_out_ref.1), custom_call_target="tpu_custom_call" | custom-call | tf_op jit(solution)/shard_map/pack/pallas_call | solution.py:478
  2.1 3.0 %collective-permute-start = (bf16[1,8,2560]{2,1,0:T(8,128)(2,1)}, bf16[1,8,2560]{2,1,0:T(8,128)(2,1)S(1)}, u32[]{:S(2)}, u32[]{:S(2)}) collective-permute-start(bf16[1,8,2560]{2,1,0:T(8,128)(2,1)} %pack.1), channel_id=1, source_target_pairs={{0,4},{1,5},{2,6},{3,7},{4,0},{5,1},{6,2},{7,3},{8,12},{9,13},{10,... | collective-permute-start | bytes 122888 | tf_op jit(solution)/shard_map/ppermute | solution.py:473
  5.1 2.6 %collective-permute-start.1 = (bf16[1,8,2560]{2,1,0:T(8,128)(2,1)}, bf16[1,8,2560]{2,1,0:T(8,128)(2,1)S(1)}, u32[]{:S(2)}, u32[]{:S(2)}) collective-permute-start(bf16[1,8,2560]{2,1,0:T(8,128)(2,1)} %pack.1), channel_id=1, source_target_pairs={{0,8},{1,9},{2,10},{3,11},{4,12},{5,13},{6,14},{7,15},{8,0},{9,1},... | collective-permute-start | bytes 122888 | tf_op jit(solution)/shard_map/ppermute | solution.py:473
  7.7 3.3 %collective-permute-done.1 = bf16[1,8,2560]{2,1,0:T(8,128)(2,1)S(1)} collective-permute-done((bf16[1,8,2560]{2,1,0:T(8,128)(2,1)}, bf16[1,8,2560]{2,1,0:T(8,128)(2,1)S(1)}, u32[]{:S(2)}, u32[]{:S(2)}) %collective-permute-start.1) | collective-permute-done | bytes 40992 | tf_op jit(solution)/shard_map/ppermute | solution.py:473
  11.0 2.7 %collective-permute-done.2 = bf16[1,8,2560]{2,1,0:T(8,128)(2,1)S(1)} collective-permute-done((bf16[1,8,2560]{2,1,0:T(8,128)(2,1)}, bf16[1,8,2560]{2,1,0:T(8,128)(2,1)S(1)}, u32[]{:S(2)}, u32[]{:S(2)}) %collective-permute-start.2) | collective-permute-done | bytes 40992 | tf_op jit(solution)/shard_map/ppermute | solution.py:473
  13.7 0.8 pad_maximum_fusion.wmine0_ref
  14.5 1.6 %collective-permute-start.3 = (bf16[4,8,2560]{2,1,0:T(8,128)(2,1)S(1)}, bf16[4,8,2560]{2,1,0:T(8,128)(2,1)S(1)}, u32[]{:S(2)}, u32[]{:S(2)}) collective-permute-start(bf16[4,8,2560]{2,1,0:T(8,128)(2,1)S(1)} %pad_maximum_fusion.wmine0_ref), channel_id=1, source_target_pairs={{0,1},{1,0},{2,3},{3,2},{4,5},{5,4},{6,7},{7,6},{8,9},{9,8},{10,11... | collective-permute-start | bytes 491528 | tf_op jit(solution)/shard_map/ppermute | solution.py:473
  16.1 1.5 %collective-permute-start.4 = (bf16[4,8,2560]{2,1,0:T(8,128)(2,1)S(1)}, bf16[4,8,2560]{2,1,0:T(8,128)(2,1)S(1)}, u32[]{:S(2)}, u32[]{:S(2)}) collective-permute-start(bf16[4,8,2560]{2,1,0:T(8,128)(2,1)S(1)} %pad_maximum_fusion.wmine0_ref), channel_id=1, source_target_pairs={{0,2},{1,3},{2,0},{3,1},{4,6},{5,7},{6,4},{7,5},{8,10},{9,11},{10,... | collective-permute-start | bytes 491528 | tf_op jit(solution)/shard_map/ppermute | solution.py:473
  17.6 0.5 collective-permute-start.5
  18.1 3.2 %collective-permute-done.3.wmine1_ref = bf16[4,8,2560]{2,1,0:T(8,128)(2,1)S(1)} collective-permute-done((bf16[4,8,2560]{2,1,0:T(8,128)(2,1)S(1)}, bf16[4,8,2560]{2,1,0:T(8,128)(2,1)S(1)}, u32[]{:S(2)}, u32[]{:S(2)}) %collective-permute-start.3) | collective-permute-done | bytes 163872 | tf_op jit(solution)/shard_map/ppermute | solution.py:473
  21.3 3.0 %collective-permute-done.4.wmine2_ref = bf16[4,8,2560]{2,1,0:T(8,128)(2,1)S(1)} collective-permute-done((bf16[4,8,2560]{2,1,0:T(8,128)(2,1)S(1)}, bf16[4,8,2560]{2,1,0:T(8,128)(2,1)S(1)}, u32[]{:S(2)}, u32[]{:S(2)}) %collective-permute-start.4) | collective-permute-done | bytes 163872 | tf_op jit(solution)/shard_map/ppermute | solution.py:473
  24.3 0.5 collective-permute-start.9
  24.8 1.7 %copy.27.patches_ref = bf16[2,4,117,128]{3,2,1,0:T(8,128)(2,1)} copy(bf16[2,4,117,128]{3,1,2,0:T(4,128)(2,1)} %param.14) | data formatting | bytes 479232 | tf_op args[0]
  26.5 1.3 %copy.28.prompts_ref = bf16[8,10,128]{2,1,0:T(8,128)(2,1)} copy(bf16[8,10,128]{2,0,1:T(8,128)(2,1)} %param.15) | data formatting | bytes 40960 | tf_op args[1]
  27.9 0.6 copy-done.6
  28.5 0.1 copy-done.7
  28.6 0.1 copy-done.8
  28.6 0.1 copy-done.9
  28.7 67.2 %tower.1 = (bf16[2,4,128,128]{3,2,1,0:T(8,128)(2,1)}, f32[2,4,117,128]{3,2,1,0:T(8,128)}, bf16[2,16,8,2560]{3,2,1,0:T(8,128)(2,1)}, f32[2,16,16,128]{3,2,1,0:T(8,128)}) custom-call(s32[2]{0:T(128)} %ids_ref.1, s32[8]{0:T(128)} %counts_ref.1, bf16[4,8,2560]{2,1,0:T(8,128)(2,1)} %copy-done.1, bf16[4,8,2560]{2,1,0:T(8,128)(2,1)} %copy-done.3, ...), custom_call_target="tpu_custom_call" | custom-call | tf_op jit(solution)/shard_map/tower/pallas_call | solution.py:408
  95.9 1.0 fusion.2
  96.9 0.1 collective-permute-start.10
  97.1 1.1 slice_bitcast_fusion
  98.2 0.5 collective-permute-start.16
  98.7 0.9 fusion.1
  99.6 1.1 collective-permute-start.11
  100.7 3.3 %collective-permute-done.11 = bf16[16,16,128]{2,1,0:T(8,128)(2,1)S(1)} collective-permute-done((bf16[16,16,128]{2,1,0:T(8,128)(2,1)S(1)}, bf16[16,16,128]{2,1,0:T(8,128)(2,1)S(1)}, u32[]{:S(2)}, u32[]{:S(2)}) %collective-permute-start.11) | collective-permute-done | bytes 65568 | tf_op jit(solution)/shard_map/ppermute | solution.py:469
  104.0 0.4 collective-permute-start.12
  104.4 3.9 %collective-permute-done.12 = bf16[16,16,128]{2,1,0:T(8,128)(2,1)S(1)} collective-permute-done((bf16[16,16,128]{2,1,0:T(8,128)(2,1)S(1)}, bf16[16,16,128]{2,1,0:T(8,128)(2,1)S(1)}, u32[]{:S(2)}, u32[]{:S(2)}) %collective-permute-start.12) | collective-permute-done | bytes 65568 | tf_op jit(solution)/shard_map/ppermute | solution.py:469
  108.4 0.1 collective-permute-start.13
  108.5 1.0 fusion
  109.4 4.9 %all-to-all-start = ((bf16[16,8,2560]{2,1,0:T(8,128)(2,1)}), bf16[16,8,2560]{2,1,0:T(8,128)(2,1)S(1)}, u32[]{:S(2)}, u32[]{:S(2)}) async-start(bf16[16,8,2560]{2,1,0:T(8,128)(2,1)} %fusion), calls=%async_computation | async-start | bytes 1310720 | tf_op jit(solution)/shard_map/all_to_all | solution.py:488
  114.4 2.0 %collective-permute-start.14 = (bf16[16,16,128]{2,1,0:T(8,128)(2,1)S(1)}, bf16[16,16,128]{2,1,0:T(8,128)(2,1)S(1)}, u32[]{:S(2)}, u32[]{:S(2)}) collective-permute-start(bf16[16,16,128]{2,1,0:T(8,128)(2,1)S(1)} %add_convert_fusion), channel_id=1, source_target_pairs={{0,4},{1,5},{2,6},{3,7},{4,0},{5,1},{6,2},{7,3},{8,12},{9,13},{10,... | collective-permute-start | bytes 196616 | tf_op jit(solution)/shard_map/ppermute | solution.py:469
  116.3 8.1 %collective-permute-done.14 = bf16[16,16,128]{2,1,0:T(8,128)(2,1)S(1)} collective-permute-done((bf16[16,16,128]{2,1,0:T(8,128)(2,1)S(1)}, bf16[16,16,128]{2,1,0:T(8,128)(2,1)S(1)}, u32[]{:S(2)}, u32[]{:S(2)}) %collective-permute-start.14) | collective-permute-done | bytes 65568 | tf_op jit(solution)/shard_map/ppermute | solution.py:469
  124.5 0.1 collective-permute-start.15
  124.6 0.9 copy.30
  125.5 0.4 collective-permute-done.15
  125.9 0.7 broadcast_select_fusion
  126.6 0.6 fusion.20
  127.2 2.6 %all-to-all-done = bf16[16,8,2560]{2,1,0:T(8,128)(2,1)S(1)} async-done(((bf16[16,8,2560]{2,1,0:T(8,128)(2,1)}), bf16[16,8,2560]{2,1,0:T(8,128)(2,1)S(1)}, u32[]{:S(2)}, u32[]{:S(2)}) %all-to-all-start) | async-done | bytes 655392 | tf_op jit(solution)/shard_map/all_to_all | solution.py:488
  129.7 0.1 convert_reduce_fusion
  129.8 0.1 collective-permute-start.17
  129.9 0.5 slice_bitcast_fusion.1
  130.4 0.6 copy.31
  131.1 0.6 copy.34
  131.7 0.6 fusion.3
  132.4 0.6 copy.33
  133.0 0.6 copy.32
  133.6 0.6 copy_bitcast_fusion
  (40 shorter events, 0.2 us)
Async XLA Ops:
  2.1 5.6 %collective-permute-start = (bf16[1,8,2560]{2,1,0:T(8,128)(2,1)}, bf16[1,8,2560]{2,1,0:T(8,128)(2,1)S(1)}, u32[]{:S(2)}, u32[]{:S(2)}) collective-permute-start(bf16[1,8,2560]{2,1,0:T(8,128)(2,1)} %pack.1), channel_id=1, source_target_pairs={{0,4},{1,5},{2,6},{3,7},{4,0},{5,1},{6,2},{7,3},{8,12},{9,13},{10,... | collective-permute-start | bytes 122888 | tf_op jit(solution)/shard_map/ppermute | solution.py:473
  5.1 5.9 %collective-permute-start.1 = (bf16[1,8,2560]{2,1,0:T(8,128)(2,1)}, bf16[1,8,2560]{2,1,0:T(8,128)(2,1)S(1)}, u32[]{:S(2)}, u32[]{:S(2)}) collective-permute-start(bf16[1,8,2560]{2,1,0:T(8,128)(2,1)} %pack.1), channel_id=1, source_target_pairs={{0,8},{1,9},{2,10},{3,11},{4,12},{5,13},{6,14},{7,15},{8,0},{9,1},... | collective-permute-start | bytes 122888 | tf_op jit(solution)/shard_map/ppermute | solution.py:473
  7.7 6.0 %collective-permute-start.2 = (bf16[1,8,2560]{2,1,0:T(8,128)(2,1)}, bf16[1,8,2560]{2,1,0:T(8,128)(2,1)S(1)}, u32[]{:S(2)}, u32[]{:S(2)}) collective-permute-start(bf16[1,8,2560]{2,1,0:T(8,128)(2,1)} %pack.1), channel_id=1, source_target_pairs={{0,12},{1,13},{2,14},{3,15},{4,8},{5,9},{6,10},{7,11},{8,4},{9,5},... | collective-permute-start | bytes 122888 | tf_op jit(solution)/shard_map/ppermute | solution.py:473
  14.5 13.4 %copy-start.1 = (bf16[4,8,2560]{2,1,0:T(8,128)(2,1)}, bf16[4,8,2560]{2,1,0:T(8,128)(2,1)S(1)}, u32[]{:S(2)}) copy-start(bf16[4,8,2560]{2,1,0:T(8,128)(2,1)S(1)} %pad_maximum_fusion.wmine0_ref) | copy-start | bytes 491524
  14.5 6.8 %collective-permute-start.3 = (bf16[4,8,2560]{2,1,0:T(8,128)(2,1)S(1)}, bf16[4,8,2560]{2,1,0:T(8,128)(2,1)S(1)}, u32[]{:S(2)}, u32[]{:S(2)}) collective-permute-start(bf16[4,8,2560]{2,1,0:T(8,128)(2,1)S(1)} %pad_maximum_fusion.wmine0_ref), channel_id=1, source_target_pairs={{0,1},{1,0},{2,3},{3,2},{4,5},{5,4},{6,7},{7,6},{8,9},{9,8},{10,11... | collective-permute-start | bytes 491528 | tf_op jit(solution)/shard_map/ppermute | solution.py:473
  16.1 8.2 %collective-permute-start.4 = (bf16[4,8,2560]{2,1,0:T(8,128)(2,1)S(1)}, bf16[4,8,2560]{2,1,0:T(8,128)(2,1)S(1)}, u32[]{:S(2)}, u32[]{:S(2)}) collective-permute-start(bf16[4,8,2560]{2,1,0:T(8,128)(2,1)S(1)} %pad_maximum_fusion.wmine0_ref), channel_id=1, source_target_pairs={{0,2},{1,3},{2,0},{3,1},{4,6},{5,7},{6,4},{7,5},{8,10},{9,11},{10,... | collective-permute-start | bytes 491528 | tf_op jit(solution)/shard_map/ppermute | solution.py:473
  17.6 6.7 %collective-permute-start.5 = (bf16[4,8,2560]{2,1,0:T(8,128)(2,1)S(1)}, bf16[4,8,2560]{2,1,0:T(8,128)(2,1)S(1)}, u32[]{:S(2)}, u32[]{:S(2)}) collective-permute-start(bf16[4,8,2560]{2,1,0:T(8,128)(2,1)S(1)} %pad_maximum_fusion.wmine0_ref), channel_id=1, source_target_pairs={{0,3},{1,2},{2,1},{3,0},{4,7},{5,6},{6,5},{7,4},{8,11},{9,10},{10,... | collective-permute-start | bytes 491528 | tf_op jit(solution)/shard_map/ppermute | solution.py:473
  18.1 9.8 %collective-permute-start.6 = (bf16[4,8,2560]{2,1,0:T(8,128)(2,1)S(1)}, bf16[4,8,2560]{2,1,0:T(8,128)(2,1)S(1)}, u32[]{:S(2)}, u32[]{:S(2)}) collective-permute-start(bf16[4,8,2560]{2,1,0:T(8,128)(2,1)S(1)} %pad_maximum_fusion.wmine0_ref), channel_id=1, source_target_pairs={{0,16},{16,0},{1,17},{17,1},{2,18},{18,2},{3,19},{19,3},{4,20},{20... | collective-permute-start | bytes 491528 | tf_op jit(solution)/shard_map/ppermute | solution.py:469
  21.3 6.6 %copy-start.3 = (bf16[4,8,2560]{2,1,0:T(8,128)(2,1)}, bf16[4,8,2560]{2,1,0:T(8,128)(2,1)S(1)}, u32[]{:S(2)}) copy-start(bf16[4,8,2560]{2,1,0:T(8,128)(2,1)S(1)} %collective-permute-done.3.wmine1_ref) | copy-start | bytes 491524
  21.3 6.5 %collective-permute-start.7 = (bf16[4,8,2560]{2,1,0:T(8,128)(2,1)S(1)}, bf16[4,8,2560]{2,1,0:T(8,128)(2,1)S(1)}, u32[]{:S(2)}, u32[]{:S(2)}) collective-permute-start(bf16[4,8,2560]{2,1,0:T(8,128)(2,1)S(1)} %collective-permute-done.3.wmine1_ref), channel_id=1, source_target_pairs={{0,16},{16,0},{1,17},{17,1},{2,18},{18,2},{3,19},{19,3},{4,20},{20... | collective-permute-start | bytes 491528 | tf_op jit(solution)/shard_map/ppermute | solution.py:469
  24.3 3.6 %copy-start.4 = (bf16[4,8,2560]{2,1,0:T(8,128)(2,1)}, bf16[4,8,2560]{2,1,0:T(8,128)(2,1)S(1)}, u32[]{:S(2)}) copy-start(bf16[4,8,2560]{2,1,0:T(8,128)(2,1)S(1)} %collective-permute-done.4.wmine2_ref) | copy-start | bytes 491524
  24.3 3.6 %collective-permute-start.8 = (bf16[4,8,2560]{2,1,0:T(8,128)(2,1)S(1)}, bf16[4,8,2560]{2,1,0:T(8,128)(2,1)S(1)}, u32[]{:S(2)}, u32[]{:S(2)}) collective-permute-start(bf16[4,8,2560]{2,1,0:T(8,128)(2,1)S(1)} %collective-permute-done.4.wmine2_ref), channel_id=1, source_target_pairs={{0,16},{16,0},{1,17},{17,1},{2,18},{18,2},{3,19},{19,3},{4,20},{20... | collective-permute-start | bytes 491528 | tf_op jit(solution)/shard_map/ppermute | solution.py:469
  24.3 3.6 %copy-start.5 = (bf16[4,8,2560]{2,1,0:T(8,128)(2,1)}, bf16[4,8,2560]{2,1,0:T(8,128)(2,1)S(1)}, u32[]{:S(2)}) copy-start(bf16[4,8,2560]{2,1,0:T(8,128)(2,1)S(1)} %collective-permute-done.5.wmine3_ref) | copy-start | bytes 491524
  24.3 3.6 %collective-permute-start.9 = (bf16[4,8,2560]{2,1,0:T(8,128)(2,1)S(1)}, bf16[4,8,2560]{2,1,0:T(8,128)(2,1)S(1)}, u32[]{:S(2)}, u32[]{:S(2)}) collective-permute-start(bf16[4,8,2560]{2,1,0:T(8,128)(2,1)S(1)} %collective-permute-done.5.wmine3_ref), channel_id=1, source_target_pairs={{0,16},{16,0},{1,17},{17,1},{2,18},{18,2},{3,19},{19,3},{4,20},{20... | collective-permute-start | bytes 491528 | tf_op jit(solution)/shard_map/ppermute | solution.py:469
  27.8 0.7 copy-start.6
  27.8 0.7 copy-start.7
  27.9 0.8 copy-start.8
  27.9 0.8 copy-start.9
  95.9 12.5 %copy-start = (bf16[2,16,8,2560]{3,2,1,0:T(8,128)(2,1)S(1)}, bf16[2,16,8,2560]{3,2,1,0:T(8,128)(2,1)}, u32[]{:S(2)}) copy-start(bf16[2,16,8,2560]{3,2,1,0:T(8,128)(2,1)} %get-tuple-element.20) | copy-start | bytes 3932164
  96.9 1.8 %collective-permute-start.10 = (bf16[16,16,128]{2,1,0:T(8,128)(2,1)S(1)}, bf16[16,16,128]{2,1,0:T(8,128)(2,1)S(1)}, u32[]{:S(2)}, u32[]{:S(2)}) collective-permute-start(bf16[16,16,128]{2,1,0:T(8,128)(2,1)S(1)} %fusion.2), channel_id=1, source_target_pairs={{0,16},{16,0},{1,17},{17,1},{2,18},{18,2},{3,19},{19,3},{4,20},{20... | collective-permute-start | bytes 196616 | tf_op jit(solution)/shard_map/ppermute | solution.py:469
  98.2 10.2 %collective-permute-start.16 = (bf16[16,8,2560]{2,1,0:T(8,128)(2,1)S(1)}, bf16[16,8,2560]{2,1,0:T(8,128)(2,1)S(1)}, u32[]{:S(2)}, u32[]{:S(2)}) collective-permute-start(bf16[16,8,2560]{2,1,0:T(8,128)(2,1)S(1)} %slice_bitcast_fusion), channel_id=1, source_target_pairs={{0,16},{16,0},{1,17},{17,1},{2,18},{18,2},{3,19},{19,3},{4,20},{20... | collective-permute-start | bytes 1966088 | tf_op jit(solution)/shard_map/ppermute | solution.py:469
  99.6 4.3 %collective-permute-start.11 = (bf16[16,16,128]{2,1,0:T(8,128)(2,1)S(1)}, bf16[16,16,128]{2,1,0:T(8,128)(2,1)S(1)}, u32[]{:S(2)}, u32[]{:S(2)}) collective-permute-start(bf16[16,16,128]{2,1,0:T(8,128)(2,1)S(1)} %fusion.1), channel_id=1, source_target_pairs={{0,2},{1,3},{2,0},{3,1},{4,6},{5,7},{6,4},{7,5},{8,10},{9,11},{10,... | collective-permute-start | bytes 196616 | tf_op jit(solution)/shard_map/ppermute | solution.py:469
  104.0 4.3 %collective-permute-start.12 = (bf16[16,16,128]{2,1,0:T(8,128)(2,1)S(1)}, bf16[16,16,128]{2,1,0:T(8,128)(2,1)S(1)}, u32[]{:S(2)}, u32[]{:S(2)}) collective-permute-start(bf16[16,16,128]{2,1,0:T(8,128)(2,1)S(1)} %add_convert_fusion.2), channel_id=1, source_target_pairs={{0,1},{1,0},{2,3},{3,2},{4,5},{5,4},{6,7},{7,6},{8,9},{9,8},{10,11... | collective-permute-start | bytes 196616 | tf_op jit(solution)/shard_map/ppermute | solution.py:469
  108.4 6.0 %collective-permute-start.13 = (bf16[16,16,128]{2,1,0:T(8,128)(2,1)S(1)}, bf16[16,16,128]{2,1,0:T(8,128)(2,1)S(1)}, u32[]{:S(2)}, u32[]{:S(2)}) collective-permute-start(bf16[16,16,128]{2,1,0:T(8,128)(2,1)S(1)} %add_convert_fusion.1), channel_id=1, source_target_pairs={{0,8},{1,9},{2,10},{3,11},{4,12},{5,13},{6,14},{7,15},{8,0},{9,1},... | collective-permute-start | bytes 196616 | tf_op jit(solution)/shard_map/ppermute | solution.py:469
  109.4 15.1 %copy-start.2 = (f32[2,4,117,128]{3,2,1,0:T(8,128)S(1)}, f32[2,4,117,128]{3,2,1,0:T(8,128)}, u32[]{:S(2)}) copy-start(f32[2,4,117,128]{3,2,1,0:T(8,128)} %get-tuple-element.22) | copy-start | bytes 1437700
  109.4 20.3 %all-to-all-start = ((bf16[16,8,2560]{2,1,0:T(8,128)(2,1)}), bf16[16,8,2560]{2,1,0:T(8,128)(2,1)S(1)}, u32[]{:S(2)}, u32[]{:S(2)}) async-start(bf16[16,8,2560]{2,1,0:T(8,128)(2,1)} %fusion), calls=%async_computation | async-start | bytes 1310720 | tf_op jit(solution)/shard_map/all_to_all | solution.py:488
  114.4 10.1 %collective-permute-start.14 = (bf16[16,16,128]{2,1,0:T(8,128)(2,1)S(1)}, bf16[16,16,128]{2,1,0:T(8,128)(2,1)S(1)}, u32[]{:S(2)}, u32[]{:S(2)}) collective-permute-start(bf16[16,16,128]{2,1,0:T(8,128)(2,1)S(1)} %add_convert_fusion), channel_id=1, source_target_pairs={{0,4},{1,5},{2,6},{3,7},{4,0},{5,1},{6,2},{7,3},{8,12},{9,13},{10,... | collective-permute-start | bytes 196616 | tf_op jit(solution)/shard_map/ppermute | solution.py:469
  124.5 1.4 %collective-permute-start.15 = (f32[16,16,128]{2,1,0:T(8,128)S(1)}, f32[16,16,128]{2,1,0:T(8,128)S(1)}, u32[]{:S(2)}, u32[]{:S(2)}) collective-permute-start(f32[16,16,128]{2,1,0:T(8,128)S(1)} %convert_add_fusion.1), channel_id=1, source_target_pairs={{0,16},{16,0},{1,17},{17,1},{2,18},{18,2},{3,19},{19,3},{4,20},{20... | collective-permute-start | bytes 393224 | tf_op jit(solution)/shard_map/ppermute | solution.py:469
  129.8 1.9 %collective-permute-start.17 = (f32[8,2560]{1,0:T(8,128)S(1)}, f32[8,2560]{1,0:T(8,128)S(1)}, u32[]{:S(2)}, u32[]{:S(2)}) collective-permute-start(f32[8,2560]{1,0:T(8,128)S(1)} %convert_reduce_fusion), channel_id=1, source_target_pairs={{0,16},{16,0},{1,17},{17,1},{2,18},{18,2},{3,19},{19,3},{4,20},{20... | collective-permute-start | bytes 245768 | tf_op jit(solution)/shard_map/ppermute | solution.py:469

commit v4 on v3

--- a/solution.py
+++ b/solution.py
@@ -62,7 +62,7 @@
     cls_ref, cot_ref, adj_ref,
     out_ref, pgrad_ref, gbig_ref, gsmall_ref,
     stage_ref, w_ref, wd_ref, wt_ref, wdt_ref, colb_ref, tokscr_ref, h_ref, g_ref, xh_ref, inv_ref,
-    qkvt_ref, pb_ref, ot_ref, qkvv_ref, pv_ref, ov_ref, pw_ref, hid_ref, du_ref, dqkv_ref,
+    qkvt_ref, pb_ref, ot_ref, qkvv_ref, pv_ref, ov_ref, pw_ref, qbd_ref, dob_ref, hid_ref, du_ref, dqkv_ref,
     dov_ref, ga_ref, gd_ref, gt_ref, gacc_ref,
 ):
     dp = lax.axis_index("dp") if split else 0
@@ -119,15 +119,12 @@
     def head_sums(left, rights):
         return dot_nn(gather_heads, jnp.concatenate([(left * right).astype(BF) for right in rights], axis=1))
 
-    blank = jnp.zeros((16, 128), BF)
-
-    def diag_pair(rows):
-        upper = jnp.concatenate([rows[:16], blank], axis=1)
-        return jnp.concatenate([upper, jnp.concatenate([blank, rows[16:]], axis=1)], axis=0)
-
-    def diag_full(pair, hp):
-        parts = [pair if at == hp else jnp.zeros_like(pair) for at in range(4)]
-        return jnp.concatenate(parts, axis=0)
+    def diag_heads(target_ref, at, rows):
+        for head in range(HEADS):
+            target_ref[at, 16 * head : 16 * head + 16, 128 * head : 128 * head + 128] = rows[16 * head : 16 * head + 16]
+
+    qbd_ref[...] = jnp.zeros_like(qbd_ref)
+    dob_ref[...] = jnp.zeros_like(dob_ref)
 
     def gain(l, k):
         return colb_ref[l * 8 + k]
@@ -153,11 +150,13 @@
         qkvt_ref[l, c, 256:384, :] = values
         for s in range(2):
             lanes = slice(128 * s, 128 * s + 128)
+            at = 2 * (c % 2) + s
+            diag_heads(qbd_ref, at, queries[:, lanes])
             key_rows = keys[:, lanes].T
             for hp in range(4):
                 span = slice(256 * hp, 256 * hp + 256)
                 rows = slice(32 * hp, 32 * hp + 32)
-                scores = dot_nn(key_rows, diag_full(diag_pair(queries[rows, lanes]), hp))
+                scores = dot_nn(key_rows, qbd_ref[at, :, span])
                 shifted = jnp.exp(scores - jnp.max(scores, axis=0, keepdims=True))
                 prob = (shifted * (1.0 / jnp.sum(shifted, axis=0, keepdims=True))).astype(BF)
                 pb_ref[l, 2 * c + s, :, span] = prob
@@ -314,20 +313,22 @@
                 ga_ref[:, COL_OUT[0] : COL_OUT[0] + 128] += dot_nt(ot_ref[l, c], dt)
         for s in range(2):
             lanes = slice(128 * s, 128 * s + 128)
+            at = 2 * (c % 2) + s
+            diag_heads(qbd_ref, at, queries[:, lanes])
             value_rows = values[:, lanes].T
+            for x in range(2):
+                diag_heads(dob_ref, 2 * at + x, grads[x][:, lanes])
             for hp in range(4):
                 span = slice(256 * hp, 256 * hp + 256)
                 rows = slice(32 * hp, 32 * hp + 32)
                 prob_bf = pb_ref[l, 2 * c + s, :, span]
                 prob = prob_bf.astype(F32)
-                query_pair = diag_pair(queries[rows, lanes])
                 for x in range(2):
-                    grad_pair = diag_pair(grads[x][rows, lanes])
-                    weighted = prob * dot_nn(value_rows, diag_full(grad_pair, hp))
+                    weighted = prob * dot_nn(value_rows, dob_ref[2 * at + x, :, span])
                     ds = (weighted - prob * jnp.sum(weighted, axis=0, keepdims=True)).astype(BF)
-                    dvalue = dot_nt(grad_pair, prob_bf)
+                    dvalue = dot_nt(dob_ref[2 * at + x, rows, span], prob_bf)
                     dquery = dot_nn(keys[rows, lanes], ds) * 0.25
-                    dkey = dot_nt(query_pair, ds)
+                    dkey = dot_nt(qbd_ref[at, rows, span], ds)
                     dqkv_ref[2 * c + x, 32 * hp : 32 * hp + 16, lanes] = dquery[:16, :128].astype(BF)
                     dqkv_ref[2 * c + x, 32 * hp + 16 : 32 * hp + 32, lanes] = dquery[16:, 128:].astype(BF)
                     dqkv_ref[2 * c + x, 128 + 32 * hp : 160 + 32 * hp, lanes] = dkey.astype(BF)
@@ -434,6 +435,8 @@
             pltpu.VMEM((2, 2, 4, 8, 512), F32),
             pltpu.VMEM((2, 4, 128, 256), BF),
             pltpu.VMEM((2, 2, 4, 128, 512), BF),
+            pltpu.VMEM((4, 128, 1024), BF),
+            pltpu.VMEM((8, 128, 1024), BF),
             pltpu.VMEM((2, 512, 256), BF),
             pltpu.VMEM((4, 1024, 256), BF),
             pltpu.VMEM((8, 384, 256), BF),

time: 135 us -> 125 us (0.926)
  Pallas kernels: 68.7 us -> 58.8 us
    pallas_call x1, Pallas kernels: 67.2 us -> 57.4 us  [run_tower(): pl.pallas_call(functools.partial(tower_kernel, split), out_shape=(jax.Sha...]
where the time goes in v4:
time: 125 us; the launch traced here: 124 us
  Pallas kernels  58.8 us (47%)
  waiting for transfers between devices  30.5 us (24%)
  starting transfers between devices  18.8 us (15%)
  local copies, waits for them, and re-layouts  10.5 us (8%)
  other arithmetic  4.85 us (4%)
    pallas_call x1, Pallas kernels, run_tower(): pl.pallas_call(functools.partial(tower_kernel, split), out_shape=(jax.Sha...  57.4 us
    ppermute x12, waiting for transfers between devices, flip(): return lax.ppermute(array, axis, [(i, i ^ 1 << bit) for i in range(size)])  15.7 us
    ppermute x6, waiting for transfers between devices, swap(): return lax.ppermute(array, 'fsdp', [(i, i ^ mask) for i in range(SHARDS)])  12.2 us
    ppermute x6, starting transfers between devices, swap(): return lax.ppermute(array, 'fsdp', [(i, i ^ mask) for i in range(SHARDS)])  9.17 us
    unnamed x27, local copies, waits for them, and re-layouts  7.2 us
    all_to_all x1, starting transfers between devices, reduce_big(): parts = lax.all_to_all(held.astype(BF), 'fsdp', 0, 0, tiled=True)  4.86 us
    ppermute x12, starting transfers between devices, flip(): return lax.ppermute(array, axis, [(i, i ^ 1 << bit) for i in range(size)])  4.8 us
    all_to_all x1, waiting for transfers between devices, reduce_big(): parts = lax.all_to_all(held.astype(BF), 'fsdp', 0, 0, tiled=True)  2.56 us
  transfers between devices with their start and end apart: 19, of which 9 were waited for; matrix products, arithmetic and copies ran while one was open for 8% of the time, Pallas kernels for 0%

profile of v4, /device:TPU:0, one launch (start us, length us, event | category | flops | bytes accessed | tf_op | source)
XLA Modules:
  0.0 124.3 jit_solution(11711115807556297223)
XLA Ops:
  0.6 1.4 %pack.1 = bf16[1,8,2560]{2,1,0:T(8,128)(2,1)} custom-call(bf16[2,2,8,384]{3,2,1,0:T(8,128)(2,1)} %attn_in_ref.1, bf16[2,2,8,128]{3,2,1,0:T(8,128)(2,1)} %attn_out_ref.1, bf16[2,8,1024]{2,1,0:T(8,128)(2,1)} %feed_in_ref.1, bf16[2,32,128]{2,1,0:T(8,128)(2,1)} %feed_out_ref.1), custom_call_target="tpu_custom_call" | custom-call | tf_op jit(solution)/shard_map/pack/pallas_call | solution.py:481
  2.1 3.0 %collective-permute-start = (bf16[1,8,2560]{2,1,0:T(8,128)(2,1)}, bf16[1,8,2560]{2,1,0:T(8,128)(2,1)S(1)}, u32[]{:S(2)}, u32[]{:S(2)}) collective-permute-start(bf16[1,8,2560]{2,1,0:T(8,128)(2,1)} %pack.1), channel_id=1, source_target_pairs={{0,4},{1,5},{2,6},{3,7},{4,0},{5,1},{6,2},{7,3},{8,12},{9,13},{10,... | collective-permute-start | bytes 122888 | tf_op jit(solution)/shard_map/ppermute | solution.py:476
  5.1 2.6 %collective-permute-start.1 = (bf16[1,8,2560]{2,1,0:T(8,128)(2,1)}, bf16[1,8,2560]{2,1,0:T(8,128)(2,1)S(1)}, u32[]{:S(2)}, u32[]{:S(2)}) collective-permute-start(bf16[1,8,2560]{2,1,0:T(8,128)(2,1)} %pack.1), channel_id=1, source_target_pairs={{0,8},{1,9},{2,10},{3,11},{4,12},{5,13},{6,14},{7,15},{8,0},{9,1},... | collective-permute-start | bytes 122888 | tf_op jit(solution)/shard_map/ppermute | solution.py:476
  7.7 3.3 %collective-permute-done.1 = bf16[1,8,2560]{2,1,0:T(8,128)(2,1)S(1)} collective-permute-done((bf16[1,8,2560]{2,1,0:T(8,128)(2,1)}, bf16[1,8,2560]{2,1,0:T(8,128)(2,1)S(1)}, u32[]{:S(2)}, u32[]{:S(2)}) %collective-permute-start.1) | collective-permute-done | bytes 40992 | tf_op jit(solution)/shard_map/ppermute | solution.py:476
  11.0 2.7 %collective-permute-done.2 = bf16[1,8,2560]{2,1,0:T(8,128)(2,1)S(1)} collective-permute-done((bf16[1,8,2560]{2,1,0:T(8,128)(2,1)}, bf16[1,8,2560]{2,1,0:T(8,128)(2,1)S(1)}, u32[]{:S(2)}, u32[]{:S(2)}) %collective-permute-start.2) | collective-permute-done | bytes 40992 | tf_op jit(solution)/shard_map/ppermute | solution.py:476
  13.7 0.8 pad_maximum_fusion.wmine0_ref
  14.5 1.6 %collective-permute-start.3 = (bf16[4,8,2560]{2,1,0:T(8,128)(2,1)S(1)}, bf16[4,8,2560]{2,1,0:T(8,128)(2,1)S(1)}, u32[]{:S(2)}, u32[]{:S(2)}) collective-permute-start(bf16[4,8,2560]{2,1,0:T(8,128)(2,1)S(1)} %pad_maximum_fusion.wmine0_ref), channel_id=1, source_target_pairs={{0,1},{1,0},{2,3},{3,2},{4,5},{5,4},{6,7},{7,6},{8,9},{9,8},{10,11... | collective-permute-start | bytes 491528 | tf_op jit(solution)/shard_map/ppermute | solution.py:476
  16.1 1.5 %collective-permute-start.4 = (bf16[4,8,2560]{2,1,0:T(8,128)(2,1)S(1)}, bf16[4,8,2560]{2,1,0:T(8,128)(2,1)S(1)}, u32[]{:S(2)}, u32[]{:S(2)}) collective-permute-start(bf16[4,8,2560]{2,1,0:T(8,128)(2,1)S(1)} %pad_maximum_fusion.wmine0_ref), channel_id=1, source_target_pairs={{0,2},{1,3},{2,0},{3,1},{4,6},{5,7},{6,4},{7,5},{8,10},{9,11},{10,... | collective-permute-start | bytes 491528 | tf_op jit(solution)/shard_map/ppermute | solution.py:476
  17.6 0.5 collective-permute-start.5
  18.1 3.2 %collective-permute-done.3.wmine1_ref = bf16[4,8,2560]{2,1,0:T(8,128)(2,1)S(1)} collective-permute-done((bf16[4,8,2560]{2,1,0:T(8,128)(2,1)S(1)}, bf16[4,8,2560]{2,1,0:T(8,128)(2,1)S(1)}, u32[]{:S(2)}, u32[]{:S(2)}) %collective-permute-start.3) | collective-permute-done | bytes 163872 | tf_op jit(solution)/shard_map/ppermute | solution.py:476
  21.3 3.0 %collective-permute-done.4.wmine2_ref = bf16[4,8,2560]{2,1,0:T(8,128)(2,1)S(1)} collective-permute-done((bf16[4,8,2560]{2,1,0:T(8,128)(2,1)S(1)}, bf16[4,8,2560]{2,1,0:T(8,128)(2,1)S(1)}, u32[]{:S(2)}, u32[]{:S(2)}) %collective-permute-start.4) | collective-permute-done | bytes 163872 | tf_op jit(solution)/shard_map/ppermute | solution.py:476
  24.3 0.5 collective-permute-start.9
  24.8 1.7 %copy.27.patches_ref = bf16[2,4,117,128]{3,2,1,0:T(8,128)(2,1)} copy(bf16[2,4,117,128]{3,1,2,0:T(4,128)(2,1)} %param.14) | data formatting | bytes 479232 | tf_op args[0]
  26.5 1.3 %copy.28.prompts_ref = bf16[8,10,128]{2,1,0:T(8,128)(2,1)} copy(bf16[8,10,128]{2,0,1:T(8,128)(2,1)} %param.15) | data formatting | bytes 40960 | tf_op args[1]
  27.9 0.6 copy-done.6
  28.5 0.1 copy-done.7
  28.6 0.1 copy-done.8
  28.6 0.1 copy-done.9
  28.7 57.4 %tower.1 = (bf16[2,4,128,128]{3,2,1,0:T(8,128)(2,1)}, f32[2,4,117,128]{3,2,1,0:T(8,128)}, bf16[2,16,8,2560]{3,2,1,0:T(8,128)(2,1)}, f32[2,16,16,128]{3,2,1,0:T(8,128)}) custom-call(s32[2]{0:T(128)} %ids_ref.1, s32[8]{0:T(128)} %counts_ref.1, bf16[4,8,2560]{2,1,0:T(8,128)(2,1)} %copy-done.1, bf16[4,8,2560]{2,1,0:T(8,128)(2,1)} %copy-done.3, ...), custom_call_target="tpu_custom_call" | custom-call | tf_op jit(solution)/shard_map/tower/pallas_call | solution.py:409
  86.0 1.0 fusion.2
  87.1 0.1 collective-permute-start.10
  87.2 1.1 slice_bitcast_fusion
  88.3 0.5 collective-permute-start.16
  88.8 0.9 fusion.1
  89.8 1.1 collective-permute-start.11
  90.8 3.3 %collective-permute-done.11 = bf16[16,16,128]{2,1,0:T(8,128)(2,1)S(1)} collective-permute-done((bf16[16,16,128]{2,1,0:T(8,128)(2,1)S(1)}, bf16[16,16,128]{2,1,0:T(8,128)(2,1)S(1)}, u32[]{:S(2)}, u32[]{:S(2)}) %collective-permute-start.11) | collective-permute-done | bytes 65568 | tf_op jit(solution)/shard_map/ppermute | solution.py:472
  94.1 0.4 collective-permute-start.12
  94.5 4.0 %collective-permute-done.12 = bf16[16,16,128]{2,1,0:T(8,128)(2,1)S(1)} collective-permute-done((bf16[16,16,128]{2,1,0:T(8,128)(2,1)S(1)}, bf16[16,16,128]{2,1,0:T(8,128)(2,1)S(1)}, u32[]{:S(2)}, u32[]{:S(2)}) %collective-permute-start.12) | collective-permute-done | bytes 65568 | tf_op jit(solution)/shard_map/ppermute | solution.py:472
  98.5 0.1 collective-permute-start.13
  98.6 1.0 fusion
  99.6 4.9 %all-to-all-start = ((bf16[16,8,2560]{2,1,0:T(8,128)(2,1)}), bf16[16,8,2560]{2,1,0:T(8,128)(2,1)S(1)}, u32[]{:S(2)}, u32[]{:S(2)}) async-start(bf16[16,8,2560]{2,1,0:T(8,128)(2,1)} %fusion), calls=%async_computation | async-start | bytes 1310720 | tf_op jit(solution)/shard_map/all_to_all | solution.py:491
  104.5 2.0 %collective-permute-start.14 = (bf16[16,16,128]{2,1,0:T(8,128)(2,1)S(1)}, bf16[16,16,128]{2,1,0:T(8,128)(2,1)S(1)}, u32[]{:S(2)}, u32[]{:S(2)}) collective-permute-start(bf16[16,16,128]{2,1,0:T(8,128)(2,1)S(1)} %add_convert_fusion), channel_id=1, source_target_pairs={{0,4},{1,5},{2,6},{3,7},{4,0},{5,1},{6,2},{7,3},{8,12},{9,13},{10,... | collective-permute-start | bytes 196616 | tf_op jit(solution)/shard_map/ppermute | solution.py:472
  106.5 8.1 %collective-permute-done.14 = bf16[16,16,128]{2,1,0:T(8,128)(2,1)S(1)} collective-permute-done((bf16[16,16,128]{2,1,0:T(8,128)(2,1)S(1)}, bf16[16,16,128]{2,1,0:T(8,128)(2,1)S(1)}, u32[]{:S(2)}, u32[]{:S(2)}) %collective-permute-start.14) | collective-permute-done | bytes 65568 | tf_op jit(solution)/shard_map/ppermute | solution.py:472
  114.6 0.1 collective-permute-start.15
  114.7 0.9 copy.30
  115.6 0.4 collective-permute-done.15
  116.0 0.7 broadcast_select_fusion
  116.7 0.6 fusion.20
  117.3 2.6 %all-to-all-done = bf16[16,8,2560]{2,1,0:T(8,128)(2,1)S(1)} async-done(((bf16[16,8,2560]{2,1,0:T(8,128)(2,1)}), bf16[16,8,2560]{2,1,0:T(8,128)(2,1)S(1)}, u32[]{:S(2)}, u32[]{:S(2)}) %all-to-all-start) | async-done | bytes 655392 | tf_op jit(solution)/shard_map/all_to_all | solution.py:491
  119.8 0.1 convert_reduce_fusion
  119.9 0.1 collective-permute-start.17
  120.0 0.5 slice_bitcast_fusion.1
  120.5 0.6 copy.31
  121.2 0.6 copy.34
  121.8 0.6 fusion.3
  122.5 0.6 copy.33
  123.1 0.6 copy.32
  123.7 0.6 copy_bitcast_fusion
  (40 shorter events, 0.2 us)
Async XLA Ops:
  2.1 5.6 %collective-permute-start = (bf16[1,8,2560]{2,1,0:T(8,128)(2,1)}, bf16[1,8,2560]{2,1,0:T(8,128)(2,1)S(1)}, u32[]{:S(2)}, u32[]{:S(2)}) collective-permute-start(bf16[1,8,2560]{2,1,0:T(8,128)(2,1)} %pack.1), channel_id=1, source_target_pairs={{0,4},{1,5},{2,6},{3,7},{4,0},{5,1},{6,2},{7,3},{8,12},{9,13},{10,... | collective-permute-start | bytes 122888 | tf_op jit(solution)/shard_map/ppermute | solution.py:476
  5.1 5.9 %collective-permute-start.1 = (bf16[1,8,2560]{2,1,0:T(8,128)(2,1)}, bf16[1,8,2560]{2,1,0:T(8,128)(2,1)S(1)}, u32[]{:S(2)}, u32[]{:S(2)}) collective-permute-start(bf16[1,8,2560]{2,1,0:T(8,128)(2,1)} %pack.1), channel_id=1, source_target_pairs={{0,8},{1,9},{2,10},{3,11},{4,12},{5,13},{6,14},{7,15},{8,0},{9,1},... | collective-permute-start | bytes 122888 | tf_op jit(solution)/shard_map/ppermute | solution.py:476
  7.7 6.0 %collective-permute-start.2 = (bf16[1,8,2560]{2,1,0:T(8,128)(2,1)}, bf16[1,8,2560]{2,1,0:T(8,128)(2,1)S(1)}, u32[]{:S(2)}, u32[]{:S(2)}) collective-permute-start(bf16[1,8,2560]{2,1,0:T(8,128)(2,1)} %pack.1), channel_id=1, source_target_pairs={{0,12},{1,13},{2,14},{3,15},{4,8},{5,9},{6,10},{7,11},{8,4},{9,5},... | collective-permute-start | bytes 122888 | tf_op jit(solution)/shard_map/ppermute | solution.py:476
  14.5 13.4 %copy-start.1 = (bf16[4,8,2560]{2,1,0:T(8,128)(2,1)}, bf16[4,8,2560]{2,1,0:T(8,128)(2,1)S(1)}, u32[]{:S(2)}) copy-start(bf16[4,8,2560]{2,1,0:T(8,128)(2,1)S(1)} %pad_maximum_fusion.wmine0_ref) | copy-start | bytes 491524
  14.5 6.8 %collective-permute-start.3 = (bf16[4,8,2560]{2,1,0:T(8,128)(2,1)S(1)}, bf16[4,8,2560]{2,1,0:T(8,128)(2,1)S(1)}, u32[]{:S(2)}, u32[]{:S(2)}) collective-permute-start(bf16[4,8,2560]{2,1,0:T(8,128)(2,1)S(1)} %pad_maximum_fusion.wmine0_ref), channel_id=1, source_target_pairs={{0,1},{1,0},{2,3},{3,2},{4,5},{5,4},{6,7},{7,6},{8,9},{9,8},{10,11... | collective-permute-start | bytes 491528 | tf_op jit(solution)/shard_map/ppermute | solution.py:476
  16.1 8.2 %collective-permute-start.4 = (bf16[4,8,2560]{2,1,0:T(8,128)(2,1)S(1)}, bf16[4,8,2560]{2,1,0:T(8,128)(2,1)S(1)}, u32[]{:S(2)}, u32[]{:S(2)}) collective-permute-start(bf16[4,8,2560]{2,1,0:T(8,128)(2,1)S(1)} %pad_maximum_fusion.wmine0_ref), channel_id=1, source_target_pairs={{0,2},{1,3},{2,0},{3,1},{4,6},{5,7},{6,4},{7,5},{8,10},{9,11},{10,... | collective-permute-start | bytes 491528 | tf_op jit(solution)/shard_map/ppermute | solution.py:476
  17.6 6.7 %collective-permute-start.5 = (bf16[4,8,2560]{2,1,0:T(8,128)(2,1)S(1)}, bf16[4,8,2560]{2,1,0:T(8,128)(2,1)S(1)}, u32[]{:S(2)}, u32[]{:S(2)}) collective-permute-start(bf16[4,8,2560]{2,1,0:T(8,128)(2,1)S(1)} %pad_maximum_fusion.wmine0_ref), channel_id=1, source_target_pairs={{0,3},{1,2},{2,1},{3,0},{4,7},{5,6},{6,5},{7,4},{8,11},{9,10},{10,... | collective-permute-start | bytes 491528 | tf_op jit(solution)/shard_map/ppermute | solution.py:476
  18.1 9.8 %collective-permute-start.6 = (bf16[4,8,2560]{2,1,0:T(8,128)(2,1)S(1)}, bf16[4,8,2560]{2,1,0:T(8,128)(2,1)S(1)}, u32[]{:S(2)}, u32[]{:S(2)}) collective-permute-start(bf16[4,8,2560]{2,1,0:T(8,128)(2,1)S(1)} %pad_maximum_fusion.wmine0_ref), channel_id=1, source_target_pairs={{0,16},{16,0},{1,17},{17,1},{2,18},{18,2},{3,19},{19,3},{4,20},{20... | collective-permute-start | bytes 491528 | tf_op jit(solution)/shard_map/ppermute | solution.py:472
  21.3 6.6 %copy-start.3 = (bf16[4,8,2560]{2,1,0:T(8,128)(2,1)}, bf16[4,8,2560]{2,1,0:T(8,128)(2,1)S(1)}, u32[]{:S(2)}) copy-start(bf16[4,8,2560]{2,1,0:T(8,128)(2,1)S(1)} %collective-permute-done.3.wmine1_ref) | copy-start | bytes 491524
  21.3 6.5 %collective-permute-start.7 = (bf16[4,8,2560]{2,1,0:T(8,128)(2,1)S(1)}, bf16[4,8,2560]{2,1,0:T(8,128)(2,1)S(1)}, u32[]{:S(2)}, u32[]{:S(2)}) collective-permute-start(bf16[4,8,2560]{2,1,0:T(8,128)(2,1)S(1)} %collective-permute-done.3.wmine1_ref), channel_id=1, source_target_pairs={{0,16},{16,0},{1,17},{17,1},{2,18},{18,2},{3,19},{19,3},{4,20},{20... | collective-permute-start | bytes 491528 | tf_op jit(solution)/shard_map/ppermute | solution.py:472
  24.3 3.6 %copy-start.4 = (bf16[4,8,2560]{2,1,0:T(8,128)(2,1)}, bf16[4,8,2560]{2,1,0:T(8,128)(2,1)S(1)}, u32[]{:S(2)}) copy-start(bf16[4,8,2560]{2,1,0:T(8,128)(2,1)S(1)} %collective-permute-done.4.wmine2_ref) | copy-start | bytes 491524
  24.3 3.6 %collective-permute-start.8 = (bf16[4,8,2560]{2,1,0:T(8,128)(2,1)S(1)}, bf16[4,8,2560]{2,1,0:T(8,128)(2,1)S(1)}, u32[]{:S(2)}, u32[]{:S(2)}) collective-permute-start(bf16[4,8,2560]{2,1,0:T(8,128)(2,1)S(1)} %collective-permute-done.4.wmine2_ref), channel_id=1, source_target_pairs={{0,16},{16,0},{1,17},{17,1},{2,18},{18,2},{3,19},{19,3},{4,20},{20... | collective-permute-start | bytes 491528 | tf_op jit(solution)/shard_map/ppermute | solution.py:472
  24.3 3.6 %copy-start.5 = (bf16[4,8,2560]{2,1,0:T(8,128)(2,1)}, bf16[4,8,2560]{2,1,0:T(8,128)(2,1)S(1)}, u32[]{:S(2)}) copy-start(bf16[4,8,2560]{2,1,0:T(8,128)(2,1)S(1)} %collective-permute-done.5.wmine3_ref) | copy-start | bytes 491524
  24.3 3.6 %collective-permute-start.9 = (bf16[4,8,2560]{2,1,0:T(8,128)(2,1)S(1)}, bf16[4,8,2560]{2,1,0:T(8,128)(2,1)S(1)}, u32[]{:S(2)}, u32[]{:S(2)}) collective-permute-start(bf16[4,8,2560]{2,1,0:T(8,128)(2,1)S(1)} %collective-permute-done.5.wmine3_ref), channel_id=1, source_target_pairs={{0,16},{16,0},{1,17},{17,1},{2,18},{18,2},{3,19},{19,3},{4,20},{20... | collective-permute-start | bytes 491528 | tf_op jit(solution)/shard_map/ppermute | solution.py:472
  27.8 0.7 copy-start.6
  27.8 0.7 copy-start.7
  27.9 0.8 copy-start.8
  27.9 0.8 copy-start.9
  86.0 12.5 %copy-start = (bf16[2,16,8,2560]{3,2,1,0:T(8,128)(2,1)S(1)}, bf16[2,16,8,2560]{3,2,1,0:T(8,128)(2,1)}, u32[]{:S(2)}) copy-start(bf16[2,16,8,2560]{3,2,1,0:T(8,128)(2,1)} %get-tuple-element.20) | copy-start | bytes 3932164
  87.1 1.8 %collective-permute-start.10 = (bf16[16,16,128]{2,1,0:T(8,128)(2,1)S(1)}, bf16[16,16,128]{2,1,0:T(8,128)(2,1)S(1)}, u32[]{:S(2)}, u32[]{:S(2)}) collective-permute-start(bf16[16,16,128]{2,1,0:T(8,128)(2,1)S(1)} %fusion.2), channel_id=1, source_target_pairs={{0,16},{16,0},{1,17},{17,1},{2,18},{18,2},{3,19},{19,3},{4,20},{20... | collective-permute-start | bytes 196616 | tf_op jit(solution)/shard_map/ppermute | solution.py:472
  88.3 10.2 %collective-permute-start.16 = (bf16[16,8,2560]{2,1,0:T(8,128)(2,1)S(1)}, bf16[16,8,2560]{2,1,0:T(8,128)(2,1)S(1)}, u32[]{:S(2)}, u32[]{:S(2)}) collective-permute-start(bf16[16,8,2560]{2,1,0:T(8,128)(2,1)S(1)} %slice_bitcast_fusion), channel_id=1, source_target_pairs={{0,16},{16,0},{1,17},{17,1},{2,18},{18,2},{3,19},{19,3},{4,20},{20... | collective-permute-start | bytes 1966088 | tf_op jit(solution)/shard_map/ppermute | solution.py:472
  89.8 4.3 %collective-permute-start.11 = (bf16[16,16,128]{2,1,0:T(8,128)(2,1)S(1)}, bf16[16,16,128]{2,1,0:T(8,128)(2,1)S(1)}, u32[]{:S(2)}, u32[]{:S(2)}) collective-permute-start(bf16[16,16,128]{2,1,0:T(8,128)(2,1)S(1)} %fusion.1), channel_id=1, source_target_pairs={{0,2},{1,3},{2,0},{3,1},{4,6},{5,7},{6,4},{7,5},{8,10},{9,11},{10,... | collective-permute-start | bytes 196616 | tf_op jit(solution)/shard_map/ppermute | solution.py:472
  94.1 4.3 %collective-permute-start.12 = (bf16[16,16,128]{2,1,0:T(8,128)(2,1)S(1)}, bf16[16,16,128]{2,1,0:T(8,128)(2,1)S(1)}, u32[]{:S(2)}, u32[]{:S(2)}) collective-permute-start(bf16[16,16,128]{2,1,0:T(8,128)(2,1)S(1)} %add_convert_fusion.2), channel_id=1, source_target_pairs={{0,1},{1,0},{2,3},{3,2},{4,5},{5,4},{6,7},{7,6},{8,9},{9,8},{10,11... | collective-permute-start | bytes 196616 | tf_op jit(solution)/shard_map/ppermute | solution.py:472
  98.5 6.0 %collective-permute-start.13 = (bf16[16,16,128]{2,1,0:T(8,128)(2,1)S(1)}, bf16[16,16,128]{2,1,0:T(8,128)(2,1)S(1)}, u32[]{:S(2)}, u32[]{:S(2)}) collective-permute-start(bf16[16,16,128]{2,1,0:T(8,128)(2,1)S(1)} %add_convert_fusion.1), channel_id=1, source_target_pairs={{0,8},{1,9},{2,10},{3,11},{4,12},{5,13},{6,14},{7,15},{8,0},{9,1},... | collective-permute-start | bytes 196616 | tf_op jit(solution)/shard_map/ppermute | solution.py:472
  99.6 15.1 %copy-start.2 = (f32[2,4,117,128]{3,2,1,0:T(8,128)S(1)}, f32[2,4,117,128]{3,2,1,0:T(8,128)}, u32[]{:S(2)}) copy-start(f32[2,4,117,128]{3,2,1,0:T(8,128)} %get-tuple-element.22) | copy-start | bytes 1437700
  99.6 20.3 %all-to-all-start = ((bf16[16,8,2560]{2,1,0:T(8,128)(2,1)}), bf16[16,8,2560]{2,1,0:T(8,128)(2,1)S(1)}, u32[]{:S(2)}, u32[]{:S(2)}) async-start(bf16[16,8,2560]{2,1,0:T(8,128)(2,1)} %fusion), calls=%async_computation | async-start | bytes 1310720 | tf_op jit(solution)/shard_map/all_to_all | solution.py:491
  104.5 10.1 %collective-permute-start.14 = (bf16[16,16,128]{2,1,0:T(8,128)(2,1)S(1)}, bf16[16,16,128]{2,1,0:T(8,128)(2,1)S(1)}, u32[]{:S(2)}, u32[]{:S(2)}) collective-permute-start(bf16[16,16,128]{2,1,0:T(8,128)(2,1)S(1)} %add_convert_fusion), channel_id=1, source_target_pairs={{0,4},{1,5},{2,6},{3,7},{4,0},{5,1},{6,2},{7,3},{8,12},{9,13},{10,... | collective-permute-start | bytes 196616 | tf_op jit(solution)/shard_map/ppermute | solution.py:472
  114.6 1.4 %collective-permute-start.15 = (f32[16,16,128]{2,1,0:T(8,128)S(1)}, f32[16,16,128]{2,1,0:T(8,128)S(1)}, u32[]{:S(2)}, u32[]{:S(2)}) collective-permute-start(f32[16,16,128]{2,1,0:T(8,128)S(1)} %convert_add_fusion.1), channel_id=1, source_target_pairs={{0,16},{16,0},{1,17},{17,1},{2,18},{18,2},{3,19},{19,3},{4,20},{20... | collective-permute-start | bytes 393224 | tf_op jit(solution)/shard_map/ppermute | solution.py:472
  119.9 1.9 %collective-permute-start.17 = (f32[8,2560]{1,0:T(8,128)S(1)}, f32[8,2560]{1,0:T(8,128)S(1)}, u32[]{:S(2)}, u32[]{:S(2)}) collective-permute-start(f32[8,2560]{1,0:T(8,128)S(1)} %convert_reduce_fusion), channel_id=1, source_target_pairs={{0,16},{16,0},{1,17},{17,1},{2,18},{18,2},{3,19},{19,3},{4,20},{20... | collective-permute-start | bytes 245768 | tf_op jit(solution)/shard_map/ppermute | solution.py:472

commit v5 on v4

--- a/solution.py
+++ b/solution.py
@@ -58,12 +58,11 @@
 def tower_kernel(
     split,
     ids_ref, counts_ref, wmine0_ref, wmine1_ref, wmine2_ref, wmine3_ref, wother0_ref, wother1_ref, wother2_ref, wother3_ref,
-    tok_ref, gains_ref, scales_ref, patches_ref, prompts_ref,
-    cls_ref, cot_ref, adj_ref,
-    out_ref, pgrad_ref, gbig_ref, gsmall_ref,
+    tok_ref, gains_ref, scales_ref, patches_ref, prompts_ref, cls_ref, cot_ref, adj_ref,
+    out_ref, pgrad_ref, bigmine_ref, bigother_ref, smallmine_ref, smallother_ref,
     stage_ref, w_ref, wd_ref, wt_ref, wdt_ref, colb_ref, tokscr_ref, h_ref, g_ref, xh_ref, inv_ref,
     qkvt_ref, pb_ref, ot_ref, qkvv_ref, pv_ref, ov_ref, pw_ref, qbd_ref, dob_ref, hid_ref, du_ref, dqkv_ref,
-    dov_ref, ga_ref, gd_ref, gt_ref, gacc_ref,
+    dov_ref, ga_ref, gf_ref, gd_ref, gt_ref, gacc_ref, gbig_ref, pacc_ref,
 ):
     dp = lax.axis_index("dp") if split else 0
     me = lax.axis_index("fsdp") if split else 0
@@ -239,7 +238,7 @@
                 dhid = dot_nn(wd_ref[l, rows, :], dz[x])
                 du_ref[2 * (c % 2) + x, 128 * z : 128 * z + 128, :] = (dhid * slope).astype(BF)
                 du_ref[2 * (c % 2) + x, 512 + 128 * z : 640 + 128 * z, :] = (dhid * act).astype(BF)
-        ga_ref[:, COL_FEED:COL_DOWN] += dot_nt(n, du_ref[2 * (c % 2)])
+        gf_ref[...] += dot_nt(du_ref[2 * (c % 2)], n)
         gd_ref[...] += dot_nt(hid_ref[c % 2], dz[0])
         for x in range(2):
             dn = dot_nn(w_ref[l, :, COL_FEED:COL_DOWN], du_ref[2 * (c % 2) + x])
@@ -355,21 +354,25 @@
 
     gacc_ref[...] = jnp.zeros_like(gacc_ref)
     gt_ref[...] = jnp.zeros_like(gt_ref)
-    gsmall_ref[...] = jnp.zeros_like(gsmall_ref)
-    rest = 1 ^ dp
+    pacc_ref[...] = jnp.zeros_like(pacc_ref)
+
     def backward_layer(step, carry):
         l = layers - 1 - step
         ga_ref[...] = jnp.zeros_like(ga_ref)
         gd_ref[...] = jnp.zeros_like(gd_ref)
+        gf_ref[...] = jnp.zeros_like(gf_ref)
         each(chunks, feed_backward, l)
         each(chunks, token_backward, l)
         each(items, var_backward, l)
         each(chunks, time_backward, l)
-        l_at = l ^ dp
+        for k in range(8):
+            turned = gf_ref[128 * k : 128 * k + 128, :].T
+            for f in range(SHARDS):
+                gbig_ref[l, f, :, COL_FEED + 128 * k : COL_FEED + 128 * k + 128] = turned[8 * f : 8 * f + 8].astype(BF)
         for f in range(SHARDS):
+            gbig_ref[l, f, :, 0:COL_FEED] = ga_ref[8 * f : 8 * f + 8, :].astype(BF)
             down = jnp.concatenate([gd_ref[32 * f + 8 * a : 32 * f + 8 * a + 8, :] for a in range(4)], axis=1)
-            block = jnp.concatenate([ga_ref[8 * f : 8 * f + 8, :], down], axis=1)
-            gbig_ref[l_at, f] = block.astype(BF)
+            gbig_ref[l, f, :, COL_DOWN:COLS] = down.astype(BF)
         gains_rows = [jnp.sum(gacc_ref[l * 4 + k].T, axis=0, keepdims=True) for k in range(4)]
         sums = [
             jnp.sum(w_ref[l, :, COL_OUT[k] : COL_OUT[k] + 128].astype(F32) * ga_ref[:, COL_OUT[k] : COL_OUT[k] + 128], axis=0, keepdims=True)
@@ -378,10 +381,8 @@
         sums.append(gains_ref[l, 2:3, :] * gains_rows[2])
         sums.append(jnp.sum(wd_ref[l].astype(F32) * gd_ref[...], axis=0, keepdims=True))
         for k in range(4):
-            gsmall_ref[rest, l * 4 + k, 10:11, :] = gains_rows[k]
-            gsmall_ref[rest, l * 4 + k, 11:12, :] = sums[k] / scales_ref[l, k : k + 1, :]
-        for block in range(8):
-            gsmall_ref[dp, 8 * l + block] = gt_ref[l, 16 * block : 16 * block + 16, :]
+            pacc_ref[0, l * 4 + k, 10:11, :] = gains_rows[k]
+            pacc_ref[0, l * 4 + k, 11:12, :] = sums[k] / scales_ref[l, k : k + 1, :]
         return carry
 
     lax.fori_loop(0, layers, backward_layer, 0)
@@ -399,24 +400,47 @@
                 cls_sum = last if cls_sum is None else cls_sum + last
                 if x == 0:
                     pgrad_ref[b, v] = tokscr_ref[4 * b + v, 10:127, :]
-            gsmall_ref[rest, 8 * x + ids_ref[b], 0:10, :] += prompt_sum
-        gsmall_ref[rest, 8 * x, 12:13, :] = cls_sum
+            pacc_ref[x, ids_ref[b], 0:10, :] += prompt_sum
+        pacc_ref[x, 0, 12:13, :] = cls_sum
+
+    for big_ref, small_ref, c in ((bigmine_ref, smallmine_ref, dp), (bigother_ref, smallother_ref, 1 - dp)):
+        for rel in range(SHARDS):
+            big_ref[rel % 4, rel // 4] = gbig_ref[c, me ^ rel]
+        for block in range(16):
+            if block < 8:
+                pair = gt_ref[c, 16 * block : 16 * block + 16, :]
+            else:
+                pair = pacc_ref[block // 4 - 2, 4 * c + block % 4]
+            lanes = slice(256 * (block % 4), 256 * (block % 4) + 256)
+            small_ref[block // 4, :, lanes] = jnp.concatenate([pair[:8], pair[8:]], axis=1)
+
+
+def call(kernel, name, out_shape, in_spaces, scratch, *operands, cost=None):
+    spaces = {"v": pltpu.VMEM, "s": pltpu.SMEM}
+    return pl.pallas_call(
+        kernel,
+        out_shape=out_shape,
+        in_specs=[pl.BlockSpec(memory_space=spaces[space]) for space in in_spaces],
+        out_specs=[pl.BlockSpec(memory_space=pltpu.VMEM)] * len(out_shape),
+        scratch_shapes=scratch,
+        compiler_params=pltpu.CompilerParams(vmem_limit_bytes=58 * 1024 * 1024),
+        cost_estimate=cost,
+        name=name,
+    )(*operands)
+
+
+def shape_of(shape, kind=F32):
+    return jax.ShapeDtypeStruct(shape, kind)
 
 
 def run_tower(split, *operands):
-    vmem = pl.BlockSpec(memory_space=pltpu.VMEM)
-    smem = pl.BlockSpec(memory_space=pltpu.SMEM)
-    return pl.pallas_call(
+    half = [shape_of((4, 4, 8, COLS), BF)] * 2 + [shape_of((4, 8, 1024))] * 2
+    return call(
         functools.partial(tower_kernel, split),
-        out_shape=(
-            jax.ShapeDtypeStruct((2, 4, 128, 128), BF),
-            jax.ShapeDtypeStruct((2, 4, 117, 128), F32),
-            jax.ShapeDtypeStruct((2, SHARDS, 8, COLS), BF),
-            jax.ShapeDtypeStruct((2, 16, 16, 128), F32),
-        ),
-        in_specs=[smem, smem] + [vmem] * 16,
-        out_specs=[vmem] * 4,
-        scratch_shapes=[
+        "tower",
+        [shape_of((2, 4, 128, 128), BF), shape_of((2, 4, 117, 128))] + half,
+        "ss" + "v" * 16,
+        [
             pltpu.VMEM((2, 128, COLS), F32),
             pltpu.VMEM((2, 128, COL_DOWN), BF),
             pltpu.VMEM((2, 512, 128), BF),
@@ -441,14 +465,17 @@
             pltpu.VMEM((4, 1024, 256), BF),
             pltpu.VMEM((8, 384, 256), BF),
             pltpu.VMEM((8, 128, 256), BF),
-            pltpu.VMEM((128, COL_DOWN), F32),
+            pltpu.VMEM((128, COL_FEED), F32),
+            pltpu.VMEM((1024, 128), F32),
             pltpu.VMEM((512, 128), F32),
             pltpu.VMEM((2, 128, 128), F32),
             pltpu.VMEM((8, 128, 128), F32),
+            pltpu.VMEM((2, SHARDS, 8, COLS), BF),
+            pltpu.VMEM((2, 8, 16, 128), F32),
         ],
-        compiler_params=pltpu.CompilerParams(vmem_limit_bytes=56 * 1024 * 1024),
-        name="tower",
-    )(*operands)
+        *operands,
+        cost=pl.CostEstimate(flops=10**10, bytes_accessed=20 * 10**6, transcendentals=0),
+    )
 
 
 def pack_rows(attn_in, attn_out, feed_in, feed_out):
@@ -477,37 +504,63 @@
 
 
 def gather_rows(attn_in, attn_out, feed_in, feed_out):
-    vmem = pl.BlockSpec(memory_space=pltpu.VMEM)
-    row = pl.pallas_call(
-        pack_kernel, out_shape=jax.ShapeDtypeStruct((1, 8, COLS), BF), in_specs=[vmem] * 4, out_specs=vmem, name="pack",
-    )(attn_in, attn_out, feed_in, feed_out)
+    row = call(pack_kernel, "pack", [shape_of((1, 8, COLS), BF)], "vvvv", [], attn_in, attn_out, feed_in, feed_out)[0]
     column = jnp.concatenate([row] + [swap(row, 4 * z) for z in range(1, 4)], axis=0)
     mine = [column] + [swap(column, xy) for xy in range(1, 4)]
     return mine + [flip(part, "dp", 0, 2) for part in mine]
 
 
-def reduce_big(big):
-    held = big[0].astype(F32) + flip(big[1], "dp", 0, 2).astype(F32)
-    parts = lax.all_to_all(held.astype(BF), "fsdp", 0, 0, tiled=True)
-    return jnp.sum(parts.astype(F32), axis=0)
-
-
-def reduce_small(small):
-    held = small[0] + flip(small[1].astype(BF), "dp", 0, 2).astype(F32)
-    for bit in STEP_BITS[::-1]:
-        mine = held.astype(BF)
-        held = mine.astype(F32) + flip(mine, "fsdp", bit, SHARDS).astype(F32)
-    return held
-
-
-def both_cores(mine, dp):
-    other = flip(mine, "dp", 0, 2)
-    return jnp.where(dp == 0, mine, other), jnp.where(dp == 0, other, mine)
+def final_kernel(big_mine, big_other, small_mine, small_other, attn_in, attn_out, feed_in, feed_out, tokens, gains, scales,
+                 prompt, cls, adjust_prompt, adjust_cls):
+    dp = lax.axis_index("dp")
+    for part, l in ((big_mine, dp), (big_other, 1 - dp)):
+        for k in range(2):
+            attn_in[l, k] = part[:, COL_IN[k] : COL_IN[k] + 384]
+            attn_out[l, k] = part[:, COL_OUT[k] : COL_OUT[k] + 128]
+        feed_in[l] = part[:, COL_FEED:COL_DOWN]
+        for a in range(4):
+            feed_out[l, 8 * a : 8 * a + 8, :] = part[:, COL_DOWN + 128 * a : COL_DOWN + 128 * a + 128]
+    for c in range(2):
+        parts = [slice(256 * k, 256 * k + 256) for k in range(16)]
+        tiles = [jnp.where(dp == c, small_mine[:, part], small_other[:, part]) for part in parts]
+        blocks = [jnp.concatenate([tile[:, :128], tile[:, 128:]], axis=0) for tile in tiles]
+        for k in range(8):
+            tokens[c, 16 * k : 16 * k + 16, :] = blocks[k]
+        for k in range(4):
+            for row in range(10):
+                prompt[row, 4 * c + k : 4 * c + k + 1, :] = blocks[8 + k][row : row + 1]
+                adjust_prompt[row, 4 * c + k : 4 * c + k + 1, :] = blocks[12 + k][row : row + 1]
+            gains[c, k : k + 1, :] = blocks[8 + k][10:11]
+            scales[c, k : k + 1, :] = blocks[8 + k][11:12]
+        if c == 0:
+            cls[...] = blocks[8][12:13]
+            adjust_cls[...] = blocks[12][12:13]
+
+
+def four(first, rest):
+    return (first.astype(F32) + rest[0].astype(F32)) + (rest[1].astype(F32) + rest[2].astype(F32))
+
+
+def reduce_all(big_mine, big_other, small_mine, small_other):
+    big = (big_mine.astype(F32) + flip(big_other, "dp", 0, 2).astype(F32)).astype(BF)
+    small = (small_mine + flip(small_other, "dp", 0, 2)).astype(BF)
+    got = [swap(jnp.concatenate([big[xy], small], axis=2), xy) for xy in range(1, 4)]
+    big = four(big[0], [part[:, :, :COLS] for part in got]).astype(BF)
+    small = four(small, [part[:, :, COLS:] for part in got]).astype(BF)
+    small = jnp.concatenate([small[at] for at in range(4)], axis=1)
+    got = [swap(jnp.concatenate([big[z], small], axis=1), 4 * z) for z in range(1, 4)]
+    big = four(big[0], [part[:, :COLS] for part in got])
+    small = four(small, [part[:, COLS:] for part in got])
+    return call(
+        final_kernel, "final",
+        [shape_of((2, 2, 8, 384)), shape_of((2, 2, 8, 128)), shape_of((2, 8, 1024)), shape_of((2, 32, 128)), shape_of((2, 128, 128)),
+         shape_of((2, 4, 128)), shape_of((2, 4, 128)), shape_of((10, 8, 128)), shape_of((1, 128)), shape_of((10, 8, 128)), shape_of((1, 128))],
+        "vvvv", [], big, flip(big, "dp", 0, 2), small, flip(small, "dp", 0, 2),
+    )
 
 
 def per_device(shard_count, patches, prompts, cls_token, attn_in, attn_out, feed_in, feed_out, token_operator,
                norm_gains, branch_scales, var_counts, dataset_ids, cotangent, adjust_cotangent):
-    dp = lax.axis_index("dp")
     fast = shard_count == SHARDS
     if fast:
         gathered = gather_rows(attn_in, attn_out, feed_in, feed_out)
@@ -522,32 +575,29 @@
         )
         rows = rows.reshape(2, SHARDS, 8, COLS).transpose(1, 0, 2, 3)
         gathered = [rows[:, l].reshape(4, 4, 8, COLS)[:, xy] for l in range(2) for xy in range(4)]
-    output, patch_grad, big, small = run_tower(
+    output, patch_grad, *sums = run_tower(
         fast, dataset_ids, var_counts, *gathered, token_operator, norm_gains, branch_scales, patches, prompts,
         cls_token.reshape(1, -1), cotangent, adjust_cotangent,
     )
     if fast:
-        layer_grads = both_cores(reduce_big(big), dp)
-        grads = unpack_rows(jnp.stack(layer_grads))
-        tokens, rest = both_cores(reduce_small(small), dp)
-    else:
-        rows = big.astype(F32).reshape(2, 128, COLS)
-        attn_in_g, attn_out_g, feed_in_g, feed_out_g = unpack_rows(rows)
-        feed_out_g = feed_out_g.reshape(2, 4, SHARDS, 8, 128).transpose(0, 2, 1, 3, 4).reshape(2, 512, 128)
-        grads = (
-            lax.psum_scatter(lax.psum(attn_in_g, "dp"), "fsdp", scatter_dimension=2, tiled=True),
-            lax.psum_scatter(lax.psum(attn_out_g, "dp"), "fsdp", scatter_dimension=2, tiled=True),
-            lax.psum_scatter(lax.psum(feed_in_g, "dp"), "fsdp", scatter_dimension=1, tiled=True),
-            lax.psum_scatter(lax.psum(feed_out_g, "dp"), "fsdp", scatter_dimension=1, tiled=True),
-        )
-        tokens, rest = lax.psum(small, ("dp", "fsdp"))
-    token_grad = tokens.reshape(2, 128, 128)
-    gains_grad = rest[:8, 10].reshape(2, 4, 128)
-    scales_grad = rest[:8, 11].reshape(2, 4, 128)
-    return (
-        output, patch_grad, rest[:8, :10], rest[0, 12], *grads, token_grad, gains_grad, scales_grad,
-        rest[8:, :10], rest[8, 12],
+        (attn_in_g, attn_out_g, feed_in_g, feed_out_g, token_g, gains_g, scales_g, prompt_g, cls_g, adjust_prompt_g,
+         adjust_cls_g) = reduce_all(*sums)
+        return (output, patch_grad, prompt_g.transpose(1, 0, 2), cls_g[0], attn_in_g, attn_out_g, feed_in_g, feed_out_g, token_g, gains_g,
+                scales_g, adjust_prompt_g.transpose(1, 0, 2), adjust_cls_g[0])
+    rows = jnp.stack(sums[:2]).transpose(0, 2, 1, 3, 4).astype(F32).reshape(2, 128, COLS)
+    attn_in_g, attn_out_g, feed_in_g, feed_out_g = unpack_rows(rows)
+    feed_out_g = feed_out_g.reshape(2, 4, SHARDS, 8, 128).transpose(0, 2, 1, 3, 4).reshape(2, 512, 128)
+    matrices = (
+        lax.psum_scatter(lax.psum(attn_in_g, "dp"), "fsdp", scatter_dimension=2, tiled=True),
+        lax.psum_scatter(lax.psum(attn_out_g, "dp"), "fsdp", scatter_dimension=2, tiled=True),
+        lax.psum_scatter(lax.psum(feed_in_g, "dp"), "fsdp", scatter_dimension=1, tiled=True),
+        lax.psum_scatter(lax.psum(feed_out_g, "dp"), "fsdp", scatter_dimension=1, tiled=True),
     )
+    small = lax.psum(jnp.stack(sums[2:]), ("dp", "fsdp"))
+    small = small.reshape(2, 4, 8, 4, 2, 128).transpose(0, 1, 3, 4, 2, 5).reshape(2, 16, 16, 128)
+    main, adjust = small[:, 8:12].reshape(8, 16, 128), small[:, 12:].reshape(8, 16, 128)
+    return (output, patch_grad, main[:, :10], main[0, 12], *matrices, small[:, :8].reshape(2, 128, 128),
+            main[:, 10].reshape(2, 4, 128), main[:, 11].reshape(2, 4, 128), adjust[:, :10], adjust[0, 12])
 
 
 def solution(mesh):

time: 125 us -> 118 us (0.944)
  local copies, waits for them, and re-layouts: 10.5 us -> 5.08 us
  other arithmetic: 4.85 us -> 3.2 us
  Pallas kernels: 58.8 us -> 60.4 us
  waiting for transfers between devices: 30.5 us -> 29.1 us
    ppermute x6 -> x12, waiting for transfers between devices: 12.2 us -> 27.1 us  [swap(): return lax.ppermute(array, 'fsdp', [(i, i ^ mask) for i in range(SHARDS)])]
    ppermute x12 -> x8, waiting for transfers between devices: 15.7 us -> 2.02 us  [flip(): return lax.ppermute(array, axis, [(i, i ^ 1 << bit) for i in range(size)])]
    ppermute x6 -> x12, starting transfers between devices: 9.17 us -> 17.2 us  [swap(): return lax.ppermute(array, 'fsdp', [(i, i ^ mask) for i in range(SHARDS)])]
    all_to_all x1 -> x0, starting transfers between devices: 4.86 us -> none  [reduce_big(): parts = lax.all_to_all(held.astype(BF), 'fsdp', 0, 0, tiled=True)]
    ppermute x12 -> x8, starting transfers between devices: 4.8 us -> 1.66 us  [flip(): return lax.ppermute(array, axis, [(i, i ^ 1 << bit) for i in range(size)])]
    all_to_all x1 -> x0, waiting for transfers between devices: 2.56 us -> none  [reduce_big(): parts = lax.all_to_all(held.astype(BF), 'fsdp', 0, 0, tiled=True)]
    unnamed x27 -> x35, local copies, waits for them, and re-layouts: 7.2 us -> 5.04 us
    pallas_call x2 -> x3, Pallas kernels: 58.8 us -> 60.4 us  [call(): pl.pallas_call(kernel, out_shape=out_shape, in_specs=[pl.BlockSpec(memory...]
  transfers between devices with their start and end apart: 19 -> 20, of which waited for: 9 -> 10; matrix products, arithmetic and copies ran while one was open for 8% -> 3% of each run, Pallas kernels for 0% -> 0%
where the time goes in v5:
time: 118 us
  Pallas kernels  60.4 us (51%)
  waiting for transfers between devices  29.1 us (25%)
  starting transfers between devices  18.8 us (16%)
  local copies, waits for them, and re-layouts  5.08 us (4%)
  other arithmetic  3.2 us (3%)
    pallas_call x3, Pallas kernels, call(): pl.pallas_call(kernel, out_shape=out_shape, in_specs=[pl.BlockSpec(memory...  60.4 us
    ppermute x12, waiting for transfers between devices, swap(): return lax.ppermute(array, 'fsdp', [(i, i ^ mask) for i in range(SHARDS)])  27.1 us
    ppermute x12, starting transfers between devices, swap(): return lax.ppermute(array, 'fsdp', [(i, i ^ mask) for i in range(SHARDS)])  17.2 us
    unnamed x35, local copies, waits for them, and re-layouts  5.04 us
  transfers between devices with their start and end apart: 20, of which 10 were waited for; matrix products, arithmetic and copies ran while one was open for 3% of the time, Pallas kernels for 0%

profile of v5, /device:TPU:0, one launch (start us, length us, event | category | flops | bytes accessed | tf_op | source)
XLA Modules:
  0.0 117.6 jit_solution(15566647019986277650)
XLA Ops:
  0.7 1.5 %pack.1 = bf16[1,8,2560]{2,1,0:T(8,128)(2,1)} custom-call(bf16[2,2,8,384]{3,2,1,0:T(8,128)(2,1)} %attn_in_ref.1, bf16[2,2,8,128]{3,2,1,0:T(8,128)(2,1)} %attn_out_ref.1, bf16[2,8,1024]{2,1,0:T(8,128)(2,1)} %feed_in_ref.1, bf16[2,32,128]{2,1,0:T(8,128)(2,1)} %feed_out_ref.1), custom_call_target="tpu_custom_call" | custom-call | tf_op jit(solution)/shard_map/pack/pallas_call | solution.py:420
  2.1 5.0 %collective-permute-start.2 = (bf16[1,8,2560]{2,1,0:T(8,128)(2,1)}, bf16[1,8,2560]{2,1,0:T(8,128)(2,1)S(1)}, u32[]{:S(2)}, u32[]{:S(2)}) collective-permute-start(bf16[1,8,2560]{2,1,0:T(8,128)(2,1)} %pack.1), channel_id=1, source_target_pairs={{0,12},{1,13},{2,14},{3,15},{4,8},{5,9},{6,10},{7,11},{8,4},{9,5},... | collective-permute-start | bytes 122888 | tf_op jit(solution)/shard_map/ppermute | solution.py:503
  7.2 0.0 collective-permute-start.1
  7.2 0.6 collective-permute-start
  7.7 1.6 %collective-permute-done.2 = bf16[1,8,2560]{2,1,0:T(8,128)(2,1)S(1)} collective-permute-done((bf16[1,8,2560]{2,1,0:T(8,128)(2,1)}, bf16[1,8,2560]{2,1,0:T(8,128)(2,1)S(1)}, u32[]{:S(2)}, u32[]{:S(2)}) %collective-permute-start.2) | collective-permute-done | bytes 40992 | tf_op jit(solution)/shard_map/ppermute | solution.py:503
  9.4 2.9 %collective-permute-done.1 = bf16[1,8,2560]{2,1,0:T(8,128)(2,1)S(1)} collective-permute-done((bf16[1,8,2560]{2,1,0:T(8,128)(2,1)}, bf16[1,8,2560]{2,1,0:T(8,128)(2,1)S(1)}, u32[]{:S(2)}, u32[]{:S(2)}) %collective-permute-start.1) | collective-permute-done | bytes 40992 | tf_op jit(solution)/shard_map/ppermute | solution.py:503
  12.3 0.0 collective-permute-done
  12.3 0.8 pad_maximum_fusion.3.wmine0_ref
  13.1 2.5 %collective-permute-start.5 = (bf16[4,8,2560]{2,1,0:T(8,128)(2,1)S(1)}, bf16[4,8,2560]{2,1,0:T(8,128)(2,1)S(1)}, u32[]{:S(2)}, u32[]{:S(2)}) collective-permute-start(bf16[4,8,2560]{2,1,0:T(8,128)(2,1)S(1)} %pad_maximum_fusion.3.wmine0_ref), channel_id=1, source_target_pairs={{0,3},{1,2},{2,1},{3,0},{4,7},{5,6},{6,5},{7,4},{8,11},{9,10},{10,... | collective-permute-start | bytes 491528 | tf_op jit(solution)/shard_map/ppermute | solution.py:503
  15.6 0.5 collective-permute-start.4
  16.1 0.5 collective-permute-start.3
  16.7 4.5 %collective-permute-done.5.wmine3_ref = bf16[4,8,2560]{2,1,0:T(8,128)(2,1)S(1)} collective-permute-done((bf16[4,8,2560]{2,1,0:T(8,128)(2,1)S(1)}, bf16[4,8,2560]{2,1,0:T(8,128)(2,1)S(1)}, u32[]{:S(2)}, u32[]{:S(2)}) %collective-permute-start.5) | collective-permute-done | bytes 163872 | tf_op jit(solution)/shard_map/ppermute | solution.py:503
  21.1 0.0 collective-permute-start.9
  21.1 0.9 collective-permute-done.4.wmine2_ref
  22.1 0.1 collective-permute-done.3.wmine1_ref
  22.1 0.5 collective-permute-start.7
  22.6 1.3 %copy.28.prompts_ref = bf16[8,10,128]{2,1,0:T(8,128)(2,1)} copy(bf16[8,10,128]{2,0,1:T(8,128)(2,1)} %param.15) | data formatting | bytes 40960 | tf_op args[1]
  24.0 0.7 copy.27.patches_ref
  24.7 0.0 collective-permute-done.8.wother2_ref
  24.8 0.6 copy-done.10
  25.4 0.1 copy-done.11
  25.4 0.1 copy-done.12
  25.5 0.0 copy-done.13
  25.5 57.1 %tower.1 = (bf16[2,4,128,128]{3,2,1,0:T(8,128)(2,1)}, f32[2,4,117,128]{3,2,1,0:T(8,128)}, bf16[4,4,8,2560]{3,2,1,0:T(8,128)(2,1)}, bf16[4,4,8,2560]{3,2,1,0:T(8,...) custom-call(s32[2]{0:T(128)} %ids_ref.1, s32[8]{0:T(128)} %counts_ref.1, bf16[4,8,2560]{2,1,0:T(8,128)(2,1)} %copy-done.4, ...), custom_call_target="tpu_custom_call" | custom-call | flops 10000000000 | bytes 20000000 | tf_op jit(solution)/shard_map/tower/pallas_call | solution.py:420
  82.6 0.1 collective-permute-start.10
  82.8 0.4 collective-permute-start.11
  83.2 2.0 %collective-permute-done.11 = f32[4,8,1024]{2,1,0:T(8,128)S(1)} collective-permute-done((f32[4,8,1024]{2,1,0:T(8,128)}, f32[4,8,1024]{2,1,0:T(8,128)S(1)}, u32[]{:S(2)}, u32[]{:S(2)}) %collective-permute-start.11) | collective-permute-done | bytes 131104 | tf_op jit(solution)/shard_map/ppermute | solution.py:499
  85.2 0.9 add_convert_fusion.2
  86.1 0.0 collective-permute-done.10
  86.1 1.2 %add_convert_fusion = bf16[4,4,8,2560]{3,2,1,0:T(8,128)(2,1)S(1)} fusion(bf16[4,4,8,2560]{3,2,1,0:T(8,128)(2,1)S(1)} %collective-permute-done.10, bf16[4,4,8,2560]{3,2,1,0:T(8,128)(2,1)} %get-tuple-element.32), kind=kLoop, calls=%fused_computation | loop fusion | flops 1310720 | bytes 1966080 | tf_op jit(solution)/shard_map/convert_element_type | solution.py:545
  87.5 1.6 %collective-permute-start.12 = (bf16[4,8,3584]{2,1,0:T(8,128)(2,1)S(1)}, bf16[4,8,3584]{2,1,0:T(8,128)(2,1)S(1)}, u32[]{:S(2)}, u32[]{:S(2)}) collective-permute-start(bf16[4,8,3584]{2,1,0:T(8,128)(2,1)S(1)} %get-tuple-element.82), channel_id=1, source_target_pairs={{0,1},{1,0},{2,3},{3,2},{4,5},{5,4},{6,7},{7,6},{8,9},{9,8},{10,11... | collective-permute-start | bytes 688136 | tf_op jit(solution)/shard_map/ppermute | solution.py:503
  89.0 0.8 collective-permute-start.13
  89.8 1.2 %collective-permute-start.14 = (bf16[4,8,3584]{2,1,0:T(8,128)(2,1)S(1)}, bf16[4,8,3584]{2,1,0:T(8,128)(2,1)S(1)}, u32[]{:S(2)}, u32[]{:S(2)}) collective-permute-start(bf16[4,8,3584]{2,1,0:T(8,128)(2,1)S(1)} %get-tuple-element.84), channel_id=1, source_target_pairs={{0,3},{1,2},{2,1},{3,0},{4,7},{5,6},{6,5},{7,4},{8,11},{9,10},{10,... | collective-permute-start | bytes 688136 | tf_op jit(solution)/shard_map/ppermute | solution.py:503
  91.0 5.0 %collective-permute-done.12 = bf16[4,8,3584]{2,1,0:T(8,128)(2,1)S(1)} collective-permute-done((bf16[4,8,3584]{2,1,0:T(8,128)(2,1)S(1)}, bf16[4,8,3584]{2,1,0:T(8,128)(2,1)S(1)}, u32[]{:S(2)}, u32[]{:S(2)}) %collective-permute-start.12) | collective-permute-done | bytes 229408 | tf_op jit(solution)/shard_map/ppermute | solution.py:503
  96.0 5.3 %collective-permute-done.13 = bf16[4,8,3584]{2,1,0:T(8,128)(2,1)S(1)} collective-permute-done((bf16[4,8,3584]{2,1,0:T(8,128)(2,1)S(1)}, bf16[4,8,3584]{2,1,0:T(8,128)(2,1)S(1)}, u32[]{:S(2)}, u32[]{:S(2)}) %collective-permute-start.13) | collective-permute-done | bytes 229408 | tf_op jit(solution)/shard_map/ppermute | solution.py:503
  101.3 0.1 fusion.1
  101.5 0.5 collective-permute-start.15
  102.0 2.1 %collective-permute-start.16 = (bf16[8,6656]{1,0:T(8,128)(2,1)S(1)}, bf16[8,6656]{1,0:T(8,128)(2,1)S(1)}, u32[]{:S(2)}, u32[]{:S(2)}) collective-permute-start(bf16[8,6656]{1,0:T(8,128)(2,1)S(1)} %get-tuple-element.71), channel_id=1, source_target_pairs={{0,8},{1,9},{2,10},{3,11},{4,12},{5,13},{6,14},{7,15},{8,0},{9,1},... | collective-permute-start | bytes 319496 | tf_op jit(solution)/shard_map/ppermute | solution.py:503
  104.1 1.9 %collective-permute-start.17 = (bf16[8,6656]{1,0:T(8,128)(2,1)S(1)}, bf16[8,6656]{1,0:T(8,128)(2,1)S(1)}, u32[]{:S(2)}, u32[]{:S(2)}) collective-permute-start(bf16[8,6656]{1,0:T(8,128)(2,1)S(1)} %get-tuple-element.72), channel_id=1, source_target_pairs={{0,12},{1,13},{2,14},{3,15},{4,8},{5,9},{6,10},{7,11},{8,4},{9,5},... | collective-permute-start | bytes 319496 | tf_op jit(solution)/shard_map/ppermute | solution.py:503
  106.0 0.7 collective-permute-done.15
  106.7 6.0 %collective-permute-done.16 = bf16[8,6656]{1,0:T(8,128)(2,1)S(1)} collective-permute-done((bf16[8,6656]{1,0:T(8,128)(2,1)S(1)}, bf16[8,6656]{1,0:T(8,128)(2,1)S(1)}, u32[]{:S(2)}, u32[]{:S(2)}) %collective-permute-start.16) | collective-permute-done | bytes 106528 | tf_op jit(solution)/shard_map/ppermute | solution.py:503
  112.8 0.1 collective-permute-start.19
  112.9 0.6 collective-permute-start.18
  113.5 0.9 copy.29
  114.4 0.0 collective-permute-done.18.big_other
  114.4 0.6 copy-done.6
  115.0 0.6 copy-done.5
  115.7 1.8 %final.1 = (f32[2,2,8,384]{3,2,1,0:T(8,128)}, f32[2,2,8,128]{3,2,1,0:T(8,128)}, f32[2,8,1024]{2,1,0:T(8,128)}, f32[2,32,128]{2,1,0:T(8,128)}, f32[2,128,128]{2,1...) custom-call(f32[8,2560]{1,0:T(8,128)} %copy-done.2, ...), custom_call_target="tpu_custom_call" | custom-call | tf_op jit(solution)/shard_map/final/pallas_call | solution.py:420
  (41 shorter events, 0.3 us)
Async XLA Ops:
  0.6 23.3 %copy-start.3 = (bf16[2,4,117,128]{3,1,2,0:T(4,128)(2,1)S(1)}, bf16[2,4,117,128]{3,1,2,0:T(4,128)(2,1)}, u32[]{:S(2)}) copy-start(bf16[2,4,117,128]{3,1,2,0:T(4,128)(2,1)} %param.14) | copy-start | bytes 718852
  2.1 7.3 %collective-permute-start.2 = (bf16[1,8,2560]{2,1,0:T(8,128)(2,1)}, bf16[1,8,2560]{2,1,0:T(8,128)(2,1)S(1)}, u32[]{:S(2)}, u32[]{:S(2)}) collective-permute-start(bf16[1,8,2560]{2,1,0:T(8,128)(2,1)} %pack.1), channel_id=1, source_target_pairs={{0,12},{1,13},{2,14},{3,15},{4,8},{5,9},{6,10},{7,11},{8,4},{9,5},... | collective-permute-start | bytes 122888 | tf_op jit(solution)/shard_map/ppermute | solution.py:503
  7.2 5.1 %collective-permute-start.1 = (bf16[1,8,2560]{2,1,0:T(8,128)(2,1)}, bf16[1,8,2560]{2,1,0:T(8,128)(2,1)S(1)}, u32[]{:S(2)}, u32[]{:S(2)}) collective-permute-start(bf16[1,8,2560]{2,1,0:T(8,128)(2,1)} %pack.1), channel_id=1, source_target_pairs={{0,8},{1,9},{2,10},{3,11},{4,12},{5,13},{6,14},{7,15},{8,0},{9,1},... | collective-permute-start | bytes 122888 | tf_op jit(solution)/shard_map/ppermute | solution.py:503
  7.2 5.1 %collective-permute-start = (bf16[1,8,2560]{2,1,0:T(8,128)(2,1)}, bf16[1,8,2560]{2,1,0:T(8,128)(2,1)S(1)}, u32[]{:S(2)}, u32[]{:S(2)}) collective-permute-start(bf16[1,8,2560]{2,1,0:T(8,128)(2,1)} %pack.1), channel_id=1, source_target_pairs={{0,4},{1,5},{2,6},{3,7},{4,0},{5,1},{6,2},{7,3},{8,12},{9,13},{10,... | collective-permute-start | bytes 122888 | tf_op jit(solution)/shard_map/ppermute | solution.py:503
  13.1 11.7 %copy-start.4 = (bf16[4,8,2560]{2,1,0:T(8,128)(2,1)}, bf16[4,8,2560]{2,1,0:T(8,128)(2,1)S(1)}, u32[]{:S(2)}) copy-start(bf16[4,8,2560]{2,1,0:T(8,128)(2,1)S(1)} %pad_maximum_fusion.3.wmine0_ref) | copy-start | bytes 491524
  13.1 8.0 %collective-permute-start.5 = (bf16[4,8,2560]{2,1,0:T(8,128)(2,1)S(1)}, bf16[4,8,2560]{2,1,0:T(8,128)(2,1)S(1)}, u32[]{:S(2)}, u32[]{:S(2)}) collective-permute-start(bf16[4,8,2560]{2,1,0:T(8,128)(2,1)S(1)} %pad_maximum_fusion.3.wmine0_ref), channel_id=1, source_target_pairs={{0,3},{1,2},{2,1},{3,0},{4,7},{5,6},{6,5},{7,4},{8,11},{9,10},{10,... | collective-permute-start | bytes 491528 | tf_op jit(solution)/shard_map/ppermute | solution.py:503
  15.6 6.5 %collective-permute-start.4 = (bf16[4,8,2560]{2,1,0:T(8,128)(2,1)S(1)}, bf16[4,8,2560]{2,1,0:T(8,128)(2,1)S(1)}, u32[]{:S(2)}, u32[]{:S(2)}) collective-permute-start(bf16[4,8,2560]{2,1,0:T(8,128)(2,1)S(1)} %pad_maximum_fusion.3.wmine0_ref), channel_id=1, source_target_pairs={{0,2},{1,3},{2,0},{3,1},{4,6},{5,7},{6,4},{7,5},{8,10},{9,11},{10,... | collective-permute-start | bytes 491528 | tf_op jit(solution)/shard_map/ppermute | solution.py:503
  16.1 6.0 %collective-permute-start.3 = (bf16[4,8,2560]{2,1,0:T(8,128)(2,1)S(1)}, bf16[4,8,2560]{2,1,0:T(8,128)(2,1)S(1)}, u32[]{:S(2)}, u32[]{:S(2)}) collective-permute-start(bf16[4,8,2560]{2,1,0:T(8,128)(2,1)S(1)} %pad_maximum_fusion.3.wmine0_ref), channel_id=1, source_target_pairs={{0,1},{1,0},{2,3},{3,2},{4,5},{5,4},{6,7},{7,6},{8,9},{9,8},{10,11... | collective-permute-start | bytes 491528 | tf_op jit(solution)/shard_map/ppermute | solution.py:503
  16.6 8.0 %collective-permute-start.6 = (bf16[4,8,2560]{2,1,0:T(8,128)(2,1)S(1)}, bf16[4,8,2560]{2,1,0:T(8,128)(2,1)S(1)}, u32[]{:S(2)}, u32[]{:S(2)}) collective-permute-start(bf16[4,8,2560]{2,1,0:T(8,128)(2,1)S(1)} %pad_maximum_fusion.3.wmine0_ref), channel_id=1, source_target_pairs={{0,16},{16,0},{1,17},{17,1},{2,18},{18,2},{3,19},{19,3},{4,20},{20... | collective-permute-start | bytes 491528 | tf_op jit(solution)/shard_map/ppermute | solution.py:499
  21.1 3.6 %copy-start.7 = (bf16[4,8,2560]{2,1,0:T(8,128)(2,1)}, bf16[4,8,2560]{2,1,0:T(8,128)(2,1)S(1)}, u32[]{:S(2)}) copy-start(bf16[4,8,2560]{2,1,0:T(8,128)(2,1)S(1)} %collective-permute-done.5.wmine3_ref) | copy-start | bytes 491524
  21.1 3.6 %collective-permute-start.9 = (bf16[4,8,2560]{2,1,0:T(8,128)(2,1)S(1)}, bf16[4,8,2560]{2,1,0:T(8,128)(2,1)S(1)}, u32[]{:S(2)}, u32[]{:S(2)}) collective-permute-start(bf16[4,8,2560]{2,1,0:T(8,128)(2,1)S(1)} %collective-permute-done.5.wmine3_ref), channel_id=1, source_target_pairs={{0,16},{16,0},{1,17},{17,1},{2,18},{18,2},{3,19},{19,3},{4,20},{20... | collective-permute-start | bytes 491528 | tf_op jit(solution)/shard_map/ppermute | solution.py:499
  22.1 2.7 %copy-start.8 = (bf16[4,8,2560]{2,1,0:T(8,128)(2,1)}, bf16[4,8,2560]{2,1,0:T(8,128)(2,1)S(1)}, u32[]{:S(2)}) copy-start(bf16[4,8,2560]{2,1,0:T(8,128)(2,1)S(1)} %collective-permute-done.4.wmine2_ref) | copy-start | bytes 491524
  22.1 2.6 %collective-permute-start.8 = (bf16[4,8,2560]{2,1,0:T(8,128)(2,1)S(1)}, bf16[4,8,2560]{2,1,0:T(8,128)(2,1)S(1)}, u32[]{:S(2)}, u32[]{:S(2)}) collective-permute-start(bf16[4,8,2560]{2,1,0:T(8,128)(2,1)S(1)} %collective-permute-done.4.wmine2_ref), channel_id=1, source_target_pairs={{0,16},{16,0},{1,17},{17,1},{2,18},{18,2},{3,19},{19,3},{4,20},{20... | collective-permute-start | bytes 491528 | tf_op jit(solution)/shard_map/ppermute | solution.py:499
  22.1 2.6 %copy-start.9 = (bf16[4,8,2560]{2,1,0:T(8,128)(2,1)}, bf16[4,8,2560]{2,1,0:T(8,128)(2,1)S(1)}, u32[]{:S(2)}) copy-start(bf16[4,8,2560]{2,1,0:T(8,128)(2,1)S(1)} %collective-permute-done.3.wmine1_ref) | copy-start | bytes 491524
  22.1 2.6 %collective-permute-start.7 = (bf16[4,8,2560]{2,1,0:T(8,128)(2,1)S(1)}, bf16[4,8,2560]{2,1,0:T(8,128)(2,1)S(1)}, u32[]{:S(2)}, u32[]{:S(2)}) collective-permute-start(bf16[4,8,2560]{2,1,0:T(8,128)(2,1)S(1)} %collective-permute-done.3.wmine1_ref), channel_id=1, source_target_pairs={{0,16},{16,0},{1,17},{17,1},{2,18},{18,2},{3,19},{19,3},{4,20},{20... | collective-permute-start | bytes 491528 | tf_op jit(solution)/shard_map/ppermute | solution.py:499
  24.7 0.7 copy-start.10
  24.7 0.7 copy-start.11
  24.7 0.8 copy-start.12
  24.7 0.8 copy-start.13
  82.6 3.5 %collective-permute-start.10 = (bf16[4,4,8,2560]{3,2,1,0:T(8,128)(2,1)}, bf16[4,4,8,2560]{3,2,1,0:T(8,128)(2,1)S(1)}, u32[]{:S(2)}, u32[]{:S(2)}) collective-permute-start(bf16[4,4,8,2560]{3,2,1,0:T(8,128)(2,1)} %get-tuple-element.33), channel_id=1, source_target_pairs={{0,16},{16,0},{1,17},{17,1},{2,18},{18,2},{3,19},{19,3},{4,20},{20... | collective-permute-start | bytes 1966088 | tf_op jit(solution)/shard_map/ppermute | solution.py:499
  82.8 2.4 %collective-permute-start.11 = (f32[4,8,1024]{2,1,0:T(8,128)}, f32[4,8,1024]{2,1,0:T(8,128)S(1)}, u32[]{:S(2)}, u32[]{:S(2)}) collective-permute-start(f32[4,8,1024]{2,1,0:T(8,128)} %get-tuple-element.35), channel_id=1, source_target_pairs={{0,16},{16,0},{1,17},{17,1},{2,18},{18,2},{3,19},{19,3},{4,20},{20... | collective-permute-start | bytes 393224 | tf_op jit(solution)/shard_map/ppermute | solution.py:499
  87.5 8.5 %collective-permute-start.12 = (bf16[4,8,3584]{2,1,0:T(8,128)(2,1)S(1)}, bf16[4,8,3584]{2,1,0:T(8,128)(2,1)S(1)}, u32[]{:S(2)}, u32[]{:S(2)}) collective-permute-start(bf16[4,8,3584]{2,1,0:T(8,128)(2,1)S(1)} %get-tuple-element.82), channel_id=1, source_target_pairs={{0,1},{1,0},{2,3},{3,2},{4,5},{5,4},{6,7},{7,6},{8,9},{9,8},{10,11... | collective-permute-start | bytes 688136 | tf_op jit(solution)/shard_map/ppermute | solution.py:503
  89.0 12.3 %collective-permute-start.13 = (bf16[4,8,3584]{2,1,0:T(8,128)(2,1)S(1)}, bf16[4,8,3584]{2,1,0:T(8,128)(2,1)S(1)}, u32[]{:S(2)}, u32[]{:S(2)}) collective-permute-start(bf16[4,8,3584]{2,1,0:T(8,128)(2,1)S(1)} %get-tuple-element.83), channel_id=1, source_target_pairs={{0,2},{1,3},{2,0},{3,1},{4,6},{5,7},{6,4},{7,5},{8,10},{9,11},{10,... | collective-permute-start | bytes 688136 | tf_op jit(solution)/shard_map/ppermute | solution.py:503
  89.8 11.5 %collective-permute-start.14 = (bf16[4,8,3584]{2,1,0:T(8,128)(2,1)S(1)}, bf16[4,8,3584]{2,1,0:T(8,128)(2,1)S(1)}, u32[]{:S(2)}, u32[]{:S(2)}) collective-permute-start(bf16[4,8,3584]{2,1,0:T(8,128)(2,1)S(1)} %get-tuple-element.84), channel_id=1, source_target_pairs={{0,3},{1,2},{2,1},{3,0},{4,7},{5,6},{6,5},{7,4},{8,11},{9,10},{10,... | collective-permute-start | bytes 688136 | tf_op jit(solution)/shard_map/ppermute | solution.py:503
  101.4 12.1 %copy-start.1 = (f32[2,4,117,128]{3,2,1,0:T(8,128)S(1)}, f32[2,4,117,128]{3,2,1,0:T(8,128)}, u32[]{:S(2)}) copy-start(f32[2,4,117,128]{3,2,1,0:T(8,128)} %get-tuple-element.48) | copy-start | bytes 1437700
  101.5 5.2 %collective-permute-start.15 = (bf16[8,6656]{1,0:T(8,128)(2,1)S(1)}, bf16[8,6656]{1,0:T(8,128)(2,1)S(1)}, u32[]{:S(2)}, u32[]{:S(2)}) collective-permute-start(bf16[8,6656]{1,0:T(8,128)(2,1)S(1)} %get-tuple-element.70), channel_id=1, source_target_pairs={{0,4},{1,5},{2,6},{3,7},{4,0},{5,1},{6,2},{7,3},{8,12},{9,13},{10,... | collective-permute-start | bytes 319496 | tf_op jit(solution)/shard_map/ppermute | solution.py:503
  102.0 10.7 %collective-permute-start.16 = (bf16[8,6656]{1,0:T(8,128)(2,1)S(1)}, bf16[8,6656]{1,0:T(8,128)(2,1)S(1)}, u32[]{:S(2)}, u32[]{:S(2)}) collective-permute-start(bf16[8,6656]{1,0:T(8,128)(2,1)S(1)} %get-tuple-element.71), channel_id=1, source_target_pairs={{0,8},{1,9},{2,10},{3,11},{4,12},{5,13},{6,14},{7,15},{8,0},{9,1},... | collective-permute-start | bytes 319496 | tf_op jit(solution)/shard_map/ppermute | solution.py:503
  104.1 8.6 %collective-permute-start.17 = (bf16[8,6656]{1,0:T(8,128)(2,1)S(1)}, bf16[8,6656]{1,0:T(8,128)(2,1)S(1)}, u32[]{:S(2)}, u32[]{:S(2)}) collective-permute-start(bf16[8,6656]{1,0:T(8,128)(2,1)S(1)} %get-tuple-element.72), channel_id=1, source_target_pairs={{0,12},{1,13},{2,14},{3,15},{4,8},{5,9},{6,10},{7,11},{8,4},{9,5},... | collective-permute-start | bytes 319496 | tf_op jit(solution)/shard_map/ppermute | solution.py:503
  112.8 1.6 %copy-start = (f32[8,4096]{1,0:T(8,128)}, f32[8,4096]{1,0:T(8,128)S(1)}, u32[]{:S(2)}) copy-start(f32[8,4096]{1,0:T(8,128)S(1)} %add_add_fusion.small_mine) | copy-start | bytes 393220
  112.8 1.6 %collective-permute-start.19 = (f32[8,4096]{1,0:T(8,128)S(1)}, f32[8,4096]{1,0:T(8,128)S(1)}, u32[]{:S(2)}, u32[]{:S(2)}) collective-permute-start(f32[8,4096]{1,0:T(8,128)S(1)} %add_add_fusion.small_mine), channel_id=1, source_target_pairs={{0,16},{16,0},{1,17},{17,1},{2,18},{18,2},{3,19},{19,3},{4,20},{20... | collective-permute-start | bytes 393224 | tf_op jit(solution)/shard_map/ppermute | solution.py:499
  112.9 1.5 %copy-start.2 = (f32[8,2560]{1,0:T(8,128)}, f32[8,2560]{1,0:T(8,128)S(1)}, u32[]{:S(2)}) copy-start(f32[8,2560]{1,0:T(8,128)S(1)} %fusion.2.big_mine) | copy-start | bytes 245764
  112.9 1.5 %collective-permute-start.18 = (f32[8,2560]{1,0:T(8,128)S(1)}, f32[8,2560]{1,0:T(8,128)S(1)}, u32[]{:S(2)}, u32[]{:S(2)}) collective-permute-start(f32[8,2560]{1,0:T(8,128)S(1)} %fusion.2.big_mine), channel_id=1, source_target_pairs={{0,16},{16,0},{1,17},{17,1},{2,18},{18,2},{3,19},{19,3},{4,20},{20... | collective-permute-start | bytes 245768 | tf_op jit(solution)/shard_map/ppermute | solution.py:499
  114.4 0.6 copy-start.6
  115.0 0.6 copy-start.5

commit v6 on v5

--- a/solution.py
+++ b/solution.py
@@ -30,6 +30,10 @@
     return lax.dot_general(a, b, (((1,), (1,)), ((), ())), preferred_element_type=F32)
 
 
+def turn(eye, x):
+    return dot_nt(eye, x)
+
+
 def norm_cols(x):
     centered = x - jnp.mean(x, axis=0, keepdims=True)
     inv = lax.rsqrt(jnp.mean(centered * centered, axis=0, keepdims=True) + EPSILON)
@@ -38,9 +42,10 @@
 
 def norm_cols_back(dn, gain, xhat, inv):
     e = dn * gain
+    both = e * xhat
     m1 = jnp.mean(e, axis=0, keepdims=True)
-    m2 = jnp.mean(e * xhat, axis=0, keepdims=True)
-    return inv * (e - m1 - xhat * m2)
+    m2 = jnp.mean(both, axis=0, keepdims=True)
+    return inv * (e - m1 - xhat * m2), both
 
 
 def fold(part):
@@ -65,6 +70,8 @@
     dov_ref, ga_ref, gf_ref, gd_ref, gt_ref, gacc_ref, gbig_ref, pacc_ref,
 ):
     dp = lax.axis_index("dp") if split else 0
+    eye_row = lax.broadcasted_iota(jnp.int32, (128, 128), 0)
+    eye = jnp.where(eye_row == lax.broadcasted_iota(jnp.int32, (128, 128), 1), 1.0, 0.0).astype(BF)
     me = lax.axis_index("fsdp") if split else 0
     layers = 2
     chunks = 4
@@ -87,9 +94,9 @@
                     [part[:, COL_DOWN + 128 * a : COL_DOWN + 128 * a + 128] for a in range(4)], axis=0
                 ).astype(BF)
         for block in range(COL_DOWN // 128):
-            wt_ref[l, 128 * block : 128 * block + 128, :] = w_ref[l, :, 128 * block : 128 * block + 128].T
+            wt_ref[l, 128 * block : 128 * block + 128, :] = turn(eye, w_ref[l, :, 128 * block : 128 * block + 128]).astype(BF)
         for block in range(4):
-            wdt_ref[l, :, 128 * block : 128 * block + 128] = wd_ref[l, 128 * block : 128 * block + 128, :].T
+            wdt_ref[l, :, 128 * block : 128 * block + 128] = turn(eye, wd_ref[l, 128 * block : 128 * block + 128, :]).astype(BF)
         for k in range(4):
             for offset, rows in ((0, gains_ref), (4, scales_ref)):
                 col = jnp.broadcast_to(rows[l, k : k + 1, :], (128, 128)).T
@@ -104,9 +111,9 @@
             tokscr_ref[bv, 10:127, :] = patches_ref[b, v].astype(F32)
             tokscr_ref[bv, 127:128, :] = cls_ref[...].astype(F32)
             lanes = slice(128 * (v % 2), 128 * (v % 2) + 128)
-            h_ref[2 * b + v // 2, :, lanes] = tokscr_ref[bv].T
-            g_ref[0, 2 * b + v // 2, :, lanes] = cot_ref[b, v].astype(F32).T
-            g_ref[1, 2 * b + v // 2, :, lanes] = adj_ref[b, v].astype(F32).T
+            h_ref[2 * b + v // 2, :, lanes] = turn(eye, tokscr_ref[bv].astype(BF))
+            g_ref[0, 2 * b + v // 2, :, lanes] = turn(eye, cot_ref[b, v])
+            g_ref[1, 2 * b + v // 2, :, lanes] = turn(eye, adj_ref[b, v])
 
     head_row = lax.broadcasted_iota(jnp.int32, (8, 128), 0)
     head_col = lax.broadcasted_iota(jnp.int32, (8, 128), 1) // 16
@@ -151,7 +158,7 @@
             lanes = slice(128 * s, 128 * s + 128)
             at = 2 * (c % 2) + s
             diag_heads(qbd_ref, at, queries[:, lanes])
-            key_rows = keys[:, lanes].T
+            key_rows = turn(eye, keys[:, lanes]).astype(BF)
             for hp in range(4):
                 span = slice(256 * hp, 256 * hp + 256)
                 rows = slice(32 * hp, 32 * hp + 32)
@@ -219,9 +226,10 @@
         return xhat, inv_ref[l * 4 + k, c], (xhat * gain(l, k)).astype(BF)
 
     def pass_on(l, k, c, x, dn, xhat, inv):
+        back, both = norm_cols_back(dn, gain(l, k), xhat, inv)
         if x == 0:
-            gacc_ref[l * 4 + k] += fold(dn * xhat)
-        g_ref[x, c] += norm_cols_back(dn, gain(l, k), xhat, inv)
+            gacc_ref[l * 4 + k] += fold(both)
+        g_ref[x, c] += back
 
     def feed_backward(l, c):
         xhat, inv, n = norm_of(l, 3, c)
@@ -253,7 +261,7 @@
                 part = dy[:, 128 * s : 128 * s + 128]
                 dn.append(dot_nn(part, tok_ref[l]))
                 if x == 0:
-                    gt_ref[l] += dot_nn(part.T, n[:, 128 * s : 128 * s + 128])
+                    gt_ref[l] += dot_nn(turn(eye, part).astype(BF), n[:, 128 * s : 128 * s + 128])
             pass_on(l, 2, c, x, jnp.concatenate(dn, axis=1), xhat, inv)
 
     def var_backward(l, b):
@@ -314,7 +322,7 @@
             lanes = slice(128 * s, 128 * s + 128)
             at = 2 * (c % 2) + s
             diag_heads(qbd_ref, at, queries[:, lanes])
-            value_rows = values[:, lanes].T
+            value_rows = turn(eye, values[:, lanes]).astype(BF)
             for x in range(2):
                 diag_heads(dob_ref, 2 * at + x, grads[x][:, lanes])
             for hp in range(4):
@@ -350,7 +358,7 @@
     for b in range(items):
         for v in range(4):
             lanes = slice(128 * (v % 2), 128 * (v % 2) + 128)
-            out_ref[b, v] = h_ref[2 * b + v // 2, :, lanes].T.astype(BF)
+            out_ref[b, v] = turn(eye, h_ref[2 * b + v // 2, :, lanes].astype(BF)).astype(BF)
 
     gacc_ref[...] = jnp.zeros_like(gacc_ref)
     gt_ref[...] = jnp.zeros_like(gt_ref)
@@ -378,10 +386,10 @@
             jnp.sum(w_ref[l, :, COL_OUT[k] : COL_OUT[k] + 128].astype(F32) * ga_ref[:, COL_OUT[k] : COL_OUT[k] + 128], axis=0, keepdims=True)
             for k in range(2)
         ]
-        sums.append(gains_ref[l, 2:3, :] * gains_rows[2])
+        sums.append(gains_rows[2])
         sums.append(jnp.sum(wd_ref[l].astype(F32) * gd_ref[...], axis=0, keepdims=True))
         for k in range(4):
-            pacc_ref[0, l * 4 + k, 10:11, :] = gains_rows[k]
+            pacc_ref[0, l * 4 + k, 10:11, :] = gains_rows[k] / gains_ref[l, k : k + 1, :]
             pacc_ref[0, l * 4 + k, 11:12, :] = sums[k] / scales_ref[l, k : k + 1, :]
         return carry
 

time: 118 us -> 124 us (1.051)
  Pallas kernels: 60.4 us -> 66.1 us
    pallas_call x3, Pallas kernels: 60.4 us -> 66.1 us  [call(): pl.pallas_call(kernel, out_shape=out_shape, in_specs=[pl.BlockSpec(memory...]
where the time goes in v6:
time: 124 us; the launch traced here: 123 us
  Pallas kernels  66.1 us (53%)
  waiting for transfers between devices  29.1 us (23%)
  starting transfers between devices  18.8 us (15%)
  local copies, waits for them, and re-layouts  5.08 us (4%)
  other arithmetic  3.2 us (3%)
    pallas_call x3, Pallas kernels, call(): pl.pallas_call(kernel, out_shape=out_shape, in_specs=[pl.BlockSpec(memory...  66.1 us
    ppermute x12, waiting for transfers between devices, swap(): return lax.ppermute(array, 'fsdp', [(i, i ^ mask) for i in range(SHARDS)])  27.1 us
    ppermute x12, starting transfers between devices, swap(): return lax.ppermute(array, 'fsdp', [(i, i ^ mask) for i in range(SHARDS)])  17.2 us
    unnamed x35, local copies, waits for them, and re-layouts  5.04 us
  transfers between devices with their start and end apart: 20, of which 10 were waited for; matrix products, arithmetic and copies ran while one was open for 3% of the time, Pallas kernels for 0%

profile of v6, /device:TPU:0, one launch (start us, length us, event | category | flops | bytes accessed | tf_op | source)
XLA Modules:
  0.0 123.3 jit_solution(14668385945304245293)
XLA Ops:
  0.7 1.5 %pack.1 = bf16[1,8,2560]{2,1,0:T(8,128)(2,1)} custom-call(bf16[2,2,8,384]{3,2,1,0:T(8,128)(2,1)} %attn_in_ref.1, bf16[2,2,8,128]{3,2,1,0:T(8,128)(2,1)} %attn_out_ref.1, bf16[2,8,1024]{2,1,0:T(8,128)(2,1)} %feed_in_ref.1, bf16[2,32,128]{2,1,0:T(8,128)(2,1)} %feed_out_ref.1), custom_call_target="tpu_custom_call" | custom-call | tf_op jit(solution)/shard_map/pack/pallas_call | solution.py:428
  2.1 5.0 %collective-permute-start.2 = (bf16[1,8,2560]{2,1,0:T(8,128)(2,1)}, bf16[1,8,2560]{2,1,0:T(8,128)(2,1)S(1)}, u32[]{:S(2)}, u32[]{:S(2)}) collective-permute-start(bf16[1,8,2560]{2,1,0:T(8,128)(2,1)} %pack.1), channel_id=1, source_target_pairs={{0,12},{1,13},{2,14},{3,15},{4,8},{5,9},{6,10},{7,11},{8,4},{9,5},... | collective-permute-start | bytes 122888 | tf_op jit(solution)/shard_map/ppermute | solution.py:511
  7.2 0.0 collective-permute-start.1
  7.2 0.6 collective-permute-start
  7.7 1.6 %collective-permute-done.2 = bf16[1,8,2560]{2,1,0:T(8,128)(2,1)S(1)} collective-permute-done((bf16[1,8,2560]{2,1,0:T(8,128)(2,1)}, bf16[1,8,2560]{2,1,0:T(8,128)(2,1)S(1)}, u32[]{:S(2)}, u32[]{:S(2)}) %collective-permute-start.2) | collective-permute-done | bytes 40992 | tf_op jit(solution)/shard_map/ppermute | solution.py:511
  9.4 2.9 %collective-permute-done.1 = bf16[1,8,2560]{2,1,0:T(8,128)(2,1)S(1)} collective-permute-done((bf16[1,8,2560]{2,1,0:T(8,128)(2,1)}, bf16[1,8,2560]{2,1,0:T(8,128)(2,1)S(1)}, u32[]{:S(2)}, u32[]{:S(2)}) %collective-permute-start.1) | collective-permute-done | bytes 40992 | tf_op jit(solution)/shard_map/ppermute | solution.py:511
  12.3 0.0 collective-permute-done
  12.3 0.8 pad_maximum_fusion.3.wmine0_ref
  13.1 2.5 %collective-permute-start.5 = (bf16[4,8,2560]{2,1,0:T(8,128)(2,1)S(1)}, bf16[4,8,2560]{2,1,0:T(8,128)(2,1)S(1)}, u32[]{:S(2)}, u32[]{:S(2)}) collective-permute-start(bf16[4,8,2560]{2,1,0:T(8,128)(2,1)S(1)} %pad_maximum_fusion.3.wmine0_ref), channel_id=1, source_target_pairs={{0,3},{1,2},{2,1},{3,0},{4,7},{5,6},{6,5},{7,4},{8,11},{9,10},{10,... | collective-permute-start | bytes 491528 | tf_op jit(solution)/shard_map/ppermute | solution.py:511
  15.6 0.5 collective-permute-start.4
  16.1 0.5 collective-permute-start.3
  16.6 0.0 collective-permute-start.6
  16.7 4.5 %collective-permute-done.5.wmine3_ref = bf16[4,8,2560]{2,1,0:T(8,128)(2,1)S(1)} collective-permute-done((bf16[4,8,2560]{2,1,0:T(8,128)(2,1)S(1)}, bf16[4,8,2560]{2,1,0:T(8,128)(2,1)S(1)}, u32[]{:S(2)}, u32[]{:S(2)}) %collective-permute-start.5) | collective-permute-done | bytes 163872 | tf_op jit(solution)/shard_map/ppermute | solution.py:511
  21.1 0.9 collective-permute-done.4.wmine2_ref
  22.1 0.1 collective-permute-done.3.wmine1_ref
  22.1 0.5 collective-permute-start.7
  22.6 1.3 %copy.28.prompts_ref = bf16[8,10,128]{2,1,0:T(8,128)(2,1)} copy(bf16[8,10,128]{2,0,1:T(8,128)(2,1)} %param.15) | data formatting | bytes 40960 | tf_op args[1]
  24.0 0.7 copy.27.patches_ref
  24.7 0.0 collective-permute-done.8.wother2_ref
  24.8 0.6 copy-done.10
  25.4 0.1 copy-done.11
  25.4 0.1 copy-done.12
  25.5 0.0 copy-done.13
  25.5 62.8 %tower.1 = (bf16[2,4,128,128]{3,2,1,0:T(8,128)(2,1)}, f32[2,4,117,128]{3,2,1,0:T(8,128)}, bf16[4,4,8,2560]{3,2,1,0:T(8,128)(2,1)}, bf16[4,4,8,2560]{3,2,1,0:T(8,...) custom-call(s32[2]{0:T(128)} %ids_ref.1, s32[8]{0:T(128)} %counts_ref.1, bf16[4,8,2560]{2,1,0:T(8,128)(2,1)} %copy-done.4, ...), custom_call_target="tpu_custom_call" | custom-call | flops 10000000000 | bytes 20000000 | tf_op jit(solution)/shard_map/tower/pallas_call | solution.py:428
  88.3 0.1 collective-permute-start.10
  88.5 0.4 collective-permute-start.11
  88.9 2.0 %collective-permute-done.11 = f32[4,8,1024]{2,1,0:T(8,128)S(1)} collective-permute-done((f32[4,8,1024]{2,1,0:T(8,128)}, f32[4,8,1024]{2,1,0:T(8,128)S(1)}, u32[]{:S(2)}, u32[]{:S(2)}) %collective-permute-start.11) | collective-permute-done | bytes 131104 | tf_op jit(solution)/shard_map/ppermute | solution.py:507
  90.9 0.9 add_convert_fusion.2
  91.8 1.2 %add_convert_fusion = bf16[4,4,8,2560]{3,2,1,0:T(8,128)(2,1)S(1)} fusion(bf16[4,4,8,2560]{3,2,1,0:T(8,128)(2,1)S(1)} %collective-permute-done.10, bf16[4,4,8,2560]{3,2,1,0:T(8,128)(2,1)} %get-tuple-element.32), kind=kLoop, calls=%fused_computation | loop fusion | flops 1310720 | bytes 1966080 | tf_op jit(solution)/shard_map/convert_element_type | solution.py:553
  93.2 1.6 %collective-permute-start.12 = (bf16[4,8,3584]{2,1,0:T(8,128)(2,1)S(1)}, bf16[4,8,3584]{2,1,0:T(8,128)(2,1)S(1)}, u32[]{:S(2)}, u32[]{:S(2)}) collective-permute-start(bf16[4,8,3584]{2,1,0:T(8,128)(2,1)S(1)} %get-tuple-element.82), channel_id=1, source_target_pairs={{0,1},{1,0},{2,3},{3,2},{4,5},{5,4},{6,7},{7,6},{8,9},{9,8},{10,11... | collective-permute-start | bytes 688136 | tf_op jit(solution)/shard_map/ppermute | solution.py:511
  94.7 0.8 collective-permute-start.13
  95.5 1.2 collective-permute-start.14
  96.7 5.0 %collective-permute-done.12 = bf16[4,8,3584]{2,1,0:T(8,128)(2,1)S(1)} collective-permute-done((bf16[4,8,3584]{2,1,0:T(8,128)(2,1)S(1)}, bf16[4,8,3584]{2,1,0:T(8,128)(2,1)S(1)}, u32[]{:S(2)}, u32[]{:S(2)}) %collective-permute-start.12) | collective-permute-done | bytes 229408 | tf_op jit(solution)/shard_map/ppermute | solution.py:511
  101.7 5.3 %collective-permute-done.13 = bf16[4,8,3584]{2,1,0:T(8,128)(2,1)S(1)} collective-permute-done((bf16[4,8,3584]{2,1,0:T(8,128)(2,1)S(1)}, bf16[4,8,3584]{2,1,0:T(8,128)(2,1)S(1)}, u32[]{:S(2)}, u32[]{:S(2)}) %collective-permute-start.13) | collective-permute-done | bytes 229408 | tf_op jit(solution)/shard_map/ppermute | solution.py:511
  107.0 0.1 fusion.1
  107.2 0.5 collective-permute-start.15
  107.7 2.1 %collective-permute-start.16 = (bf16[8,6656]{1,0:T(8,128)(2,1)S(1)}, bf16[8,6656]{1,0:T(8,128)(2,1)S(1)}, u32[]{:S(2)}, u32[]{:S(2)}) collective-permute-start(bf16[8,6656]{1,0:T(8,128)(2,1)S(1)} %get-tuple-element.71), channel_id=1, source_target_pairs={{0,8},{1,9},{2,10},{3,11},{4,12},{5,13},{6,14},{7,15},{8,0},{9,1},... | collective-permute-start | bytes 319496 | tf_op jit(solution)/shard_map/ppermute | solution.py:511
  109.8 1.9 %collective-permute-start.17 = (bf16[8,6656]{1,0:T(8,128)(2,1)S(1)}, bf16[8,6656]{1,0:T(8,128)(2,1)S(1)}, u32[]{:S(2)}, u32[]{:S(2)}) collective-permute-start(bf16[8,6656]{1,0:T(8,128)(2,1)S(1)} %get-tuple-element.72), channel_id=1, source_target_pairs={{0,12},{1,13},{2,14},{3,15},{4,8},{5,9},{6,10},{7,11},{8,4},{9,5},... | collective-permute-start | bytes 319496 | tf_op jit(solution)/shard_map/ppermute | solution.py:511
  111.7 0.7 collective-permute-done.15
  112.4 6.0 %collective-permute-done.16 = bf16[8,6656]{1,0:T(8,128)(2,1)S(1)} collective-permute-done((bf16[8,6656]{1,0:T(8,128)(2,1)S(1)}, bf16[8,6656]{1,0:T(8,128)(2,1)S(1)}, u32[]{:S(2)}, u32[]{:S(2)}) %collective-permute-start.16) | collective-permute-done | bytes 106528 | tf_op jit(solution)/shard_map/ppermute | solution.py:511
  118.5 0.1 collective-permute-start.19
  118.6 0.6 collective-permute-start.18
  119.2 0.9 copy.29
  120.1 0.0 collective-permute-done.18.big_other
  120.1 0.0 collective-permute-done.19.small_other
  120.1 0.6 copy-done.6
  120.7 0.6 copy-done.5
  121.4 1.8 %final.1 = (f32[2,2,8,384]{3,2,1,0:T(8,128)}, f32[2,2,8,128]{3,2,1,0:T(8,128)}, f32[2,8,1024]{2,1,0:T(8,128)}, f32[2,32,128]{2,1,0:T(8,128)}, f32[2,128,128]{2,1...) custom-call(f32[8,2560]{1,0:T(8,128)} %copy-done.2, ...), custom_call_target="tpu_custom_call" | custom-call | tf_op jit(solution)/shard_map/final/pallas_call | solution.py:428
  (41 shorter events, 0.3 us)
Async XLA Ops:
  0.6 23.3 %copy-start.3 = (bf16[2,4,117,128]{3,1,2,0:T(4,128)(2,1)S(1)}, bf16[2,4,117,128]{3,1,2,0:T(4,128)(2,1)}, u32[]{:S(2)}) copy-start(bf16[2,4,117,128]{3,1,2,0:T(4,128)(2,1)} %param.14) | copy-start | bytes 718852
  2.1 7.3 %collective-permute-start.2 = (bf16[1,8,2560]{2,1,0:T(8,128)(2,1)}, bf16[1,8,2560]{2,1,0:T(8,128)(2,1)S(1)}, u32[]{:S(2)}, u32[]{:S(2)}) collective-permute-start(bf16[1,8,2560]{2,1,0:T(8,128)(2,1)} %pack.1), channel_id=1, source_target_pairs={{0,12},{1,13},{2,14},{3,15},{4,8},{5,9},{6,10},{7,11},{8,4},{9,5},... | collective-permute-start | bytes 122888 | tf_op jit(solution)/shard_map/ppermute | solution.py:511
  7.2 5.1 %collective-permute-start.1 = (bf16[1,8,2560]{2,1,0:T(8,128)(2,1)}, bf16[1,8,2560]{2,1,0:T(8,128)(2,1)S(1)}, u32[]{:S(2)}, u32[]{:S(2)}) collective-permute-start(bf16[1,8,2560]{2,1,0:T(8,128)(2,1)} %pack.1), channel_id=1, source_target_pairs={{0,8},{1,9},{2,10},{3,11},{4,12},{5,13},{6,14},{7,15},{8,0},{9,1},... | collective-permute-start | bytes 122888 | tf_op jit(solution)/shard_map/ppermute | solution.py:511
  7.2 5.1 %collective-permute-start = (bf16[1,8,2560]{2,1,0:T(8,128)(2,1)}, bf16[1,8,2560]{2,1,0:T(8,128)(2,1)S(1)}, u32[]{:S(2)}, u32[]{:S(2)}) collective-permute-start(bf16[1,8,2560]{2,1,0:T(8,128)(2,1)} %pack.1), channel_id=1, source_target_pairs={{0,4},{1,5},{2,6},{3,7},{4,0},{5,1},{6,2},{7,3},{8,12},{9,13},{10,... | collective-permute-start | bytes 122888 | tf_op jit(solution)/shard_map/ppermute | solution.py:511
  13.1 11.7 %copy-start.4 = (bf16[4,8,2560]{2,1,0:T(8,128)(2,1)}, bf16[4,8,2560]{2,1,0:T(8,128)(2,1)S(1)}, u32[]{:S(2)}) copy-start(bf16[4,8,2560]{2,1,0:T(8,128)(2,1)S(1)} %pad_maximum_fusion.3.wmine0_ref) | copy-start | bytes 491524
  13.1 8.0 %collective-permute-start.5 = (bf16[4,8,2560]{2,1,0:T(8,128)(2,1)S(1)}, bf16[4,8,2560]{2,1,0:T(8,128)(2,1)S(1)}, u32[]{:S(2)}, u32[]{:S(2)}) collective-permute-start(bf16[4,8,2560]{2,1,0:T(8,128)(2,1)S(1)} %pad_maximum_fusion.3.wmine0_ref), channel_id=1, source_target_pairs={{0,3},{1,2},{2,1},{3,0},{4,7},{5,6},{6,5},{7,4},{8,11},{9,10},{10,... | collective-permute-start | bytes 491528 | tf_op jit(solution)/shard_map/ppermute | solution.py:511
  15.6 6.5 %collective-permute-start.4 = (bf16[4,8,2560]{2,1,0:T(8,128)(2,1)S(1)}, bf16[4,8,2560]{2,1,0:T(8,128)(2,1)S(1)}, u32[]{:S(2)}, u32[]{:S(2)}) collective-permute-start(bf16[4,8,2560]{2,1,0:T(8,128)(2,1)S(1)} %pad_maximum_fusion.3.wmine0_ref), channel_id=1, source_target_pairs={{0,2},{1,3},{2,0},{3,1},{4,6},{5,7},{6,4},{7,5},{8,10},{9,11},{10,... | collective-permute-start | bytes 491528 | tf_op jit(solution)/shard_map/ppermute | solution.py:511
  16.1 6.0 %collective-permute-start.3 = (bf16[4,8,2560]{2,1,0:T(8,128)(2,1)S(1)}, bf16[4,8,2560]{2,1,0:T(8,128)(2,1)S(1)}, u32[]{:S(2)}, u32[]{:S(2)}) collective-permute-start(bf16[4,8,2560]{2,1,0:T(8,128)(2,1)S(1)} %pad_maximum_fusion.3.wmine0_ref), channel_id=1, source_target_pairs={{0,1},{1,0},{2,3},{3,2},{4,5},{5,4},{6,7},{7,6},{8,9},{9,8},{10,11... | collective-permute-start | bytes 491528 | tf_op jit(solution)/shard_map/ppermute | solution.py:511
  16.6 8.0 %collective-permute-start.6 = (bf16[4,8,2560]{2,1,0:T(8,128)(2,1)S(1)}, bf16[4,8,2560]{2,1,0:T(8,128)(2,1)S(1)}, u32[]{:S(2)}, u32[]{:S(2)}) collective-permute-start(bf16[4,8,2560]{2,1,0:T(8,128)(2,1)S(1)} %pad_maximum_fusion.3.wmine0_ref), channel_id=1, source_target_pairs={{0,16},{16,0},{1,17},{17,1},{2,18},{18,2},{3,19},{19,3},{4,20},{20... | collective-permute-start | bytes 491528 | tf_op jit(solution)/shard_map/ppermute | solution.py:507
  21.1 3.6 %copy-start.7 = (bf16[4,8,2560]{2,1,0:T(8,128)(2,1)}, bf16[4,8,2560]{2,1,0:T(8,128)(2,1)S(1)}, u32[]{:S(2)}) copy-start(bf16[4,8,2560]{2,1,0:T(8,128)(2,1)S(1)} %collective-permute-done.5.wmine3_ref) | copy-start | bytes 491524
  21.1 3.6 %collective-permute-start.9 = (bf16[4,8,2560]{2,1,0:T(8,128)(2,1)S(1)}, bf16[4,8,2560]{2,1,0:T(8,128)(2,1)S(1)}, u32[]{:S(2)}, u32[]{:S(2)}) collective-permute-start(bf16[4,8,2560]{2,1,0:T(8,128)(2,1)S(1)} %collective-permute-done.5.wmine3_ref), channel_id=1, source_target_pairs={{0,16},{16,0},{1,17},{17,1},{2,18},{18,2},{3,19},{19,3},{4,20},{20... | collective-permute-start | bytes 491528 | tf_op jit(solution)/shard_map/ppermute | solution.py:507
  22.1 2.7 %copy-start.8 = (bf16[4,8,2560]{2,1,0:T(8,128)(2,1)}, bf16[4,8,2560]{2,1,0:T(8,128)(2,1)S(1)}, u32[]{:S(2)}) copy-start(bf16[4,8,2560]{2,1,0:T(8,128)(2,1)S(1)} %collective-permute-done.4.wmine2_ref) | copy-start | bytes 491524
  22.1 2.6 %collective-permute-start.8 = (bf16[4,8,2560]{2,1,0:T(8,128)(2,1)S(1)}, bf16[4,8,2560]{2,1,0:T(8,128)(2,1)S(1)}, u32[]{:S(2)}, u32[]{:S(2)}) collective-permute-start(bf16[4,8,2560]{2,1,0:T(8,128)(2,1)S(1)} %collective-permute-done.4.wmine2_ref), channel_id=1, source_target_pairs={{0,16},{16,0},{1,17},{17,1},{2,18},{18,2},{3,19},{19,3},{4,20},{20... | collective-permute-start | bytes 491528 | tf_op jit(solution)/shard_map/ppermute | solution.py:507
  22.1 2.6 %copy-start.9 = (bf16[4,8,2560]{2,1,0:T(8,128)(2,1)}, bf16[4,8,2560]{2,1,0:T(8,128)(2,1)S(1)}, u32[]{:S(2)}) copy-start(bf16[4,8,2560]{2,1,0:T(8,128)(2,1)S(1)} %collective-permute-done.3.wmine1_ref) | copy-start | bytes 491524
  22.1 2.6 %collective-permute-start.7 = (bf16[4,8,2560]{2,1,0:T(8,128)(2,1)S(1)}, bf16[4,8,2560]{2,1,0:T(8,128)(2,1)S(1)}, u32[]{:S(2)}, u32[]{:S(2)}) collective-permute-start(bf16[4,8,2560]{2,1,0:T(8,128)(2,1)S(1)} %collective-permute-done.3.wmine1_ref), channel_id=1, source_target_pairs={{0,16},{16,0},{1,17},{17,1},{2,18},{18,2},{3,19},{19,3},{4,20},{20... | collective-permute-start | bytes 491528 | tf_op jit(solution)/shard_map/ppermute | solution.py:507
  24.7 0.7 copy-start.10
  24.7 0.7 copy-start.11
  24.7 0.8 copy-start.12
  24.7 0.8 copy-start.13
  88.3 3.5 %collective-permute-start.10 = (bf16[4,4,8,2560]{3,2,1,0:T(8,128)(2,1)}, bf16[4,4,8,2560]{3,2,1,0:T(8,128)(2,1)S(1)}, u32[]{:S(2)}, u32[]{:S(2)}) collective-permute-start(bf16[4,4,8,2560]{3,2,1,0:T(8,128)(2,1)} %get-tuple-element.33), channel_id=1, source_target_pairs={{0,16},{16,0},{1,17},{17,1},{2,18},{18,2},{3,19},{19,3},{4,20},{20... | collective-permute-start | bytes 1966088 | tf_op jit(solution)/shard_map/ppermute | solution.py:507
  88.5 2.4 %collective-permute-start.11 = (f32[4,8,1024]{2,1,0:T(8,128)}, f32[4,8,1024]{2,1,0:T(8,128)S(1)}, u32[]{:S(2)}, u32[]{:S(2)}) collective-permute-start(f32[4,8,1024]{2,1,0:T(8,128)} %get-tuple-element.35), channel_id=1, source_target_pairs={{0,16},{16,0},{1,17},{17,1},{2,18},{18,2},{3,19},{19,3},{4,20},{20... | collective-permute-start | bytes 393224 | tf_op jit(solution)/shard_map/ppermute | solution.py:507
  93.2 8.5 %collective-permute-start.12 = (bf16[4,8,3584]{2,1,0:T(8,128)(2,1)S(1)}, bf16[4,8,3584]{2,1,0:T(8,128)(2,1)S(1)}, u32[]{:S(2)}, u32[]{:S(2)}) collective-permute-start(bf16[4,8,3584]{2,1,0:T(8,128)(2,1)S(1)} %get-tuple-element.82), channel_id=1, source_target_pairs={{0,1},{1,0},{2,3},{3,2},{4,5},{5,4},{6,7},{7,6},{8,9},{9,8},{10,11... | collective-permute-start | bytes 688136 | tf_op jit(solution)/shard_map/ppermute | solution.py:511
  94.7 12.3 %collective-permute-start.13 = (bf16[4,8,3584]{2,1,0:T(8,128)(2,1)S(1)}, bf16[4,8,3584]{2,1,0:T(8,128)(2,1)S(1)}, u32[]{:S(2)}, u32[]{:S(2)}) collective-permute-start(bf16[4,8,3584]{2,1,0:T(8,128)(2,1)S(1)} %get-tuple-element.83), channel_id=1, source_target_pairs={{0,2},{1,3},{2,0},{3,1},{4,6},{5,7},{6,4},{7,5},{8,10},{9,11},{10,... | collective-permute-start | bytes 688136 | tf_op jit(solution)/shard_map/ppermute | solution.py:511
  95.5 11.5 %collective-permute-start.14 = (bf16[4,8,3584]{2,1,0:T(8,128)(2,1)S(1)}, bf16[4,8,3584]{2,1,0:T(8,128)(2,1)S(1)}, u32[]{:S(2)}, u32[]{:S(2)}) collective-permute-start(bf16[4,8,3584]{2,1,0:T(8,128)(2,1)S(1)} %get-tuple-element.84), channel_id=1, source_target_pairs={{0,3},{1,2},{2,1},{3,0},{4,7},{5,6},{6,5},{7,4},{8,11},{9,10},{10,... | collective-permute-start | bytes 688136 | tf_op jit(solution)/shard_map/ppermute | solution.py:511
  107.1 12.1 %copy-start.1 = (f32[2,4,117,128]{3,2,1,0:T(8,128)S(1)}, f32[2,4,117,128]{3,2,1,0:T(8,128)}, u32[]{:S(2)}) copy-start(f32[2,4,117,128]{3,2,1,0:T(8,128)} %get-tuple-element.48) | copy-start | bytes 1437700
  107.2 5.2 %collective-permute-start.15 = (bf16[8,6656]{1,0:T(8,128)(2,1)S(1)}, bf16[8,6656]{1,0:T(8,128)(2,1)S(1)}, u32[]{:S(2)}, u32[]{:S(2)}) collective-permute-start(bf16[8,6656]{1,0:T(8,128)(2,1)S(1)} %get-tuple-element.70), channel_id=1, source_target_pairs={{0,4},{1,5},{2,6},{3,7},{4,0},{5,1},{6,2},{7,3},{8,12},{9,13},{10,... | collective-permute-start | bytes 319496 | tf_op jit(solution)/shard_map/ppermute | solution.py:511
  107.7 10.7 %collective-permute-start.16 = (bf16[8,6656]{1,0:T(8,128)(2,1)S(1)}, bf16[8,6656]{1,0:T(8,128)(2,1)S(1)}, u32[]{:S(2)}, u32[]{:S(2)}) collective-permute-start(bf16[8,6656]{1,0:T(8,128)(2,1)S(1)} %get-tuple-element.71), channel_id=1, source_target_pairs={{0,8},{1,9},{2,10},{3,11},{4,12},{5,13},{6,14},{7,15},{8,0},{9,1},... | collective-permute-start | bytes 319496 | tf_op jit(solution)/shard_map/ppermute | solution.py:511
  109.8 8.6 %collective-permute-start.17 = (bf16[8,6656]{1,0:T(8,128)(2,1)S(1)}, bf16[8,6656]{1,0:T(8,128)(2,1)S(1)}, u32[]{:S(2)}, u32[]{:S(2)}) collective-permute-start(bf16[8,6656]{1,0:T(8,128)(2,1)S(1)} %get-tuple-element.72), channel_id=1, source_target_pairs={{0,12},{1,13},{2,14},{3,15},{4,8},{5,9},{6,10},{7,11},{8,4},{9,5},... | collective-permute-start | bytes 319496 | tf_op jit(solution)/shard_map/ppermute | solution.py:511
  118.5 1.6 %copy-start = (f32[8,4096]{1,0:T(8,128)}, f32[8,4096]{1,0:T(8,128)S(1)}, u32[]{:S(2)}) copy-start(f32[8,4096]{1,0:T(8,128)S(1)} %add_add_fusion.small_mine) | copy-start | bytes 393220
  118.5 1.6 %collective-permute-start.19 = (f32[8,4096]{1,0:T(8,128)S(1)}, f32[8,4096]{1,0:T(8,128)S(1)}, u32[]{:S(2)}, u32[]{:S(2)}) collective-permute-start(f32[8,4096]{1,0:T(8,128)S(1)} %add_add_fusion.small_mine), channel_id=1, source_target_pairs={{0,16},{16,0},{1,17},{17,1},{2,18},{18,2},{3,19},{19,3},{4,20},{20... | collective-permute-start | bytes 393224 | tf_op jit(solution)/shard_map/ppermute | solution.py:507
  118.6 1.5 %copy-start.2 = (f32[8,2560]{1,0:T(8,128)}, f32[8,2560]{1,0:T(8,128)S(1)}, u32[]{:S(2)}) copy-start(f32[8,2560]{1,0:T(8,128)S(1)} %fusion.2.big_mine) | copy-start | bytes 245764
  118.6 1.5 %collective-permute-start.18 = (f32[8,2560]{1,0:T(8,128)S(1)}, f32[8,2560]{1,0:T(8,128)S(1)}, u32[]{:S(2)}, u32[]{:S(2)}) collective-permute-start(f32[8,2560]{1,0:T(8,128)S(1)} %fusion.2.big_mine), channel_id=1, source_target_pairs={{0,16},{16,0},{1,17},{17,1},{2,18},{18,2},{3,19},{19,3},{4,20},{20... | collective-permute-start | bytes 245768 | tf_op jit(solution)/shard_map/ppermute | solution.py:507
  120.1 0.6 copy-start.6
  120.7 0.6 copy-start.5

commit v7 on v5

--- a/solution.py
+++ b/solution.py
@@ -38,9 +38,10 @@
 
 def norm_cols_back(dn, gain, xhat, inv):
     e = dn * gain
+    both = e * xhat
     m1 = jnp.mean(e, axis=0, keepdims=True)
-    m2 = jnp.mean(e * xhat, axis=0, keepdims=True)
-    return inv * (e - m1 - xhat * m2)
+    m2 = jnp.mean(both, axis=0, keepdims=True)
+    return inv * (e - m1 - xhat * m2), both
 
 
 def fold(part):
@@ -62,7 +63,7 @@
     out_ref, pgrad_ref, bigmine_ref, bigother_ref, smallmine_ref, smallother_ref,
     stage_ref, w_ref, wd_ref, wt_ref, wdt_ref, colb_ref, tokscr_ref, h_ref, g_ref, xh_ref, inv_ref,
     qkvt_ref, pb_ref, ot_ref, qkvv_ref, pv_ref, ov_ref, pw_ref, qbd_ref, dob_ref, hid_ref, du_ref, dqkv_ref,
-    dov_ref, ga_ref, gf_ref, gd_ref, gt_ref, gacc_ref, gbig_ref, pacc_ref,
+    dov_ref, ga_ref, gd_ref, gt_ref, gacc_ref, gbig_ref, pacc_ref, spread_ref, act_ref, slope_ref, gdt_ref,
 ):
     dp = lax.axis_index("dp") if split else 0
     me = lax.axis_index("fsdp") if split else 0
@@ -111,9 +112,9 @@
     head_row = lax.broadcasted_iota(jnp.int32, (8, 128), 0)
     head_col = lax.broadcasted_iota(jnp.int32, (8, 128), 1) // 16
     gather_heads = jnp.where(head_row == head_col, 1.0, 0.0).astype(BF)
-    spread_row = lax.broadcasted_iota(jnp.int32, (128, 8), 0) // 16
-    spread_col = lax.broadcasted_iota(jnp.int32, (128, 8), 1)
-    spread_heads = jnp.where(spread_row == spread_col, 1.0, 0.0).astype(BF)
+    def spread_of(at, j):
+        lanes = slice(128 * j, 128 * j + 128)
+        return jnp.concatenate([jnp.broadcast_to(spread_ref[at, h : h + 1, lanes], (16, 128)) for h in range(HEADS)], axis=0)
 
     def head_sums(left, rights):
         return dot_nn(gather_heads, jnp.concatenate([(left * right).astype(BF) for right in rights], axis=1))
@@ -189,11 +190,12 @@
             total = 1.0 / ((shifted[0] + shifted[1]) + (shifted[2] + shifted[3]))
             prob = jnp.concatenate([part * total for part in shifted], axis=1)
             pv_ref[l, b, i] = prob
-            spread = dot_nn(spread_heads, prob.astype(BF))
-            pw_ref[l, b, i] = spread.astype(BF)
-            mixed = spread[:, :128] * value_slots[0]
-            for j in range(1, 4):
-                mixed = mixed + spread[:, 128 * j : 128 * j + 128] * value_slots[j]
+            spread_ref[4 * b + i] = prob.astype(BF).astype(F32)
+            mixed = None
+            for j in range(4):
+                spread = spread_of(4 * b + i, j)
+                pw_ref[l, b, i, :, 128 * j : 128 * j + 128] = spread.astype(BF)
+                mixed = spread * value_slots[j] if mixed is None else mixed + spread * value_slots[j]
             lanes = slice(128 * (i % 2), 128 * (i % 2) + 128)
             ov_ref[l, 2 * b + i // 2, :, lanes] = mixed.astype(BF)
         for cc in range(2):
@@ -208,38 +210,39 @@
         x = x + scale(l, 2) * jnp.concatenate(mix, axis=1)
         n = keep_norm(l, 3, c, x)
         for z in range(4):
+            rows = slice(128 * z, 128 * z + 128)
             gate = dot_nn(wt_ref[l, COL_FEED + 128 * z : COL_FEED + 128 * z + 128, :], n)
             up = dot_nn(wt_ref[l, COL_FEED + 512 + 128 * z : COL_FEED + 640 + 128 * z, :], n)
             sig = 0.5 * jnp.tanh(0.5 * gate) + 0.5
-            hid_ref[c % 2, 128 * z : 128 * z + 128, :] = (gate * sig * up).astype(BF)
-        h_ref[c] = x + scale(l, 3) * dot_nn(wdt_ref[l], hid_ref[c % 2])
+            act = gate * sig
+            hid_ref[l, c, rows, :] = (act * up).astype(BF)
+            act_ref[l, c, rows, :] = act.astype(BF)
+            slope_ref[l, c, rows, :] = (up * (sig * (1.0 + gate * (1.0 - sig)))).astype(BF)
+        h_ref[c] = x + scale(l, 3) * dot_nn(wdt_ref[l], hid_ref[l, c])
 
     def norm_of(l, k, c):
         xhat = xh_ref[l * 4 + k, c]
         return xhat, inv_ref[l * 4 + k, c], (xhat * gain(l, k)).astype(BF)
 
     def pass_on(l, k, c, x, dn, xhat, inv):
+        back, both = norm_cols_back(dn, gain(l, k), xhat, inv)
         if x == 0:
-            gacc_ref[l * 4 + k] += fold(dn * xhat)
-        g_ref[x, c] += norm_cols_back(dn, gain(l, k), xhat, inv)
+            gacc_ref[l * 4 + k] += fold(both)
+        g_ref[x, c] += back
 
     def feed_backward(l, c):
         xhat, inv, n = norm_of(l, 3, c)
         dz = [(scale(l, 3) * g_ref[x, c]).astype(BF) for x in range(2)]
         for z in range(4):
             rows = slice(128 * z, 128 * z + 128)
-            gate = dot_nn(wt_ref[l, COL_FEED + 128 * z : COL_FEED + 128 * z + 128, :], n)
-            up = dot_nn(wt_ref[l, COL_FEED + 512 + 128 * z : COL_FEED + 640 + 128 * z, :], n)
-            sig = 0.5 * jnp.tanh(0.5 * gate) + 0.5
-            act = gate * sig
-            hid_ref[c % 2, rows, :] = (act * up).astype(BF)
-            slope = up * (sig * (1.0 + gate * (1.0 - sig)))
+            act = act_ref[l, c, rows, :].astype(F32)
+            slope = slope_ref[l, c, rows, :].astype(F32)
             for x in range(2):
                 dhid = dot_nn(wd_ref[l, rows, :], dz[x])
                 du_ref[2 * (c % 2) + x, 128 * z : 128 * z + 128, :] = (dhid * slope).astype(BF)
                 du_ref[2 * (c % 2) + x, 512 + 128 * z : 640 + 128 * z, :] = (dhid * act).astype(BF)
-        gf_ref[...] += dot_nt(du_ref[2 * (c % 2)], n)
-        gd_ref[...] += dot_nt(hid_ref[c % 2], dz[0])
+        ga_ref[:, COL_FEED:COL_DOWN] += dot_nt(n, du_ref[2 * (c % 2)])
+        gdt_ref[...] += dot_nt(dz[0], hid_ref[l, c])
         for x in range(2):
             dn = dot_nn(w_ref[l, :, COL_FEED:COL_DOWN], du_ref[2 * (c % 2) + x])
             pass_on(l, 3, c, x, dn, xhat, inv)
@@ -248,12 +251,10 @@
         xhat, inv, n = norm_of(l, 2, c)
         for x in range(2):
             dy = (scale(l, 2) * g_ref[x, c]).astype(BF)
-            dn = []
-            for s in range(2):
-                part = dy[:, 128 * s : 128 * s + 128]
-                dn.append(dot_nn(part, tok_ref[l]))
-                if x == 0:
-                    gt_ref[l] += dot_nn(part.T, n[:, 128 * s : 128 * s + 128])
+            if x == 0:
+                turned = jnp.concatenate([dy[:, :128].T, dy[:, 128:].T], axis=1)
+                gt_ref[l] += dot_nn(turned, jnp.concatenate([n[:, :128], n[:, 128:]], axis=0))
+            dn = [dot_nn(dy[:, 128 * s : 128 * s + 128], tok_ref[l]) for s in range(2)]
             pass_on(l, 2, c, x, jnp.concatenate(dn, axis=1), xhat, inv)
 
     def var_backward(l, b):
@@ -279,8 +280,8 @@
                 weighted = prob * head_sums(grad, value_slots)
                 total = (weighted[:, :128] + weighted[:, 128:256]) + (weighted[:, 256:384] + weighted[:, 384:])
                 ds = weighted - prob * jnp.concatenate([total] * 4, axis=1)
-                ds_wide = dot_nn(spread_heads, ds.astype(BF))
-                ds_slots = [ds_wide[:, 128 * j : 128 * j + 128] for j in range(4)]
+                spread_ref[8 * b + 4 * x + i] = ds.astype(BF).astype(F32)
+                ds_slots = [spread_of(8 * b + 4 * x + i, j) for j in range(4)]
                 terms = [ds_slots[j] * slot(128, j) for j in range(4)]
                 dquery = (terms[0] + terms[1]) + (terms[2] + terms[3])
                 for j in range(4):
@@ -359,29 +360,26 @@
     def backward_layer(step, carry):
         l = layers - 1 - step
         ga_ref[...] = jnp.zeros_like(ga_ref)
-        gd_ref[...] = jnp.zeros_like(gd_ref)
-        gf_ref[...] = jnp.zeros_like(gf_ref)
+        gdt_ref[...] = jnp.zeros_like(gdt_ref)
         each(chunks, feed_backward, l)
         each(chunks, token_backward, l)
         each(items, var_backward, l)
         each(chunks, time_backward, l)
-        for k in range(8):
-            turned = gf_ref[128 * k : 128 * k + 128, :].T
-            for f in range(SHARDS):
-                gbig_ref[l, f, :, COL_FEED + 128 * k : COL_FEED + 128 * k + 128] = turned[8 * f : 8 * f + 8].astype(BF)
+        for k in range(4):
+            gd_ref[128 * k : 128 * k + 128, :] = gdt_ref[:, 128 * k : 128 * k + 128].T
         for f in range(SHARDS):
-            gbig_ref[l, f, :, 0:COL_FEED] = ga_ref[8 * f : 8 * f + 8, :].astype(BF)
             down = jnp.concatenate([gd_ref[32 * f + 8 * a : 32 * f + 8 * a + 8, :] for a in range(4)], axis=1)
-            gbig_ref[l, f, :, COL_DOWN:COLS] = down.astype(BF)
+            block = jnp.concatenate([ga_ref[8 * f : 8 * f + 8, :], down], axis=1)
+            gbig_ref[l, f] = block.astype(BF)
         gains_rows = [jnp.sum(gacc_ref[l * 4 + k].T, axis=0, keepdims=True) for k in range(4)]
         sums = [
             jnp.sum(w_ref[l, :, COL_OUT[k] : COL_OUT[k] + 128].astype(F32) * ga_ref[:, COL_OUT[k] : COL_OUT[k] + 128], axis=0, keepdims=True)
             for k in range(2)
         ]
-        sums.append(gains_ref[l, 2:3, :] * gains_rows[2])
+        sums.append(gains_rows[2])
         sums.append(jnp.sum(wd_ref[l].astype(F32) * gd_ref[...], axis=0, keepdims=True))
         for k in range(4):
-            pacc_ref[0, l * 4 + k, 10:11, :] = gains_rows[k]
+            pacc_ref[0, l * 4 + k, 10:11, :] = gains_rows[k] / gains_ref[l, k : k + 1, :]
             pacc_ref[0, l * 4 + k, 11:12, :] = sums[k] / scales_ref[l, k : k + 1, :]
         return carry
 
@@ -461,17 +459,20 @@
             pltpu.VMEM((2, 2, 4, 128, 512), BF),
             pltpu.VMEM((4, 128, 1024), BF),
             pltpu.VMEM((8, 128, 1024), BF),
-            pltpu.VMEM((2, 512, 256), BF),
+            pltpu.VMEM((2, 4, 512, 256), BF),
             pltpu.VMEM((4, 1024, 256), BF),
             pltpu.VMEM((8, 384, 256), BF),
             pltpu.VMEM((8, 128, 256), BF),
-            pltpu.VMEM((128, COL_FEED), F32),
-            pltpu.VMEM((1024, 128), F32),
+            pltpu.VMEM((128, COL_DOWN), F32),
             pltpu.VMEM((512, 128), F32),
             pltpu.VMEM((2, 128, 128), F32),
             pltpu.VMEM((8, 128, 128), F32),
             pltpu.VMEM((2, SHARDS, 8, COLS), BF),
             pltpu.VMEM((2, 8, 16, 128), F32),
+            pltpu.VMEM((16, 8, 512), F32),
+            pltpu.VMEM((2, 4, 512, 256), BF),
+            pltpu.VMEM((2, 4, 512, 256), BF),
+            pltpu.VMEM((128, 512), F32),
         ],
         *operands,
         cost=pl.CostEstimate(flops=10**10, bytes_accessed=20 * 10**6, transcendentals=0),

time: 118 us -> 112 us (0.949)
  Pallas kernels: 60.4 us -> 54.6 us
    pallas_call x3, Pallas kernels: 60.4 us -> 54.6 us  [call(): pl.pallas_call(kernel, out_shape=out_shape, in_specs=[pl.BlockSpec(memory...]
  transfers between devices with their start and end apart: 20 -> 20, of which waited for: 10 -> 10; matrix products, arithmetic and copies ran while one was open for 3% -> 4% of each run, Pallas kernels for 0% -> 0%
where the time goes in v7:
time: 112 us
  Pallas kernels  54.6 us (49%)
  waiting for transfers between devices  29.1 us (26%)
  starting transfers between devices  18.8 us (17%)
  local copies, waits for them, and re-layouts  5.08 us (5%)
  other arithmetic  3.2 us (3%)
    pallas_call x3, Pallas kernels, call(): pl.pallas_call(kernel, out_shape=out_shape, in_specs=[pl.BlockSpec(memory...  54.6 us
    ppermute x12, waiting for transfers between devices, swap(): return lax.ppermute(array, 'fsdp', [(i, i ^ mask) for i in range(SHARDS)])  27.1 us
    ppermute x12, starting transfers between devices, swap(): return lax.ppermute(array, 'fsdp', [(i, i ^ mask) for i in range(SHARDS)])  17.2 us
    unnamed x35, local copies, waits for them, and re-layouts  5.04 us
  transfers between devices with their start and end apart: 20, of which 10 were waited for; matrix products, arithmetic and copies ran while one was open for 4% of the time, Pallas kernels for 0%

profile of v7, /device:TPU:0, one launch (start us, length us, event | category | flops | bytes accessed | tf_op | source)
XLA Modules:
  0.0 111.8 jit_solution(3668067432545889442)
XLA Ops:
  0.7 1.5 %pack.1 = bf16[1,8,2560]{2,1,0:T(8,128)(2,1)} custom-call(bf16[2,2,8,384]{3,2,1,0:T(8,128)(2,1)} %attn_in_ref.1, bf16[2,2,8,128]{3,2,1,0:T(8,128)(2,1)} %attn_out_ref.1, bf16[2,8,1024]{2,1,0:T(8,128)(2,1)} %feed_in_ref.1, bf16[2,32,128]{2,1,0:T(8,128)(2,1)} %feed_out_ref.1), custom_call_target="tpu_custom_call" | custom-call | tf_op jit(solution)/shard_map/pack/pallas_call | solution.py:418
  2.1 5.0 %collective-permute-start.2 = (bf16[1,8,2560]{2,1,0:T(8,128)(2,1)}, bf16[1,8,2560]{2,1,0:T(8,128)(2,1)S(1)}, u32[]{:S(2)}, u32[]{:S(2)}) collective-permute-start(bf16[1,8,2560]{2,1,0:T(8,128)(2,1)} %pack.1), channel_id=1, source_target_pairs={{0,12},{1,13},{2,14},{3,15},{4,8},{5,9},{6,10},{7,11},{8,4},{9,5},... | collective-permute-start | bytes 122888 | tf_op jit(solution)/shard_map/ppermute | solution.py:504
  7.2 0.0 collective-permute-start.1
  7.2 0.6 collective-permute-start
  7.7 1.6 %collective-permute-done.2 = bf16[1,8,2560]{2,1,0:T(8,128)(2,1)S(1)} collective-permute-done((bf16[1,8,2560]{2,1,0:T(8,128)(2,1)}, bf16[1,8,2560]{2,1,0:T(8,128)(2,1)S(1)}, u32[]{:S(2)}, u32[]{:S(2)}) %collective-permute-start.2) | collective-permute-done | bytes 40992 | tf_op jit(solution)/shard_map/ppermute | solution.py:504
  9.4 2.9 %collective-permute-done.1 = bf16[1,8,2560]{2,1,0:T(8,128)(2,1)S(1)} collective-permute-done((bf16[1,8,2560]{2,1,0:T(8,128)(2,1)}, bf16[1,8,2560]{2,1,0:T(8,128)(2,1)S(1)}, u32[]{:S(2)}, u32[]{:S(2)}) %collective-permute-start.1) | collective-permute-done | bytes 40992 | tf_op jit(solution)/shard_map/ppermute | solution.py:504
  12.3 0.0 collective-permute-done
  12.3 0.8 pad_maximum_fusion.3.wmine0_ref
  13.1 2.5 %collective-permute-start.5 = (bf16[4,8,2560]{2,1,0:T(8,128)(2,1)S(1)}, bf16[4,8,2560]{2,1,0:T(8,128)(2,1)S(1)}, u32[]{:S(2)}, u32[]{:S(2)}) collective-permute-start(bf16[4,8,2560]{2,1,0:T(8,128)(2,1)S(1)} %pad_maximum_fusion.3.wmine0_ref), channel_id=1, source_target_pairs={{0,3},{1,2},{2,1},{3,0},{4,7},{5,6},{6,5},{7,4},{8,11},{9,10},{10,... | collective-permute-start | bytes 491528 | tf_op jit(solution)/shard_map/ppermute | solution.py:504
  15.6 0.5 collective-permute-start.4
  16.1 0.5 collective-permute-start.3
  16.7 4.5 %collective-permute-done.5.wmine3_ref = bf16[4,8,2560]{2,1,0:T(8,128)(2,1)S(1)} collective-permute-done((bf16[4,8,2560]{2,1,0:T(8,128)(2,1)S(1)}, bf16[4,8,2560]{2,1,0:T(8,128)(2,1)S(1)}, u32[]{:S(2)}, u32[]{:S(2)}) %collective-permute-start.5) | collective-permute-done | bytes 163872 | tf_op jit(solution)/shard_map/ppermute | solution.py:504
  21.1 0.9 collective-permute-done.4.wmine2_ref
  22.1 0.1 collective-permute-done.3.wmine1_ref
  22.1 0.5 collective-permute-start.7
  22.6 1.3 %copy.28.prompts_ref = bf16[8,10,128]{2,1,0:T(8,128)(2,1)} copy(bf16[8,10,128]{2,0,1:T(8,128)(2,1)} %param.15) | data formatting | bytes 40960 | tf_op args[1]
  24.0 0.7 copy.27.patches_ref
  24.7 0.0 collective-permute-done.8.wother2_ref
  24.8 0.6 copy-done.10
  25.4 0.1 copy-done.11
  25.4 0.1 copy-done.12
  25.5 0.0 copy-done.13
  25.5 51.3 %tower.1 = (bf16[2,4,128,128]{3,2,1,0:T(8,128)(2,1)}, f32[2,4,117,128]{3,2,1,0:T(8,128)}, bf16[4,4,8,2560]{3,2,1,0:T(8,128)(2,1)}, bf16[4,4,8,2560]{3,2,1,0:T(8,...) custom-call(s32[2]{0:T(128)} %ids_ref.1, s32[8]{0:T(128)} %counts_ref.1, bf16[4,8,2560]{2,1,0:T(8,128)(2,1)} %copy-done.4, ...), custom_call_target="tpu_custom_call" | custom-call | flops 10000000000 | bytes 20000000 | tf_op jit(solution)/shard_map/tower/pallas_call | solution.py:418
  76.8 0.1 collective-permute-start.10
  76.9 0.4 collective-permute-start.11
  77.4 2.0 %collective-permute-done.11 = f32[4,8,1024]{2,1,0:T(8,128)S(1)} collective-permute-done((f32[4,8,1024]{2,1,0:T(8,128)}, f32[4,8,1024]{2,1,0:T(8,128)S(1)}, u32[]{:S(2)}, u32[]{:S(2)}) %collective-permute-start.11) | collective-permute-done | bytes 131104 | tf_op jit(solution)/shard_map/ppermute | solution.py:500
  79.3 0.9 add_convert_fusion.2
  80.3 0.0 collective-permute-done.10
  80.3 1.2 %add_convert_fusion = bf16[4,4,8,2560]{3,2,1,0:T(8,128)(2,1)S(1)} fusion(bf16[4,4,8,2560]{3,2,1,0:T(8,128)(2,1)S(1)} %collective-permute-done.10, bf16[4,4,8,2560]{3,2,1,0:T(8,128)(2,1)} %get-tuple-element.32), kind=kLoop, calls=%fused_computation | loop fusion | flops 1310720 | bytes 1966080 | tf_op jit(solution)/shard_map/convert_element_type | solution.py:546
  81.6 1.6 %collective-permute-start.12 = (bf16[4,8,3584]{2,1,0:T(8,128)(2,1)S(1)}, bf16[4,8,3584]{2,1,0:T(8,128)(2,1)S(1)}, u32[]{:S(2)}, u32[]{:S(2)}) collective-permute-start(bf16[4,8,3584]{2,1,0:T(8,128)(2,1)S(1)} %get-tuple-element.82), channel_id=1, source_target_pairs={{0,1},{1,0},{2,3},{3,2},{4,5},{5,4},{6,7},{7,6},{8,9},{9,8},{10,11... | collective-permute-start | bytes 688136 | tf_op jit(solution)/shard_map/ppermute | solution.py:504
  83.2 0.8 collective-permute-start.13
  84.0 1.2 %collective-permute-start.14 = (bf16[4,8,3584]{2,1,0:T(8,128)(2,1)S(1)}, bf16[4,8,3584]{2,1,0:T(8,128)(2,1)S(1)}, u32[]{:S(2)}, u32[]{:S(2)}) collective-permute-start(bf16[4,8,3584]{2,1,0:T(8,128)(2,1)S(1)} %get-tuple-element.84), channel_id=1, source_target_pairs={{0,3},{1,2},{2,1},{3,0},{4,7},{5,6},{6,5},{7,4},{8,11},{9,10},{10,... | collective-permute-start | bytes 688136 | tf_op jit(solution)/shard_map/ppermute | solution.py:504
  85.2 5.0 %collective-permute-done.12 = bf16[4,8,3584]{2,1,0:T(8,128)(2,1)S(1)} collective-permute-done((bf16[4,8,3584]{2,1,0:T(8,128)(2,1)S(1)}, bf16[4,8,3584]{2,1,0:T(8,128)(2,1)S(1)}, u32[]{:S(2)}, u32[]{:S(2)}) %collective-permute-start.12) | collective-permute-done | bytes 229408 | tf_op jit(solution)/shard_map/ppermute | solution.py:504
  90.1 5.3 %collective-permute-done.13 = bf16[4,8,3584]{2,1,0:T(8,128)(2,1)S(1)} collective-permute-done((bf16[4,8,3584]{2,1,0:T(8,128)(2,1)S(1)}, bf16[4,8,3584]{2,1,0:T(8,128)(2,1)S(1)}, u32[]{:S(2)}, u32[]{:S(2)}) %collective-permute-start.13) | collective-permute-done | bytes 229408 | tf_op jit(solution)/shard_map/ppermute | solution.py:504
  95.5 0.1 fusion.1
  95.7 0.5 collective-permute-start.15
  96.1 2.1 %collective-permute-start.16 = (bf16[8,6656]{1,0:T(8,128)(2,1)S(1)}, bf16[8,6656]{1,0:T(8,128)(2,1)S(1)}, u32[]{:S(2)}, u32[]{:S(2)}) collective-permute-start(bf16[8,6656]{1,0:T(8,128)(2,1)S(1)} %get-tuple-element.71), channel_id=1, source_target_pairs={{0,8},{1,9},{2,10},{3,11},{4,12},{5,13},{6,14},{7,15},{8,0},{9,1},... | collective-permute-start | bytes 319496 | tf_op jit(solution)/shard_map/ppermute | solution.py:504
  98.2 1.9 %collective-permute-start.17 = (bf16[8,6656]{1,0:T(8,128)(2,1)S(1)}, bf16[8,6656]{1,0:T(8,128)(2,1)S(1)}, u32[]{:S(2)}, u32[]{:S(2)}) collective-permute-start(bf16[8,6656]{1,0:T(8,128)(2,1)S(1)} %get-tuple-element.72), channel_id=1, source_target_pairs={{0,12},{1,13},{2,14},{3,15},{4,8},{5,9},{6,10},{7,11},{8,4},{9,5},... | collective-permute-start | bytes 319496 | tf_op jit(solution)/shard_map/ppermute | solution.py:504
  100.1 0.7 collective-permute-done.15
  100.9 6.0 %collective-permute-done.16 = bf16[8,6656]{1,0:T(8,128)(2,1)S(1)} collective-permute-done((bf16[8,6656]{1,0:T(8,128)(2,1)S(1)}, bf16[8,6656]{1,0:T(8,128)(2,1)S(1)}, u32[]{:S(2)}, u32[]{:S(2)}) %collective-permute-start.16) | collective-permute-done | bytes 106528 | tf_op jit(solution)/shard_map/ppermute | solution.py:504
  106.9 0.1 collective-permute-start.19
  107.1 0.6 collective-permute-start.18
  107.6 0.9 copy.29
  108.5 0.0 collective-permute-done.18.big_other
  108.5 0.0 collective-permute-done.19.small_other
  108.6 0.6 copy-done.6
  109.2 0.6 copy-done.5
  109.8 1.8 %final.1 = (f32[2,2,8,384]{3,2,1,0:T(8,128)}, f32[2,2,8,128]{3,2,1,0:T(8,128)}, f32[2,8,1024]{2,1,0:T(8,128)}, f32[2,32,128]{2,1,0:T(8,128)}, f32[2,128,128]{2,1...) custom-call(f32[8,2560]{1,0:T(8,128)} %copy-done.2, ...), custom_call_target="tpu_custom_call" | custom-call | tf_op jit(solution)/shard_map/final/pallas_call | solution.py:418
  (41 shorter events, 0.3 us)
Async XLA Ops:
  0.6 23.3 %copy-start.3 = (bf16[2,4,117,128]{3,1,2,0:T(4,128)(2,1)S(1)}, bf16[2,4,117,128]{3,1,2,0:T(4,128)(2,1)}, u32[]{:S(2)}) copy-start(bf16[2,4,117,128]{3,1,2,0:T(4,128)(2,1)} %param.14) | copy-start | bytes 718852
  2.1 7.3 %collective-permute-start.2 = (bf16[1,8,2560]{2,1,0:T(8,128)(2,1)}, bf16[1,8,2560]{2,1,0:T(8,128)(2,1)S(1)}, u32[]{:S(2)}, u32[]{:S(2)}) collective-permute-start(bf16[1,8,2560]{2,1,0:T(8,128)(2,1)} %pack.1), channel_id=1, source_target_pairs={{0,12},{1,13},{2,14},{3,15},{4,8},{5,9},{6,10},{7,11},{8,4},{9,5},... | collective-permute-start | bytes 122888 | tf_op jit(solution)/shard_map/ppermute | solution.py:504
  7.2 5.1 %collective-permute-start.1 = (bf16[1,8,2560]{2,1,0:T(8,128)(2,1)}, bf16[1,8,2560]{2,1,0:T(8,128)(2,1)S(1)}, u32[]{:S(2)}, u32[]{:S(2)}) collective-permute-start(bf16[1,8,2560]{2,1,0:T(8,128)(2,1)} %pack.1), channel_id=1, source_target_pairs={{0,8},{1,9},{2,10},{3,11},{4,12},{5,13},{6,14},{7,15},{8,0},{9,1},... | collective-permute-start | bytes 122888 | tf_op jit(solution)/shard_map/ppermute | solution.py:504
  7.2 5.1 %collective-permute-start = (bf16[1,8,2560]{2,1,0:T(8,128)(2,1)}, bf16[1,8,2560]{2,1,0:T(8,128)(2,1)S(1)}, u32[]{:S(2)}, u32[]{:S(2)}) collective-permute-start(bf16[1,8,2560]{2,1,0:T(8,128)(2,1)} %pack.1), channel_id=1, source_target_pairs={{0,4},{1,5},{2,6},{3,7},{4,0},{5,1},{6,2},{7,3},{8,12},{9,13},{10,... | collective-permute-start | bytes 122888 | tf_op jit(solution)/shard_map/ppermute | solution.py:504
  13.1 11.7 %copy-start.4 = (bf16[4,8,2560]{2,1,0:T(8,128)(2,1)}, bf16[4,8,2560]{2,1,0:T(8,128)(2,1)S(1)}, u32[]{:S(2)}) copy-start(bf16[4,8,2560]{2,1,0:T(8,128)(2,1)S(1)} %pad_maximum_fusion.3.wmine0_ref) | copy-start | bytes 491524
  13.1 8.0 %collective-permute-start.5 = (bf16[4,8,2560]{2,1,0:T(8,128)(2,1)S(1)}, bf16[4,8,2560]{2,1,0:T(8,128)(2,1)S(1)}, u32[]{:S(2)}, u32[]{:S(2)}) collective-permute-start(bf16[4,8,2560]{2,1,0:T(8,128)(2,1)S(1)} %pad_maximum_fusion.3.wmine0_ref), channel_id=1, source_target_pairs={{0,3},{1,2},{2,1},{3,0},{4,7},{5,6},{6,5},{7,4},{8,11},{9,10},{10,... | collective-permute-start | bytes 491528 | tf_op jit(solution)/shard_map/ppermute | solution.py:504
  15.6 6.5 %collective-permute-start.4 = (bf16[4,8,2560]{2,1,0:T(8,128)(2,1)S(1)}, bf16[4,8,2560]{2,1,0:T(8,128)(2,1)S(1)}, u32[]{:S(2)}, u32[]{:S(2)}) collective-permute-start(bf16[4,8,2560]{2,1,0:T(8,128)(2,1)S(1)} %pad_maximum_fusion.3.wmine0_ref), channel_id=1, source_target_pairs={{0,2},{1,3},{2,0},{3,1},{4,6},{5,7},{6,4},{7,5},{8,10},{9,11},{10,... | collective-permute-start | bytes 491528 | tf_op jit(solution)/shard_map/ppermute | solution.py:504
  16.1 6.0 %collective-permute-start.3 = (bf16[4,8,2560]{2,1,0:T(8,128)(2,1)S(1)}, bf16[4,8,2560]{2,1,0:T(8,128)(2,1)S(1)}, u32[]{:S(2)}, u32[]{:S(2)}) collective-permute-start(bf16[4,8,2560]{2,1,0:T(8,128)(2,1)S(1)} %pad_maximum_fusion.3.wmine0_ref), channel_id=1, source_target_pairs={{0,1},{1,0},{2,3},{3,2},{4,5},{5,4},{6,7},{7,6},{8,9},{9,8},{10,11... | collective-permute-start | bytes 491528 | tf_op jit(solution)/shard_map/ppermute | solution.py:504
  16.6 8.0 %collective-permute-start.6 = (bf16[4,8,2560]{2,1,0:T(8,128)(2,1)S(1)}, bf16[4,8,2560]{2,1,0:T(8,128)(2,1)S(1)}, u32[]{:S(2)}, u32[]{:S(2)}) collective-permute-start(bf16[4,8,2560]{2,1,0:T(8,128)(2,1)S(1)} %pad_maximum_fusion.3.wmine0_ref), channel_id=1, source_target_pairs={{0,16},{16,0},{1,17},{17,1},{2,18},{18,2},{3,19},{19,3},{4,20},{20... | collective-permute-start | bytes 491528 | tf_op jit(solution)/shard_map/ppermute | solution.py:500
  21.1 3.6 %copy-start.7 = (bf16[4,8,2560]{2,1,0:T(8,128)(2,1)}, bf16[4,8,2560]{2,1,0:T(8,128)(2,1)S(1)}, u32[]{:S(2)}) copy-start(bf16[4,8,2560]{2,1,0:T(8,128)(2,1)S(1)} %collective-permute-done.5.wmine3_ref) | copy-start | bytes 491524
  21.1 3.6 %collective-permute-start.9 = (bf16[4,8,2560]{2,1,0:T(8,128)(2,1)S(1)}, bf16[4,8,2560]{2,1,0:T(8,128)(2,1)S(1)}, u32[]{:S(2)}, u32[]{:S(2)}) collective-permute-start(bf16[4,8,2560]{2,1,0:T(8,128)(2,1)S(1)} %collective-permute-done.5.wmine3_ref), channel_id=1, source_target_pairs={{0,16},{16,0},{1,17},{17,1},{2,18},{18,2},{3,19},{19,3},{4,20},{20... | collective-permute-start | bytes 491528 | tf_op jit(solution)/shard_map/ppermute | solution.py:500
  22.1 2.7 %copy-start.8 = (bf16[4,8,2560]{2,1,0:T(8,128)(2,1)}, bf16[4,8,2560]{2,1,0:T(8,128)(2,1)S(1)}, u32[]{:S(2)}) copy-start(bf16[4,8,2560]{2,1,0:T(8,128)(2,1)S(1)} %collective-permute-done.4.wmine2_ref) | copy-start | bytes 491524
  22.1 2.6 %collective-permute-start.8 = (bf16[4,8,2560]{2,1,0:T(8,128)(2,1)S(1)}, bf16[4,8,2560]{2,1,0:T(8,128)(2,1)S(1)}, u32[]{:S(2)}, u32[]{:S(2)}) collective-permute-start(bf16[4,8,2560]{2,1,0:T(8,128)(2,1)S(1)} %collective-permute-done.4.wmine2_ref), channel_id=1, source_target_pairs={{0,16},{16,0},{1,17},{17,1},{2,18},{18,2},{3,19},{19,3},{4,20},{20... | collective-permute-start | bytes 491528 | tf_op jit(solution)/shard_map/ppermute | solution.py:500
  22.1 2.6 %copy-start.9 = (bf16[4,8,2560]{2,1,0:T(8,128)(2,1)}, bf16[4,8,2560]{2,1,0:T(8,128)(2,1)S(1)}, u32[]{:S(2)}) copy-start(bf16[4,8,2560]{2,1,0:T(8,128)(2,1)S(1)} %collective-permute-done.3.wmine1_ref) | copy-start | bytes 491524
  22.1 2.6 %collective-permute-start.7 = (bf16[4,8,2560]{2,1,0:T(8,128)(2,1)S(1)}, bf16[4,8,2560]{2,1,0:T(8,128)(2,1)S(1)}, u32[]{:S(2)}, u32[]{:S(2)}) collective-permute-start(bf16[4,8,2560]{2,1,0:T(8,128)(2,1)S(1)} %collective-permute-done.3.wmine1_ref), channel_id=1, source_target_pairs={{0,16},{16,0},{1,17},{17,1},{2,18},{18,2},{3,19},{19,3},{4,20},{20... | collective-permute-start | bytes 491528 | tf_op jit(solution)/shard_map/ppermute | solution.py:500
  24.7 0.7 copy-start.10
  24.7 0.7 copy-start.11
  24.7 0.8 copy-start.12
  24.7 0.8 copy-start.13
  76.8 3.5 %collective-permute-start.10 = (bf16[4,4,8,2560]{3,2,1,0:T(8,128)(2,1)}, bf16[4,4,8,2560]{3,2,1,0:T(8,128)(2,1)S(1)}, u32[]{:S(2)}, u32[]{:S(2)}) collective-permute-start(bf16[4,4,8,2560]{3,2,1,0:T(8,128)(2,1)} %get-tuple-element.33), channel_id=1, source_target_pairs={{0,16},{16,0},{1,17},{17,1},{2,18},{18,2},{3,19},{19,3},{4,20},{20... | collective-permute-start | bytes 1966088 | tf_op jit(solution)/shard_map/ppermute | solution.py:500
  76.9 2.4 %collective-permute-start.11 = (f32[4,8,1024]{2,1,0:T(8,128)}, f32[4,8,1024]{2,1,0:T(8,128)S(1)}, u32[]{:S(2)}, u32[]{:S(2)}) collective-permute-start(f32[4,8,1024]{2,1,0:T(8,128)} %get-tuple-element.35), channel_id=1, source_target_pairs={{0,16},{16,0},{1,17},{17,1},{2,18},{18,2},{3,19},{19,3},{4,20},{20... | collective-permute-start | bytes 393224 | tf_op jit(solution)/shard_map/ppermute | solution.py:500
  81.6 8.5 %collective-permute-start.12 = (bf16[4,8,3584]{2,1,0:T(8,128)(2,1)S(1)}, bf16[4,8,3584]{2,1,0:T(8,128)(2,1)S(1)}, u32[]{:S(2)}, u32[]{:S(2)}) collective-permute-start(bf16[4,8,3584]{2,1,0:T(8,128)(2,1)S(1)} %get-tuple-element.82), channel_id=1, source_target_pairs={{0,1},{1,0},{2,3},{3,2},{4,5},{5,4},{6,7},{7,6},{8,9},{9,8},{10,11... | collective-permute-start | bytes 688136 | tf_op jit(solution)/shard_map/ppermute | solution.py:504
  83.2 12.3 %collective-permute-start.13 = (bf16[4,8,3584]{2,1,0:T(8,128)(2,1)S(1)}, bf16[4,8,3584]{2,1,0:T(8,128)(2,1)S(1)}, u32[]{:S(2)}, u32[]{:S(2)}) collective-permute-start(bf16[4,8,3584]{2,1,0:T(8,128)(2,1)S(1)} %get-tuple-element.83), channel_id=1, source_target_pairs={{0,2},{1,3},{2,0},{3,1},{4,6},{5,7},{6,4},{7,5},{8,10},{9,11},{10,... | collective-permute-start | bytes 688136 | tf_op jit(solution)/shard_map/ppermute | solution.py:504
  84.0 11.5 %collective-permute-start.14 = (bf16[4,8,3584]{2,1,0:T(8,128)(2,1)S(1)}, bf16[4,8,3584]{2,1,0:T(8,128)(2,1)S(1)}, u32[]{:S(2)}, u32[]{:S(2)}) collective-permute-start(bf16[4,8,3584]{2,1,0:T(8,128)(2,1)S(1)} %get-tuple-element.84), channel_id=1, source_target_pairs={{0,3},{1,2},{2,1},{3,0},{4,7},{5,6},{6,5},{7,4},{8,11},{9,10},{10,... | collective-permute-start | bytes 688136 | tf_op jit(solution)/shard_map/ppermute | solution.py:504
  95.6 12.1 %copy-start.1 = (f32[2,4,117,128]{3,2,1,0:T(8,128)S(1)}, f32[2,4,117,128]{3,2,1,0:T(8,128)}, u32[]{:S(2)}) copy-start(f32[2,4,117,128]{3,2,1,0:T(8,128)} %get-tuple-element.48) | copy-start | bytes 1437700
  95.7 5.2 %collective-permute-start.15 = (bf16[8,6656]{1,0:T(8,128)(2,1)S(1)}, bf16[8,6656]{1,0:T(8,128)(2,1)S(1)}, u32[]{:S(2)}, u32[]{:S(2)}) collective-permute-start(bf16[8,6656]{1,0:T(8,128)(2,1)S(1)} %get-tuple-element.70), channel_id=1, source_target_pairs={{0,4},{1,5},{2,6},{3,7},{4,0},{5,1},{6,2},{7,3},{8,12},{9,13},{10,... | collective-permute-start | bytes 319496 | tf_op jit(solution)/shard_map/ppermute | solution.py:504
  96.1 10.7 %collective-permute-start.16 = (bf16[8,6656]{1,0:T(8,128)(2,1)S(1)}, bf16[8,6656]{1,0:T(8,128)(2,1)S(1)}, u32[]{:S(2)}, u32[]{:S(2)}) collective-permute-start(bf16[8,6656]{1,0:T(8,128)(2,1)S(1)} %get-tuple-element.71), channel_id=1, source_target_pairs={{0,8},{1,9},{2,10},{3,11},{4,12},{5,13},{6,14},{7,15},{8,0},{9,1},... | collective-permute-start | bytes 319496 | tf_op jit(solution)/shard_map/ppermute | solution.py:504
  98.2 8.6 %collective-permute-start.17 = (bf16[8,6656]{1,0:T(8,128)(2,1)S(1)}, bf16[8,6656]{1,0:T(8,128)(2,1)S(1)}, u32[]{:S(2)}, u32[]{:S(2)}) collective-permute-start(bf16[8,6656]{1,0:T(8,128)(2,1)S(1)} %get-tuple-element.72), channel_id=1, source_target_pairs={{0,12},{1,13},{2,14},{3,15},{4,8},{5,9},{6,10},{7,11},{8,4},{9,5},... | collective-permute-start | bytes 319496 | tf_op jit(solution)/shard_map/ppermute | solution.py:504
  106.9 1.6 %copy-start = (f32[8,4096]{1,0:T(8,128)}, f32[8,4096]{1,0:T(8,128)S(1)}, u32[]{:S(2)}) copy-start(f32[8,4096]{1,0:T(8,128)S(1)} %add_add_fusion.small_mine) | copy-start | bytes 393220
  106.9 1.6 %collective-permute-start.19 = (f32[8,4096]{1,0:T(8,128)S(1)}, f32[8,4096]{1,0:T(8,128)S(1)}, u32[]{:S(2)}, u32[]{:S(2)}) collective-permute-start(f32[8,4096]{1,0:T(8,128)S(1)} %add_add_fusion.small_mine), channel_id=1, source_target_pairs={{0,16},{16,0},{1,17},{17,1},{2,18},{18,2},{3,19},{19,3},{4,20},{20... | collective-permute-start | bytes 393224 | tf_op jit(solution)/shard_map/ppermute | solution.py:500
  107.1 1.5 %copy-start.2 = (f32[8,2560]{1,0:T(8,128)}, f32[8,2560]{1,0:T(8,128)S(1)}, u32[]{:S(2)}) copy-start(f32[8,2560]{1,0:T(8,128)S(1)} %fusion.2.big_mine) | copy-start | bytes 245764
  107.1 1.5 %collective-permute-start.18 = (f32[8,2560]{1,0:T(8,128)S(1)}, f32[8,2560]{1,0:T(8,128)S(1)}, u32[]{:S(2)}, u32[]{:S(2)}) collective-permute-start(f32[8,2560]{1,0:T(8,128)S(1)} %fusion.2.big_mine), channel_id=1, source_target_pairs={{0,16},{16,0},{1,17},{17,1},{2,18},{18,2},{3,19},{19,3},{4,20},{20... | collective-permute-start | bytes 245768 | tf_op jit(solution)/shard_map/ppermute | solution.py:500
  108.5 0.6 copy-start.6
  109.2 0.6 copy-start.5

commit v8 on v7

--- a/solution.py
+++ b/solution.py
@@ -56,14 +56,28 @@
     out_ref[0] = jnp.concatenate(parts, axis=1).astype(BF)
 
 
+def prepare_kernel(ids_ref, patches_ref, prompts_ref, cls_ref, cot_ref, adj_ref, turned_ref, tok_ref):
+    for b in range(2):
+        ident = ids_ref[b]
+        for v in range(4):
+            at = 4 * b + v
+            lanes = slice(128 * (v % 2), 128 * (v % 2) + 128)
+            tok_ref[at, 0:10, :] = prompts_ref[ident].astype(F32)
+            tok_ref[at, 10:127, :] = patches_ref[b, v].astype(F32)
+            tok_ref[at, 127:128, :] = cls_ref[...].astype(F32)
+            turned_ref[0, 2 * b + v // 2, :, lanes] = tok_ref[at].T.astype(BF)
+            turned_ref[1, 2 * b + v // 2, :, lanes] = cot_ref[b, v].T
+            turned_ref[2, 2 * b + v // 2, :, lanes] = adj_ref[b, v].T
+
+
 def tower_kernel(
     split,
     ids_ref, counts_ref, wmine0_ref, wmine1_ref, wmine2_ref, wmine3_ref, wother0_ref, wother1_ref, wother2_ref, wother3_ref,
-    tok_ref, gains_ref, scales_ref, patches_ref, prompts_ref, cls_ref, cot_ref, adj_ref,
+    tok_ref, gains_ref, scales_ref, turned_ref,
     out_ref, pgrad_ref, bigmine_ref, bigother_ref, smallmine_ref, smallother_ref,
     stage_ref, w_ref, wd_ref, wt_ref, wdt_ref, colb_ref, tokscr_ref, h_ref, g_ref, xh_ref, inv_ref,
     qkvt_ref, pb_ref, ot_ref, qkvv_ref, pv_ref, ov_ref, pw_ref, qbd_ref, dob_ref, hid_ref, du_ref, dqkv_ref,
-    dov_ref, ga_ref, gd_ref, gt_ref, gacc_ref, gbig_ref, pacc_ref, spread_ref, act_ref, slope_ref, gdt_ref,
+    dov_ref, ga_ref, gd_ref, gt_ref, gacc_ref, gbig_ref, pacc_ref, spread_ref, act_ref, slope_ref, gdt_ref, both_ref,
 ):
     dp = lax.axis_index("dp") if split else 0
     me = lax.axis_index("fsdp") if split else 0
@@ -97,17 +111,8 @@
                 colb_ref[l * 8 + offset + k, :, 0:128] = col
                 colb_ref[l * 8 + offset + k, :, 128:256] = col
 
-    for b in range(items):
-        ident = ids_ref[b]
-        for v in range(4):
-            bv = 4 * b + v
-            tokscr_ref[bv, 0:10, :] = prompts_ref[ident].astype(F32)
-            tokscr_ref[bv, 10:127, :] = patches_ref[b, v].astype(F32)
-            tokscr_ref[bv, 127:128, :] = cls_ref[...].astype(F32)
-            lanes = slice(128 * (v % 2), 128 * (v % 2) + 128)
-            h_ref[2 * b + v // 2, :, lanes] = tokscr_ref[bv].T
-            g_ref[0, 2 * b + v // 2, :, lanes] = cot_ref[b, v].astype(F32).T
-            g_ref[1, 2 * b + v // 2, :, lanes] = adj_ref[b, v].astype(F32).T
+    h_ref[...] = turned_ref[0].astype(F32)
+    g_ref[...] = turned_ref[1:3].astype(F32)
 
     head_row = lax.broadcasted_iota(jnp.int32, (8, 128), 0)
     head_col = lax.broadcasted_iota(jnp.int32, (8, 128), 1) // 16
@@ -123,6 +128,9 @@
         for head in range(HEADS):
             target_ref[at, 16 * head : 16 * head + 16, 128 * head : 128 * head + 128] = rows[16 * head : 16 * head + 16]
 
+    both_ref[...] = jnp.zeros_like(both_ref)
+    for half in range(2):
+        both_ref[:, 128 * half : 128 * half + 128, 128 * half : 128 * half + 128] = tok_ref[...]
     qbd_ref[...] = jnp.zeros_like(qbd_ref)
     dob_ref[...] = jnp.zeros_like(dob_ref)
 
@@ -206,8 +214,7 @@
     def tail_forward(l, c):
         x = h_ref[c]
         n = keep_norm(l, 2, c, x)
-        mix = [dot_nt(n[:, 128 * s : 128 * s + 128], tok_ref[l]) for s in range(2)]
-        x = x + scale(l, 2) * jnp.concatenate(mix, axis=1)
+        x = x + scale(l, 2) * dot_nt(n, both_ref[l])
         n = keep_norm(l, 3, c, x)
         for z in range(4):
             rows = slice(128 * z, 128 * z + 128)
@@ -254,8 +261,7 @@
             if x == 0:
                 turned = jnp.concatenate([dy[:, :128].T, dy[:, 128:].T], axis=1)
                 gt_ref[l] += dot_nn(turned, jnp.concatenate([n[:, :128], n[:, 128:]], axis=0))
-            dn = [dot_nn(dy[:, 128 * s : 128 * s + 128], tok_ref[l]) for s in range(2)]
-            pass_on(l, 2, c, x, jnp.concatenate(dn, axis=1), xhat, inv)
+            pass_on(l, 2, c, x, dot_nn(dy, both_ref[l]), xhat, inv)
 
     def var_backward(l, b):
         def slot(first, i):
@@ -437,7 +443,7 @@
         functools.partial(tower_kernel, split),
         "tower",
         [shape_of((2, 4, 128, 128), BF), shape_of((2, 4, 117, 128))] + half,
-        "ss" + "v" * 16,
+        "ss" + "v" * 12,
         [
             pltpu.VMEM((2, 128, COLS), F32),
             pltpu.VMEM((2, 128, COL_DOWN), BF),
@@ -473,6 +479,7 @@
             pltpu.VMEM((2, 4, 512, 256), BF),
             pltpu.VMEM((2, 4, 512, 256), BF),
             pltpu.VMEM((128, 512), F32),
+            pltpu.VMEM((2, 256, 256), BF),
         ],
         *operands,
         cost=pl.CostEstimate(flops=10**10, bytes_accessed=20 * 10**6, transcendentals=0),
@@ -504,11 +511,12 @@
     return lax.ppermute(array, "fsdp", [(i, i ^ mask) for i in range(SHARDS)])
 
 
-def gather_rows(attn_in, attn_out, feed_in, feed_out):
+def gather_rows(attn_in, attn_out, feed_in, feed_out, turned):
     row = call(pack_kernel, "pack", [shape_of((1, 8, COLS), BF)], "vvvv", [], attn_in, attn_out, feed_in, feed_out)[0]
     column = jnp.concatenate([row] + [swap(row, 4 * z) for z in range(1, 4)], axis=0)
     mine = [column] + [swap(column, xy) for xy in range(1, 4)]
-    return mine + [flip(part, "dp", 0, 2) for part in mine]
+    mine, turned = lax.optimization_barrier((mine, turned))
+    return mine + [flip(part, "dp", 0, 2) for part in mine], turned
 
 
 def final_kernel(big_mine, big_other, small_mine, small_other, attn_in, attn_out, feed_in, feed_out, tokens, gains, scales,
@@ -563,8 +571,13 @@
 def per_device(shard_count, patches, prompts, cls_token, attn_in, attn_out, feed_in, feed_out, token_operator,
                norm_gains, branch_scales, var_counts, dataset_ids, cotangent, adjust_cotangent):
     fast = shard_count == SHARDS
+    turned = call(
+        prepare_kernel, "prepare", [shape_of((3, 4, 128, 256), BF)], "svvvvv", [pltpu.VMEM((8, 128, 128), F32)],
+        dataset_ids, patches, prompts, cls_token.reshape(1, -1), cotangent, adjust_cotangent,
+        cost=pl.CostEstimate(flops=10**6, bytes_accessed=8 * 10**6, transcendentals=0),
+    )[0]
     if fast:
-        gathered = gather_rows(attn_in, attn_out, feed_in, feed_out)
+        gathered, turned = gather_rows(attn_in, attn_out, feed_in, feed_out, turned)
     else:
         whole_down = lax.all_gather(feed_out, "fsdp", axis=1, tiled=True)
         whole_down = whole_down.reshape(2, SHARDS, 4, 8, 128).transpose(0, 2, 1, 3, 4).reshape(2, 512, 128)
@@ -577,8 +590,7 @@
         rows = rows.reshape(2, SHARDS, 8, COLS).transpose(1, 0, 2, 3)
         gathered = [rows[:, l].reshape(4, 4, 8, COLS)[:, xy] for l in range(2) for xy in range(4)]
     output, patch_grad, *sums = run_tower(
-        fast, dataset_ids, var_counts, *gathered, token_operator, norm_gains, branch_scales, patches, prompts,
-        cls_token.reshape(1, -1), cotangent, adjust_cotangent,
+        fast, dataset_ids, var_counts, *gathered, token_operator, norm_gains, branch_scales, turned
     )
     if fast:
         (attn_in_g, attn_out_g, feed_in_g, feed_out_g, token_g, gains_g, scales_g, prompt_g, cls_g, adjust_prompt_g,

time: 112 us -> 112 us (level)
  waiting for transfers between devices: 29.1 us -> 25 us
  Pallas kernels: 54.6 us -> 56.3 us
  local copies, waits for them, and re-layouts: 5.08 us -> 6.36 us
    ppermute x12, waiting for transfers between devices: 27.1 us -> 21.8 us  [swap(): return lax.ppermute(array, 'fsdp', [(i, i ^ mask) for i in range(SHARDS)])]
    pallas_call x3 -> x4, Pallas kernels: 54.6 us -> 56.3 us  [call(): pl.pallas_call(kernel, out_shape=out_shape, in_specs=[pl.BlockSpec(memory...]
    unnamed x35 -> x33, local copies, waits for them, and re-layouts: 5.04 us -> 6.31 us
  transfers between devices with their start and end apart: 20 -> 20, of which waited for: 10 -> 12; matrix products, arithmetic and copies ran while one was open for 4% -> 4% of each run, Pallas kernels for 0% -> 2%
where the time goes in v8:
time: 112 us; the launch traced here: 111 us
  Pallas kernels  56.3 us (50%)
  waiting for transfers between devices  25 us (22%)
  starting transfers between devices  19.4 us (17%)
  local copies, waits for them, and re-layouts  6.36 us (6%)
  other arithmetic  3.2 us (3%)
    pallas_call x4, Pallas kernels, call(): pl.pallas_call(kernel, out_shape=out_shape, in_specs=[pl.BlockSpec(memory...  56.3 us
    ppermute x12, waiting for transfers between devices, swap(): return lax.ppermute(array, 'fsdp', [(i, i ^ mask) for i in range(SHARDS)])  21.8 us
    ppermute x12, starting transfers between devices, swap(): return lax.ppermute(array, 'fsdp', [(i, i ^ mask) for i in range(SHARDS)])  17.2 us
    unnamed x33, local copies, waits for them, and re-layouts  6.31 us
    ppermute x8, waiting for transfers between devices, flip(): return lax.ppermute(array, axis, [(i, i ^ 1 << bit) for i in range(size)])  3.12 us
  transfers between devices with their start and end apart: 20, of which 12 were waited for; matrix products, arithmetic and copies ran while one was open for 4% of the time, Pallas kernels for 2%

profile of v8, /device:TPU:0, one launch (start us, length us, event | category | flops | bytes accessed | tf_op | source)
XLA Modules:
  0.0 111.2 jit_solution(15973834962166337177)
XLA Ops:
  0.6 1.4 %pack.1 = bf16[1,8,2560]{2,1,0:T(8,128)(2,1)} custom-call(bf16[2,2,8,384]{3,2,1,0:T(8,128)(2,1)} %attn_in_ref.1, bf16[2,2,8,128]{3,2,1,0:T(8,128)(2,1)} %attn_out_ref.1, bf16[2,8,1024]{2,1,0:T(8,128)(2,1)} %feed_in_ref.1, bf16[2,32,128]{2,1,0:T(8,128)(2,1)} %feed_out_ref.1), custom_call_target="tpu_custom_call" | custom-call | tf_op jit(solution)/shard_map/pack/pallas_call | solution.py:424
  2.1 5.0 %collective-permute-start.2 = (bf16[1,8,2560]{2,1,0:T(8,128)(2,1)}, bf16[1,8,2560]{2,1,0:T(8,128)(2,1)S(1)}, u32[]{:S(2)}, u32[]{:S(2)}) collective-permute-start(bf16[1,8,2560]{2,1,0:T(8,128)(2,1)} %pack.1), channel_id=1, source_target_pairs={{0,12},{1,13},{2,14},{3,15},{4,8},{5,9},{6,10},{7,11},{8,4},{9,5},... | collective-permute-start | bytes 122888 | tf_op jit(solution)/shard_map/ppermute | solution.py:511
  7.1 0.6 collective-permute-start
  7.7 1.6 %collective-permute-done.2 = bf16[1,8,2560]{2,1,0:T(8,128)(2,1)S(1)} collective-permute-done((bf16[1,8,2560]{2,1,0:T(8,128)(2,1)}, bf16[1,8,2560]{2,1,0:T(8,128)(2,1)S(1)}, u32[]{:S(2)}, u32[]{:S(2)}) %collective-permute-start.2) | collective-permute-done | bytes 40992 | tf_op jit(solution)/shard_map/ppermute | solution.py:511
  9.3 2.9 %collective-permute-done.1 = bf16[1,8,2560]{2,1,0:T(8,128)(2,1)S(1)} collective-permute-done((bf16[1,8,2560]{2,1,0:T(8,128)(2,1)}, bf16[1,8,2560]{2,1,0:T(8,128)(2,1)S(1)}, u32[]{:S(2)}, u32[]{:S(2)}) %collective-permute-start.1) | collective-permute-done | bytes 40992 | tf_op jit(solution)/shard_map/ppermute | solution.py:511
  12.2 0.8 pad_maximum_fusion.3.wmine0_ref
  13.0 2.5 %collective-permute-start.5 = (bf16[4,8,2560]{2,1,0:T(8,128)(2,1)S(1)}, bf16[4,8,2560]{2,1,0:T(8,128)(2,1)S(1)}, u32[]{:S(2)}, u32[]{:S(2)}) collective-permute-start(bf16[4,8,2560]{2,1,0:T(8,128)(2,1)S(1)} %pad_maximum_fusion.3.wmine0_ref), channel_id=1, source_target_pairs={{0,3},{1,2},{2,1},{3,0},{4,7},{5,6},{6,5},{7,4},{8,11},{9,10},{10,... | collective-permute-start | bytes 491528 | tf_op jit(solution)/shard_map/ppermute | solution.py:511
  15.6 0.5 collective-permute-start.4
  16.1 0.5 collective-permute-start.3
  16.6 1.3 %copy.28.prompts_ref = bf16[8,10,128]{2,1,0:T(8,128)(2,1)} copy(bf16[8,10,128]{2,0,1:T(8,128)(2,1)} %param.15) | data formatting | bytes 40960 | tf_op args[1]
  17.9 1.7 %copy.27.patches_ref = bf16[2,4,117,128]{3,2,1,0:T(8,128)(2,1)} copy(bf16[2,4,117,128]{3,1,2,0:T(4,128)(2,1)} %param.14) | data formatting | bytes 479232 | tf_op args[0]
  19.6 2.4 %prepare.1.turned_ref = bf16[3,4,128,256]{3,2,1,0:T(8,128)(2,1)} custom-call(s32[2]{0:T(128)} %ids_ref.3, bf16[2,4,117,128]{3,2,1,0:T(8,128)(2,1)} %copy.27.patches_ref, bf16[8,10,128]{2,1,0:T(8,128)(2,1)} %copy.28.prompts_ref, bf16[1,128]{1,0:T(2,128)(2,1)} %bitcast.65, bf16[2,4,128,128]{3,2,1,0:T(8,128)(2,1)} %cot_ref.1, bf16[2,4,128,128]{3,2,1,0:T(8,128)(2,1)} %adj_ref.1), custom_call_target="tpu_custom_call" | custom-call | flops 1000000 | bytes 8000000 | tf_op jit(solution)/shard_map/prepare/pallas_call | solution.py:424
  22.0 0.1 collective-permute-done.3.wmine1_ref
  22.1 0.0 collective-permute-start.6
  22.2 0.5 collective-permute-start.7
  22.6 0.1 collective-permute-start.8
  22.7 0.4 collective-permute-start.9
  23.2 0.4 collective-permute-done.6.wother0_ref
  23.5 0.2 collective-permute-done.7.wother1_ref
  23.8 0.3 collective-permute-done.8.wother2_ref
  24.0 0.2 collective-permute-done.9.wother3_ref
  24.3 0.1 copy-done.10
  24.4 0.3 copy-done.11
  24.7 0.6 copy-done.12
  25.4 50.7 %tower.1 = (bf16[2,4,128,128]{3,2,1,0:T(8,128)(2,1)}, f32[2,4,117,128]{3,2,1,0:T(8,128)}, bf16[4,4,8,2560]{3,2,1,0:T(8,128)(2,1)}, bf16[4,4,8,2560]{3,2,1,0:T(8,...) custom-call(s32[2]{0:T(128)} %ids_ref.3, s32[8]{0:T(128)} %counts_ref.1, bf16[4,8,2560]{2,1,0:T(8,128)(2,1)} %copy-done.3, ...), custom_call_target="tpu_custom_call" | custom-call | flops 10000000000 | bytes 20000000 | tf_op jit(solution)/shard_map/tower/pallas_call | solution.py:424
  76.0 0.2 collective-permute-start.10
  76.3 0.3 collective-permute-start.11
  76.6 2.0 %collective-permute-done.11 = f32[4,8,1024]{2,1,0:T(8,128)S(1)} collective-permute-done((f32[4,8,1024]{2,1,0:T(8,128)}, f32[4,8,1024]{2,1,0:T(8,128)S(1)}, u32[]{:S(2)}, u32[]{:S(2)}) %collective-permute-start.11) | collective-permute-done | bytes 131104 | tf_op jit(solution)/shard_map/ppermute | solution.py:507
  78.5 0.9 add_convert_fusion.2
  79.5 1.2 %add_convert_fusion = bf16[4,4,8,2560]{3,2,1,0:T(8,128)(2,1)S(1)} fusion(bf16[4,4,8,2560]{3,2,1,0:T(8,128)(2,1)S(1)} %collective-permute-done.10, bf16[4,4,8,2560]{3,2,1,0:T(8,128)(2,1)} %get-tuple-element.42), kind=kLoop, calls=%fused_computation | loop fusion | flops 1310720 | bytes 1966080 | tf_op jit(solution)/shard_map/convert_element_type | solution.py:554
  80.8 1.6 %collective-permute-start.12 = (bf16[4,8,3584]{2,1,0:T(8,128)(2,1)S(1)}, bf16[4,8,3584]{2,1,0:T(8,128)(2,1)S(1)}, u32[]{:S(2)}, u32[]{:S(2)}) collective-permute-start(bf16[4,8,3584]{2,1,0:T(8,128)(2,1)S(1)} %get-tuple-element.92), channel_id=1, source_target_pairs={{0,1},{1,0},{2,3},{3,2},{4,5},{5,4},{6,7},{7,6},{8,9},{9,8},{10,11... | collective-permute-start | bytes 688136 | tf_op jit(solution)/shard_map/ppermute | solution.py:511
  82.4 1.5 %collective-permute-start.13 = (bf16[4,8,3584]{2,1,0:T(8,128)(2,1)S(1)}, bf16[4,8,3584]{2,1,0:T(8,128)(2,1)S(1)}, u32[]{:S(2)}, u32[]{:S(2)}) collective-permute-start(bf16[4,8,3584]{2,1,0:T(8,128)(2,1)S(1)} %get-tuple-element.93), channel_id=1, source_target_pairs={{0,2},{1,3},{2,0},{3,1},{4,6},{5,7},{6,4},{7,5},{8,10},{9,11},{10,... | collective-permute-start | bytes 688136 | tf_op jit(solution)/shard_map/ppermute | solution.py:511
  83.9 0.5 collective-permute-start.14
  84.4 4.9 %collective-permute-done.12 = bf16[4,8,3584]{2,1,0:T(8,128)(2,1)S(1)} collective-permute-done((bf16[4,8,3584]{2,1,0:T(8,128)(2,1)S(1)}, bf16[4,8,3584]{2,1,0:T(8,128)(2,1)S(1)}, u32[]{:S(2)}, u32[]{:S(2)}) %collective-permute-start.12) | collective-permute-done | bytes 229408 | tf_op jit(solution)/shard_map/ppermute | solution.py:511
  89.3 5.5 %collective-permute-done.13 = bf16[4,8,3584]{2,1,0:T(8,128)(2,1)S(1)} collective-permute-done((bf16[4,8,3584]{2,1,0:T(8,128)(2,1)S(1)}, bf16[4,8,3584]{2,1,0:T(8,128)(2,1)S(1)}, u32[]{:S(2)}, u32[]{:S(2)}) %collective-permute-start.13) | collective-permute-done | bytes 229408 | tf_op jit(solution)/shard_map/ppermute | solution.py:511
  94.8 0.1 fusion.1
  95.0 0.5 collective-permute-start.15
  95.5 2.1 %collective-permute-start.16 = (bf16[8,6656]{1,0:T(8,128)(2,1)S(1)}, bf16[8,6656]{1,0:T(8,128)(2,1)S(1)}, u32[]{:S(2)}, u32[]{:S(2)}) collective-permute-start(bf16[8,6656]{1,0:T(8,128)(2,1)S(1)} %get-tuple-element.81), channel_id=1, source_target_pairs={{0,8},{1,9},{2,10},{3,11},{4,12},{5,13},{6,14},{7,15},{8,0},{9,1},... | collective-permute-start | bytes 319496 | tf_op jit(solution)/shard_map/ppermute | solution.py:511
  97.6 1.9 %collective-permute-start.17 = (bf16[8,6656]{1,0:T(8,128)(2,1)S(1)}, bf16[8,6656]{1,0:T(8,128)(2,1)S(1)}, u32[]{:S(2)}, u32[]{:S(2)}) collective-permute-start(bf16[8,6656]{1,0:T(8,128)(2,1)S(1)} %get-tuple-element.82), channel_id=1, source_target_pairs={{0,12},{1,13},{2,14},{3,15},{4,8},{5,9},{6,10},{7,11},{8,4},{9,5},... | collective-permute-start | bytes 319496 | tf_op jit(solution)/shard_map/ppermute | solution.py:511
  99.4 0.8 collective-permute-done.15
  100.3 6.0 %collective-permute-done.16 = bf16[8,6656]{1,0:T(8,128)(2,1)S(1)} collective-permute-done((bf16[8,6656]{1,0:T(8,128)(2,1)S(1)}, bf16[8,6656]{1,0:T(8,128)(2,1)S(1)}, u32[]{:S(2)}, u32[]{:S(2)}) %collective-permute-start.16) | collective-permute-done | bytes 106528 | tf_op jit(solution)/shard_map/ppermute | solution.py:511
  106.3 0.1 collective-permute-start.19
  106.5 0.6 collective-permute-start.18
  107.0 0.9 copy.29
  107.9 0.0 collective-permute-done.18.big_other
  107.9 0.6 copy-done.5
  108.6 0.6 copy-done.4
  109.2 1.8 %final.1 = (f32[2,2,8,384]{3,2,1,0:T(8,128)}, f32[2,2,8,128]{3,2,1,0:T(8,128)}, f32[2,8,1024]{2,1,0:T(8,128)}, f32[2,32,128]{2,1,0:T(8,128)}, f32[2,128,128]{2,1...) custom-call(f32[8,2560]{1,0:T(8,128)} %copy-done.2, ...), custom_call_target="tpu_custom_call" | custom-call | tf_op jit(solution)/shard_map/final/pallas_call | solution.py:424
  (40 shorter events, 0.3 us)
Async XLA Ops:
  2.1 7.3 %collective-permute-start.2 = (bf16[1,8,2560]{2,1,0:T(8,128)(2,1)}, bf16[1,8,2560]{2,1,0:T(8,128)(2,1)S(1)}, u32[]{:S(2)}, u32[]{:S(2)}) collective-permute-start(bf16[1,8,2560]{2,1,0:T(8,128)(2,1)} %pack.1), channel_id=1, source_target_pairs={{0,12},{1,13},{2,14},{3,15},{4,8},{5,9},{6,10},{7,11},{8,4},{9,5},... | collective-permute-start | bytes 122888 | tf_op jit(solution)/shard_map/ppermute | solution.py:511
  7.1 5.1 %collective-permute-start.1 = (bf16[1,8,2560]{2,1,0:T(8,128)(2,1)}, bf16[1,8,2560]{2,1,0:T(8,128)(2,1)S(1)}, u32[]{:S(2)}, u32[]{:S(2)}) collective-permute-start(bf16[1,8,2560]{2,1,0:T(8,128)(2,1)} %pack.1), channel_id=1, source_target_pairs={{0,8},{1,9},{2,10},{3,11},{4,12},{5,13},{6,14},{7,15},{8,0},{9,1},... | collective-permute-start | bytes 122888 | tf_op jit(solution)/shard_map/ppermute | solution.py:511
  7.1 5.1 %collective-permute-start = (bf16[1,8,2560]{2,1,0:T(8,128)(2,1)}, bf16[1,8,2560]{2,1,0:T(8,128)(2,1)S(1)}, u32[]{:S(2)}, u32[]{:S(2)}) collective-permute-start(bf16[1,8,2560]{2,1,0:T(8,128)(2,1)} %pack.1), channel_id=1, source_target_pairs={{0,4},{1,5},{2,6},{3,7},{4,0},{5,1},{6,2},{7,3},{8,12},{9,13},{10,... | collective-permute-start | bytes 122888 | tf_op jit(solution)/shard_map/ppermute | solution.py:511
  13.0 9.1 %copy-start.3 = (bf16[4,8,2560]{2,1,0:T(8,128)(2,1)}, bf16[4,8,2560]{2,1,0:T(8,128)(2,1)S(1)}, u32[]{:S(2)}) copy-start(bf16[4,8,2560]{2,1,0:T(8,128)(2,1)S(1)} %pad_maximum_fusion.3.wmine0_ref) | copy-start | bytes 491524
  13.0 9.0 %collective-permute-start.5 = (bf16[4,8,2560]{2,1,0:T(8,128)(2,1)S(1)}, bf16[4,8,2560]{2,1,0:T(8,128)(2,1)S(1)}, u32[]{:S(2)}, u32[]{:S(2)}) collective-permute-start(bf16[4,8,2560]{2,1,0:T(8,128)(2,1)S(1)} %pad_maximum_fusion.3.wmine0_ref), channel_id=1, source_target_pairs={{0,3},{1,2},{2,1},{3,0},{4,7},{5,6},{6,5},{7,4},{8,11},{9,10},{10,... | collective-permute-start | bytes 491528 | tf_op jit(solution)/shard_map/ppermute | solution.py:511
  15.6 6.5 %collective-permute-start.4 = (bf16[4,8,2560]{2,1,0:T(8,128)(2,1)S(1)}, bf16[4,8,2560]{2,1,0:T(8,128)(2,1)S(1)}, u32[]{:S(2)}, u32[]{:S(2)}) collective-permute-start(bf16[4,8,2560]{2,1,0:T(8,128)(2,1)S(1)} %pad_maximum_fusion.3.wmine0_ref), channel_id=1, source_target_pairs={{0,2},{1,3},{2,0},{3,1},{4,6},{5,7},{6,4},{7,5},{8,10},{9,11},{10,... | collective-permute-start | bytes 491528 | tf_op jit(solution)/shard_map/ppermute | solution.py:511
  16.1 6.0 %collective-permute-start.3 = (bf16[4,8,2560]{2,1,0:T(8,128)(2,1)S(1)}, bf16[4,8,2560]{2,1,0:T(8,128)(2,1)S(1)}, u32[]{:S(2)}, u32[]{:S(2)}) collective-permute-start(bf16[4,8,2560]{2,1,0:T(8,128)(2,1)S(1)} %pad_maximum_fusion.3.wmine0_ref), channel_id=1, source_target_pairs={{0,1},{1,0},{2,3},{3,2},{4,5},{5,4},{6,7},{7,6},{8,9},{9,8},{10,11... | collective-permute-start | bytes 491528 | tf_op jit(solution)/shard_map/ppermute | solution.py:511
  22.0 2.3 %copy-start.6 = (bf16[4,8,2560]{2,1,0:T(8,128)(2,1)}, bf16[4,8,2560]{2,1,0:T(8,128)(2,1)S(1)}, u32[]{:S(2)}) copy-start(bf16[4,8,2560]{2,1,0:T(8,128)(2,1)S(1)} %collective-permute-done.5.wmine3_ref) | copy-start | bytes 491524
  22.0 2.2 %copy-start.7 = (bf16[4,8,2560]{2,1,0:T(8,128)(2,1)}, bf16[4,8,2560]{2,1,0:T(8,128)(2,1)S(1)}, u32[]{:S(2)}) copy-start(bf16[4,8,2560]{2,1,0:T(8,128)(2,1)S(1)} %collective-permute-done.4.wmine2_ref) | copy-start | bytes 491524
  22.1 2.2 %copy-start.8 = (bf16[4,8,2560]{2,1,0:T(8,128)(2,1)}, bf16[4,8,2560]{2,1,0:T(8,128)(2,1)S(1)}, u32[]{:S(2)}) copy-start(bf16[4,8,2560]{2,1,0:T(8,128)(2,1)S(1)} %collective-permute-done.3.wmine1_ref) | copy-start | bytes 491524
  22.1 1.4 %collective-permute-start.6 = (bf16[4,8,2560]{2,1,0:T(8,128)(2,1)S(1)}, bf16[4,8,2560]{2,1,0:T(8,128)(2,1)S(1)}, u32[]{:S(2)}, u32[]{:S(2)}) collective-permute-start(bf16[4,8,2560]{2,1,0:T(8,128)(2,1)S(1)} %pad_maximum_fusion.3.wmine0_ref), channel_id=1, source_target_pairs={{0,16},{16,0},{1,17},{17,1},{2,18},{18,2},{3,19},{19,3},{4,20},{20... | collective-permute-start | bytes 491528 | tf_op jit(solution)/shard_map/ppermute | solution.py:507
  22.2 1.6 %collective-permute-start.7 = (bf16[4,8,2560]{2,1,0:T(8,128)(2,1)S(1)}, bf16[4,8,2560]{2,1,0:T(8,128)(2,1)S(1)}, u32[]{:S(2)}, u32[]{:S(2)}) collective-permute-start(bf16[4,8,2560]{2,1,0:T(8,128)(2,1)S(1)} %collective-permute-done.3.wmine1_ref), channel_id=1, source_target_pairs={{0,16},{16,0},{1,17},{17,1},{2,18},{18,2},{3,19},{19,3},{4,20},{20... | collective-permute-start | bytes 491528 | tf_op jit(solution)/shard_map/ppermute | solution.py:507
  22.6 1.4 %collective-permute-start.8 = (bf16[4,8,2560]{2,1,0:T(8,128)(2,1)S(1)}, bf16[4,8,2560]{2,1,0:T(8,128)(2,1)S(1)}, u32[]{:S(2)}, u32[]{:S(2)}) collective-permute-start(bf16[4,8,2560]{2,1,0:T(8,128)(2,1)S(1)} %collective-permute-done.4.wmine2_ref), channel_id=1, source_target_pairs={{0,16},{16,0},{1,17},{17,1},{2,18},{18,2},{3,19},{19,3},{4,20},{20... | collective-permute-start | bytes 491528 | tf_op jit(solution)/shard_map/ppermute | solution.py:507
  22.7 1.6 %collective-permute-start.9 = (bf16[4,8,2560]{2,1,0:T(8,128)(2,1)S(1)}, bf16[4,8,2560]{2,1,0:T(8,128)(2,1)S(1)}, u32[]{:S(2)}, u32[]{:S(2)}) collective-permute-start(bf16[4,8,2560]{2,1,0:T(8,128)(2,1)S(1)} %collective-permute-done.5.wmine3_ref), channel_id=1, source_target_pairs={{0,16},{16,0},{1,17},{17,1},{2,18},{18,2},{3,19},{19,3},{4,20},{20... | collective-permute-start | bytes 491528 | tf_op jit(solution)/shard_map/ppermute | solution.py:507
  23.5 0.8 copy-start.9
  23.8 0.7 copy-start.10
  24.0 0.7 copy-start.11
  24.7 0.7 copy-start.12
  76.0 3.4 %collective-permute-start.10 = (bf16[4,4,8,2560]{3,2,1,0:T(8,128)(2,1)}, bf16[4,4,8,2560]{3,2,1,0:T(8,128)(2,1)S(1)}, u32[]{:S(2)}, u32[]{:S(2)}) collective-permute-start(bf16[4,4,8,2560]{3,2,1,0:T(8,128)(2,1)} %get-tuple-element.43), channel_id=1, source_target_pairs={{0,16},{16,0},{1,17},{17,1},{2,18},{18,2},{3,19},{19,3},{4,20},{20... | collective-permute-start | bytes 1966088 | tf_op jit(solution)/shard_map/ppermute | solution.py:507
  76.3 2.3 %collective-permute-start.11 = (f32[4,8,1024]{2,1,0:T(8,128)}, f32[4,8,1024]{2,1,0:T(8,128)S(1)}, u32[]{:S(2)}, u32[]{:S(2)}) collective-permute-start(f32[4,8,1024]{2,1,0:T(8,128)} %get-tuple-element.45), channel_id=1, source_target_pairs={{0,16},{16,0},{1,17},{17,1},{2,18},{18,2},{3,19},{19,3},{4,20},{20... | collective-permute-start | bytes 393224 | tf_op jit(solution)/shard_map/ppermute | solution.py:507
  80.8 8.5 %collective-permute-start.12 = (bf16[4,8,3584]{2,1,0:T(8,128)(2,1)S(1)}, bf16[4,8,3584]{2,1,0:T(8,128)(2,1)S(1)}, u32[]{:S(2)}, u32[]{:S(2)}) collective-permute-start(bf16[4,8,3584]{2,1,0:T(8,128)(2,1)S(1)} %get-tuple-element.92), channel_id=1, source_target_pairs={{0,1},{1,0},{2,3},{3,2},{4,5},{5,4},{6,7},{7,6},{8,9},{9,8},{10,11... | collective-permute-start | bytes 688136 | tf_op jit(solution)/shard_map/ppermute | solution.py:511
  82.4 12.4 %collective-permute-start.13 = (bf16[4,8,3584]{2,1,0:T(8,128)(2,1)S(1)}, bf16[4,8,3584]{2,1,0:T(8,128)(2,1)S(1)}, u32[]{:S(2)}, u32[]{:S(2)}) collective-permute-start(bf16[4,8,3584]{2,1,0:T(8,128)(2,1)S(1)} %get-tuple-element.93), channel_id=1, source_target_pairs={{0,2},{1,3},{2,0},{3,1},{4,6},{5,7},{6,4},{7,5},{8,10},{9,11},{10,... | collective-permute-start | bytes 688136 | tf_op jit(solution)/shard_map/ppermute | solution.py:511
  83.9 10.9 %collective-permute-start.14 = (bf16[4,8,3584]{2,1,0:T(8,128)(2,1)S(1)}, bf16[4,8,3584]{2,1,0:T(8,128)(2,1)S(1)}, u32[]{:S(2)}, u32[]{:S(2)}) collective-permute-start(bf16[4,8,3584]{2,1,0:T(8,128)(2,1)S(1)} %get-tuple-element.94), channel_id=1, source_target_pairs={{0,3},{1,2},{2,1},{3,0},{4,7},{5,6},{6,5},{7,4},{8,11},{9,10},{10,... | collective-permute-start | bytes 688136 | tf_op jit(solution)/shard_map/ppermute | solution.py:511
  94.9 12.2 %copy-start.1 = (f32[2,4,117,128]{3,2,1,0:T(8,128)S(1)}, f32[2,4,117,128]{3,2,1,0:T(8,128)}, u32[]{:S(2)}) copy-start(f32[2,4,117,128]{3,2,1,0:T(8,128)} %get-tuple-element.58) | copy-start | bytes 1437700
  95.0 5.3 %collective-permute-start.15 = (bf16[8,6656]{1,0:T(8,128)(2,1)S(1)}, bf16[8,6656]{1,0:T(8,128)(2,1)S(1)}, u32[]{:S(2)}, u32[]{:S(2)}) collective-permute-start(bf16[8,6656]{1,0:T(8,128)(2,1)S(1)} %get-tuple-element.80), channel_id=1, source_target_pairs={{0,4},{1,5},{2,6},{3,7},{4,0},{5,1},{6,2},{7,3},{8,12},{9,13},{10,... | collective-permute-start | bytes 319496 | tf_op jit(solution)/shard_map/ppermute | solution.py:511
  95.5 10.8 %collective-permute-start.16 = (bf16[8,6656]{1,0:T(8,128)(2,1)S(1)}, bf16[8,6656]{1,0:T(8,128)(2,1)S(1)}, u32[]{:S(2)}, u32[]{:S(2)}) collective-permute-start(bf16[8,6656]{1,0:T(8,128)(2,1)S(1)} %get-tuple-element.81), channel_id=1, source_target_pairs={{0,8},{1,9},{2,10},{3,11},{4,12},{5,13},{6,14},{7,15},{8,0},{9,1},... | collective-permute-start | bytes 319496 | tf_op jit(solution)/shard_map/ppermute | solution.py:511
  97.6 8.7 %collective-permute-start.17 = (bf16[8,6656]{1,0:T(8,128)(2,1)S(1)}, bf16[8,6656]{1,0:T(8,128)(2,1)S(1)}, u32[]{:S(2)}, u32[]{:S(2)}) collective-permute-start(bf16[8,6656]{1,0:T(8,128)(2,1)S(1)} %get-tuple-element.82), channel_id=1, source_target_pairs={{0,12},{1,13},{2,14},{3,15},{4,8},{5,9},{6,10},{7,11},{8,4},{9,5},... | collective-permute-start | bytes 319496 | tf_op jit(solution)/shard_map/ppermute | solution.py:511
  106.3 1.6 %copy-start = (f32[8,4096]{1,0:T(8,128)}, f32[8,4096]{1,0:T(8,128)S(1)}, u32[]{:S(2)}) copy-start(f32[8,4096]{1,0:T(8,128)S(1)} %add_add_fusion.small_mine) | copy-start | bytes 393220
  106.3 1.6 %collective-permute-start.19 = (f32[8,4096]{1,0:T(8,128)S(1)}, f32[8,4096]{1,0:T(8,128)S(1)}, u32[]{:S(2)}, u32[]{:S(2)}) collective-permute-start(f32[8,4096]{1,0:T(8,128)S(1)} %add_add_fusion.small_mine), channel_id=1, source_target_pairs={{0,16},{16,0},{1,17},{17,1},{2,18},{18,2},{3,19},{19,3},{4,20},{20... | collective-permute-start | bytes 393224 | tf_op jit(solution)/shard_map/ppermute | solution.py:507
  106.4 1.5 %copy-start.2 = (f32[8,2560]{1,0:T(8,128)}, f32[8,2560]{1,0:T(8,128)S(1)}, u32[]{:S(2)}) copy-start(f32[8,2560]{1,0:T(8,128)S(1)} %fusion.2.big_mine) | copy-start | bytes 245764
  106.5 1.5 %collective-permute-start.18 = (f32[8,2560]{1,0:T(8,128)S(1)}, f32[8,2560]{1,0:T(8,128)S(1)}, u32[]{:S(2)}, u32[]{:S(2)}) collective-permute-start(f32[8,2560]{1,0:T(8,128)S(1)} %fusion.2.big_mine), channel_id=1, source_target_pairs={{0,16},{16,0},{1,17},{17,1},{2,18},{18,2},{3,19},{19,3},{4,20},{20... | collective-permute-start | bytes 245768 | tf_op jit(solution)/shard_map/ppermute | solution.py:507
  107.9 0.6 copy-start.5
  108.6 0.6 copy-start.4

commit v9 on v8

--- a/solution.py
+++ b/solution.py
@@ -70,11 +70,20 @@
             turned_ref[2, 2 * b + v // 2, :, lanes] = adj_ref[b, v].T
 
 
+def leave_kernel(last_ref, gradient_ref, out_ref, pgrad_ref, tok_ref):
+    for b in range(2):
+        for v in range(4):
+            lanes = slice(128 * (v % 2), 128 * (v % 2) + 128)
+            out_ref[b, v] = last_ref[2 * b + v // 2, :, lanes].T
+            tok_ref[4 * b + v] = gradient_ref[2 * b + v // 2, :, lanes].T
+            pgrad_ref[b, v] = tok_ref[4 * b + v, 10:127, :]
+
+
 def tower_kernel(
     split,
     ids_ref, counts_ref, wmine0_ref, wmine1_ref, wmine2_ref, wmine3_ref, wother0_ref, wother1_ref, wother2_ref, wother3_ref,
     tok_ref, gains_ref, scales_ref, turned_ref,
-    out_ref, pgrad_ref, bigmine_ref, bigother_ref, smallmine_ref, smallother_ref,
+    last_ref, gradient_ref, bigmine_ref, bigother_ref, smallmine_ref, smallother_ref,
     stage_ref, w_ref, wd_ref, wt_ref, wdt_ref, colb_ref, tokscr_ref, h_ref, g_ref, xh_ref, inv_ref,
     qkvt_ref, pb_ref, ot_ref, qkvv_ref, pv_ref, ov_ref, pw_ref, qbd_ref, dob_ref, hid_ref, du_ref, dqkv_ref,
     dov_ref, ga_ref, gd_ref, gt_ref, gacc_ref, gbig_ref, pacc_ref, spread_ref, act_ref, slope_ref, gdt_ref, both_ref,
@@ -354,10 +363,7 @@
         return carry
 
     lax.fori_loop(0, layers, forward_layer, 0)
-    for b in range(items):
-        for v in range(4):
-            lanes = slice(128 * (v % 2), 128 * (v % 2) + 128)
-            out_ref[b, v] = h_ref[2 * b + v // 2, :, lanes].T.astype(BF)
+    last_ref[...] = h_ref[...].astype(BF)
 
     gacc_ref[...] = jnp.zeros_like(gacc_ref)
     gt_ref[...] = jnp.zeros_like(gt_ref)
@@ -391,21 +397,13 @@
 
     lax.fori_loop(0, layers, backward_layer, 0)
 
+    gradient_ref[...] = g_ref[0]
     for x in range(2):
-        cls_sum = None
         for b in range(items):
-            prompt_sum = None
-            for v in range(4):
-                lanes = slice(128 * (v % 2), 128 * (v % 2) + 128)
-                tokscr_ref[4 * b + v] = g_ref[x, 2 * b + v // 2, :, lanes].T
-                head = tokscr_ref[4 * b + v, 0:10, :]
-                last = tokscr_ref[4 * b + v, 127:128, :]
-                prompt_sum = head if prompt_sum is None else prompt_sum + head
-                cls_sum = last if cls_sum is None else cls_sum + last
-                if x == 0:
-                    pgrad_ref[b, v] = tokscr_ref[4 * b + v, 10:127, :]
-            pacc_ref[x, ids_ref[b], 0:10, :] += prompt_sum
-        pacc_ref[x, 0, 12:13, :] = cls_sum
+            slots = g_ref[x, 2 * b] + g_ref[x, 2 * b + 1]
+            tokscr_ref[2 * x + b] = (slots[:, :128] + slots[:, 128:]).T
+            pacc_ref[x, ids_ref[b], 0:10, :] += tokscr_ref[2 * x + b, 0:10, :]
+        pacc_ref[x, 0, 12:13, :] = tokscr_ref[2 * x, 127:128, :] + tokscr_ref[2 * x + 1, 127:128, :]
 
     for big_ref, small_ref, c in ((bigmine_ref, smallmine_ref, dp), (bigother_ref, smallother_ref, 1 - dp)):
         for rel in range(SHARDS):
@@ -442,7 +440,7 @@
     return call(
         functools.partial(tower_kernel, split),
         "tower",
-        [shape_of((2, 4, 128, 128), BF), shape_of((2, 4, 117, 128))] + half,
+        [shape_of((4, 128, 256), BF), shape_of((4, 128, 256))] + half,
         "ss" + "v" * 12,
         [
             pltpu.VMEM((2, 128, COLS), F32),
@@ -550,22 +548,33 @@
     return (first.astype(F32) + rest[0].astype(F32)) + (rest[1].astype(F32) + rest[2].astype(F32))
 
 
-def reduce_all(big_mine, big_other, small_mine, small_other):
+def leave(last, gradient):
+    return call(
+        leave_kernel, "leave", [shape_of((2, 4, 128, 128), BF), shape_of((2, 4, 117, 128))], "vv", [pltpu.VMEM((8, 128, 128), F32)],
+        last, gradient, cost=pl.CostEstimate(flops=10**6, bytes_accessed=16 * 10**6, transcendentals=0),
+    )
+
+
+def reduce_all(big_mine, big_other, small_mine, small_other, last, gradient):
     big = (big_mine.astype(F32) + flip(big_other, "dp", 0, 2).astype(F32)).astype(BF)
     small = (small_mine + flip(small_other, "dp", 0, 2)).astype(BF)
+    big, small, last, gradient = lax.optimization_barrier((big, small, last, gradient))
+    local = leave(last, gradient)
     got = [swap(jnp.concatenate([big[xy], small], axis=2), xy) for xy in range(1, 4)]
     big = four(big[0], [part[:, :, :COLS] for part in got]).astype(BF)
     small = four(small, [part[:, :, COLS:] for part in got]).astype(BF)
     small = jnp.concatenate([small[at] for at in range(4)], axis=1)
+    big, small, local = lax.optimization_barrier((big, small, local))
     got = [swap(jnp.concatenate([big[z], small], axis=1), 4 * z) for z in range(1, 4)]
     big = four(big[0], [part[:, :COLS] for part in got])
     small = four(small, [part[:, COLS:] for part in got])
-    return call(
+    reduced = call(
         final_kernel, "final",
         [shape_of((2, 2, 8, 384)), shape_of((2, 2, 8, 128)), shape_of((2, 8, 1024)), shape_of((2, 32, 128)), shape_of((2, 128, 128)),
          shape_of((2, 4, 128)), shape_of((2, 4, 128)), shape_of((10, 8, 128)), shape_of((1, 128)), shape_of((10, 8, 128)), shape_of((1, 128))],
         "vvvv", [], big, flip(big, "dp", 0, 2), small, flip(small, "dp", 0, 2),
     )
+    return local, reduced
 
 
 def per_device(shard_count, patches, prompts, cls_token, attn_in, attn_out, feed_in, feed_out, token_operator,
@@ -589,14 +598,16 @@
         )
         rows = rows.reshape(2, SHARDS, 8, COLS).transpose(1, 0, 2, 3)
         gathered = [rows[:, l].reshape(4, 4, 8, COLS)[:, xy] for l in range(2) for xy in range(4)]
-    output, patch_grad, *sums = run_tower(
+    last, gradient, *sums = run_tower(
         fast, dataset_ids, var_counts, *gathered, token_operator, norm_gains, branch_scales, turned
     )
     if fast:
+        (output, patch_grad), reduced = reduce_all(*sums, last, gradient)
         (attn_in_g, attn_out_g, feed_in_g, feed_out_g, token_g, gains_g, scales_g, prompt_g, cls_g, adjust_prompt_g,
-         adjust_cls_g) = reduce_all(*sums)
+         adjust_cls_g) = reduced
         return (output, patch_grad, prompt_g.transpose(1, 0, 2), cls_g[0], attn_in_g, attn_out_g, feed_in_g, feed_out_g, token_g, gains_g,
                 scales_g, adjust_prompt_g.transpose(1, 0, 2), adjust_cls_g[0])
+    output, patch_grad = leave(last, gradient)
     rows = jnp.stack(sums[:2]).transpose(0, 2, 1, 3, 4).astype(F32).reshape(2, 128, COLS)
     attn_in_g, attn_out_g, feed_in_g, feed_out_g = unpack_rows(rows)
     feed_out_g = feed_out_g.reshape(2, 4, SHARDS, 8, 128).transpose(0, 2, 1, 3, 4).reshape(2, 512, 128)

time: 112 us -> 111 us (level)
  waiting for transfers between devices: 25 us -> 22.6 us
  Pallas kernels: 56.3 us -> 58.5 us
    ppermute x12, waiting for transfers between devices: 21.8 us -> 19.5 us  [swap(): return lax.ppermute(array, 'fsdp', [(i, i ^ mask) for i in range(SHARDS)])]
    pallas_call x4 -> x5, Pallas kernels: 56.3 us -> 58.5 us  [call(): pl.pallas_call(kernel, out_shape=out_shape, in_specs=[pl.BlockSpec(memory...]
    unnamed x33 -> x29, local copies, waits for them, and re-layouts: 6.31 us -> 6.27 us
  transfers between devices with their start and end apart: 20 -> 20, of which waited for: 12 -> 12; matrix products, arithmetic and copies ran while one was open for 4% -> 4% of each run, Pallas kernels for 2% -> 4%
where the time goes in v9:
time: 111 us
  Pallas kernels  58.5 us (53%)
  waiting for transfers between devices  22.6 us (20%)
  starting transfers between devices  19.4 us (17%)
  local copies, waits for them, and re-layouts  6.32 us (6%)
  other arithmetic  3.23 us (3%)
    pallas_call x5, Pallas kernels, call(): pl.pallas_call(kernel, out_shape=out_shape, in_specs=[pl.BlockSpec(memory...  58.5 us
    ppermute x12, waiting for transfers between devices, swap(): return lax.ppermute(array, 'fsdp', [(i, i ^ mask) for i in range(SHARDS)])  19.5 us
    ppermute x12, starting transfers between devices, swap(): return lax.ppermute(array, 'fsdp', [(i, i ^ mask) for i in range(SHARDS)])  17.2 us
    unnamed x29, local copies, waits for them, and re-layouts  6.27 us
    ppermute x8, waiting for transfers between devices, flip(): return lax.ppermute(array, axis, [(i, i ^ 1 << bit) for i in range(size)])  3.12 us
  transfers between devices with their start and end apart: 20, of which 12 were waited for; matrix products, arithmetic and copies ran while one was open for 4% of the time, Pallas kernels for 4%

profile of v9, /device:TPU:0, one launch (start us, length us, event | category | flops | bytes accessed | tf_op | source)
XLA Modules:
  0.0 111.0 jit_solution(412549403343220923)
XLA Ops:
  0.6 1.4 %pack.1 = bf16[1,8,2560]{2,1,0:T(8,128)(2,1)} custom-call(bf16[2,2,8,384]{3,2,1,0:T(8,128)(2,1)} %attn_in_ref.1, bf16[2,2,8,128]{3,2,1,0:T(8,128)(2,1)} %attn_out_ref.1, bf16[2,8,1024]{2,1,0:T(8,128)(2,1)} %feed_in_ref.1, bf16[2,32,128]{2,1,0:T(8,128)(2,1)} %feed_out_ref.1), custom_call_target="tpu_custom_call" | custom-call | tf_op jit(solution)/shard_map/pack/pallas_call | solution.py:422
  2.1 5.0 %collective-permute-start.2 = (bf16[1,8,2560]{2,1,0:T(8,128)(2,1)}, bf16[1,8,2560]{2,1,0:T(8,128)(2,1)S(1)}, u32[]{:S(2)}, u32[]{:S(2)}) collective-permute-start(bf16[1,8,2560]{2,1,0:T(8,128)(2,1)} %pack.1), channel_id=1, source_target_pairs={{0,12},{1,13},{2,14},{3,15},{4,8},{5,9},{6,10},{7,11},{8,4},{9,5},... | collective-permute-start | bytes 122888 | tf_op jit(solution)/shard_map/ppermute | solution.py:509
  7.1 0.6 collective-permute-start
  7.7 1.6 %collective-permute-done.2 = bf16[1,8,2560]{2,1,0:T(8,128)(2,1)S(1)} collective-permute-done((bf16[1,8,2560]{2,1,0:T(8,128)(2,1)}, bf16[1,8,2560]{2,1,0:T(8,128)(2,1)S(1)}, u32[]{:S(2)}, u32[]{:S(2)}) %collective-permute-start.2) | collective-permute-done | bytes 40992 | tf_op jit(solution)/shard_map/ppermute | solution.py:509
  9.3 2.9 %collective-permute-done.1 = bf16[1,8,2560]{2,1,0:T(8,128)(2,1)S(1)} collective-permute-done((bf16[1,8,2560]{2,1,0:T(8,128)(2,1)}, bf16[1,8,2560]{2,1,0:T(8,128)(2,1)S(1)}, u32[]{:S(2)}, u32[]{:S(2)}) %collective-permute-start.1) | collective-permute-done | bytes 40992 | tf_op jit(solution)/shard_map/ppermute | solution.py:509
  12.2 0.8 pad_maximum_fusion.3.wmine0_ref
  13.0 2.5 %collective-permute-start.5 = (bf16[4,8,2560]{2,1,0:T(8,128)(2,1)S(1)}, bf16[4,8,2560]{2,1,0:T(8,128)(2,1)S(1)}, u32[]{:S(2)}, u32[]{:S(2)}) collective-permute-start(bf16[4,8,2560]{2,1,0:T(8,128)(2,1)S(1)} %pad_maximum_fusion.3.wmine0_ref), channel_id=1, source_target_pairs={{0,3},{1,2},{2,1},{3,0},{4,7},{5,6},{6,5},{7,4},{8,11},{9,10},{10,... | collective-permute-start | bytes 491528 | tf_op jit(solution)/shard_map/ppermute | solution.py:509
  15.6 0.5 collective-permute-start.4
  16.1 0.5 collective-permute-start.3
  16.6 1.3 %copy.28.prompts_ref = bf16[8,10,128]{2,1,0:T(8,128)(2,1)} copy(bf16[8,10,128]{2,0,1:T(8,128)(2,1)} %param.15) | data formatting | bytes 40960 | tf_op args[1]
  17.9 1.7 %copy.27.patches_ref = bf16[2,4,117,128]{3,2,1,0:T(8,128)(2,1)} copy(bf16[2,4,117,128]{3,1,2,0:T(4,128)(2,1)} %param.14) | data formatting | bytes 479232 | tf_op args[0]
  19.6 2.4 %prepare.1.turned_ref = bf16[3,4,128,256]{3,2,1,0:T(8,128)(2,1)} custom-call(s32[2]{0:T(128)} %ids_ref.3, bf16[2,4,117,128]{3,2,1,0:T(8,128)(2,1)} %copy.27.patches_ref, bf16[8,10,128]{2,1,0:T(8,128)(2,1)} %copy.28.prompts_ref, bf16[1,128]{1,0:T(2,128)(2,1)} %bitcast.31, bf16[2,4,128,128]{3,2,1,0:T(8,128)(2,1)} %cot_ref.1, bf16[2,4,128,128]{3,2,1,0:T(8,128)(2,1)} %adj_ref.1), custom_call_target="tpu_custom_call" | custom-call | flops 1000000 | bytes 8000000 | tf_op jit(solution)/shard_map/prepare/pallas_call | solution.py:422
  22.0 0.1 collective-permute-done.3.wmine1_ref
  22.1 0.0 collective-permute-start.6
  22.1 0.5 collective-permute-start.7
  22.6 0.1 collective-permute-start.8
  22.7 0.4 collective-permute-start.9
  23.1 0.4 collective-permute-done.6.wother0_ref
  23.5 0.2 collective-permute-done.7.wother1_ref
  23.8 0.3 collective-permute-done.8.wother2_ref
  24.0 0.2 collective-permute-done.9.wother3_ref
  24.3 0.1 copy-done.10
  24.4 0.3 copy-done.11
  24.7 0.6 copy-done.12
  25.3 50.5 %tower.1 = (bf16[4,128,256]{2,1,0:T(8,128)(2,1)}, f32[4,128,256]{2,1,0:T(8,128)}, bf16[4,4,8,2560]{3,2,1,0:T(8,128)(2,1)}, bf16[4,4,8,2560]{3,2,1,0:T(8,128)(2,1...) custom-call(s32[2]{0:T(128)} %ids_ref.3, s32[8]{0:T(128)} %counts_ref.1, bf16[4,8,2560]{2,1,0:T(8,128)(2,1)} %copy-done.3, ...), custom_call_target="tpu_custom_call" | custom-call | flops 10000000000 | bytes 20000000 | tf_op jit(solution)/shard_map/tower/pallas_call | solution.py:422
  75.9 0.2 collective-permute-start.10
  76.1 0.3 collective-permute-start.11
  76.4 2.0 %collective-permute-done.11 = f32[4,8,1024]{2,1,0:T(8,128)S(1)} collective-permute-done((f32[4,8,1024]{2,1,0:T(8,128)}, f32[4,8,1024]{2,1,0:T(8,128)S(1)}, u32[]{:S(2)}, u32[]{:S(2)}) %collective-permute-start.11) | collective-permute-done | bytes 131104 | tf_op jit(solution)/shard_map/ppermute | solution.py:505
  78.3 0.9 add_convert_fusion.2
  79.3 1.2 %add_convert_fusion = bf16[4,4,8,2560]{3,2,1,0:T(8,128)(2,1)S(1)} fusion(bf16[4,4,8,2560]{3,2,1,0:T(8,128)(2,1)S(1)} %collective-permute-done.10, bf16[4,4,8,2560]{3,2,1,0:T(8,128)(2,1)} %get-tuple-element.50), kind=kLoop, calls=%fused_computation | loop fusion | flops 1310720 | bytes 1966080 | tf_op jit(solution)/shard_map/convert_element_type | solution.py:559
  80.6 1.6 %collective-permute-start.12 = (bf16[4,8,3584]{2,1,0:T(8,128)(2,1)S(1)}, bf16[4,8,3584]{2,1,0:T(8,128)(2,1)S(1)}, u32[]{:S(2)}, u32[]{:S(2)}) collective-permute-start(bf16[4,8,3584]{2,1,0:T(8,128)(2,1)S(1)} %get-tuple-element.103), channel_id=1, source_target_pairs={{0,1},{1,0},{2,3},{3,2},{4,5},{5,4},{6,7},{7,6},{8,9},{9,8},{10,11... | collective-permute-start | bytes 688136 | tf_op jit(solution)/shard_map/ppermute | solution.py:509
  82.2 1.5 %collective-permute-start.13 = (bf16[4,8,3584]{2,1,0:T(8,128)(2,1)S(1)}, bf16[4,8,3584]{2,1,0:T(8,128)(2,1)S(1)}, u32[]{:S(2)}, u32[]{:S(2)}) collective-permute-start(bf16[4,8,3584]{2,1,0:T(8,128)(2,1)S(1)} %get-tuple-element.104), channel_id=1, source_target_pairs={{0,2},{1,3},{2,0},{3,1},{4,6},{5,7},{6,4},{7,5},{8,10},{9,11},{10,... | collective-permute-start | bytes 688136 | tf_op jit(solution)/shard_map/ppermute | solution.py:509
  83.7 0.5 collective-permute-start.14
  84.2 2.4 %leave.1 = (bf16[2,4,128,128]{3,2,1,0:T(8,128)(2,1)}, f32[2,4,117,128]{3,2,1,0:T(8,128)}) custom-call(bf16[4,128,256]{2,1,0:T(8,128)(2,1)} %get-tuple-element.58.last_ref, f32[4,128,256]{2,1,0:T(8,128)} %get-tuple-element.59.gradient_ref), custom_call_target="tpu_custom_call" | custom-call | flops 1000000 | bytes 16000000 | tf_op jit(solution)/shard_map/leave/pallas_call | solution.py:422
  86.6 2.6 %collective-permute-done.12 = bf16[4,8,3584]{2,1,0:T(8,128)(2,1)S(1)} collective-permute-done((bf16[4,8,3584]{2,1,0:T(8,128)(2,1)S(1)}, bf16[4,8,3584]{2,1,0:T(8,128)(2,1)S(1)}, u32[]{:S(2)}, u32[]{:S(2)}) %collective-permute-start.12) | collective-permute-done | bytes 229408 | tf_op jit(solution)/shard_map/ppermute | solution.py:509
  89.1 5.4 %collective-permute-done.13 = bf16[4,8,3584]{2,1,0:T(8,128)(2,1)S(1)} collective-permute-done((bf16[4,8,3584]{2,1,0:T(8,128)(2,1)S(1)}, bf16[4,8,3584]{2,1,0:T(8,128)(2,1)S(1)}, u32[]{:S(2)}, u32[]{:S(2)}) %collective-permute-start.13) | collective-permute-done | bytes 229408 | tf_op jit(solution)/shard_map/ppermute | solution.py:509
  94.6 0.1 fusion.1
  94.8 0.5 collective-permute-start.15
  95.3 2.1 %collective-permute-start.16 = (bf16[8,6656]{1,0:T(8,128)(2,1)S(1)}, bf16[8,6656]{1,0:T(8,128)(2,1)S(1)}, u32[]{:S(2)}, u32[]{:S(2)}) collective-permute-start(bf16[8,6656]{1,0:T(8,128)(2,1)S(1)} %get-tuple-element.97), channel_id=1, source_target_pairs={{0,8},{1,9},{2,10},{3,11},{4,12},{5,13},{6,14},{7,15},{8,0},{9,1},... | collective-permute-start | bytes 319496 | tf_op jit(solution)/shard_map/ppermute | solution.py:509
  97.4 1.9 %collective-permute-start.17 = (bf16[8,6656]{1,0:T(8,128)(2,1)S(1)}, bf16[8,6656]{1,0:T(8,128)(2,1)S(1)}, u32[]{:S(2)}, u32[]{:S(2)}) collective-permute-start(bf16[8,6656]{1,0:T(8,128)(2,1)S(1)} %get-tuple-element.98), channel_id=1, source_target_pairs={{0,12},{1,13},{2,14},{3,15},{4,8},{5,9},{6,10},{7,11},{8,4},{9,5},... | collective-permute-start | bytes 319496 | tf_op jit(solution)/shard_map/ppermute | solution.py:509
  99.2 0.8 collective-permute-done.15
  100.1 6.0 %collective-permute-done.16 = bf16[8,6656]{1,0:T(8,128)(2,1)S(1)} collective-permute-done((bf16[8,6656]{1,0:T(8,128)(2,1)S(1)}, bf16[8,6656]{1,0:T(8,128)(2,1)S(1)}, u32[]{:S(2)}, u32[]{:S(2)}) %collective-permute-start.16) | collective-permute-done | bytes 106528 | tf_op jit(solution)/shard_map/ppermute | solution.py:509
  106.1 0.1 collective-permute-start.19
  106.3 0.6 collective-permute-start.18
  106.8 0.9 copy.29
  107.8 0.6 copy-done.5
  108.4 0.7 copy-done.4
  109.0 1.8 %final.1 = (f32[2,2,8,384]{3,2,1,0:T(8,128)}, f32[2,2,8,128]{3,2,1,0:T(8,128)}, f32[2,8,1024]{2,1,0:T(8,128)}, f32[2,32,128]{2,1,0:T(8,128)}, f32[2,128,128]{2,1...) custom-call(f32[8,2560]{1,0:T(8,128)} %copy-done.2, ...), custom_call_target="tpu_custom_call" | custom-call | tf_op jit(solution)/shard_map/final/pallas_call | solution.py:422
  (39 shorter events, 0.3 us)
Async XLA Ops:
  2.1 7.3 %collective-permute-start.2 = (bf16[1,8,2560]{2,1,0:T(8,128)(2,1)}, bf16[1,8,2560]{2,1,0:T(8,128)(2,1)S(1)}, u32[]{:S(2)}, u32[]{:S(2)}) collective-permute-start(bf16[1,8,2560]{2,1,0:T(8,128)(2,1)} %pack.1), channel_id=1, source_target_pairs={{0,12},{1,13},{2,14},{3,15},{4,8},{5,9},{6,10},{7,11},{8,4},{9,5},... | collective-permute-start | bytes 122888 | tf_op jit(solution)/shard_map/ppermute | solution.py:509
  7.1 5.1 %collective-permute-start.1 = (bf16[1,8,2560]{2,1,0:T(8,128)(2,1)}, bf16[1,8,2560]{2,1,0:T(8,128)(2,1)S(1)}, u32[]{:S(2)}, u32[]{:S(2)}) collective-permute-start(bf16[1,8,2560]{2,1,0:T(8,128)(2,1)} %pack.1), channel_id=1, source_target_pairs={{0,8},{1,9},{2,10},{3,11},{4,12},{5,13},{6,14},{7,15},{8,0},{9,1},... | collective-permute-start | bytes 122888 | tf_op jit(solution)/shard_map/ppermute | solution.py:509
  7.1 5.1 %collective-permute-start = (bf16[1,8,2560]{2,1,0:T(8,128)(2,1)}, bf16[1,8,2560]{2,1,0:T(8,128)(2,1)S(1)}, u32[]{:S(2)}, u32[]{:S(2)}) collective-permute-start(bf16[1,8,2560]{2,1,0:T(8,128)(2,1)} %pack.1), channel_id=1, source_target_pairs={{0,4},{1,5},{2,6},{3,7},{4,0},{5,1},{6,2},{7,3},{8,12},{9,13},{10,... | collective-permute-start | bytes 122888 | tf_op jit(solution)/shard_map/ppermute | solution.py:509
  13.0 9.1 %copy-start.3 = (bf16[4,8,2560]{2,1,0:T(8,128)(2,1)}, bf16[4,8,2560]{2,1,0:T(8,128)(2,1)S(1)}, u32[]{:S(2)}) copy-start(bf16[4,8,2560]{2,1,0:T(8,128)(2,1)S(1)} %pad_maximum_fusion.3.wmine0_ref) | copy-start | bytes 491524
  13.0 9.0 %collective-permute-start.5 = (bf16[4,8,2560]{2,1,0:T(8,128)(2,1)S(1)}, bf16[4,8,2560]{2,1,0:T(8,128)(2,1)S(1)}, u32[]{:S(2)}, u32[]{:S(2)}) collective-permute-start(bf16[4,8,2560]{2,1,0:T(8,128)(2,1)S(1)} %pad_maximum_fusion.3.wmine0_ref), channel_id=1, source_target_pairs={{0,3},{1,2},{2,1},{3,0},{4,7},{5,6},{6,5},{7,4},{8,11},{9,10},{10,... | collective-permute-start | bytes 491528 | tf_op jit(solution)/shard_map/ppermute | solution.py:509
  15.6 6.5 %collective-permute-start.4 = (bf16[4,8,2560]{2,1,0:T(8,128)(2,1)S(1)}, bf16[4,8,2560]{2,1,0:T(8,128)(2,1)S(1)}, u32[]{:S(2)}, u32[]{:S(2)}) collective-permute-start(bf16[4,8,2560]{2,1,0:T(8,128)(2,1)S(1)} %pad_maximum_fusion.3.wmine0_ref), channel_id=1, source_target_pairs={{0,2},{1,3},{2,0},{3,1},{4,6},{5,7},{6,4},{7,5},{8,10},{9,11},{10,... | collective-permute-start | bytes 491528 | tf_op jit(solution)/shard_map/ppermute | solution.py:509
  16.1 6.0 %collective-permute-start.3 = (bf16[4,8,2560]{2,1,0:T(8,128)(2,1)S(1)}, bf16[4,8,2560]{2,1,0:T(8,128)(2,1)S(1)}, u32[]{:S(2)}, u32[]{:S(2)}) collective-permute-start(bf16[4,8,2560]{2,1,0:T(8,128)(2,1)S(1)} %pad_maximum_fusion.3.wmine0_ref), channel_id=1, source_target_pairs={{0,1},{1,0},{2,3},{3,2},{4,5},{5,4},{6,7},{7,6},{8,9},{9,8},{10,11... | collective-permute-start | bytes 491528 | tf_op jit(solution)/shard_map/ppermute | solution.py:509
  22.0 2.3 %copy-start.6 = (bf16[4,8,2560]{2,1,0:T(8,128)(2,1)}, bf16[4,8,2560]{2,1,0:T(8,128)(2,1)S(1)}, u32[]{:S(2)}) copy-start(bf16[4,8,2560]{2,1,0:T(8,128)(2,1)S(1)} %collective-permute-done.5.wmine3_ref) | copy-start | bytes 491524
  22.0 2.2 %copy-start.7 = (bf16[4,8,2560]{2,1,0:T(8,128)(2,1)}, bf16[4,8,2560]{2,1,0:T(8,128)(2,1)S(1)}, u32[]{:S(2)}) copy-start(bf16[4,8,2560]{2,1,0:T(8,128)(2,1)S(1)} %collective-permute-done.4.wmine2_ref) | copy-start | bytes 491524
  22.1 2.2 %copy-start.8 = (bf16[4,8,2560]{2,1,0:T(8,128)(2,1)}, bf16[4,8,2560]{2,1,0:T(8,128)(2,1)S(1)}, u32[]{:S(2)}) copy-start(bf16[4,8,2560]{2,1,0:T(8,128)(2,1)S(1)} %collective-permute-done.3.wmine1_ref) | copy-start | bytes 491524
  22.1 1.4 %collective-permute-start.6 = (bf16[4,8,2560]{2,1,0:T(8,128)(2,1)S(1)}, bf16[4,8,2560]{2,1,0:T(8,128)(2,1)S(1)}, u32[]{:S(2)}, u32[]{:S(2)}) collective-permute-start(bf16[4,8,2560]{2,1,0:T(8,128)(2,1)S(1)} %pad_maximum_fusion.3.wmine0_ref), channel_id=1, source_target_pairs={{0,16},{16,0},{1,17},{17,1},{2,18},{18,2},{3,19},{19,3},{4,20},{20... | collective-permute-start | bytes 491528 | tf_op jit(solution)/shard_map/ppermute | solution.py:505
  22.1 1.6 %collective-permute-start.7 = (bf16[4,8,2560]{2,1,0:T(8,128)(2,1)S(1)}, bf16[4,8,2560]{2,1,0:T(8,128)(2,1)S(1)}, u32[]{:S(2)}, u32[]{:S(2)}) collective-permute-start(bf16[4,8,2560]{2,1,0:T(8,128)(2,1)S(1)} %collective-permute-done.3.wmine1_ref), channel_id=1, source_target_pairs={{0,16},{16,0},{1,17},{17,1},{2,18},{18,2},{3,19},{19,3},{4,20},{20... | collective-permute-start | bytes 491528 | tf_op jit(solution)/shard_map/ppermute | solution.py:505
  22.6 1.4 %collective-permute-start.8 = (bf16[4,8,2560]{2,1,0:T(8,128)(2,1)S(1)}, bf16[4,8,2560]{2,1,0:T(8,128)(2,1)S(1)}, u32[]{:S(2)}, u32[]{:S(2)}) collective-permute-start(bf16[4,8,2560]{2,1,0:T(8,128)(2,1)S(1)} %collective-permute-done.4.wmine2_ref), channel_id=1, source_target_pairs={{0,16},{16,0},{1,17},{17,1},{2,18},{18,2},{3,19},{19,3},{4,20},{20... | collective-permute-start | bytes 491528 | tf_op jit(solution)/shard_map/ppermute | solution.py:505
  22.7 1.6 %collective-permute-start.9 = (bf16[4,8,2560]{2,1,0:T(8,128)(2,1)S(1)}, bf16[4,8,2560]{2,1,0:T(8,128)(2,1)S(1)}, u32[]{:S(2)}, u32[]{:S(2)}) collective-permute-start(bf16[4,8,2560]{2,1,0:T(8,128)(2,1)S(1)} %collective-permute-done.5.wmine3_ref), channel_id=1, source_target_pairs={{0,16},{16,0},{1,17},{17,1},{2,18},{18,2},{3,19},{19,3},{4,20},{20... | collective-permute-start | bytes 491528 | tf_op jit(solution)/shard_map/ppermute | solution.py:505
  23.5 0.8 copy-start.9
  23.8 0.7 copy-start.10
  24.0 0.7 copy-start.11
  24.7 0.7 copy-start.12
  75.9 3.4 %collective-permute-start.10 = (bf16[4,4,8,2560]{3,2,1,0:T(8,128)(2,1)}, bf16[4,4,8,2560]{3,2,1,0:T(8,128)(2,1)S(1)}, u32[]{:S(2)}, u32[]{:S(2)}) collective-permute-start(bf16[4,4,8,2560]{3,2,1,0:T(8,128)(2,1)} %get-tuple-element.51), channel_id=1, source_target_pairs={{0,16},{16,0},{1,17},{17,1},{2,18},{18,2},{3,19},{19,3},{4,20},{20... | collective-permute-start | bytes 1966088 | tf_op jit(solution)/shard_map/ppermute | solution.py:505
  76.1 2.3 %collective-permute-start.11 = (f32[4,8,1024]{2,1,0:T(8,128)}, f32[4,8,1024]{2,1,0:T(8,128)S(1)}, u32[]{:S(2)}, u32[]{:S(2)}) collective-permute-start(f32[4,8,1024]{2,1,0:T(8,128)} %get-tuple-element.53), channel_id=1, source_target_pairs={{0,16},{16,0},{1,17},{17,1},{2,18},{18,2},{3,19},{19,3},{4,20},{20... | collective-permute-start | bytes 393224 | tf_op jit(solution)/shard_map/ppermute | solution.py:505
  80.6 8.5 %collective-permute-start.12 = (bf16[4,8,3584]{2,1,0:T(8,128)(2,1)S(1)}, bf16[4,8,3584]{2,1,0:T(8,128)(2,1)S(1)}, u32[]{:S(2)}, u32[]{:S(2)}) collective-permute-start(bf16[4,8,3584]{2,1,0:T(8,128)(2,1)S(1)} %get-tuple-element.103), channel_id=1, source_target_pairs={{0,1},{1,0},{2,3},{3,2},{4,5},{5,4},{6,7},{7,6},{8,9},{9,8},{10,11... | collective-permute-start | bytes 688136 | tf_op jit(solution)/shard_map/ppermute | solution.py:509
  82.2 12.4 %collective-permute-start.13 = (bf16[4,8,3584]{2,1,0:T(8,128)(2,1)S(1)}, bf16[4,8,3584]{2,1,0:T(8,128)(2,1)S(1)}, u32[]{:S(2)}, u32[]{:S(2)}) collective-permute-start(bf16[4,8,3584]{2,1,0:T(8,128)(2,1)S(1)} %get-tuple-element.104), channel_id=1, source_target_pairs={{0,2},{1,3},{2,0},{3,1},{4,6},{5,7},{6,4},{7,5},{8,10},{9,11},{10,... | collective-permute-start | bytes 688136 | tf_op jit(solution)/shard_map/ppermute | solution.py:509
  83.7 10.9 %collective-permute-start.14 = (bf16[4,8,3584]{2,1,0:T(8,128)(2,1)S(1)}, bf16[4,8,3584]{2,1,0:T(8,128)(2,1)S(1)}, u32[]{:S(2)}, u32[]{:S(2)}) collective-permute-start(bf16[4,8,3584]{2,1,0:T(8,128)(2,1)S(1)} %get-tuple-element.105), channel_id=1, source_target_pairs={{0,3},{1,2},{2,1},{3,0},{4,7},{5,6},{6,5},{7,4},{8,11},{9,10},{10,... | collective-permute-start | bytes 688136 | tf_op jit(solution)/shard_map/ppermute | solution.py:509
  94.7 12.1 %copy-start.1 = (f32[2,4,117,128]{3,2,1,0:T(8,128)S(1)}, f32[2,4,117,128]{3,2,1,0:T(8,128)}, u32[]{:S(2)}) copy-start(f32[2,4,117,128]{3,2,1,0:T(8,128)} %get-tuple-element.78) | copy-start | bytes 1437700
  94.8 5.3 %collective-permute-start.15 = (bf16[8,6656]{1,0:T(8,128)(2,1)S(1)}, bf16[8,6656]{1,0:T(8,128)(2,1)S(1)}, u32[]{:S(2)}, u32[]{:S(2)}) collective-permute-start(bf16[8,6656]{1,0:T(8,128)(2,1)S(1)} %get-tuple-element.96), channel_id=1, source_target_pairs={{0,4},{1,5},{2,6},{3,7},{4,0},{5,1},{6,2},{7,3},{8,12},{9,13},{10,... | collective-permute-start | bytes 319496 | tf_op jit(solution)/shard_map/ppermute | solution.py:509
  95.3 10.8 %collective-permute-start.16 = (bf16[8,6656]{1,0:T(8,128)(2,1)S(1)}, bf16[8,6656]{1,0:T(8,128)(2,1)S(1)}, u32[]{:S(2)}, u32[]{:S(2)}) collective-permute-start(bf16[8,6656]{1,0:T(8,128)(2,1)S(1)} %get-tuple-element.97), channel_id=1, source_target_pairs={{0,8},{1,9},{2,10},{3,11},{4,12},{5,13},{6,14},{7,15},{8,0},{9,1},... | collective-permute-start | bytes 319496 | tf_op jit(solution)/shard_map/ppermute | solution.py:509
  97.4 8.7 %collective-permute-start.17 = (bf16[8,6656]{1,0:T(8,128)(2,1)S(1)}, bf16[8,6656]{1,0:T(8,128)(2,1)S(1)}, u32[]{:S(2)}, u32[]{:S(2)}) collective-permute-start(bf16[8,6656]{1,0:T(8,128)(2,1)S(1)} %get-tuple-element.98), channel_id=1, source_target_pairs={{0,12},{1,13},{2,14},{3,15},{4,8},{5,9},{6,10},{7,11},{8,4},{9,5},... | collective-permute-start | bytes 319496 | tf_op jit(solution)/shard_map/ppermute | solution.py:509
  106.1 1.6 %copy-start = (f32[8,4096]{1,0:T(8,128)}, f32[8,4096]{1,0:T(8,128)S(1)}, u32[]{:S(2)}) copy-start(f32[8,4096]{1,0:T(8,128)S(1)} %add_add_fusion.small_mine) | copy-start | bytes 393220
  106.1 1.6 %collective-permute-start.19 = (f32[8,4096]{1,0:T(8,128)S(1)}, f32[8,4096]{1,0:T(8,128)S(1)}, u32[]{:S(2)}, u32[]{:S(2)}) collective-permute-start(f32[8,4096]{1,0:T(8,128)S(1)} %add_add_fusion.small_mine), channel_id=1, source_target_pairs={{0,16},{16,0},{1,17},{17,1},{2,18},{18,2},{3,19},{19,3},{4,20},{20... | collective-permute-start | bytes 393224 | tf_op jit(solution)/shard_map/ppermute | solution.py:505
  106.3 1.5 %copy-start.2 = (f32[8,2560]{1,0:T(8,128)}, f32[8,2560]{1,0:T(8,128)S(1)}, u32[]{:S(2)}) copy-start(f32[8,2560]{1,0:T(8,128)S(1)} %fusion.2.big_mine) | copy-start | bytes 245764
  106.3 1.5 %collective-permute-start.18 = (f32[8,2560]{1,0:T(8,128)S(1)}, f32[8,2560]{1,0:T(8,128)S(1)}, u32[]{:S(2)}, u32[]{:S(2)}) collective-permute-start(f32[8,2560]{1,0:T(8,128)S(1)} %fusion.2.big_mine), channel_id=1, source_target_pairs={{0,16},{16,0},{1,17},{17,1},{2,18},{18,2},{3,19},{19,3},{4,20},{20... | collective-permute-start | bytes 245768 | tf_op jit(solution)/shard_map/ppermute | solution.py:505
  107.7 0.6 copy-start.5
  108.4 0.7 copy-start.4

commit v10 on v8

--- a/solution.py
+++ b/solution.py
@@ -92,19 +92,6 @@
         stage_ref[dp, rows, :] = mine_ref[rel // 4].astype(F32)
         stage_ref[1 - dp, rows, :] = other_ref[rel // 4].astype(F32)
     for l in range(layers):
-        for pair in range(SHARDS // 2):
-            lo = stage_ref[l, 16 * pair : 16 * pair + 8, :]
-            hi = stage_ref[l, 16 * pair + 8 : 16 * pair + 16, :]
-            w_ref[l, 16 * pair : 16 * pair + 16, :] = jnp.concatenate([lo[:, :COL_DOWN], hi[:, :COL_DOWN]], axis=0).astype(BF)
-            for half, part in enumerate((lo, hi)):
-                base = 64 * pair + 32 * half
-                wd_ref[l, base : base + 32, :] = jnp.concatenate(
-                    [part[:, COL_DOWN + 128 * a : COL_DOWN + 128 * a + 128] for a in range(4)], axis=0
-                ).astype(BF)
-        for block in range(COL_DOWN // 128):
-            wt_ref[l, 128 * block : 128 * block + 128, :] = w_ref[l, :, 128 * block : 128 * block + 128].T
-        for block in range(4):
-            wdt_ref[l, :, 128 * block : 128 * block + 128] = wd_ref[l, 128 * block : 128 * block + 128, :].T
         for k in range(4):
             for offset, rows in ((0, gains_ref), (4, scales_ref)):
                 col = jnp.broadcast_to(rows[l, k : k + 1, :], (128, 128)).T
@@ -348,6 +335,19 @@
             stage(l, i)
 
     def forward_layer(l, carry):
+        for pair in range(SHARDS // 2):
+            lo = stage_ref[l, 16 * pair : 16 * pair + 8, :]
+            hi = stage_ref[l, 16 * pair + 8 : 16 * pair + 16, :]
+            w_ref[l, 16 * pair : 16 * pair + 16, :] = jnp.concatenate([lo[:, :COL_DOWN], hi[:, :COL_DOWN]], axis=0).astype(BF)
+            for half, part in enumerate((lo, hi)):
+                base = 64 * pair + 32 * half
+                wd_ref[l, base : base + 32, :] = jnp.concatenate(
+                    [part[:, COL_DOWN + 128 * a : COL_DOWN + 128 * a + 128] for a in range(4)], axis=0
+                ).astype(BF)
+        for block in range(COL_DOWN // 128):
+            wt_ref[l, 128 * block : 128 * block + 128, :] = w_ref[l, :, 128 * block : 128 * block + 128].T
+        for block in range(4):
+            wdt_ref[l, :, 128 * block : 128 * block + 128] = wd_ref[l, 128 * block : 128 * block + 128, :].T
         each(chunks, time_forward, l)
         each(items, var_forward, l)
         each(chunks, tail_forward, l)

time: 112 us -> 111 us (level)
  no operation moved by 1% of the time
where the time goes in v10:
time: 111 us
  Pallas kernels  56.2 us (51%)
  waiting for transfers between devices  25 us (23%)
  starting transfers between devices  19.4 us (17%)
  local copies, waits for them, and re-layouts  6.36 us (6%)
  other arithmetic  3.2 us (3%)
    pallas_call x4, Pallas kernels, call(): pl.pallas_call(kernel, out_shape=out_shape, in_specs=[pl.BlockSpec(memory...  56.2 us
    ppermute x12, waiting for transfers between devices, swap(): return lax.ppermute(array, 'fsdp', [(i, i ^ mask) for i in range(SHARDS)])  21.8 us
    ppermute x12, starting transfers between devices, swap(): return lax.ppermute(array, 'fsdp', [(i, i ^ mask) for i in range(SHARDS)])  17.2 us
    unnamed x33, local copies, waits for them, and re-layouts  6.31 us
    ppermute x8, waiting for transfers between devices, flip(): return lax.ppermute(array, axis, [(i, i ^ 1 << bit) for i in range(size)])  3.12 us
  transfers between devices with their start and end apart: 20, of which 12 were waited for; matrix products, arithmetic and copies ran while one was open for 4% of the time, Pallas kernels for 2%

profile of v10, /device:TPU:0, one launch (start us, length us, event | category | flops | bytes accessed | tf_op | source)
XLA Modules:
  0.0 111.0 jit_solution(7131964702352410069)
XLA Ops:
  0.6 1.4 %pack.1 = bf16[1,8,2560]{2,1,0:T(8,128)(2,1)} custom-call(bf16[2,2,8,384]{3,2,1,0:T(8,128)(2,1)} %attn_in_ref.1, bf16[2,2,8,128]{3,2,1,0:T(8,128)(2,1)} %attn_out_ref.1, bf16[2,8,1024]{2,1,0:T(8,128)(2,1)} %feed_in_ref.1, bf16[2,32,128]{2,1,0:T(8,128)(2,1)} %feed_out_ref.1), custom_call_target="tpu_custom_call" | custom-call | tf_op jit(solution)/shard_map/pack/pallas_call | solution.py:424
  2.1 5.0 %collective-permute-start.2 = (bf16[1,8,2560]{2,1,0:T(8,128)(2,1)}, bf16[1,8,2560]{2,1,0:T(8,128)(2,1)S(1)}, u32[]{:S(2)}, u32[]{:S(2)}) collective-permute-start(bf16[1,8,2560]{2,1,0:T(8,128)(2,1)} %pack.1), channel_id=1, source_target_pairs={{0,12},{1,13},{2,14},{3,15},{4,8},{5,9},{6,10},{7,11},{8,4},{9,5},... | collective-permute-start | bytes 122888 | tf_op jit(solution)/shard_map/ppermute | solution.py:511
  7.1 0.6 collective-permute-start
  7.7 1.6 %collective-permute-done.2 = bf16[1,8,2560]{2,1,0:T(8,128)(2,1)S(1)} collective-permute-done((bf16[1,8,2560]{2,1,0:T(8,128)(2,1)}, bf16[1,8,2560]{2,1,0:T(8,128)(2,1)S(1)}, u32[]{:S(2)}, u32[]{:S(2)}) %collective-permute-start.2) | collective-permute-done | bytes 40992 | tf_op jit(solution)/shard_map/ppermute | solution.py:511
  9.3 2.9 %collective-permute-done.1 = bf16[1,8,2560]{2,1,0:T(8,128)(2,1)S(1)} collective-permute-done((bf16[1,8,2560]{2,1,0:T(8,128)(2,1)}, bf16[1,8,2560]{2,1,0:T(8,128)(2,1)S(1)}, u32[]{:S(2)}, u32[]{:S(2)}) %collective-permute-start.1) | collective-permute-done | bytes 40992 | tf_op jit(solution)/shard_map/ppermute | solution.py:511
  12.2 0.8 pad_maximum_fusion.3.wmine0_ref
  13.0 2.5 %collective-permute-start.5 = (bf16[4,8,2560]{2,1,0:T(8,128)(2,1)S(1)}, bf16[4,8,2560]{2,1,0:T(8,128)(2,1)S(1)}, u32[]{:S(2)}, u32[]{:S(2)}) collective-permute-start(bf16[4,8,2560]{2,1,0:T(8,128)(2,1)S(1)} %pad_maximum_fusion.3.wmine0_ref), channel_id=1, source_target_pairs={{0,3},{1,2},{2,1},{3,0},{4,7},{5,6},{6,5},{7,4},{8,11},{9,10},{10,... | collective-permute-start | bytes 491528 | tf_op jit(solution)/shard_map/ppermute | solution.py:511
  15.6 0.5 collective-permute-start.4
  16.1 0.5 collective-permute-start.3
  16.6 1.3 %copy.28.prompts_ref = bf16[8,10,128]{2,1,0:T(8,128)(2,1)} copy(bf16[8,10,128]{2,0,1:T(8,128)(2,1)} %param.15) | data formatting | bytes 40960 | tf_op args[1]
  17.9 1.7 %copy.27.patches_ref = bf16[2,4,117,128]{3,2,1,0:T(8,128)(2,1)} copy(bf16[2,4,117,128]{3,1,2,0:T(4,128)(2,1)} %param.14) | data formatting | bytes 479232 | tf_op args[0]
  19.6 2.4 %prepare.1.turned_ref = bf16[3,4,128,256]{3,2,1,0:T(8,128)(2,1)} custom-call(s32[2]{0:T(128)} %ids_ref.3, bf16[2,4,117,128]{3,2,1,0:T(8,128)(2,1)} %copy.27.patches_ref, bf16[8,10,128]{2,1,0:T(8,128)(2,1)} %copy.28.prompts_ref, bf16[1,128]{1,0:T(2,128)(2,1)} %bitcast.65, bf16[2,4,128,128]{3,2,1,0:T(8,128)(2,1)} %cot_ref.1, bf16[2,4,128,128]{3,2,1,0:T(8,128)(2,1)} %adj_ref.1), custom_call_target="tpu_custom_call" | custom-call | flops 1000000 | bytes 8000000 | tf_op jit(solution)/shard_map/prepare/pallas_call | solution.py:424
  22.0 0.1 collective-permute-done.3.wmine1_ref
  22.1 0.0 collective-permute-start.6
  22.1 0.5 collective-permute-start.7
  22.6 0.1 collective-permute-start.8
  22.7 0.4 collective-permute-start.9
  23.2 0.4 collective-permute-done.6.wother0_ref
  23.5 0.2 collective-permute-done.7.wother1_ref
  23.8 0.3 collective-permute-done.8.wother2_ref
  24.0 0.2 collective-permute-done.9.wother3_ref
  24.3 0.1 copy-done.10
  24.4 0.3 copy-done.11
  24.7 0.6 copy-done.12
  25.4 50.5 %tower.1 = (bf16[2,4,128,128]{3,2,1,0:T(8,128)(2,1)}, f32[2,4,117,128]{3,2,1,0:T(8,128)}, bf16[4,4,8,2560]{3,2,1,0:T(8,128)(2,1)}, bf16[4,4,8,2560]{3,2,1,0:T(8,...) custom-call(s32[2]{0:T(128)} %ids_ref.3, s32[8]{0:T(128)} %counts_ref.1, bf16[4,8,2560]{2,1,0:T(8,128)(2,1)} %copy-done.3, ...), custom_call_target="tpu_custom_call" | custom-call | flops 10000000000 | bytes 20000000 | tf_op jit(solution)/shard_map/tower/pallas_call | solution.py:424
  75.9 0.2 collective-permute-start.10
  76.1 0.3 collective-permute-start.11
  76.4 2.0 %collective-permute-done.11 = f32[4,8,1024]{2,1,0:T(8,128)S(1)} collective-permute-done((f32[4,8,1024]{2,1,0:T(8,128)}, f32[4,8,1024]{2,1,0:T(8,128)S(1)}, u32[]{:S(2)}, u32[]{:S(2)}) %collective-permute-start.11) | collective-permute-done | bytes 131104 | tf_op jit(solution)/shard_map/ppermute | solution.py:507
  78.4 0.9 add_convert_fusion.2
  79.3 1.2 %add_convert_fusion = bf16[4,4,8,2560]{3,2,1,0:T(8,128)(2,1)S(1)} fusion(bf16[4,4,8,2560]{3,2,1,0:T(8,128)(2,1)S(1)} %collective-permute-done.10, bf16[4,4,8,2560]{3,2,1,0:T(8,128)(2,1)} %get-tuple-element.42), kind=kLoop, calls=%fused_computation | loop fusion | flops 1310720 | bytes 1966080 | tf_op jit(solution)/shard_map/convert_element_type | solution.py:554
  80.6 1.6 %collective-permute-start.12 = (bf16[4,8,3584]{2,1,0:T(8,128)(2,1)S(1)}, bf16[4,8,3584]{2,1,0:T(8,128)(2,1)S(1)}, u32[]{:S(2)}, u32[]{:S(2)}) collective-permute-start(bf16[4,8,3584]{2,1,0:T(8,128)(2,1)S(1)} %get-tuple-element.92), channel_id=1, source_target_pairs={{0,1},{1,0},{2,3},{3,2},{4,5},{5,4},{6,7},{7,6},{8,9},{9,8},{10,11... | collective-permute-start | bytes 688136 | tf_op jit(solution)/shard_map/ppermute | solution.py:511
  82.2 1.5 %collective-permute-start.13 = (bf16[4,8,3584]{2,1,0:T(8,128)(2,1)S(1)}, bf16[4,8,3584]{2,1,0:T(8,128)(2,1)S(1)}, u32[]{:S(2)}, u32[]{:S(2)}) collective-permute-start(bf16[4,8,3584]{2,1,0:T(8,128)(2,1)S(1)} %get-tuple-element.93), channel_id=1, source_target_pairs={{0,2},{1,3},{2,0},{3,1},{4,6},{5,7},{6,4},{7,5},{8,10},{9,11},{10,... | collective-permute-start | bytes 688136 | tf_op jit(solution)/shard_map/ppermute | solution.py:511
  83.7 0.5 collective-permute-start.14
  84.2 4.9 %collective-permute-done.12 = bf16[4,8,3584]{2,1,0:T(8,128)(2,1)S(1)} collective-permute-done((bf16[4,8,3584]{2,1,0:T(8,128)(2,1)S(1)}, bf16[4,8,3584]{2,1,0:T(8,128)(2,1)S(1)}, u32[]{:S(2)}, u32[]{:S(2)}) %collective-permute-start.12) | collective-permute-done | bytes 229408 | tf_op jit(solution)/shard_map/ppermute | solution.py:511
  89.1 5.4 %collective-permute-done.13 = bf16[4,8,3584]{2,1,0:T(8,128)(2,1)S(1)} collective-permute-done((bf16[4,8,3584]{2,1,0:T(8,128)(2,1)S(1)}, bf16[4,8,3584]{2,1,0:T(8,128)(2,1)S(1)}, u32[]{:S(2)}, u32[]{:S(2)}) %collective-permute-start.13) | collective-permute-done | bytes 229408 | tf_op jit(solution)/shard_map/ppermute | solution.py:511
  94.6 0.1 fusion.1
  94.8 0.5 collective-permute-start.15
  95.3 2.1 %collective-permute-start.16 = (bf16[8,6656]{1,0:T(8,128)(2,1)S(1)}, bf16[8,6656]{1,0:T(8,128)(2,1)S(1)}, u32[]{:S(2)}, u32[]{:S(2)}) collective-permute-start(bf16[8,6656]{1,0:T(8,128)(2,1)S(1)} %get-tuple-element.81), channel_id=1, source_target_pairs={{0,8},{1,9},{2,10},{3,11},{4,12},{5,13},{6,14},{7,15},{8,0},{9,1},... | collective-permute-start | bytes 319496 | tf_op jit(solution)/shard_map/ppermute | solution.py:511
  97.4 1.9 %collective-permute-start.17 = (bf16[8,6656]{1,0:T(8,128)(2,1)S(1)}, bf16[8,6656]{1,0:T(8,128)(2,1)S(1)}, u32[]{:S(2)}, u32[]{:S(2)}) collective-permute-start(bf16[8,6656]{1,0:T(8,128)(2,1)S(1)} %get-tuple-element.82), channel_id=1, source_target_pairs={{0,12},{1,13},{2,14},{3,15},{4,8},{5,9},{6,10},{7,11},{8,4},{9,5},... | collective-permute-start | bytes 319496 | tf_op jit(solution)/shard_map/ppermute | solution.py:511
  99.3 0.8 collective-permute-done.15
  100.1 6.0 %collective-permute-done.16 = bf16[8,6656]{1,0:T(8,128)(2,1)S(1)} collective-permute-done((bf16[8,6656]{1,0:T(8,128)(2,1)S(1)}, bf16[8,6656]{1,0:T(8,128)(2,1)S(1)}, u32[]{:S(2)}, u32[]{:S(2)}) %collective-permute-start.16) | collective-permute-done | bytes 106528 | tf_op jit(solution)/shard_map/ppermute | solution.py:511
  106.2 0.1 collective-permute-start.19
  106.3 0.6 collective-permute-start.18
  106.8 0.9 copy.29
  107.7 0.0 collective-permute-done.18.big_other
  107.8 0.6 copy-done.5
  108.4 0.6 copy-done.4
  109.0 1.8 %final.1 = (f32[2,2,8,384]{3,2,1,0:T(8,128)}, f32[2,2,8,128]{3,2,1,0:T(8,128)}, f32[2,8,1024]{2,1,0:T(8,128)}, f32[2,32,128]{2,1,0:T(8,128)}, f32[2,128,128]{2,1...) custom-call(f32[8,2560]{1,0:T(8,128)} %copy-done.2, ...), custom_call_target="tpu_custom_call" | custom-call | tf_op jit(solution)/shard_map/final/pallas_call | solution.py:424
  (40 shorter events, 0.3 us)
Async XLA Ops:
  2.1 7.3 %collective-permute-start.2 = (bf16[1,8,2560]{2,1,0:T(8,128)(2,1)}, bf16[1,8,2560]{2,1,0:T(8,128)(2,1)S(1)}, u32[]{:S(2)}, u32[]{:S(2)}) collective-permute-start(bf16[1,8,2560]{2,1,0:T(8,128)(2,1)} %pack.1), channel_id=1, source_target_pairs={{0,12},{1,13},{2,14},{3,15},{4,8},{5,9},{6,10},{7,11},{8,4},{9,5},... | collective-permute-start | bytes 122888 | tf_op jit(solution)/shard_map/ppermute | solution.py:511
  7.1 5.1 %collective-permute-start.1 = (bf16[1,8,2560]{2,1,0:T(8,128)(2,1)}, bf16[1,8,2560]{2,1,0:T(8,128)(2,1)S(1)}, u32[]{:S(2)}, u32[]{:S(2)}) collective-permute-start(bf16[1,8,2560]{2,1,0:T(8,128)(2,1)} %pack.1), channel_id=1, source_target_pairs={{0,8},{1,9},{2,10},{3,11},{4,12},{5,13},{6,14},{7,15},{8,0},{9,1},... | collective-permute-start | bytes 122888 | tf_op jit(solution)/shard_map/ppermute | solution.py:511
  7.1 5.1 %collective-permute-start = (bf16[1,8,2560]{2,1,0:T(8,128)(2,1)}, bf16[1,8,2560]{2,1,0:T(8,128)(2,1)S(1)}, u32[]{:S(2)}, u32[]{:S(2)}) collective-permute-start(bf16[1,8,2560]{2,1,0:T(8,128)(2,1)} %pack.1), channel_id=1, source_target_pairs={{0,4},{1,5},{2,6},{3,7},{4,0},{5,1},{6,2},{7,3},{8,12},{9,13},{10,... | collective-permute-start | bytes 122888 | tf_op jit(solution)/shard_map/ppermute | solution.py:511
  13.0 9.1 %copy-start.3 = (bf16[4,8,2560]{2,1,0:T(8,128)(2,1)}, bf16[4,8,2560]{2,1,0:T(8,128)(2,1)S(1)}, u32[]{:S(2)}) copy-start(bf16[4,8,2560]{2,1,0:T(8,128)(2,1)S(1)} %pad_maximum_fusion.3.wmine0_ref) | copy-start | bytes 491524
  13.0 9.0 %collective-permute-start.5 = (bf16[4,8,2560]{2,1,0:T(8,128)(2,1)S(1)}, bf16[4,8,2560]{2,1,0:T(8,128)(2,1)S(1)}, u32[]{:S(2)}, u32[]{:S(2)}) collective-permute-start(bf16[4,8,2560]{2,1,0:T(8,128)(2,1)S(1)} %pad_maximum_fusion.3.wmine0_ref), channel_id=1, source_target_pairs={{0,3},{1,2},{2,1},{3,0},{4,7},{5,6},{6,5},{7,4},{8,11},{9,10},{10,... | collective-permute-start | bytes 491528 | tf_op jit(solution)/shard_map/ppermute | solution.py:511
  15.6 6.5 %collective-permute-start.4 = (bf16[4,8,2560]{2,1,0:T(8,128)(2,1)S(1)}, bf16[4,8,2560]{2,1,0:T(8,128)(2,1)S(1)}, u32[]{:S(2)}, u32[]{:S(2)}) collective-permute-start(bf16[4,8,2560]{2,1,0:T(8,128)(2,1)S(1)} %pad_maximum_fusion.3.wmine0_ref), channel_id=1, source_target_pairs={{0,2},{1,3},{2,0},{3,1},{4,6},{5,7},{6,4},{7,5},{8,10},{9,11},{10,... | collective-permute-start | bytes 491528 | tf_op jit(solution)/shard_map/ppermute | solution.py:511
  16.1 6.0 %collective-permute-start.3 = (bf16[4,8,2560]{2,1,0:T(8,128)(2,1)S(1)}, bf16[4,8,2560]{2,1,0:T(8,128)(2,1)S(1)}, u32[]{:S(2)}, u32[]{:S(2)}) collective-permute-start(bf16[4,8,2560]{2,1,0:T(8,128)(2,1)S(1)} %pad_maximum_fusion.3.wmine0_ref), channel_id=1, source_target_pairs={{0,1},{1,0},{2,3},{3,2},{4,5},{5,4},{6,7},{7,6},{8,9},{9,8},{10,11... | collective-permute-start | bytes 491528 | tf_op jit(solution)/shard_map/ppermute | solution.py:511
  22.0 2.3 %copy-start.6 = (bf16[4,8,2560]{2,1,0:T(8,128)(2,1)}, bf16[4,8,2560]{2,1,0:T(8,128)(2,1)S(1)}, u32[]{:S(2)}) copy-start(bf16[4,8,2560]{2,1,0:T(8,128)(2,1)S(1)} %collective-permute-done.5.wmine3_ref) | copy-start | bytes 491524
  22.0 2.2 %copy-start.7 = (bf16[4,8,2560]{2,1,0:T(8,128)(2,1)}, bf16[4,8,2560]{2,1,0:T(8,128)(2,1)S(1)}, u32[]{:S(2)}) copy-start(bf16[4,8,2560]{2,1,0:T(8,128)(2,1)S(1)} %collective-permute-done.4.wmine2_ref) | copy-start | bytes 491524
  22.1 2.2 %copy-start.8 = (bf16[4,8,2560]{2,1,0:T(8,128)(2,1)}, bf16[4,8,2560]{2,1,0:T(8,128)(2,1)S(1)}, u32[]{:S(2)}) copy-start(bf16[4,8,2560]{2,1,0:T(8,128)(2,1)S(1)} %collective-permute-done.3.wmine1_ref) | copy-start | bytes 491524
  22.1 1.4 %collective-permute-start.6 = (bf16[4,8,2560]{2,1,0:T(8,128)(2,1)S(1)}, bf16[4,8,2560]{2,1,0:T(8,128)(2,1)S(1)}, u32[]{:S(2)}, u32[]{:S(2)}) collective-permute-start(bf16[4,8,2560]{2,1,0:T(8,128)(2,1)S(1)} %pad_maximum_fusion.3.wmine0_ref), channel_id=1, source_target_pairs={{0,16},{16,0},{1,17},{17,1},{2,18},{18,2},{3,19},{19,3},{4,20},{20... | collective-permute-start | bytes 491528 | tf_op jit(solution)/shard_map/ppermute | solution.py:507
  22.1 1.6 %collective-permute-start.7 = (bf16[4,8,2560]{2,1,0:T(8,128)(2,1)S(1)}, bf16[4,8,2560]{2,1,0:T(8,128)(2,1)S(1)}, u32[]{:S(2)}, u32[]{:S(2)}) collective-permute-start(bf16[4,8,2560]{2,1,0:T(8,128)(2,1)S(1)} %collective-permute-done.3.wmine1_ref), channel_id=1, source_target_pairs={{0,16},{16,0},{1,17},{17,1},{2,18},{18,2},{3,19},{19,3},{4,20},{20... | collective-permute-start | bytes 491528 | tf_op jit(solution)/shard_map/ppermute | solution.py:507
  22.6 1.4 %collective-permute-start.8 = (bf16[4,8,2560]{2,1,0:T(8,128)(2,1)S(1)}, bf16[4,8,2560]{2,1,0:T(8,128)(2,1)S(1)}, u32[]{:S(2)}, u32[]{:S(2)}) collective-permute-start(bf16[4,8,2560]{2,1,0:T(8,128)(2,1)S(1)} %collective-permute-done.4.wmine2_ref), channel_id=1, source_target_pairs={{0,16},{16,0},{1,17},{17,1},{2,18},{18,2},{3,19},{19,3},{4,20},{20... | collective-permute-start | bytes 491528 | tf_op jit(solution)/shard_map/ppermute | solution.py:507
  22.7 1.6 %collective-permute-start.9 = (bf16[4,8,2560]{2,1,0:T(8,128)(2,1)S(1)}, bf16[4,8,2560]{2,1,0:T(8,128)(2,1)S(1)}, u32[]{:S(2)}, u32[]{:S(2)}) collective-permute-start(bf16[4,8,2560]{2,1,0:T(8,128)(2,1)S(1)} %collective-permute-done.5.wmine3_ref), channel_id=1, source_target_pairs={{0,16},{16,0},{1,17},{17,1},{2,18},{18,2},{3,19},{19,3},{4,20},{20... | collective-permute-start | bytes 491528 | tf_op jit(solution)/shard_map/ppermute | solution.py:507
  23.5 0.8 copy-start.9
  23.8 0.7 copy-start.10
  24.0 0.7 copy-start.11
  24.7 0.7 copy-start.12
  75.9 3.4 %collective-permute-start.10 = (bf16[4,4,8,2560]{3,2,1,0:T(8,128)(2,1)}, bf16[4,4,8,2560]{3,2,1,0:T(8,128)(2,1)S(1)}, u32[]{:S(2)}, u32[]{:S(2)}) collective-permute-start(bf16[4,4,8,2560]{3,2,1,0:T(8,128)(2,1)} %get-tuple-element.43), channel_id=1, source_target_pairs={{0,16},{16,0},{1,17},{17,1},{2,18},{18,2},{3,19},{19,3},{4,20},{20... | collective-permute-start | bytes 1966088 | tf_op jit(solution)/shard_map/ppermute | solution.py:507
  76.1 2.3 %collective-permute-start.11 = (f32[4,8,1024]{2,1,0:T(8,128)}, f32[4,8,1024]{2,1,0:T(8,128)S(1)}, u32[]{:S(2)}, u32[]{:S(2)}) collective-permute-start(f32[4,8,1024]{2,1,0:T(8,128)} %get-tuple-element.45), channel_id=1, source_target_pairs={{0,16},{16,0},{1,17},{17,1},{2,18},{18,2},{3,19},{19,3},{4,20},{20... | collective-permute-start | bytes 393224 | tf_op jit(solution)/shard_map/ppermute | solution.py:507
  80.6 8.5 %collective-permute-start.12 = (bf16[4,8,3584]{2,1,0:T(8,128)(2,1)S(1)}, bf16[4,8,3584]{2,1,0:T(8,128)(2,1)S(1)}, u32[]{:S(2)}, u32[]{:S(2)}) collective-permute-start(bf16[4,8,3584]{2,1,0:T(8,128)(2,1)S(1)} %get-tuple-element.92), channel_id=1, source_target_pairs={{0,1},{1,0},{2,3},{3,2},{4,5},{5,4},{6,7},{7,6},{8,9},{9,8},{10,11... | collective-permute-start | bytes 688136 | tf_op jit(solution)/shard_map/ppermute | solution.py:511
  82.2 12.4 %collective-permute-start.13 = (bf16[4,8,3584]{2,1,0:T(8,128)(2,1)S(1)}, bf16[4,8,3584]{2,1,0:T(8,128)(2,1)S(1)}, u32[]{:S(2)}, u32[]{:S(2)}) collective-permute-start(bf16[4,8,3584]{2,1,0:T(8,128)(2,1)S(1)} %get-tuple-element.93), channel_id=1, source_target_pairs={{0,2},{1,3},{2,0},{3,1},{4,6},{5,7},{6,4},{7,5},{8,10},{9,11},{10,... | collective-permute-start | bytes 688136 | tf_op jit(solution)/shard_map/ppermute | solution.py:511
  83.7 10.9 %collective-permute-start.14 = (bf16[4,8,3584]{2,1,0:T(8,128)(2,1)S(1)}, bf16[4,8,3584]{2,1,0:T(8,128)(2,1)S(1)}, u32[]{:S(2)}, u32[]{:S(2)}) collective-permute-start(bf16[4,8,3584]{2,1,0:T(8,128)(2,1)S(1)} %get-tuple-element.94), channel_id=1, source_target_pairs={{0,3},{1,2},{2,1},{3,0},{4,7},{5,6},{6,5},{7,4},{8,11},{9,10},{10,... | collective-permute-start | bytes 688136 | tf_op jit(solution)/shard_map/ppermute | solution.py:511
  94.7 12.2 %copy-start.1 = (f32[2,4,117,128]{3,2,1,0:T(8,128)S(1)}, f32[2,4,117,128]{3,2,1,0:T(8,128)}, u32[]{:S(2)}) copy-start(f32[2,4,117,128]{3,2,1,0:T(8,128)} %get-tuple-element.58) | copy-start | bytes 1437700
  94.8 5.3 %collective-permute-start.15 = (bf16[8,6656]{1,0:T(8,128)(2,1)S(1)}, bf16[8,6656]{1,0:T(8,128)(2,1)S(1)}, u32[]{:S(2)}, u32[]{:S(2)}) collective-permute-start(bf16[8,6656]{1,0:T(8,128)(2,1)S(1)} %get-tuple-element.80), channel_id=1, source_target_pairs={{0,4},{1,5},{2,6},{3,7},{4,0},{5,1},{6,2},{7,3},{8,12},{9,13},{10,... | collective-permute-start | bytes 319496 | tf_op jit(solution)/shard_map/ppermute | solution.py:511
  95.3 10.8 %collective-permute-start.16 = (bf16[8,6656]{1,0:T(8,128)(2,1)S(1)}, bf16[8,6656]{1,0:T(8,128)(2,1)S(1)}, u32[]{:S(2)}, u32[]{:S(2)}) collective-permute-start(bf16[8,6656]{1,0:T(8,128)(2,1)S(1)} %get-tuple-element.81), channel_id=1, source_target_pairs={{0,8},{1,9},{2,10},{3,11},{4,12},{5,13},{6,14},{7,15},{8,0},{9,1},... | collective-permute-start | bytes 319496 | tf_op jit(solution)/shard_map/ppermute | solution.py:511
  97.4 8.7 %collective-permute-start.17 = (bf16[8,6656]{1,0:T(8,128)(2,1)S(1)}, bf16[8,6656]{1,0:T(8,128)(2,1)S(1)}, u32[]{:S(2)}, u32[]{:S(2)}) collective-permute-start(bf16[8,6656]{1,0:T(8,128)(2,1)S(1)} %get-tuple-element.82), channel_id=1, source_target_pairs={{0,12},{1,13},{2,14},{3,15},{4,8},{5,9},{6,10},{7,11},{8,4},{9,5},... | collective-permute-start | bytes 319496 | tf_op jit(solution)/shard_map/ppermute | solution.py:511
  106.1 1.6 %copy-start = (f32[8,4096]{1,0:T(8,128)}, f32[8,4096]{1,0:T(8,128)S(1)}, u32[]{:S(2)}) copy-start(f32[8,4096]{1,0:T(8,128)S(1)} %add_add_fusion.small_mine) | copy-start | bytes 393220
  106.2 1.6 %collective-permute-start.19 = (f32[8,4096]{1,0:T(8,128)S(1)}, f32[8,4096]{1,0:T(8,128)S(1)}, u32[]{:S(2)}, u32[]{:S(2)}) collective-permute-start(f32[8,4096]{1,0:T(8,128)S(1)} %add_add_fusion.small_mine), channel_id=1, source_target_pairs={{0,16},{16,0},{1,17},{17,1},{2,18},{18,2},{3,19},{19,3},{4,20},{20... | collective-permute-start | bytes 393224 | tf_op jit(solution)/shard_map/ppermute | solution.py:507
  106.3 1.5 %copy-start.2 = (f32[8,2560]{1,0:T(8,128)}, f32[8,2560]{1,0:T(8,128)S(1)}, u32[]{:S(2)}) copy-start(f32[8,2560]{1,0:T(8,128)S(1)} %fusion.2.big_mine) | copy-start | bytes 245764
  106.3 1.5 %collective-permute-start.18 = (f32[8,2560]{1,0:T(8,128)S(1)}, f32[8,2560]{1,0:T(8,128)S(1)}, u32[]{:S(2)}, u32[]{:S(2)}) collective-permute-start(f32[8,2560]{1,0:T(8,128)S(1)} %fusion.2.big_mine), channel_id=1, source_target_pairs={{0,16},{16,0},{1,17},{17,1},{2,18},{18,2},{3,19},{19,3},{4,20},{20... | collective-permute-start | bytes 245768 | tf_op jit(solution)/shard_map/ppermute | solution.py:507
  107.8 0.6 copy-start.5
  108.4 0.6 copy-start.4

commit v11 on v10

--- a/solution.py
+++ b/solution.py
@@ -77,7 +77,7 @@
     out_ref, pgrad_ref, bigmine_ref, bigother_ref, smallmine_ref, smallother_ref,
     stage_ref, w_ref, wd_ref, wt_ref, wdt_ref, colb_ref, tokscr_ref, h_ref, g_ref, xh_ref, inv_ref,
     qkvt_ref, pb_ref, ot_ref, qkvv_ref, pv_ref, ov_ref, pw_ref, qbd_ref, dob_ref, hid_ref, du_ref, dqkv_ref,
-    dov_ref, ga_ref, gd_ref, gt_ref, gacc_ref, gbig_ref, pacc_ref, spread_ref, act_ref, slope_ref, gdt_ref, both_ref,
+    dov_ref, ga_ref, gd_ref, gt_ref, gacc_ref, gbig_ref, pacc_ref, spread_ref, act_ref, slope_ref, gdt_ref, both_ref, dop_ref,
 ):
     dp = lax.axis_index("dp") if split else 0
     me = lax.axis_index("fsdp") if split else 0
@@ -118,6 +118,7 @@
     both_ref[...] = jnp.zeros_like(both_ref)
     for half in range(2):
         both_ref[:, 128 * half : 128 * half + 128, 128 * half : 128 * half + 128] = tok_ref[...]
+    dop_ref[...] = jnp.zeros_like(dop_ref)
     qbd_ref[...] = jnp.zeros_like(qbd_ref)
     dob_ref[...] = jnp.zeros_like(dob_ref)
 
@@ -311,21 +312,25 @@
             value_rows = values[:, lanes].T
             for x in range(2):
                 diag_heads(dob_ref, 2 * at + x, grads[x][:, lanes])
+                for head in range(HEADS):
+                    first = 64 * (head // 2) + 32 * x + 16 * (head % 2)
+                    half = slice(128 * (head % 2), 128 * (head % 2) + 128)
+                    dop_ref[at, first : first + 16, half] = grads[x][16 * head : 16 * head + 16, lanes]
             for hp in range(4):
                 span = slice(256 * hp, 256 * hp + 256)
                 rows = slice(32 * hp, 32 * hp + 32)
                 prob_bf = pb_ref[l, 2 * c + s, :, span]
                 prob = prob_bf.astype(F32)
+                dvalue = dot_nt(dop_ref[at, 64 * hp : 64 * hp + 64, :], prob_bf).astype(BF)
                 for x in range(2):
                     weighted = prob * dot_nn(value_rows, dob_ref[2 * at + x, :, span])
                     ds = (weighted - prob * jnp.sum(weighted, axis=0, keepdims=True)).astype(BF)
-                    dvalue = dot_nt(dob_ref[2 * at + x, rows, span], prob_bf)
                     dquery = dot_nn(keys[rows, lanes], ds) * 0.25
                     dkey = dot_nt(qbd_ref[at, rows, span], ds)
                     dqkv_ref[2 * c + x, 32 * hp : 32 * hp + 16, lanes] = dquery[:16, :128].astype(BF)
                     dqkv_ref[2 * c + x, 32 * hp + 16 : 32 * hp + 32, lanes] = dquery[16:, 128:].astype(BF)
                     dqkv_ref[2 * c + x, 128 + 32 * hp : 160 + 32 * hp, lanes] = dkey.astype(BF)
-                    dqkv_ref[2 * c + x, 256 + 32 * hp : 288 + 32 * hp, lanes] = dvalue.astype(BF)
+                    dqkv_ref[2 * c + x, 256 + 32 * hp : 288 + 32 * hp, lanes] = dvalue[32 * x : 32 * x + 32]
         ga_ref[:, COL_IN[0] : COL_IN[0] + 384] += dot_nt(n, dqkv_ref[2 * c])
         for x in range(2):
             pass_on(l, 0, c, x, dot_nn(w_ref[l, :, COL_IN[0] : COL_IN[0] + 384], dqkv_ref[2 * c + x]), xhat, inv)
@@ -480,6 +485,7 @@
             pltpu.VMEM((2, 4, 512, 256), BF),
             pltpu.VMEM((128, 512), F32),
             pltpu.VMEM((2, 256, 256), BF),
+            pltpu.VMEM((4, 256, 256), BF),
         ],
         *operands,
         cost=pl.CostEstimate(flops=10**10, bytes_accessed=20 * 10**6, transcendentals=0),

time: 111 us -> 128 us (1.15)
  Pallas kernels: 56.2 us -> 72.5 us
    pallas_call x4, Pallas kernels: 56.2 us -> 72.5 us  [call(): pl.pallas_call(kernel, out_shape=out_shape, in_specs=[pl.BlockSpec(memory...]
where the time goes in v11:
time: 128 us; the launch traced here: 127 us
  Pallas kernels  72.5 us (57%)
  waiting for transfers between devices  25 us (20%)
  starting transfers between devices  19.4 us (15%)
  local copies, waits for them, and re-layouts  6.36 us (5%)
  other arithmetic  3.2 us (2%)
    pallas_call x4, Pallas kernels, call(): pl.pallas_call(kernel, out_shape=out_shape, in_specs=[pl.BlockSpec(memory...  72.5 us
    ppermute x12, waiting for transfers between devices, swap(): return lax.ppermute(array, 'fsdp', [(i, i ^ mask) for i in range(SHARDS)])  21.8 us
    ppermute x12, starting transfers between devices, swap(): return lax.ppermute(array, 'fsdp', [(i, i ^ mask) for i in range(SHARDS)])  17.2 us
    unnamed x33, local copies, waits for them, and re-layouts  6.31 us
    ppermute x8, waiting for transfers between devices, flip(): return lax.ppermute(array, axis, [(i, i ^ 1 << bit) for i in range(size)])  3.12 us
  transfers between devices with their start and end apart: 20, of which 12 were waited for; matrix products, arithmetic and copies ran while one was open for 4% of the time, Pallas kernels for 2%

profile of v11, /device:TPU:0, one launch (start us, length us, event | category | flops | bytes accessed | tf_op | source)
XLA Modules:
  0.0 127.4 jit_solution(6367059841975202106)
XLA Ops:
  0.6 1.4 %pack.1 = bf16[1,8,2560]{2,1,0:T(8,128)(2,1)} custom-call(bf16[2,2,8,384]{3,2,1,0:T(8,128)(2,1)} %attn_in_ref.1, bf16[2,2,8,128]{3,2,1,0:T(8,128)(2,1)} %attn_out_ref.1, bf16[2,8,1024]{2,1,0:T(8,128)(2,1)} %feed_in_ref.1, bf16[2,32,128]{2,1,0:T(8,128)(2,1)} %feed_out_ref.1), custom_call_target="tpu_custom_call" | custom-call | tf_op jit(solution)/shard_map/pack/pallas_call | solution.py:429
  2.1 5.0 %collective-permute-start.2 = (bf16[1,8,2560]{2,1,0:T(8,128)(2,1)}, bf16[1,8,2560]{2,1,0:T(8,128)(2,1)S(1)}, u32[]{:S(2)}, u32[]{:S(2)}) collective-permute-start(bf16[1,8,2560]{2,1,0:T(8,128)(2,1)} %pack.1), channel_id=1, source_target_pairs={{0,12},{1,13},{2,14},{3,15},{4,8},{5,9},{6,10},{7,11},{8,4},{9,5},... | collective-permute-start | bytes 122888 | tf_op jit(solution)/shard_map/ppermute | solution.py:517
  7.1 0.6 collective-permute-start
  7.7 1.6 %collective-permute-done.2 = bf16[1,8,2560]{2,1,0:T(8,128)(2,1)S(1)} collective-permute-done((bf16[1,8,2560]{2,1,0:T(8,128)(2,1)}, bf16[1,8,2560]{2,1,0:T(8,128)(2,1)S(1)}, u32[]{:S(2)}, u32[]{:S(2)}) %collective-permute-start.2) | collective-permute-done | bytes 40992 | tf_op jit(solution)/shard_map/ppermute | solution.py:517
  9.3 2.9 %collective-permute-done.1 = bf16[1,8,2560]{2,1,0:T(8,128)(2,1)S(1)} collective-permute-done((bf16[1,8,2560]{2,1,0:T(8,128)(2,1)}, bf16[1,8,2560]{2,1,0:T(8,128)(2,1)S(1)}, u32[]{:S(2)}, u32[]{:S(2)}) %collective-permute-start.1) | collective-permute-done | bytes 40992 | tf_op jit(solution)/shard_map/ppermute | solution.py:517
  12.2 0.8 pad_maximum_fusion.3.wmine0_ref
  13.0 2.5 %collective-permute-start.5 = (bf16[4,8,2560]{2,1,0:T(8,128)(2,1)S(1)}, bf16[4,8,2560]{2,1,0:T(8,128)(2,1)S(1)}, u32[]{:S(2)}, u32[]{:S(2)}) collective-permute-start(bf16[4,8,2560]{2,1,0:T(8,128)(2,1)S(1)} %pad_maximum_fusion.3.wmine0_ref), channel_id=1, source_target_pairs={{0,3},{1,2},{2,1},{3,0},{4,7},{5,6},{6,5},{7,4},{8,11},{9,10},{10,... | collective-permute-start | bytes 491528 | tf_op jit(solution)/shard_map/ppermute | solution.py:517
  15.6 0.5 collective-permute-start.4
  16.1 0.5 collective-permute-start.3
  16.6 1.3 %copy.28.prompts_ref = bf16[8,10,128]{2,1,0:T(8,128)(2,1)} copy(bf16[8,10,128]{2,0,1:T(8,128)(2,1)} %param.15) | data formatting | bytes 40960 | tf_op args[1]
  17.9 1.7 %copy.27.patches_ref = bf16[2,4,117,128]{3,2,1,0:T(8,128)(2,1)} copy(bf16[2,4,117,128]{3,1,2,0:T(4,128)(2,1)} %param.14) | data formatting | bytes 479232 | tf_op args[0]
  19.6 2.4 %prepare.1.turned_ref = bf16[3,4,128,256]{3,2,1,0:T(8,128)(2,1)} custom-call(s32[2]{0:T(128)} %ids_ref.3, bf16[2,4,117,128]{3,2,1,0:T(8,128)(2,1)} %copy.27.patches_ref, bf16[8,10,128]{2,1,0:T(8,128)(2,1)} %copy.28.prompts_ref, bf16[1,128]{1,0:T(2,128)(2,1)} %bitcast.65, bf16[2,4,128,128]{3,2,1,0:T(8,128)(2,1)} %cot_ref.1, bf16[2,4,128,128]{3,2,1,0:T(8,128)(2,1)} %adj_ref.1), custom_call_target="tpu_custom_call" | custom-call | flops 1000000 | bytes 8000000 | tf_op jit(solution)/shard_map/prepare/pallas_call | solution.py:429
  22.0 0.1 collective-permute-done.3.wmine1_ref
  22.1 0.0 collective-permute-start.6
  22.1 0.5 collective-permute-start.7
  22.6 0.1 collective-permute-start.8
  22.7 0.4 collective-permute-start.9
  23.2 0.4 collective-permute-done.6.wother0_ref
  23.5 0.2 collective-permute-done.7.wother1_ref
  23.8 0.3 collective-permute-done.8.wother2_ref
  24.0 0.2 collective-permute-done.9.wother3_ref
  24.3 0.1 copy-done.10
  24.4 0.3 copy-done.11
  24.7 0.6 copy-done.12
  25.4 66.9 %tower.1 = (bf16[2,4,128,128]{3,2,1,0:T(8,128)(2,1)}, f32[2,4,117,128]{3,2,1,0:T(8,128)}, bf16[4,4,8,2560]{3,2,1,0:T(8,128)(2,1)}, bf16[4,4,8,2560]{3,2,1,0:T(8,...) custom-call(s32[2]{0:T(128)} %ids_ref.3, s32[8]{0:T(128)} %counts_ref.1, bf16[4,8,2560]{2,1,0:T(8,128)(2,1)} %copy-done.3, ...), custom_call_target="tpu_custom_call" | custom-call | flops 10000000000 | bytes 20000000 | tf_op jit(solution)/shard_map/tower/pallas_call | solution.py:429
  92.2 0.2 collective-permute-start.10
  92.5 0.3 collective-permute-start.11
  92.8 2.0 %collective-permute-done.11 = f32[4,8,1024]{2,1,0:T(8,128)S(1)} collective-permute-done((f32[4,8,1024]{2,1,0:T(8,128)}, f32[4,8,1024]{2,1,0:T(8,128)S(1)}, u32[]{:S(2)}, u32[]{:S(2)}) %collective-permute-start.11) | collective-permute-done | bytes 131104 | tf_op jit(solution)/shard_map/ppermute | solution.py:513
  94.7 0.9 add_convert_fusion.2
  95.7 1.2 add_convert_fusion
  97.0 1.6 %collective-permute-start.12 = (bf16[4,8,3584]{2,1,0:T(8,128)(2,1)S(1)}, bf16[4,8,3584]{2,1,0:T(8,128)(2,1)S(1)}, u32[]{:S(2)}, u32[]{:S(2)}) collective-permute-start(bf16[4,8,3584]{2,1,0:T(8,128)(2,1)S(1)} %get-tuple-element.92), channel_id=1, source_target_pairs={{0,1},{1,0},{2,3},{3,2},{4,5},{5,4},{6,7},{7,6},{8,9},{9,8},{10,11... | collective-permute-start | bytes 688136 | tf_op jit(solution)/shard_map/ppermute | solution.py:517
  98.6 1.5 %collective-permute-start.13 = (bf16[4,8,3584]{2,1,0:T(8,128)(2,1)S(1)}, bf16[4,8,3584]{2,1,0:T(8,128)(2,1)S(1)}, u32[]{:S(2)}, u32[]{:S(2)}) collective-permute-start(bf16[4,8,3584]{2,1,0:T(8,128)(2,1)S(1)} %get-tuple-element.93), channel_id=1, source_target_pairs={{0,2},{1,3},{2,0},{3,1},{4,6},{5,7},{6,4},{7,5},{8,10},{9,11},{10,... | collective-permute-start | bytes 688136 | tf_op jit(solution)/shard_map/ppermute | solution.py:517
  100.1 0.5 collective-permute-start.14
  100.6 4.9 %collective-permute-done.12 = bf16[4,8,3584]{2,1,0:T(8,128)(2,1)S(1)} collective-permute-done((bf16[4,8,3584]{2,1,0:T(8,128)(2,1)S(1)}, bf16[4,8,3584]{2,1,0:T(8,128)(2,1)S(1)}, u32[]{:S(2)}, u32[]{:S(2)}) %collective-permute-start.12) | collective-permute-done | bytes 229408 | tf_op jit(solution)/shard_map/ppermute | solution.py:517
  105.5 5.5 %collective-permute-done.13 = bf16[4,8,3584]{2,1,0:T(8,128)(2,1)S(1)} collective-permute-done((bf16[4,8,3584]{2,1,0:T(8,128)(2,1)S(1)}, bf16[4,8,3584]{2,1,0:T(8,128)(2,1)S(1)}, u32[]{:S(2)}, u32[]{:S(2)}) %collective-permute-start.13) | collective-permute-done | bytes 229408 | tf_op jit(solution)/shard_map/ppermute | solution.py:517
  111.0 0.1 fusion.1
  111.2 0.5 collective-permute-start.15
  111.7 2.1 %collective-permute-start.16 = (bf16[8,6656]{1,0:T(8,128)(2,1)S(1)}, bf16[8,6656]{1,0:T(8,128)(2,1)S(1)}, u32[]{:S(2)}, u32[]{:S(2)}) collective-permute-start(bf16[8,6656]{1,0:T(8,128)(2,1)S(1)} %get-tuple-element.81), channel_id=1, source_target_pairs={{0,8},{1,9},{2,10},{3,11},{4,12},{5,13},{6,14},{7,15},{8,0},{9,1},... | collective-permute-start | bytes 319496 | tf_op jit(solution)/shard_map/ppermute | solution.py:517
  113.8 1.9 %collective-permute-start.17 = (bf16[8,6656]{1,0:T(8,128)(2,1)S(1)}, bf16[8,6656]{1,0:T(8,128)(2,1)S(1)}, u32[]{:S(2)}, u32[]{:S(2)}) collective-permute-start(bf16[8,6656]{1,0:T(8,128)(2,1)S(1)} %get-tuple-element.82), channel_id=1, source_target_pairs={{0,12},{1,13},{2,14},{3,15},{4,8},{5,9},{6,10},{7,11},{8,4},{9,5},... | collective-permute-start | bytes 319496 | tf_op jit(solution)/shard_map/ppermute | solution.py:517
  115.7 0.8 collective-permute-done.15
  116.5 6.0 %collective-permute-done.16 = bf16[8,6656]{1,0:T(8,128)(2,1)S(1)} collective-permute-done((bf16[8,6656]{1,0:T(8,128)(2,1)S(1)}, bf16[8,6656]{1,0:T(8,128)(2,1)S(1)}, u32[]{:S(2)}, u32[]{:S(2)}) %collective-permute-start.16) | collective-permute-done | bytes 106528 | tf_op jit(solution)/shard_map/ppermute | solution.py:517
  122.5 0.1 collective-permute-start.19
  122.6 0.6 collective-permute-start.18
  123.2 0.9 copy.29
  124.1 0.0 collective-permute-done.18.big_other
  124.1 0.6 copy-done.5
  124.8 0.6 copy-done.4
  125.4 1.8 %final.1 = (f32[2,2,8,384]{3,2,1,0:T(8,128)}, f32[2,2,8,128]{3,2,1,0:T(8,128)}, f32[2,8,1024]{2,1,0:T(8,128)}, f32[2,32,128]{2,1,0:T(8,128)}, f32[2,128,128]{2,1...) custom-call(f32[8,2560]{1,0:T(8,128)} %copy-done.2, ...), custom_call_target="tpu_custom_call" | custom-call | tf_op jit(solution)/shard_map/final/pallas_call | solution.py:429
  (40 shorter events, 0.3 us)
Async XLA Ops:
  2.1 7.3 %collective-permute-start.2 = (bf16[1,8,2560]{2,1,0:T(8,128)(2,1)}, bf16[1,8,2560]{2,1,0:T(8,128)(2,1)S(1)}, u32[]{:S(2)}, u32[]{:S(2)}) collective-permute-start(bf16[1,8,2560]{2,1,0:T(8,128)(2,1)} %pack.1), channel_id=1, source_target_pairs={{0,12},{1,13},{2,14},{3,15},{4,8},{5,9},{6,10},{7,11},{8,4},{9,5},... | collective-permute-start | bytes 122888 | tf_op jit(solution)/shard_map/ppermute | solution.py:517
  7.1 5.1 %collective-permute-start.1 = (bf16[1,8,2560]{2,1,0:T(8,128)(2,1)}, bf16[1,8,2560]{2,1,0:T(8,128)(2,1)S(1)}, u32[]{:S(2)}, u32[]{:S(2)}) collective-permute-start(bf16[1,8,2560]{2,1,0:T(8,128)(2,1)} %pack.1), channel_id=1, source_target_pairs={{0,8},{1,9},{2,10},{3,11},{4,12},{5,13},{6,14},{7,15},{8,0},{9,1},... | collective-permute-start | bytes 122888 | tf_op jit(solution)/shard_map/ppermute | solution.py:517
  7.1 5.1 %collective-permute-start = (bf16[1,8,2560]{2,1,0:T(8,128)(2,1)}, bf16[1,8,2560]{2,1,0:T(8,128)(2,1)S(1)}, u32[]{:S(2)}, u32[]{:S(2)}) collective-permute-start(bf16[1,8,2560]{2,1,0:T(8,128)(2,1)} %pack.1), channel_id=1, source_target_pairs={{0,4},{1,5},{2,6},{3,7},{4,0},{5,1},{6,2},{7,3},{8,12},{9,13},{10,... | collective-permute-start | bytes 122888 | tf_op jit(solution)/shard_map/ppermute | solution.py:517
  13.0 9.1 %copy-start.3 = (bf16[4,8,2560]{2,1,0:T(8,128)(2,1)}, bf16[4,8,2560]{2,1,0:T(8,128)(2,1)S(1)}, u32[]{:S(2)}) copy-start(bf16[4,8,2560]{2,1,0:T(8,128)(2,1)S(1)} %pad_maximum_fusion.3.wmine0_ref) | copy-start | bytes 491524
  13.0 9.0 %collective-permute-start.5 = (bf16[4,8,2560]{2,1,0:T(8,128)(2,1)S(1)}, bf16[4,8,2560]{2,1,0:T(8,128)(2,1)S(1)}, u32[]{:S(2)}, u32[]{:S(2)}) collective-permute-start(bf16[4,8,2560]{2,1,0:T(8,128)(2,1)S(1)} %pad_maximum_fusion.3.wmine0_ref), channel_id=1, source_target_pairs={{0,3},{1,2},{2,1},{3,0},{4,7},{5,6},{6,5},{7,4},{8,11},{9,10},{10,... | collective-permute-start | bytes 491528 | tf_op jit(solution)/shard_map/ppermute | solution.py:517
  15.6 6.5 %collective-permute-start.4 = (bf16[4,8,2560]{2,1,0:T(8,128)(2,1)S(1)}, bf16[4,8,2560]{2,1,0:T(8,128)(2,1)S(1)}, u32[]{:S(2)}, u32[]{:S(2)}) collective-permute-start(bf16[4,8,2560]{2,1,0:T(8,128)(2,1)S(1)} %pad_maximum_fusion.3.wmine0_ref), channel_id=1, source_target_pairs={{0,2},{1,3},{2,0},{3,1},{4,6},{5,7},{6,4},{7,5},{8,10},{9,11},{10,... | collective-permute-start | bytes 491528 | tf_op jit(solution)/shard_map/ppermute | solution.py:517
  16.1 6.0 %collective-permute-start.3 = (bf16[4,8,2560]{2,1,0:T(8,128)(2,1)S(1)}, bf16[4,8,2560]{2,1,0:T(8,128)(2,1)S(1)}, u32[]{:S(2)}, u32[]{:S(2)}) collective-permute-start(bf16[4,8,2560]{2,1,0:T(8,128)(2,1)S(1)} %pad_maximum_fusion.3.wmine0_ref), channel_id=1, source_target_pairs={{0,1},{1,0},{2,3},{3,2},{4,5},{5,4},{6,7},{7,6},{8,9},{9,8},{10,11... | collective-permute-start | bytes 491528 | tf_op jit(solution)/shard_map/ppermute | solution.py:517
  22.0 2.3 %copy-start.6 = (bf16[4,8,2560]{2,1,0:T(8,128)(2,1)}, bf16[4,8,2560]{2,1,0:T(8,128)(2,1)S(1)}, u32[]{:S(2)}) copy-start(bf16[4,8,2560]{2,1,0:T(8,128)(2,1)S(1)} %collective-permute-done.5.wmine3_ref) | copy-start | bytes 491524
  22.0 2.2 %copy-start.7 = (bf16[4,8,2560]{2,1,0:T(8,128)(2,1)}, bf16[4,8,2560]{2,1,0:T(8,128)(2,1)S(1)}, u32[]{:S(2)}) copy-start(bf16[4,8,2560]{2,1,0:T(8,128)(2,1)S(1)} %collective-permute-done.4.wmine2_ref) | copy-start | bytes 491524
  22.1 2.2 %copy-start.8 = (bf16[4,8,2560]{2,1,0:T(8,128)(2,1)}, bf16[4,8,2560]{2,1,0:T(8,128)(2,1)S(1)}, u32[]{:S(2)}) copy-start(bf16[4,8,2560]{2,1,0:T(8,128)(2,1)S(1)} %collective-permute-done.3.wmine1_ref) | copy-start | bytes 491524
  22.1 1.4 %collective-permute-start.6 = (bf16[4,8,2560]{2,1,0:T(8,128)(2,1)S(1)}, bf16[4,8,2560]{2,1,0:T(8,128)(2,1)S(1)}, u32[]{:S(2)}, u32[]{:S(2)}) collective-permute-start(bf16[4,8,2560]{2,1,0:T(8,128)(2,1)S(1)} %pad_maximum_fusion.3.wmine0_ref), channel_id=1, source_target_pairs={{0,16},{16,0},{1,17},{17,1},{2,18},{18,2},{3,19},{19,3},{4,20},{20... | collective-permute-start | bytes 491528 | tf_op jit(solution)/shard_map/ppermute | solution.py:513
  22.1 1.6 %collective-permute-start.7 = (bf16[4,8,2560]{2,1,0:T(8,128)(2,1)S(1)}, bf16[4,8,2560]{2,1,0:T(8,128)(2,1)S(1)}, u32[]{:S(2)}, u32[]{:S(2)}) collective-permute-start(bf16[4,8,2560]{2,1,0:T(8,128)(2,1)S(1)} %collective-permute-done.3.wmine1_ref), channel_id=1, source_target_pairs={{0,16},{16,0},{1,17},{17,1},{2,18},{18,2},{3,19},{19,3},{4,20},{20... | collective-permute-start | bytes 491528 | tf_op jit(solution)/shard_map/ppermute | solution.py:513
  22.6 1.4 %collective-permute-start.8 = (bf16[4,8,2560]{2,1,0:T(8,128)(2,1)S(1)}, bf16[4,8,2560]{2,1,0:T(8,128)(2,1)S(1)}, u32[]{:S(2)}, u32[]{:S(2)}) collective-permute-start(bf16[4,8,2560]{2,1,0:T(8,128)(2,1)S(1)} %collective-permute-done.4.wmine2_ref), channel_id=1, source_target_pairs={{0,16},{16,0},{1,17},{17,1},{2,18},{18,2},{3,19},{19,3},{4,20},{20... | collective-permute-start | bytes 491528 | tf_op jit(solution)/shard_map/ppermute | solution.py:513
  22.7 1.6 %collective-permute-start.9 = (bf16[4,8,2560]{2,1,0:T(8,128)(2,1)S(1)}, bf16[4,8,2560]{2,1,0:T(8,128)(2,1)S(1)}, u32[]{:S(2)}, u32[]{:S(2)}) collective-permute-start(bf16[4,8,2560]{2,1,0:T(8,128)(2,1)S(1)} %collective-permute-done.5.wmine3_ref), channel_id=1, source_target_pairs={{0,16},{16,0},{1,17},{17,1},{2,18},{18,2},{3,19},{19,3},{4,20},{20... | collective-permute-start | bytes 491528 | tf_op jit(solution)/shard_map/ppermute | solution.py:513
  23.5 0.8 copy-start.9
  23.8 0.7 copy-start.10
  24.0 0.7 copy-start.11
  24.7 0.7 copy-start.12
  92.2 3.4 %collective-permute-start.10 = (bf16[4,4,8,2560]{3,2,1,0:T(8,128)(2,1)}, bf16[4,4,8,2560]{3,2,1,0:T(8,128)(2,1)S(1)}, u32[]{:S(2)}, u32[]{:S(2)}) collective-permute-start(bf16[4,4,8,2560]{3,2,1,0:T(8,128)(2,1)} %get-tuple-element.43), channel_id=1, source_target_pairs={{0,16},{16,0},{1,17},{17,1},{2,18},{18,2},{3,19},{19,3},{4,20},{20... | collective-permute-start | bytes 1966088 | tf_op jit(solution)/shard_map/ppermute | solution.py:513
  92.5 2.3 %collective-permute-start.11 = (f32[4,8,1024]{2,1,0:T(8,128)}, f32[4,8,1024]{2,1,0:T(8,128)S(1)}, u32[]{:S(2)}, u32[]{:S(2)}) collective-permute-start(f32[4,8,1024]{2,1,0:T(8,128)} %get-tuple-element.45), channel_id=1, source_target_pairs={{0,16},{16,0},{1,17},{17,1},{2,18},{18,2},{3,19},{19,3},{4,20},{20... | collective-permute-start | bytes 393224 | tf_op jit(solution)/shard_map/ppermute | solution.py:513
  97.0 8.5 %collective-permute-start.12 = (bf16[4,8,3584]{2,1,0:T(8,128)(2,1)S(1)}, bf16[4,8,3584]{2,1,0:T(8,128)(2,1)S(1)}, u32[]{:S(2)}, u32[]{:S(2)}) collective-permute-start(bf16[4,8,3584]{2,1,0:T(8,128)(2,1)S(1)} %get-tuple-element.92), channel_id=1, source_target_pairs={{0,1},{1,0},{2,3},{3,2},{4,5},{5,4},{6,7},{7,6},{8,9},{9,8},{10,11... | collective-permute-start | bytes 688136 | tf_op jit(solution)/shard_map/ppermute | solution.py:517
  98.6 12.4 %collective-permute-start.13 = (bf16[4,8,3584]{2,1,0:T(8,128)(2,1)S(1)}, bf16[4,8,3584]{2,1,0:T(8,128)(2,1)S(1)}, u32[]{:S(2)}, u32[]{:S(2)}) collective-permute-start(bf16[4,8,3584]{2,1,0:T(8,128)(2,1)S(1)} %get-tuple-element.93), channel_id=1, source_target_pairs={{0,2},{1,3},{2,0},{3,1},{4,6},{5,7},{6,4},{7,5},{8,10},{9,11},{10,... | collective-permute-start | bytes 688136 | tf_op jit(solution)/shard_map/ppermute | solution.py:517
  100.1 10.9 %collective-permute-start.14 = (bf16[4,8,3584]{2,1,0:T(8,128)(2,1)S(1)}, bf16[4,8,3584]{2,1,0:T(8,128)(2,1)S(1)}, u32[]{:S(2)}, u32[]{:S(2)}) collective-permute-start(bf16[4,8,3584]{2,1,0:T(8,128)(2,1)S(1)} %get-tuple-element.94), channel_id=1, source_target_pairs={{0,3},{1,2},{2,1},{3,0},{4,7},{5,6},{6,5},{7,4},{8,11},{9,10},{10,... | collective-permute-start | bytes 688136 | tf_op jit(solution)/shard_map/ppermute | solution.py:517
  111.1 12.1 %copy-start.1 = (f32[2,4,117,128]{3,2,1,0:T(8,128)S(1)}, f32[2,4,117,128]{3,2,1,0:T(8,128)}, u32[]{:S(2)}) copy-start(f32[2,4,117,128]{3,2,1,0:T(8,128)} %get-tuple-element.58) | copy-start | bytes 1437700
  111.2 5.3 %collective-permute-start.15 = (bf16[8,6656]{1,0:T(8,128)(2,1)S(1)}, bf16[8,6656]{1,0:T(8,128)(2,1)S(1)}, u32[]{:S(2)}, u32[]{:S(2)}) collective-permute-start(bf16[8,6656]{1,0:T(8,128)(2,1)S(1)} %get-tuple-element.80), channel_id=1, source_target_pairs={{0,4},{1,5},{2,6},{3,7},{4,0},{5,1},{6,2},{7,3},{8,12},{9,13},{10,... | collective-permute-start | bytes 319496 | tf_op jit(solution)/shard_map/ppermute | solution.py:517
  111.7 10.8 %collective-permute-start.16 = (bf16[8,6656]{1,0:T(8,128)(2,1)S(1)}, bf16[8,6656]{1,0:T(8,128)(2,1)S(1)}, u32[]{:S(2)}, u32[]{:S(2)}) collective-permute-start(bf16[8,6656]{1,0:T(8,128)(2,1)S(1)} %get-tuple-element.81), channel_id=1, source_target_pairs={{0,8},{1,9},{2,10},{3,11},{4,12},{5,13},{6,14},{7,15},{8,0},{9,1},... | collective-permute-start | bytes 319496 | tf_op jit(solution)/shard_map/ppermute | solution.py:517
  113.8 8.7 %collective-permute-start.17 = (bf16[8,6656]{1,0:T(8,128)(2,1)S(1)}, bf16[8,6656]{1,0:T(8,128)(2,1)S(1)}, u32[]{:S(2)}, u32[]{:S(2)}) collective-permute-start(bf16[8,6656]{1,0:T(8,128)(2,1)S(1)} %get-tuple-element.82), channel_id=1, source_target_pairs={{0,12},{1,13},{2,14},{3,15},{4,8},{5,9},{6,10},{7,11},{8,4},{9,5},... | collective-permute-start | bytes 319496 | tf_op jit(solution)/shard_map/ppermute | solution.py:517
  122.5 1.6 %copy-start = (f32[8,4096]{1,0:T(8,128)}, f32[8,4096]{1,0:T(8,128)S(1)}, u32[]{:S(2)}) copy-start(f32[8,4096]{1,0:T(8,128)S(1)} %add_add_fusion.small_mine) | copy-start | bytes 393220
  122.5 1.6 %collective-permute-start.19 = (f32[8,4096]{1,0:T(8,128)S(1)}, f32[8,4096]{1,0:T(8,128)S(1)}, u32[]{:S(2)}, u32[]{:S(2)}) collective-permute-start(f32[8,4096]{1,0:T(8,128)S(1)} %add_add_fusion.small_mine), channel_id=1, source_target_pairs={{0,16},{16,0},{1,17},{17,1},{2,18},{18,2},{3,19},{19,3},{4,20},{20... | collective-permute-start | bytes 393224 | tf_op jit(solution)/shard_map/ppermute | solution.py:513
  122.6 1.5 %copy-start.2 = (f32[8,2560]{1,0:T(8,128)}, f32[8,2560]{1,0:T(8,128)S(1)}, u32[]{:S(2)}) copy-start(f32[8,2560]{1,0:T(8,128)S(1)} %fusion.2.big_mine) | copy-start | bytes 245764
  122.6 1.5 %collective-permute-start.18 = (f32[8,2560]{1,0:T(8,128)S(1)}, f32[8,2560]{1,0:T(8,128)S(1)}, u32[]{:S(2)}, u32[]{:S(2)}) collective-permute-start(f32[8,2560]{1,0:T(8,128)S(1)} %fusion.2.big_mine), channel_id=1, source_target_pairs={{0,16},{16,0},{1,17},{17,1},{2,18},{18,2},{3,19},{19,3},{4,20},{20... | collective-permute-start | bytes 245768 | tf_op jit(solution)/shard_map/ppermute | solution.py:513
  124.1 0.6 copy-start.5
  124.8 0.6 copy-start.4
